TPU v7x, 32 devices: a whole 2x2x4 slice. The times are simulated.
32 devices in a mesh: rows: 8 (over z, x), tm: 4 (over y, core).
Axes of the slice: x: 2, y: 2, z: 4, core: 2. Of those that a mesh axis runs over, the one named last changes fastest.
Arguments:
- frames: bfloat16 [16, 16, 32, 256], P('tm', 'rows'), may hold values from -45 to 45, as said below
- norm_gain: float32 [256], replicated, may hold values from 0.1 to 1.9
- conv_weight: bfloat16 [3, 3, 3, 256, 256], replicated, may hold values from -0.078125 to 0.078125
- conv_bias: float32 [256], replicated, may hold values from -3 to 3
- latent_grad: bfloat16 [16, 8, 16, 256], P('tm', None, 'rows'), may hold values from -6 to 6
Outputs:
- latent: bfloat16 [16, 8, 16, 256], P('tm', None, 'rows')
- frames_grad: bfloat16 [16, 16, 32, 256], P('tm', 'rows')
- weight_grad: float32 [3, 3, 3, 256, 256], P(None, None, None, 'tm')
- gain_grad: float32 [256], P('tm')
- bias_grad: float32 [256], P('tm')
Inputs may be any that keep to these rules, and one draw needn't show every extreme that they name: `frames`: features of the clip.
All inputs are finite; a program needn't handle non-finite values.
Results may differ from a plain program's by a relative error of at most 0.0045.
Values may be sent and summed in bfloat16 or wider, within the bound.
No kernel may reach another device: no remote copies, remote signals or barrier semaphores. Data moves between devices by JAX's collectives and lax.ppermute only.
A program may use at most 128 MiB of HBM per device.

v0:
```python
import functools

import jax
import jax.numpy as jnp
from jax import lax
from jax.experimental import pallas as pl
from jax.experimental.pallas import tpu as pltpu
from jax.sharding import PartitionSpec as P

EPS = 1e-06
TAPS = [(a, b, c) for a in range(3) for b in range(3) for c in range(3)]
VMEM_LIMIT = 48 * 1024 * 1024


def shifted(value, axis, steps):
    count = lax.axis_size(axis)
    leading, last = (max(0, -steps), min(count, count - steps))
    return lax.ppermute(value, axis, [(source, source + steps) for source in range(leading, last)])


def contract_out(grad_piece, weight_tap):
    return lax.dot_general(
        grad_piece, weight_tap, (((1,), (1,)), ((), ())), preferred_element_type=jnp.float32
    )


def reduced_form(frames, norm_gain, conv_weight, conv_bias, latent_grad):
    signal = frames.astype(jnp.float32)
    inv_rms = lax.rsqrt(jnp.mean(signal * signal, axis=-1, keepdims=True) + EPS)
    unit = signal * inv_rms
    normed = unit * norm_gain
    hidden = jax.nn.silu(normed).astype(jnp.bfloat16)
    frame_count, row_count, col_count, channels = hidden.shape
    lat_rows = row_count // 2
    lat_cols = col_count // 2
    cached = shifted(hidden[frame_count - 2 :], "tm", 1)
    stacked = jnp.concatenate([cached, hidden], axis=0)
    row_under = shifted(stacked[:, :1], "rows", -1)
    extended = jnp.concatenate([stacked, row_under], axis=1)
    extended = jnp.pad(extended, ((0, 0), (0, 0), (0, 1), (0, 0)))
    grad_rows = lax.all_to_all(latent_grad, "rows", split_axis=1, concat_axis=2, tiled=True)
    grad_flat = grad_rows.reshape(-1, channels)
    running = jnp.zeros((frame_count * lat_rows * lat_cols, channels), jnp.float32)
    blocks = []
    for tap_t, tap_r, tap_c in TAPS:
        window_piece = extended[
            tap_t : tap_t + frame_count,
            tap_r : tap_r + 2 * lat_rows : 2,
            tap_c : tap_c + 2 * lat_cols : 2,
        ]
        window_piece = window_piece.reshape(-1, channels)
        running = running + jnp.dot(
            window_piece, conv_weight[tap_t, tap_r, tap_c], preferred_element_type=jnp.float32
        )
        blocks.append(
            lax.dot_general(
                window_piece,
                grad_flat,
                (((0,), (0,)), ((), ())),
                preferred_element_type=jnp.float32,
            )
        )
    latent_rows = (
        (running + conv_bias)
        .reshape(frame_count, lat_rows, lat_cols, channels)
        .astype(jnp.bfloat16)
    )
    latent = lax.all_to_all(latent_rows, "rows", split_axis=2, concat_axis=1, tiled=True)
    weight_local = jnp.stack(blocks).reshape(3, 3, 3, channels, channels)
    bias_local = jnp.sum(grad_flat.astype(jnp.float32), axis=0)
    following = shifted(grad_rows[:2], "tm", -1)
    grad_ext = jnp.concatenate([grad_rows, following], axis=0)
    above_row = shifted(grad_ext, "rows", 1)
    grad_ext = jnp.concatenate([above_row, grad_ext], axis=1)
    grad_ext = jnp.pad(grad_ext, ((0, 0), (0, 0), (1, 0), (0, 0)))
    parity_sums = {}
    for tap_t, tap_r, tap_c in TAPS:
        row_start = 1 - tap_r // 2
        col_start = 1 - tap_c // 2
        grad_piece = grad_ext[
            2 - tap_t : 2 - tap_t + frame_count,
            row_start : row_start + lat_rows,
            col_start : col_start + lat_cols,
        ]
        term = contract_out(grad_piece.reshape(-1, channels), conv_weight[tap_t, tap_r, tap_c])
        label = (tap_r % 2, tap_c % 2)
        parity_sums[label] = parity_sums[label] + term if label in parity_sums else term
    shaped = {}
    for label in parity_sums:
        shaped[label] = parity_sums[label].reshape(frame_count, lat_rows, lat_cols, channels)
    even_rows = jnp.stack([shaped[0, 0], shaped[0, 1]], axis=3)
    odd_rows = jnp.stack([shaped[1, 0], shaped[1, 1]], axis=3)
    hidden_grad = jnp.stack([even_rows, odd_rows], axis=2).reshape(
        frame_count, row_count, col_count, channels
    )
    sigma = jax.nn.sigmoid(normed)
    normed_grad = hidden_grad * sigma * (1.0 + normed * (1.0 - sigma))
    gain_local = jnp.sum(normed_grad * unit, axis=(0, 1, 2))
    unit_grad = normed_grad * norm_gain
    frames_grad = inv_rms * (unit_grad - unit * jnp.mean(unit_grad * unit, axis=-1, keepdims=True))
    totals = lax.psum((weight_local, gain_local, bias_local), "rows")
    weight_grad, gain_grad, bias_grad = (
        lax.psum_scatter(totals[0], "tm", scatter_dimension=3, tiled=True),
        lax.psum_scatter(totals[1], "tm", scatter_dimension=0, tiled=True),
        lax.psum_scatter(totals[2], "tm", scatter_dimension=0, tiled=True),
    )
    return (latent, frames_grad.astype(jnp.bfloat16), weight_grad, gain_grad, bias_grad)


def partners(value, axis, bits):
    count = lax.axis_size(axis)
    return lax.ppermute(value, axis, [(source, source ^ bits) for source in range(count)])


def exchanged(value, axis):
    blocks = [value]
    for k in range(1, lax.axis_size(axis)):
        if k % 2 == 0:
            blocks.append(partners(value, axis, k))
        else:
            blocks.append(partners(blocks[k - 1], axis, 1))
    return blocks


def mm(left, right):
    return jnp.dot(left, right, preferred_element_type=jnp.float32)


def mm_t(left, right):
    return lax.dot_general(
        left, right, (((1,), (1,)), ((), ())), preferred_element_type=jnp.float32
    )


def normalised(frames, gain):
    signal = frames.astype(jnp.float32)
    inv_rms = lax.rsqrt(jnp.mean(signal * signal, axis=-1, keepdims=True) + EPS)
    unit = signal * inv_rms
    return inv_rms, unit, unit * gain


def hidden_kernel(F, J, T, place, frames, gain, planes, cached, under, corner, *rest):
    sends, tmp = rest[:T], rest[T]
    channels = frames.shape[1]
    part = channels // T
    _, _, normed = normalised(frames[...], gain[...])
    value = normed / (1.0 + jnp.exp(-normed))
    tmp[0] = value[:, : channels // 2]
    tmp[1] = value[:, channels // 2 :]
    block = place[1]
    for rp in range(2):
        pair = []
        for cp in range(2):
            rows = [
                jnp.concatenate(
                    [
                        tmp[half, pl.ds((t * 2 + rp) * 2 * J + cp, J, stride=2), :]
                        for half in range(2)
                    ],
                    axis=1,
                )
                for t in range(F)
            ]
            plane = jnp.concatenate(rows, axis=0)
            pair.append(plane)
            plane = plane.astype(jnp.bfloat16)
            planes[rp, cp] = plane
            cached[rp, cp] = plane[(F - 2) * J :]
            if rp == 0:
                under[cp] = plane
                corner[cp] = plane[(F - 2) * J :]
        pieces = [
            jnp.concatenate([p[:, d * part : (d + 1) * part] for p in pair], axis=1)
            for d in range(T)
        ]
        for k in range(T):
            chosen = pieces[0]
            for d in range(1, T):
                chosen = jnp.where(block == d ^ k, pieces[d], chosen)
            sends[k][rp] = chosen.astype(jnp.bfloat16)


def permutation(shape, meet):
    row = lax.broadcasted_iota(jnp.int32, shape, 0)
    col = lax.broadcasted_iota(jnp.int32, shape, 1)
    return jnp.where(meet(row, col), 1.0, 0.0).astype(jnp.bfloat16)


def latent_kernel(F, J, R, planes, cached, under, corner, weight, bias, out, ext):
    rows = (F + 2) * J
    last = lax.broadcasted_iota(jnp.int32, (rows, 1), 0) % J == J - 1
    for b in range(3):
        for cp in range(2):
            before, now = (corner[cp], under[cp]) if b == 2 else (cached[b, cp], planes[b, cp])
            full = jnp.concatenate([before, now], axis=0)
            ext[b, cp] = full
            if cp == 0:
                moved = pltpu.roll(full.astype(jnp.float32), rows - 1, 0)
                ext[b, 2] = jnp.where(last, 0.0, moved).astype(jnp.bfloat16)
    total = jnp.zeros(out.shape, jnp.float32) + bias[...]
    for n, (a, b, c) in enumerate(TAPS):
        total = total + mm(ext[b, c, a * J : (a + F) * J, :], weight[n])
    jl = J // R
    order = permutation(
        (F * J, F * J),
        lambda o, s: (o // jl % F == s // J) & (o // (F * jl) * jl + o % jl == s % J),
    )
    out[...] = mm(order, total.astype(jnp.bfloat16)).astype(jnp.bfloat16)


def shard_rows(source, start, count, R):
    return jnp.concatenate([source[s, start : start + count, :] for s in range(R)], axis=0)


def shard_order(J, R, rows, first, moved):
    jl = J // R
    return permutation(
        (rows * 2 * J, 2 * R * J),
        lambda o, s: (o // (2 * J) + first == s // jl % R)
        & (o // J % 2 == s // (jl * R) % 2)
        & (o % J == s // (2 * jl * R) * jl + s % jl + moved),
    )


def frames_kernel(
    F, J, R, place, gathered, following, weight, frames, gain, frames_grad, gain_part, near, tmp
):
    channels = frames.shape[1]
    pair_rows = 2 * R * (J // R)
    orders = [shard_order(J, R, 2, place[0] - 1, moved) for moved in range(2)]
    for pair in range(F // 2 + 1):
        if pair < F // 2:
            source = shard_rows(gathered, pair * pair_rows, pair_rows, R)
        else:
            source = shard_rows(following, 0, pair_rows, R)
        for moved in range(2):
            value = mm(orders[moved], source).astype(jnp.bfloat16)
            for i in range(2):
                near[moved, i, pair * 2 * J : (pair + 1) * 2 * J, :] = value[
                    i * 2 * J : (i + 1) * 2 * J
                ]
    sums = {}
    for n, (a, b, c) in enumerate(TAPS):
        piece = near[c // 2, 1 - b // 2, (2 - a) * J : (2 - a + F) * J, :]
        term = mm_t(piece, weight[n])
        key = (b % 2, c % 2)
        sums[key] = sums[key] + term if key in sums else term
    for (rp, cp), value in sums.items():
        for t in range(F):
            for half in range(2):
                lanes = slice(half * channels // 2, (half + 1) * channels // 2)
                tmp[half, pl.ds((t * 2 + rp) * 2 * J + cp, J, stride=2), :] = value[
                    t * J : (t + 1) * J, lanes
                ]
    hidden_grad = jnp.concatenate([tmp[0], tmp[1]], axis=1)
    inv_rms, unit, normed = normalised(frames[...], gain[...])
    sigma = 1.0 / (1.0 + jnp.exp(-normed))
    normed_grad = hidden_grad * sigma * (1.0 + normed * (1.0 - sigma))
    gain_part[...] = jnp.sum(normed_grad * unit, axis=0, keepdims=True)
    unit_grad = normed_grad * gain[...]
    mean = jnp.mean(unit_grad * unit, axis=-1, keepdims=True)
    frames_grad[...] = (inv_rms * (unit_grad - unit * mean)).astype(jnp.bfloat16)


def weight_kernel(F, J, R, T, part, place, *refs):
    gathered, hidden = refs[:T], refs[T : T + R]
    out, bias_sum, grads, even, odd = refs[T + R :]
    channels = gathered[0].shape[-1]
    span = F * J
    depth = T * span
    lanes = 2 * part
    row, block = place[0], place[1]
    pair_rows = 2 * R * (J // R)
    grads[:, :, depth:, :] = jnp.zeros((2, R, 2 * J, channels), jnp.bfloat16)
    even[:, R * depth :] = jnp.zeros((lanes, depth), jnp.bfloat16)
    orders = [shard_order(J, R, R, 0, moved) for moved in range(2)]
    total = jnp.zeros((1, channels), jnp.float32)
    for k in range(T):
        for pair in range(F // 2):
            source = shard_rows(gathered[k], pair * pair_rows, pair_rows, R)
            total = total + jnp.sum(source.astype(jnp.float32), axis=0, keepdims=True)
            at = pl.multiple_of((block ^ k) * span + pair * 2 * J, 16)
            for moved in range(2):
                value = mm(orders[moved], source).astype(jnp.bfloat16)
                for i in range(R):
                    grads[moved, i, pl.ds(at, 2 * J), :] = value[i * 2 * J : (i + 1) * 2 * J]
    bias_sum[...] = total
    for k in range(R):
        at = pl.multiple_of((row ^ k) * depth, 128)
        for rp, turned in ((0, even), (1, odd)):
            turned[:, pl.ds(at, depth)] = hidden[k][rp].T
    for a in range(3):
        start = (2 - a) * J
        for moved in range(2):
            right = grads[moved, :, start : start + depth, :].reshape(R * depth, channels)
            size = part if moved else lanes
            left = jnp.concatenate(
                [
                    even[:size, : R * depth],
                    odd[:size, :],
                    even[:size, depth:],
                ],
                axis=0,
            )
            value = mm(left, right)
            for b in range(3):
                if moved:
                    out[(a * 3 + b) * 3 + 2] = value[b * part : (b + 1) * part]
                else:
                    for cp in range(2):
                        at = b * lanes + cp * part
                        out[(a * 3 + b) * 3 + cp] = value[at : at + part]


def call(kernel, outs, scratch, flops, moved, smem=0, operands=0):
    vmem = pl.BlockSpec(memory_space=pltpu.VMEM)
    specs = [pl.BlockSpec(memory_space=pltpu.SMEM)] * smem + [vmem] * (operands - smem)
    return pl.pallas_call(
        kernel,
        out_shape=[jax.ShapeDtypeStruct(s, d) for s, d in outs],
        in_specs=specs,
        out_specs=[vmem] * len(outs),
        scratch_shapes=[pltpu.VMEM(s, d) for s, d in scratch],
        compiler_params=pltpu.CompilerParams(vmem_limit_bytes=VMEM_LIMIT),
        cost_estimate=pl.CostEstimate(flops=flops, bytes_accessed=moved, transcendentals=0),
    )


def gathered_form(frames, norm_gain, conv_weight, conv_bias, latent_grad):
    bf16, f32 = jnp.bfloat16, jnp.float32
    F, row_count, col_count, C = frames.shape
    R, T = lax.axis_size("rows"), lax.axis_size("tm")
    J = col_count // 2
    span = F * J
    part = C // T
    gain = norm_gain.reshape(1, C)
    bias = conv_bias.reshape(1, C)
    flat = frames.reshape(-1, C)
    weight = conv_weight.reshape(27, C, C)
    place = jnp.stack([lax.axis_index("rows"), lax.axis_index("tm")]).astype(jnp.int32)

    grad_rows = lax.all_gather(latent_grad.reshape(-1, C), "rows", axis=0)

    planes, cached, under, corner, *sends = call(
        functools.partial(hidden_kernel, F, J, T),
        [
            ((2, 2, span, C), bf16),
            ((2, 2, 2 * J, C), bf16),
            ((2, span, C), bf16),
            ((2, 2 * J, C), bf16),
        ]
        + [((2, span, 2 * part), bf16)] * T,
        [((2, 4 * span, C // 2), f32)],
        10 * 4 * span * C, 16 * span * C, smem=1, operands=3,
    )(place, flat, gain)

    parts = [sends[0]] + [partners(sends[k], "tm", k) for k in range(1, T)]
    block = lax.axis_index("tm")
    ordered = jnp.stack(parts)
    ordered = jnp.stack(
        [lax.dynamic_index_in_dim(ordered, block ^ t, keepdims=False) for t in range(T)], axis=1
    )
    hidden_all = exchanged(ordered.reshape(2, T * span, 2 * part), "rows")

    cached = shifted(cached, "tm", 1)
    under = shifted(under, "rows", -1)
    steps = [
        ((r + 1) * T + t, r * T + t + 1) for r in range(R - 1) for t in range(T - 1)
    ]
    corner = lax.ppermute(corner, ("rows", "tm"), steps)

    (latent_send,) = call(
        functools.partial(latent_kernel, F, J, R),
        [((span, C), bf16)],
        [((3, 3, (F + 2) * J, C), bf16)],
        2 * 27 * span * C * C, 2 * 27 * C * C, operands=6,
    )(planes, cached, under, corner, weight, bias)
    latent = lax.all_to_all(
        latent_send.reshape(R, span // R, C), "rows", split_axis=0, concat_axis=0, tiled=True
    )
    latent = latent.reshape(R, F, J // R, C).transpose(1, 0, 2, 3)

    following = shifted(grad_rows[:, : 2 * J], "tm", -1)
    grad_all = exchanged(grad_rows, "tm")
    frames_grad, gain_part = call(
        functools.partial(frames_kernel, F, J, R),
        [((4 * span, C), bf16), ((1, C), f32)],
        [((2, 2, (F + 2) * J, C), bf16), ((2, 4 * span, C // 2), f32)],
        2 * 27 * span * C * C, 2 * 27 * C * C, smem=1, operands=6,
    )(place, grad_rows, following, weight, flat, gain)

    weight_grad, bias_sum = call(
        functools.partial(weight_kernel, F, J, R, T, part),
        [((27, part, C), f32), ((1, C), f32)],
        [
            ((2, R, (F * T + 2) * J, C), bf16),
            ((2 * part, (R + 1) * T * span), bf16),
            ((2 * part, R * T * span), bf16),
        ],
        2 * 27 * R * T * span * part * C, 8 * 27 * part * C, smem=1, operands=1 + T + R,
    )(place, *grad_all, *hidden_all)

    gain_grad = lax.psum(gain_part, ("rows", "tm"))
    start = lax.axis_index("tm") * part
    gain_grad = lax.dynamic_slice(gain_grad.reshape(C), (start,), (part,))
    bias_grad = lax.dynamic_slice(bias_sum.reshape(C), (start,), (part,))
    return (
        latent,
        frames_grad.reshape(frames.shape),
        weight_grad.reshape(3, 3, 3, part, C),
        gain_grad,
        bias_grad,
    )


def on_device(frames, norm_gain, conv_weight, conv_bias, latent_grad):
    rows, shares = lax.axis_size("rows"), lax.axis_size("tm")
    operand_bytes = 2 * rows * shares * (frames.size // shares + latent_grad.size)
    result_bytes = 4 * conv_weight.size
    powers = (rows & (rows - 1)) == 0 and (shares & (shares - 1)) == 0
    if powers and frames.shape[1] == 2 and operand_bytes <= result_bytes:
        form = gathered_form
    else:
        form = reduced_form
    return form(frames, norm_gain, conv_weight, conv_bias, latent_grad)


def solution(mesh):
    placed = (P("tm", "rows", None, None), P(), P(), P(), P("tm", None, "rows", None))
    return jax.shard_map(
        on_device,
        mesh=mesh,
        in_specs=placed,
        out_specs=(
            P("tm", None, "rows", None),
            P("tm", "rows", None, None),
            P(None, None, None, "tm", None),
            P("tm"),
            P("tm"),
        ),
        check_vma=False,
    )
```

profile of v0, /device:TPU:0, one launch (start us, length us, event | category | flops | bytes accessed | tf_op | source)
XLA Modules:
  0.0 137.2 jit_solution(6437950525967502894)
XLA Ops:
  0.6 0.0 copy-start.10
  0.6 0.1 pad_add_fusion.place
  0.7 0.9 copy-done.2
  1.6 0.7 copy-done.9
  2.3 0.8 shard_map.92
  3.2 0.0 copy-start.7
  3.2 0.6 copy-done.7
  3.8 0.5 collective-permute-start.7
  4.3 2.5 %collective-permute-start.8 = (bf16[2,64,128]{2,1,0:T(8,128)(2,1)S(1)}, bf16[2,64,128]{2,1,0:T(8,128)(2,1)S(1)}, u32[]{:S(2)}, u32[]{:S(2)}) collective-permute-start(bf16[2,64,128]{2,1,0:T(8,128)(2,1)S(1)} %get-tuple-element.24), channel_id=1, source_target_pairs={{0,2},{1,3},{2,0},{3,1},{4,6},{5,7},{6,4},{7,5},{8,10},{9,11},{10,... | collective-permute-start | bytes 98312 | tf_op jit(solution)/shard_map/ppermute | solution.py:112
  6.8 0.1 collective-permute-start.9
  6.9 0.8 all_gather_reshape.3
  7.7 33.3 %all_gather.3.gathered.refs_0_ = bf16[8,64,256]{2,1,0:T(8,128)(2,1)} all-gather(bf16[1,64,256]{2,1,0:T(8,128)(2,1)S(1)} %all_gather_reshape.3), channel_id=1, replica_groups=mesh['rows'=8,'tm'=4] {'rows'}, dimensions={0}, use_global_device_ids=true | all-gather | bytes 294912 | tf_op jit(solution)/shard_map/all_gather | solution.py:342
  41.0 1.5 %collective-permute-start.5 = (bf16[8,64,256]{2,1,0:T(8,128)(2,1)}, bf16[8,64,256]{2,1,0:T(8,128)(2,1)}, u32[]{:S(2)}, u32[]{:S(2)}) collective-permute-start(bf16[8,64,256]{2,1,0:T(8,128)(2,1)} %all_gather.3.gathered.refs_0_), channel_id=1, source_target_pairs={{0,2},{1,3},{2,0},{3,1},{4,6},{5,7},{6,4},{7,5},{8,10},{9,11},{10,... | collective-permute-start | bytes 786440 | tf_op jit(solution)/shard_map/ppermute | solution.py:112
  42.5 0.9 slice.4
  43.5 1.3 collective-permute-start.3
  44.8 0.0 collective-permute-done.7
  44.8 0.0 collective-permute-done.8
  44.8 0.0 collective-permute-done.9
  44.9 0.7 pad_maximum_fusion.1
  45.5 0.6 collective-permute-start.15
  46.1 0.7 collective-permute-start.2
  46.8 3.4 %collective-permute-start = (bf16[2,2,32,256]{3,2,1,0:T(8,128)(2,1)S(1)}, bf16[2,2,32,256]{3,2,1,0:T(8,128)(2,1)S(1)}, u32[]{:S(2)}, u32[]{:S(2)}) collective-permute-start(bf16[2,2,32,256]{3,2,1,0:T(8,128)(2,1)S(1)} %get-tuple-element.18), channel_id=1, source_target_pairs={{0,1},{1,2},{2,3},{4,5},{5,6},{6,7},{8,9},{9,10},{10,11},{12,13},{... | collective-permute-start | bytes 196616 | tf_op jit(solution)/shard_map/ppermute | solution.py:18
  50.2 0.0 collective-permute-done.2.corner
  50.2 1.3 collective-permute-start.1
  51.5 0.0 collective-permute-done.cached
  51.5 4.7 %collective-permute-start.13 = (bf16[2,256,128]{2,1,0:T(8,128)(2,1)}, bf16[2,256,128]{2,1,0:T(8,128)(2,1)}, u32[]{:S(2)}, u32[]{:S(2)}) collective-permute-start(bf16[2,256,128]{2,1,0:T(8,128)(2,1)} %bitcast.18.refs_4_), channel_id=1, source_target_pairs={{0,16},{4,20},{8,24},{12,28},{16,0},{20,4},{24,8},{28,12},{1,17},{... | collective-permute-start | bytes 393224 | tf_op jit(solution)/shard_map/ppermute | solution.py:112
  56.2 3.1 %collective-permute-done.1.under = bf16[2,64,256]{2,1,0:T(8,128)(2,1)S(1)} collective-permute-done((bf16[2,64,256]{2,1,0:T(8,128)(2,1)S(1)}, bf16[2,64,256]{2,1,0:T(8,128)(2,1)S(1)}, u32[]{:S(2)}, u32[]{:S(2)}) %collective-permute-start.1) | collective-permute-done | bytes 65568 | tf_op jit(solution)/shard_map/ppermute | solution.py:18
  59.3 3.4 %collective-permute-start.11 = (bf16[2,256,128]{2,1,0:T(8,128)(2,1)}, bf16[2,256,128]{2,1,0:T(8,128)(2,1)}, u32[]{:S(2)}, u32[]{:S(2)}) collective-permute-start(bf16[2,256,128]{2,1,0:T(8,128)(2,1)} %bitcast.18.refs_4_), channel_id=1, source_target_pairs={{0,8},{4,12},{8,0},{12,4},{16,24},{20,28},{24,16},{28,20},{1,9},{5... | collective-permute-start | bytes 393224 | tf_op jit(solution)/shard_map/ppermute | solution.py:112
  62.7 0.0 collective-permute-done.3.following
  62.7 0.7 copy-done.5
  63.4 1.0 collective-permute-start.10
  64.3 0.0 collective-permute-done.15.refs_10_
  64.3 0.2 collective-permute-start.4
  64.5 0.0 collective-permute-done.5.refs_2_
  64.5 0.3 collective-permute-start.6
  64.9 2.0 %copy-done = bf16[3,3,3,256,256]{4,3,2,1,0:T(8,128)(2,1)S(1)} copy-done((bf16[3,3,3,256,256]{4,3,2,1,0:T(8,128)(2,1)S(1)}, bf16[3,3,3,256,256]{4,3,2,1,0:T(8,128)(2,1)}, u32[]{:S(2)}) %copy-start) | copy-done | bytes 3538968
  66.9 0.9 copy-done.8
  67.8 0.7 copy-done.11
  68.4 0.9 shard_map.93
  69.3 0.0 copy-start.4
  69.3 0.6 copy-done.4
  69.9 4.0 %all-to-all-start = ((bf16[8,8,256]{2,1,0:T(8,128)(2,1)}), bf16[8,8,256]{2,1,0:T(8,128)(2,1)}, u32[]{:S(2)}, u32[]{:S(2)}) async-start(bf16[8,8,256]{2,1,0:T(8,128)(2,1)} %bitcast.33), calls=%async_computation | async-start | bytes 65536 | tf_op jit(solution)/shard_map/all_to_all | solution.py:378
  73.9 6.7 %all-to-all-done = bf16[8,8,256]{2,1,0:T(8,128)(2,1)} async-done(((bf16[8,8,256]{2,1,0:T(8,128)(2,1)}), bf16[8,8,256]{2,1,0:T(8,128)(2,1)}, u32[]{:S(2)}, u32[]{:S(2)}) %all-to-all-start) | async-done | bytes 32800 | tf_op jit(solution)/shard_map/all_to_all | solution.py:378
  80.6 0.8 copy.12
  81.4 0.6 copy.13
  82.0 0.0 collective-permute-done.13.refs_8_
  82.0 0.5 collective-permute-start.16
  82.5 0.0 collective-permute-done.11.refs_6_
  82.5 1.6 %collective-permute-start.14 = (bf16[2,256,128]{2,1,0:T(8,128)(2,1)}, bf16[2,256,128]{2,1,0:T(8,128)(2,1)}, u32[]{:S(2)}, u32[]{:S(2)}) collective-permute-start(bf16[2,256,128]{2,1,0:T(8,128)(2,1)} %collective-permute-done.13.refs_8_), channel_id=1, source_target_pairs={{0,4},{4,0},{8,12},{12,8},{16,20},{20,16},{24,28},{28,24},{1,5},{5... | collective-permute-start | bytes 393224 | tf_op jit(solution)/shard_map/ppermute | solution.py:112
  84.1 0.0 collective-permute-done.10.refs_5_
  84.1 0.5 collective-permute-start.12
  84.5 0.0 copy-done.10
  84.6 0.9 copy-done.3
  85.5 0.9 copy-done.6
  86.4 3.1 %shard_map.94 = (bf16[256,256]{1,0:T(8,128)(2,1)}, f32[1,256]{1,0:T(1,128)S(1)}) custom-call(s32[2]{0:T(128)S(1)} %pad_add_fusion.place, bf16[8,64,256]{2,1,0:T(8,128)(2,1)} %all_gather.3.gathered.refs_0_, bf16[8,32,256]{2,1,0:T(8,128)(2,1)S(1)} %copy-done.6, bf16[27,256,256]{2,1,0:T(8,128)(2,1)S(1)} %bitcast.30, bf16[256,256]{1,0:T(8,128)(2,1)S(1)} %bitcast.32, ...), custom_call_target="tpu_custom_call" | custom-call | flops 226492416 | bytes 3538944 | tf_op jit(solution)/shard_map/pallas_call | solution.py:385
  89.5 41.1 %psum.7 = f32[1,256]{1,0:T(1,128)S(1)} all-reduce(f32[1,256]{1,0:T(1,128)S(1)} %get-tuple-element.27), channel_id=1, replica_groups=mesh['rows'=8,'tm'=4] {'rows','tm'}, use_global_device_ids=true, to_apply=%region_0.1 | all-reduce | flops 256 | bytes 2048 | tf_op jit(solution)/shard_map/psum | solution.py:403
  130.5 0.6 fusion
  131.1 0.0 collective-permute-done.4.refs_1_
  131.1 0.0 collective-permute-done.16.refs_11_
  131.1 0.0 collective-permute-done.14.refs_9_
  131.1 0.0 collective-permute-done.12.refs_7_
  131.1 0.0 collective-permute-done.6.refs_3_
  131.1 5.5 %shard_map.95 = (f32[27,64,256]{2,1,0:T(8,128)}, f32[1,256]{1,0:T(1,128)S(1)}) custom-call(s32[2]{0:T(128)S(1)} %pad_add_fusion.place, bf16[8,64,256]{2,1,0:T(8,128)(2,1)} %all_gather.3.gathered.refs_0_, bf16[8,64,256]{2,1,0:T(8,128)(2,1)} %collective-permute-done.4.refs_1_, bf16[8,64,256]{2,1,0:T(8,128)(2,1)} %collective-permute-done.5.refs_2_, ...), custom_call_target="tpu_custom_call" | custom-call | flops 1811939328 | bytes 3538944 | tf_op jit(solution)/shard_map/pallas_call | solution.py:392
  136.7 0.6 fusion.1
  (12 shorter events, 0.1 us)
Async XLA Ops:
  0.6 83.9 %copy-start.10 = (f32[256]{0:T(256)S(1)}, f32[256]{0:T(256)}, u32[]{:S(2)}) copy-start(f32[256]{0:T(256)} %param.6) | copy-start | bytes 3076
  0.7 0.9 copy-start.2
  1.6 0.7 copy-start.9
  3.2 0.7 copy-start.7
  3.8 41.0 %collective-permute-start.7 = (bf16[2,64,128]{2,1,0:T(8,128)(2,1)S(1)}, bf16[2,64,128]{2,1,0:T(8,128)(2,1)S(1)}, u32[]{:S(2)}, u32[]{:S(2)}) collective-permute-start(bf16[2,64,128]{2,1,0:T(8,128)(2,1)S(1)} %get-tuple-element.23), channel_id=1, source_target_pairs={{0,1},{1,0},{2,3},{3,2},{4,5},{5,4},{6,7},{7,6},{8,9},{9,8},{10,11... | collective-permute-start | bytes 98312 | tf_op jit(solution)/shard_map/ppermute | solution.py:112
  4.3 40.5 %collective-permute-start.8 = (bf16[2,64,128]{2,1,0:T(8,128)(2,1)S(1)}, bf16[2,64,128]{2,1,0:T(8,128)(2,1)S(1)}, u32[]{:S(2)}, u32[]{:S(2)}) collective-permute-start(bf16[2,64,128]{2,1,0:T(8,128)(2,1)S(1)} %get-tuple-element.24), channel_id=1, source_target_pairs={{0,2},{1,3},{2,0},{3,1},{4,6},{5,7},{6,4},{7,5},{8,10},{9,11},{10,... | collective-permute-start | bytes 98312 | tf_op jit(solution)/shard_map/ppermute | solution.py:112
  6.8 38.0 %collective-permute-start.9 = (bf16[2,64,128]{2,1,0:T(8,128)(2,1)S(1)}, bf16[2,64,128]{2,1,0:T(8,128)(2,1)S(1)}, u32[]{:S(2)}, u32[]{:S(2)}) collective-permute-start(bf16[2,64,128]{2,1,0:T(8,128)(2,1)S(1)} %get-tuple-element.25), channel_id=1, source_target_pairs={{0,3},{1,2},{2,1},{3,0},{4,7},{5,6},{6,5},{7,4},{8,11},{9,10},{10,... | collective-permute-start | bytes 98312 | tf_op jit(solution)/shard_map/ppermute | solution.py:112
  41.0 23.5 %collective-permute-start.5 = (bf16[8,64,256]{2,1,0:T(8,128)(2,1)}, bf16[8,64,256]{2,1,0:T(8,128)(2,1)}, u32[]{:S(2)}, u32[]{:S(2)}) collective-permute-start(bf16[8,64,256]{2,1,0:T(8,128)(2,1)} %all_gather.3.gathered.refs_0_), channel_id=1, source_target_pairs={{0,2},{1,3},{2,0},{3,1},{4,6},{5,7},{6,4},{7,5},{8,10},{9,11},{10,... | collective-permute-start | bytes 786440 | tf_op jit(solution)/shard_map/ppermute | solution.py:112
  43.5 19.3 %collective-permute-start.3 = (bf16[8,32,256]{2,1,0:T(8,128)(2,1)S(1)}, bf16[8,32,256]{2,1,0:T(8,128)(2,1)S(1)}, u32[]{:S(2)}, u32[]{:S(2)}) collective-permute-start(bf16[8,32,256]{2,1,0:T(8,128)(2,1)S(1)} %slice.4), channel_id=1, source_target_pairs={{1,0},{2,1},{3,2},{5,4},{6,5},{7,6},{9,8},{10,9},{11,10},{13,12},{... | collective-permute-start | bytes 393224 | tf_op jit(solution)/shard_map/ppermute | solution.py:18
  45.5 18.8 %collective-permute-start.15 = (bf16[2,256,128]{2,1,0:T(8,128)(2,1)}, bf16[2,256,128]{2,1,0:T(8,128)(2,1)}, u32[]{:S(2)}, u32[]{:S(2)}) collective-permute-start(bf16[2,256,128]{2,1,0:T(8,128)(2,1)} %bitcast.18.refs_4_), channel_id=1, source_target_pairs={{0,24},{4,28},{8,16},{12,20},{16,8},{20,12},{24,0},{28,4},{1,25},{... | collective-permute-start | bytes 393224 | tf_op jit(solution)/shard_map/ppermute | solution.py:112
  46.1 4.1 %collective-permute-start.2 = (bf16[2,32,256]{2,1,0:T(8,128)(2,1)S(1)}, bf16[2,32,256]{2,1,0:T(8,128)(2,1)S(1)}, u32[]{:S(2)}, u32[]{:S(2)}) collective-permute-start(bf16[2,32,256]{2,1,0:T(8,128)(2,1)S(1)} %get-tuple-element.20), channel_id=1, source_target_pairs={{4,1},{5,2},{6,3},{8,5},{9,6},{10,7},{12,9},{13,10},{14,11},{16,13... | collective-permute-start | bytes 98312 | tf_op jit(solution)/shard_map/ppermute | solution.py:370
  46.8 4.7 %collective-permute-start = (bf16[2,2,32,256]{3,2,1,0:T(8,128)(2,1)S(1)}, bf16[2,2,32,256]{3,2,1,0:T(8,128)(2,1)S(1)}, u32[]{:S(2)}, u32[]{:S(2)}) collective-permute-start(bf16[2,2,32,256]{3,2,1,0:T(8,128)(2,1)S(1)} %get-tuple-element.18), channel_id=1, source_target_pairs={{0,1},{1,2},{2,3},{4,5},{5,6},{6,7},{8,9},{9,10},{10,11},{12,13},{... | collective-permute-start | bytes 196616 | tf_op jit(solution)/shard_map/ppermute | solution.py:18
  50.2 9.1 %collective-permute-start.1 = (bf16[2,64,256]{2,1,0:T(8,128)(2,1)S(1)}, bf16[2,64,256]{2,1,0:T(8,128)(2,1)S(1)}, u32[]{:S(2)}, u32[]{:S(2)}) collective-permute-start(bf16[2,64,256]{2,1,0:T(8,128)(2,1)S(1)} %get-tuple-element.19), channel_id=1, source_target_pairs={{4,0},{8,4},{12,8},{16,12},{20,16},{24,20},{28,24},{5,1},{9,5},{13... | collective-permute-start | bytes 196616 | tf_op jit(solution)/shard_map/ppermute | solution.py:18
  51.5 30.6 %collective-permute-start.13 = (bf16[2,256,128]{2,1,0:T(8,128)(2,1)}, bf16[2,256,128]{2,1,0:T(8,128)(2,1)}, u32[]{:S(2)}, u32[]{:S(2)}) collective-permute-start(bf16[2,256,128]{2,1,0:T(8,128)(2,1)} %bitcast.18.refs_4_), channel_id=1, source_target_pairs={{0,16},{4,20},{8,24},{12,28},{16,0},{20,4},{24,8},{28,12},{1,17},{... | collective-permute-start | bytes 393224 | tf_op jit(solution)/shard_map/ppermute | solution.py:112
  59.3 23.2 %collective-permute-start.11 = (bf16[2,256,128]{2,1,0:T(8,128)(2,1)}, bf16[2,256,128]{2,1,0:T(8,128)(2,1)}, u32[]{:S(2)}, u32[]{:S(2)}) collective-permute-start(bf16[2,256,128]{2,1,0:T(8,128)(2,1)} %bitcast.18.refs_4_), channel_id=1, source_target_pairs={{0,8},{4,12},{8,0},{12,4},{16,24},{20,28},{24,16},{28,20},{1,9},{5... | collective-permute-start | bytes 393224 | tf_op jit(solution)/shard_map/ppermute | solution.py:112
  62.7 0.7 copy-start.5
  63.4 20.7 %collective-permute-start.10 = (bf16[2,256,128]{2,1,0:T(8,128)(2,1)}, bf16[2,256,128]{2,1,0:T(8,128)(2,1)}, u32[]{:S(2)}, u32[]{:S(2)}) collective-permute-start(bf16[2,256,128]{2,1,0:T(8,128)(2,1)} %bitcast.18.refs_4_), channel_id=1, source_target_pairs={{0,4},{4,0},{8,12},{12,8},{16,20},{20,16},{24,28},{28,24},{1,5},{5... | collective-permute-start | bytes 393224 | tf_op jit(solution)/shard_map/ppermute | solution.py:112
  64.3 66.7 %collective-permute-start.4 = (bf16[8,64,256]{2,1,0:T(8,128)(2,1)}, bf16[8,64,256]{2,1,0:T(8,128)(2,1)}, u32[]{:S(2)}, u32[]{:S(2)}) collective-permute-start(bf16[8,64,256]{2,1,0:T(8,128)(2,1)} %all_gather.3.gathered.refs_0_), channel_id=1, source_target_pairs={{0,1},{1,0},{2,3},{3,2},{4,5},{5,4},{6,7},{7,6},{8,9},{9,8},{10,11... | collective-permute-start | bytes 786440 | tf_op jit(solution)/shard_map/ppermute | solution.py:112
  64.5 66.6 %collective-permute-start.6 = (bf16[8,64,256]{2,1,0:T(8,128)(2,1)}, bf16[8,64,256]{2,1,0:T(8,128)(2,1)}, u32[]{:S(2)}, u32[]{:S(2)}) collective-permute-start(bf16[8,64,256]{2,1,0:T(8,128)(2,1)} %collective-permute-done.5.refs_2_), channel_id=1, source_target_pairs={{0,1},{1,0},{2,3},{3,2},{4,5},{5,4},{6,7},{7,6},{8,9},{9,8},{10,11... | collective-permute-start | bytes 786440 | tf_op jit(solution)/shard_map/ppermute | solution.py:112
  64.9 2.0 %copy-start = (bf16[3,3,3,256,256]{4,3,2,1,0:T(8,128)(2,1)S(1)}, bf16[3,3,3,256,256]{4,3,2,1,0:T(8,128)(2,1)}, u32[]{:S(2)}) copy-start(bf16[3,3,3,256,256]{4,3,2,1,0:T(8,128)(2,1)} %param.7) | copy-start | bytes 10616836
  66.9 0.9 copy-start.8
  67.8 0.7 copy-start.11
  68.4 16.1 %copy-start.1 = (bf16[3,3,3,256,256]{4,3,2,1,0:T(8,128)(2,1)S(1)}, bf16[3,3,3,256,256]{4,3,2,1,0:T(8,128)(2,1)}, u32[]{:S(2)}) copy-start(bf16[3,3,3,256,256]{4,3,2,1,0:T(8,128)(2,1)} %param.7) | copy-start | bytes 10616836
  69.3 0.6 copy-start.4
  69.9 10.7 %all-to-all-start = ((bf16[8,8,256]{2,1,0:T(8,128)(2,1)}), bf16[8,8,256]{2,1,0:T(8,128)(2,1)}, u32[]{:S(2)}, u32[]{:S(2)}) async-start(bf16[8,8,256]{2,1,0:T(8,128)(2,1)} %bitcast.33), calls=%async_computation | async-start | bytes 65536 | tf_op jit(solution)/shard_map/all_to_all | solution.py:378
  82.0 49.1 %collective-permute-start.16 = (bf16[2,256,128]{2,1,0:T(8,128)(2,1)}, bf16[2,256,128]{2,1,0:T(8,128)(2,1)}, u32[]{:S(2)}, u32[]{:S(2)}) collective-permute-start(bf16[2,256,128]{2,1,0:T(8,128)(2,1)} %collective-permute-done.15.refs_10_), channel_id=1, source_target_pairs={{0,4},{4,0},{8,12},{12,8},{16,20},{20,16},{24,28},{28,24},{1,5},{5... | collective-permute-start | bytes 393224 | tf_op jit(solution)/shard_map/ppermute | solution.py:112
  82.5 48.6 %collective-permute-start.14 = (bf16[2,256,128]{2,1,0:T(8,128)(2,1)}, bf16[2,256,128]{2,1,0:T(8,128)(2,1)}, u32[]{:S(2)}, u32[]{:S(2)}) collective-permute-start(bf16[2,256,128]{2,1,0:T(8,128)(2,1)} %collective-permute-done.13.refs_8_), channel_id=1, source_target_pairs={{0,4},{4,0},{8,12},{12,8},{16,20},{20,16},{24,28},{28,24},{1,5},{5... | collective-permute-start | bytes 393224 | tf_op jit(solution)/shard_map/ppermute | solution.py:112
  84.1 47.0 %collective-permute-start.12 = (bf16[2,256,128]{2,1,0:T(8,128)(2,1)}, bf16[2,256,128]{2,1,0:T(8,128)(2,1)}, u32[]{:S(2)}, u32[]{:S(2)}) collective-permute-start(bf16[2,256,128]{2,1,0:T(8,128)(2,1)} %collective-permute-done.11.refs_6_), channel_id=1, source_target_pairs={{0,4},{4,0},{8,12},{12,8},{16,20},{20,16},{24,28},{28,24},{1,5},{5... | collective-permute-start | bytes 393224 | tf_op jit(solution)/shard_map/ppermute | solution.py:112
  84.5 0.9 copy-start.3
  85.5 0.9 copy-start.6
where the time goes:
time: 138 us; the launch traced here: 137 us
  blocking collectives  74.3 us (54%)
  starting transfers between devices  27.9 us (20%)
  local copies, waits for them, and re-layouts  13.2 us (10%)
  Pallas kernels  10.3 us (7%)
  waiting for transfers between devices  9.83 us (7%)
    psum x1, blocking collectives, gathered_form(): gain_grad = lax.psum(gain_part, ('rows', 'tm'))  41.1 us
    all_gather x1, blocking collectives, gathered_form(): grad_rows = lax.all_gather(latent_grad.reshape(-1, C), 'rows', axis=0)  33.3 us
    ppermute x13, starting transfers between devices, partners(): lax.ppermute(value, axis, [(source, source ^ bits) for source in range(co...  17.3 us
    unnamed x25, local copies, waits for them, and re-layouts  9.54 us
    all_to_all x1, waiting for transfers between devices, gathered_form(): lax.all_to_all(latent_send.reshape(R, span // R, C), 'rows', split_axis=0...  6.7 us
    ppermute x3, starting transfers between devices, shifted(): lax.ppermute(value, axis, [(source, source + steps) for source in range(l...  5.97 us
    pallas_call x1, Pallas kernels, gathered_form(): call(functools.partial(weight_kernel, F, J, R, T, part), [((27, part, C),...  5.53 us
    all_to_all x1, starting transfers between devices, gathered_form(): lax.all_to_all(latent_send.reshape(R, span // R, C), 'rows', split_axis=0...  3.96 us
  transfers between devices with their start and end apart: 18, of which 2 were waited for; matrix products, arithmetic and copies ran while one was open for 3% of the time, Pallas kernels for 3%

commit v1 on v0

--- a/solution.py
+++ b/solution.py
@@ -139,8 +139,16 @@
     return inv_rms, unit, unit * gain
 
 
-def hidden_kernel(F, J, T, place, frames, gain, planes, cached, under, corner, *rest):
-    sends, tmp = rest[:T], rest[T]
+def hidden_kernel(F, J, T, place, frames_hbm, gain_hbm, planes, *rest):
+    sends, (frames, gain, tmp, sem) = rest[:T], rest[T:]
+    copies = [
+        pltpu.make_async_copy(frames_hbm, frames, sem.at[0]),
+        pltpu.make_async_copy(gain_hbm, gain, sem.at[1]),
+    ]
+    for copy in copies:
+        copy.start()
+    for copy in copies:
+        copy.wait()
     channels = frames.shape[1]
     part = channels // T
     _, _, normed = normalised(frames[...], gain[...])
@@ -165,10 +173,12 @@
             pair.append(plane)
             plane = plane.astype(jnp.bfloat16)
             planes[rp, cp] = plane
-            cached[rp, cp] = plane[(F - 2) * J :]
-            if rp == 0:
-                under[cp] = plane
-                corner[cp] = plane[(F - 2) * J :]
+            late = plane[(F - 2) * J :]
+            for k in range(1, T, 2):
+                for half in range(2):
+                    at = (((rp * 2 + cp) * 2) + half) * 2 * J
+                    lanes = slice(half * channels // 2, (half + 1) * channels // 2)
+                    sends[k][2 * F * J + at : 2 * F * J + at + 2 * J] = late[:, lanes]
         pieces = [
             jnp.concatenate([p[:, d * part : (d + 1) * part] for p in pair], axis=1)
             for d in range(T)
@@ -177,7 +187,31 @@
             chosen = pieces[0]
             for d in range(1, T):
                 chosen = jnp.where(block == d ^ k, pieces[d], chosen)
-            sends[k][rp] = chosen.astype(jnp.bfloat16)
+            sends[k][rp * F * J : (rp + 1) * F * J] = chosen.astype(jnp.bfloat16)
+
+
+def join_kernel(F, J, T, place, planes, *refs):
+    messages, (joined, cached, under) = refs[:T], refs[T:]
+    span = F * J
+    block = place[1]
+    for k in range(T):
+        for rp in range(2):
+            joined[k, rp] = messages[k][rp * span : (rp + 1) * span, :]
+    for rp in range(2):
+        for cp in range(2):
+            halves = []
+            for half in range(2):
+                start = 2 * span + ((rp * 2 + cp) * 2 + half) * 2 * J
+                value = jnp.zeros((2 * J, messages[1].shape[1]), jnp.bfloat16)
+                for k in range(1, T, 2):
+                    found = (block > 0) & (block ^ k == block - 1)
+                    value = jnp.where(found, messages[k][start : start + 2 * J, :], value)
+                halves.append(value)
+            before = jnp.concatenate(halves, axis=1)
+            cached[rp, cp] = before
+            if rp == 0:
+                under[cp, : 2 * J] = before
+                under[cp, 2 * J :] = planes[0, cp]
 
 
 def permutation(shape, meet):
@@ -186,62 +220,78 @@
     return jnp.where(meet(row, col), 1.0, 0.0).astype(jnp.bfloat16)
 
 
-def latent_kernel(F, J, R, planes, cached, under, corner, weight, bias, out, ext):
+def shard_order(J, R, moved):
+    jl = J // R
+    return permutation(
+        (R * 2 * J, R * 2 * J),
+        lambda o, s: (o // (2 * J) == s // jl % R)
+        & (o // J % 2 == s // (jl * R) % 2)
+        & (o % J == s // (2 * jl * R) * jl + s % jl + moved),
+    )
+
+
+def slab_kernel(
+    F, J, R, T, slot, place, planes, cached, under, weight_hbm, bias_hbm, frames_hbm, gain_hbm, *refs
+):
+    gathered = refs[:T]
+    out, frames_grad, bias_sum, grads = refs[T : T + 4]
+    weight, bias, frames, gain, ext, tmp, sem = refs[T + 4 :]
+    row, block = place[0], place[1]
+    channels = frames.shape[1]
+    span = F * J
+    taps_a = [
+        pltpu.make_async_copy(weight_hbm.at[pl.ds(a * 9, 9)], weight.at[pl.ds(a * 9, 9)], sem.at[a])
+        for a in range(3)
+    ]
+    others = [
+        pltpu.make_async_copy(source, target, sem.at[3 + n])
+        for n, (source, target) in enumerate(
+            ((bias_hbm, bias), (frames_hbm, frames), (gain_hbm, gain))
+        )
+    ]
+    for copy in taps_a + others:
+        copy.start()
+
+    pair_rows = 2 * R * (J // R)
+    grads[:, 0] = jnp.zeros((2,) + grads.shape[2:], jnp.bfloat16)
+    grads[:, :, T * span :, :] = jnp.zeros((2, R + 1, 2 * J, channels), jnp.bfloat16)
+    orders = [shard_order(J, R, moved) for moved in range(2)]
+    total = jnp.zeros((1, channels), jnp.float32)
+    for k in range(T):
+        for pair in range(F // 2):
+            start = pair * pair_rows
+            source = jnp.concatenate(
+                [gathered[k][s, start : start + pair_rows, :] for s in range(R)], axis=0
+            )
+            total = total + jnp.sum(source.astype(jnp.float32), axis=0, keepdims=True)
+            at = pl.multiple_of((block ^ k) * span + pair * 2 * J, 16)
+            for moved in range(2):
+                value = mm(orders[moved], source).astype(jnp.bfloat16)
+                for i in range(R):
+                    grads[moved, i + 1, pl.ds(at, 2 * J), :] = value[i * 2 * J : (i + 1) * 2 * J]
+    bias_sum[...] = total
+
     rows = (F + 2) * J
     last = lax.broadcasted_iota(jnp.int32, (rows, 1), 0) % J == J - 1
     for b in range(3):
         for cp in range(2):
-            before, now = (corner[cp], under[cp]) if b == 2 else (cached[b, cp], planes[b, cp])
-            full = jnp.concatenate([before, now], axis=0)
+            if b == 2:
+                full = under[cp]
+            else:
+                full = jnp.concatenate([cached[b, cp], planes[b, cp]], axis=0)
             ext[b, cp] = full
             if cp == 0:
                 moved = pltpu.roll(full.astype(jnp.float32), rows - 1, 0)
                 ext[b, 2] = jnp.where(last, 0.0, moved).astype(jnp.bfloat16)
-    total = jnp.zeros(out.shape, jnp.float32) + bias[...]
-    for n, (a, b, c) in enumerate(TAPS):
-        total = total + mm(ext[b, c, a * J : (a + F) * J, :], weight[n])
-    jl = J // R
-    order = permutation(
-        (F * J, F * J),
-        lambda o, s: (o // jl % F == s // J) & (o // (F * jl) * jl + o % jl == s % J),
-    )
-    out[...] = mm(order, total.astype(jnp.bfloat16)).astype(jnp.bfloat16)
-
-
-def shard_rows(source, start, count, R):
-    return jnp.concatenate([source[s, start : start + count, :] for s in range(R)], axis=0)
-
-
-def shard_order(J, R, rows, first, moved):
-    jl = J // R
-    return permutation(
-        (rows * 2 * J, 2 * R * J),
-        lambda o, s: (o // (2 * J) + first == s // jl % R)
-        & (o // J % 2 == s // (jl * R) % 2)
-        & (o % J == s // (2 * jl * R) * jl + s % jl + moved),
-    )
-
-
-def frames_kernel(
-    F, J, R, place, gathered, following, weight, frames, gain, frames_grad, gain_part, near, tmp
-):
-    channels = frames.shape[1]
-    pair_rows = 2 * R * (J // R)
-    orders = [shard_order(J, R, 2, place[0] - 1, moved) for moved in range(2)]
-    for pair in range(F // 2 + 1):
-        if pair < F // 2:
-            source = shard_rows(gathered, pair * pair_rows, pair_rows, R)
-        else:
-            source = shard_rows(following, 0, pair_rows, R)
-        for moved in range(2):
-            value = mm(orders[moved], source).astype(jnp.bfloat16)
-            for i in range(2):
-                near[moved, i, pair * 2 * J : (pair + 1) * 2 * J, :] = value[
-                    i * 2 * J : (i + 1) * 2 * J
-                ]
+
+    latent = jnp.zeros((span, channels), jnp.float32)
     sums = {}
     for n, (a, b, c) in enumerate(TAPS):
-        piece = near[c // 2, 1 - b // 2, (2 - a) * J : (2 - a + F) * J, :]
+        if n % 9 == 0:
+            taps_a[a].wait()
+        latent = latent + mm(ext[b, c, a * J : (a + F) * J, :], weight[n])
+        start = pl.multiple_of((block * F + 2 - a) * J, 16)
+        piece = grads[c // 2, row + 1 - b // 2, pl.ds(start, span), :]
         term = mm_t(piece, weight[n])
         key = (b % 2, c % 2)
         sums[key] = sums[key] + term if key in sums else term
@@ -252,55 +302,55 @@
                 tmp[half, pl.ds((t * 2 + rp) * 2 * J + cp, J, stride=2), :] = value[
                     t * J : (t + 1) * J, lanes
                 ]
+    for copy in others:
+        copy.wait()
     hidden_grad = jnp.concatenate([tmp[0], tmp[1]], axis=1)
     inv_rms, unit, normed = normalised(frames[...], gain[...])
     sigma = 1.0 / (1.0 + jnp.exp(-normed))
     normed_grad = hidden_grad * sigma * (1.0 + normed * (1.0 - sigma))
-    gain_part[...] = jnp.sum(normed_grad * unit, axis=0, keepdims=True)
+    gain_part = jnp.sum(normed_grad * unit, axis=0, keepdims=True)
     unit_grad = normed_grad * gain[...]
     mean = jnp.mean(unit_grad * unit, axis=-1, keepdims=True)
     frames_grad[...] = (inv_rms * (unit_grad - unit * mean)).astype(jnp.bfloat16)
 
-
-def weight_kernel(F, J, R, T, part, place, *refs):
-    gathered, hidden = refs[:T], refs[T : T + R]
-    out, bias_sum, grads, even, odd = refs[T + R :]
-    channels = gathered[0].shape[-1]
-    span = F * J
-    depth = T * span
+    jl = J // R
+    used = span // R
+    order = permutation(
+        (R * slot, span),
+        lambda o, s: (o % slot < used)
+        & (o % slot // jl == s // J)
+        & (o // slot * jl + o % jl == s % J),
+    )
+    value = mm(order, (latent + bias[...]).astype(jnp.bfloat16))
+    line = lax.broadcasted_iota(jnp.int32, (R * slot, 1), 0) % slot
+    rest = gain_part
+    for n in range(3):
+        term = rest.astype(jnp.bfloat16).astype(jnp.float32)
+        rest = rest - term
+        value = jnp.where(line == used + n, term, value)
+    out[...] = value.astype(jnp.bfloat16)
+
+
+def weight_kernel(F, J, R, T, part, place, grads, *refs):
+    hidden = refs[:R]
+    out, even, odd = refs[R:]
+    channels = grads.shape[-1]
+    depth = T * F * J
     lanes = 2 * part
     row, block = place[0], place[1]
-    pair_rows = 2 * R * (J // R)
-    grads[:, :, depth:, :] = jnp.zeros((2, R, 2 * J, channels), jnp.bfloat16)
     even[:, R * depth :] = jnp.zeros((lanes, depth), jnp.bfloat16)
-    orders = [shard_order(J, R, R, 0, moved) for moved in range(2)]
-    total = jnp.zeros((1, channels), jnp.float32)
-    for k in range(T):
-        for pair in range(F // 2):
-            source = shard_rows(gathered[k], pair * pair_rows, pair_rows, R)
-            total = total + jnp.sum(source.astype(jnp.float32), axis=0, keepdims=True)
-            at = pl.multiple_of((block ^ k) * span + pair * 2 * J, 16)
-            for moved in range(2):
-                value = mm(orders[moved], source).astype(jnp.bfloat16)
-                for i in range(R):
-                    grads[moved, i, pl.ds(at, 2 * J), :] = value[i * 2 * J : (i + 1) * 2 * J]
-    bias_sum[...] = total
     for k in range(R):
         at = pl.multiple_of((row ^ k) * depth, 128)
         for rp, turned in ((0, even), (1, odd)):
-            turned[:, pl.ds(at, depth)] = hidden[k][rp].T
+            value = jnp.concatenate([hidden[k][block ^ t, rp] for t in range(T)], axis=0)
+            turned[:, pl.ds(at, depth)] = value.T
     for a in range(3):
         start = (2 - a) * J
         for moved in range(2):
-            right = grads[moved, :, start : start + depth, :].reshape(R * depth, channels)
+            right = grads[moved, 1:, start : start + depth, :].reshape(R * depth, channels)
             size = part if moved else lanes
             left = jnp.concatenate(
-                [
-                    even[:size, : R * depth],
-                    odd[:size, :],
-                    even[:size, depth:],
-                ],
-                axis=0,
+                [even[:size, : R * depth], odd[:size, :], even[:size, depth:]], axis=0
             )
             value = mm(left, right)
             for b in range(3):
@@ -312,15 +362,14 @@
                         out[(a * 3 + b) * 3 + cp] = value[at : at + part]
 
 
-def call(kernel, outs, scratch, flops, moved, smem=0, operands=0):
-    vmem = pl.BlockSpec(memory_space=pltpu.VMEM)
-    specs = [pl.BlockSpec(memory_space=pltpu.SMEM)] * smem + [vmem] * (operands - smem)
+def call(kernel, outs, scratch, flops, moved, places):
+    kinds = {"s": pltpu.SMEM, "v": pltpu.VMEM, "a": pl.ANY}
     return pl.pallas_call(
         kernel,
         out_shape=[jax.ShapeDtypeStruct(s, d) for s, d in outs],
-        in_specs=specs,
-        out_specs=[vmem] * len(outs),
-        scratch_shapes=[pltpu.VMEM(s, d) for s, d in scratch],
+        in_specs=[pl.BlockSpec(memory_space=kinds[p]) for p in places],
+        out_specs=[pl.BlockSpec(memory_space=pltpu.VMEM)] * len(outs),
+        scratch_shapes=scratch,
         compiler_params=pltpu.CompilerParams(vmem_limit_bytes=VMEM_LIMIT),
         cost_estimate=pl.CostEstimate(flops=flops, bytes_accessed=moved, transcendentals=0),
     )
@@ -333,76 +382,83 @@
     J = col_count // 2
     span = F * J
     part = C // T
+    used = span // R
+    slot = -(-(used + 3) // 16) * 16
     gain = norm_gain.reshape(1, C)
     bias = conv_bias.reshape(1, C)
     flat = frames.reshape(-1, C)
     weight = conv_weight.reshape(27, C, C)
     place = jnp.stack([lax.axis_index("rows"), lax.axis_index("tm")]).astype(jnp.int32)
 
-    grad_rows = lax.all_gather(latent_grad.reshape(-1, C), "rows", axis=0)
-
-    planes, cached, under, corner, *sends = call(
+    own = latent_grad.reshape(1, -1, C)
+    grad_rows = lax.all_to_all(
+        jnp.broadcast_to(own, (R,) + own.shape[1:]), "rows", 0, 0, tiled=True
+    )
+
+    sizes = [(2 * span + (16 * J if k % 2 else 0), 2 * part) for k in range(T)]
+    planes, *sends = call(
         functools.partial(hidden_kernel, F, J, T),
+        [((2, 2, span, C), bf16)] + [(size, bf16) for size in sizes],
         [
-            ((2, 2, span, C), bf16),
+            pltpu.VMEM((4 * span, C), bf16),
+            pltpu.VMEM((1, C), f32),
+            pltpu.VMEM((2, 4 * span, C // 2), f32),
+            pltpu.SemaphoreType.DMA((2,)),
+        ],
+        10 * 4 * span * C, 16 * span * C, "saa",
+    )(place, flat, gain)
+    messages = [sends[0]] + [partners(sends[k], "tm", k) for k in range(1, T)]
+    joined, cached, under = call(
+        functools.partial(join_kernel, F, J, T),
+        [
+            ((T, 2, span, 2 * part), bf16),
             ((2, 2, 2 * J, C), bf16),
-            ((2, span, C), bf16),
-            ((2, 2 * J, C), bf16),
-        ]
-        + [((2, span, 2 * part), bf16)] * T,
-        [((2, 4 * span, C // 2), f32)],
-        10 * 4 * span * C, 16 * span * C, smem=1, operands=3,
-    )(place, flat, gain)
-
-    parts = [sends[0]] + [partners(sends[k], "tm", k) for k in range(1, T)]
-    block = lax.axis_index("tm")
-    ordered = jnp.stack(parts)
-    ordered = jnp.stack(
-        [lax.dynamic_index_in_dim(ordered, block ^ t, keepdims=False) for t in range(T)], axis=1
-    )
-    hidden_all = exchanged(ordered.reshape(2, T * span, 2 * part), "rows")
-
-    cached = shifted(cached, "tm", 1)
+            ((2, 2 * J + span, C), bf16),
+        ],
+        [],
+        4 * span * C, 16 * span * C, "sv" + "v" * T,
+    )(place, planes, *messages)
     under = shifted(under, "rows", -1)
-    steps = [
-        ((r + 1) * T + t, r * T + t + 1) for r in range(R - 1) for t in range(T - 1)
-    ]
-    corner = lax.ppermute(corner, ("rows", "tm"), steps)
-
-    (latent_send,) = call(
-        functools.partial(latent_kernel, F, J, R),
-        [((span, C), bf16)],
-        [((3, 3, (F + 2) * J, C), bf16)],
-        2 * 27 * span * C * C, 2 * 27 * C * C, operands=6,
-    )(planes, cached, under, corner, weight, bias)
-    latent = lax.all_to_all(
-        latent_send.reshape(R, span // R, C), "rows", split_axis=0, concat_axis=0, tiled=True
-    )
-    latent = latent.reshape(R, F, J // R, C).transpose(1, 0, 2, 3)
-
-    following = shifted(grad_rows[:, : 2 * J], "tm", -1)
+    hidden_all = exchanged(joined, "rows")
     grad_all = exchanged(grad_rows, "tm")
-    frames_grad, gain_part = call(
-        functools.partial(frames_kernel, F, J, R),
-        [((4 * span, C), bf16), ((1, C), f32)],
-        [((2, 2, (F + 2) * J, C), bf16), ((2, 4 * span, C // 2), f32)],
-        2 * 27 * span * C * C, 2 * 27 * C * C, smem=1, operands=6,
-    )(place, grad_rows, following, weight, flat, gain)
-
-    weight_grad, bias_sum = call(
+
+    packed, frames_grad, bias_sum, grads = call(
+        functools.partial(slab_kernel, F, J, R, T, slot),
+        [
+            ((R * slot, C), bf16),
+            ((4 * span, C), bf16),
+            ((1, C), f32),
+            ((2, R + 1, (F * T + 2) * J, C), bf16),
+        ],
+        [
+            pltpu.VMEM((27, C, C), bf16),
+            pltpu.VMEM((1, C), f32),
+            pltpu.VMEM((4 * span, C), bf16),
+            pltpu.VMEM((1, C), f32),
+            pltpu.VMEM((3, 3, (F + 2) * J, C), bf16),
+            pltpu.VMEM((2, 4 * span, C // 2), f32),
+            pltpu.SemaphoreType.DMA((6,)),
+        ],
+        4 * 27 * span * C * C, 2 * 27 * C * C, "svvvaaaa" + "v" * T,
+    )(place, planes, cached, under, weight, bias, flat, gain, *grad_all)
+
+    packed = lax.all_to_all(packed.reshape(R, slot, C), "rows", 0, 0, tiled=True)
+    latent = packed[:, :used].reshape(R, F, J // R, C).transpose(1, 0, 2, 3)
+    gain_sum = jnp.sum(packed[:, used : used + 3].astype(f32), axis=(0, 1)).reshape(1, C)
+    gain_sum = sum(partners(gain_sum, "tm", k) for k in range(1, T)) + gain_sum
+
+    (weight_grad,) = call(
         functools.partial(weight_kernel, F, J, R, T, part),
-        [((27, part, C), f32), ((1, C), f32)],
+        [((27, part, C), f32)],
         [
-            ((2, R, (F * T + 2) * J, C), bf16),
-            ((2 * part, (R + 1) * T * span), bf16),
-            ((2 * part, R * T * span), bf16),
+            pltpu.VMEM((2 * part, (R + 1) * T * span), bf16),
+            pltpu.VMEM((2 * part, R * T * span), bf16),
         ],
-        2 * 27 * R * T * span * part * C, 8 * 27 * part * C, smem=1, operands=1 + T + R,
-    )(place, *grad_all, *hidden_all)
-
-    gain_grad = lax.psum(gain_part, ("rows", "tm"))
+        2 * 27 * R * T * span * part * C, 8 * 27 * part * C, "sv" + "v" * R,
+    )(place, grads, *hidden_all)
+
     start = lax.axis_index("tm") * part
-    gain_grad = lax.dynamic_slice(gain_grad.reshape(C), (start,), (part,))
+    gain_grad = lax.dynamic_slice(gain_sum.reshape(C), (start,), (part,))
     bias_grad = lax.dynamic_slice(bias_sum.reshape(C), (start,), (part,))
     return (
         latent,

time: 138 us -> 73.9 us (0.54)
  blocking collectives: 74.3 us -> 0 us
  waiting for transfers between devices: 9.83 us -> 17.6 us
  starting transfers between devices: 27.9 us -> 34.1 us
  local copies, waits for them, and re-layouts: 13.2 us -> 9.84 us
    psum x1 -> x0, blocking collectives: 41.1 us -> none  [gathered_form(): gain_grad = lax.psum(gain_part, ('rows', 'tm'))]
    all_gather x1 -> x0, blocking collectives: 33.3 us -> none  [gathered_form(): grad_rows = lax.all_gather(latent_grad.reshape(-1, C), 'rows', axis=0)]
    ppermute x13 -> x16, waiting for transfers between devices: 0.03 us -> 7.57 us  [partners(): lax.ppermute(value, axis, [(source, source ^ bits) for source in range(co...]
    all_to_all x1 -> x2, starting transfers between devices: 3.96 us -> 10.8 us  [the longest x1 7.25 us: gathered_form(): lax.all_to_all(jnp.broadcast_to(own, (R,) + own.shape[1:]), 'rows', 0, 0,...]
    ppermute x3 -> x1, starting transfers between devices: 5.97 us -> 1.29 us  [shifted(): lax.ppermute(value, axis, [(source, source + steps) for source in range(l...]
    ppermute x13 -> x16, starting transfers between devices: 17.3 us -> 22 us  [partners(): lax.ppermute(value, axis, [(source, source ^ bits) for source in range(co...]
    all_to_all x1 -> x2, waiting for transfers between devices: 6.7 us -> 9.98 us  [the longest x1 8.92 us: gathered_form(): lax.all_to_all(jnp.broadcast_to(own, (R,) + own.shape[1:]), 'rows', 0, 0,...]
    ppermute x3 -> x1, waiting for transfers between devices: 3.1 us -> 0.1 us  [shifted(): lax.ppermute(value, axis, [(source, source + steps) for source in range(l...]
  transfers between devices with their start and end apart: 18 -> 19, of which waited for: 2 -> 6; matrix products, arithmetic and copies ran while one was open for 3% -> 2% of each run, Pallas kernels for 3% -> 14%
where the time goes in v1:
time: 73.9 us; the launch traced here: 73.4 us
  starting transfers between devices  34.1 us (46%)
  waiting for transfers between devices  17.6 us (24%)
  Pallas kernels  10.3 us (14%)
  local copies, waits for them, and re-layouts  9.84 us (13%)
  between operations  0.76 us (1%)
    ppermute x16, starting transfers between devices, partners(): lax.ppermute(value, axis, [(source, source ^ bits) for source in range(co...  22 us
    all_to_all x1, waiting for transfers between devices, gathered_form(): lax.all_to_all(jnp.broadcast_to(own, (R,) + own.shape[1:]), 'rows', 0, 0,...  8.92 us
    unnamed x16, local copies, waits for them, and re-layouts  7.76 us
    ppermute x16, waiting for transfers between devices, partners(): lax.ppermute(value, axis, [(source, source ^ bits) for source in range(co...  7.57 us
    all_to_all x1, starting transfers between devices, gathered_form(): lax.all_to_all(jnp.broadcast_to(own, (R,) + own.shape[1:]), 'rows', 0, 0,...  7.25 us
    pallas_call x1, Pallas kernels, gathered_form(): call(functools.partial(slab_kernel, F, J, R, T, slot), [((R * slot, C), b...  4.66 us
    pallas_call x1, Pallas kernels, gathered_form(): call(functools.partial(weight_kernel, F, J, R, T, part), [((27, part, C),...  4.05 us
    all_to_all x1, starting transfers between devices, gathered_form(): lax.all_to_all(packed.reshape(R, slot, C), 'rows', 0, 0, tiled=True)  3.56 us
  transfers between devices with their start and end apart: 19, of which 6 were waited for; matrix products, arithmetic and copies ran while one was open for 2% of the time, Pallas kernels for 14%

profile of v1, /device:TPU:0, one launch (start us, length us, event | category | flops | bytes accessed | tf_op | source)
XLA Modules:
  0.0 73.4 jit_solution(15500516953696745745)
XLA Ops:
  0.6 0.8 %broadcast_in_dim.7 = bf16[64,256]{1,0:T(8,128)(2,1)S(1)} reshape(bf16[4,8,2,256]{3,2,1,0:T(2,128)(2,1)} %param.9) | data formatting | bytes 65536 | tf_op jit(solution)/shard_map/broadcast_in_dim | solution.py:395
  1.4 0.7 broadcast_in_dim.8
  2.1 7.3 %all-to-all-start = ((bf16[8,64,256]{2,1,0:T(8,128)(2,1)}), bf16[8,64,256]{2,1,0:T(8,128)(2,1)S(1)}, u32[]{:S(2)}, u32[]{:S(2)}) async-start(bf16[8,64,256]{2,1,0:T(8,128)(2,1)} %broadcast_in_dim.8), calls=%async_computation | async-start | bytes 524288 | tf_op jit(solution)/shard_map/all_to_all | solution.py:394
  9.4 8.9 %all-to-all-done.refs_0_ = bf16[8,64,256]{2,1,0:T(8,128)(2,1)S(1)} async-done(((bf16[8,64,256]{2,1,0:T(8,128)(2,1)}), bf16[8,64,256]{2,1,0:T(8,128)(2,1)S(1)}, u32[]{:S(2)}, u32[]{:S(2)}) %all-to-all-start) | async-done | bytes 262176 | tf_op jit(solution)/shard_map/all_to_all | solution.py:394
  18.3 1.5 %collective-permute-start.5 = (bf16[8,64,256]{2,1,0:T(8,128)(2,1)S(1)}, bf16[8,64,256]{2,1,0:T(8,128)(2,1)S(1)}, u32[]{:S(2)}, u32[]{:S(2)}) collective-permute-start(bf16[8,64,256]{2,1,0:T(8,128)(2,1)S(1)} %all-to-all-done.refs_0_), channel_id=1, source_target_pairs={{0,2},{1,3},{2,0},{3,1},{4,6},{5,7},{6,4},{7,5},{8,10},{9,11},{10,... | collective-permute-start | bytes 786440 | tf_op jit(solution)/shard_map/ppermute | solution.py:112
  19.8 0.1 pad_add_fusion.place
  19.9 0.0 copy-start
  19.9 0.9 %copy-done = bf16[4,2,32,256]{3,2,1,0:T(8,128)(2,1)S(1)} copy-done((bf16[4,2,32,256]{3,2,1,0:T(8,128)(2,1)S(1)}, bf16[4,2,32,256]{3,2,1,0:T(8,128)(2,1)}, u32[]{:S(2)}) %copy-start) | copy-done | bytes 131096
  20.8 0.0 copy-start.2
  20.8 0.7 copy-done.2
  21.5 1.0 %shard_map.92 = (bf16[2,2,64,256]{3,2,1,0:T(8,128)(2,1)S(1)}, bf16[128,128]{1,0:T(8,128)(2,1)S(1)}, bf16[384,128]{1,0:T(8,128)(2,1)S(1)}, bf16[128,128]{1,0:T(8,128)(2,1)S(1)}, bf16[384,128]{1,0:T(8,128)(2,1)S(1)}) custom-call(s32[2]{0:T(128)S(1)} %pad_add_fusion.place, bf16[256,256]{1,0:T(8,128)(2,1)S(1)} %bitcast.17, f32[1,256]{1,0:T(1,128)S(1)} %bitcast.19), custom_call_target="tpu_custom_call" | custom-call | flops 655360 | bytes 262144 | tf_op jit(solution)/shard_map/pallas_call | solution.py:399
  22.5 0.1 collective-permute-start
  22.6 0.6 collective-permute-start.2
  23.2 1.5 %collective-permute-start.1 = (bf16[128,128]{1,0:T(8,128)(2,1)S(1)}, bf16[128,128]{1,0:T(8,128)(2,1)S(1)}, u32[]{:S(2)}, u32[]{:S(2)}) collective-permute-start(bf16[128,128]{1,0:T(8,128)(2,1)S(1)} %get-tuple-element.20), channel_id=1, source_target_pairs={{0,2},{1,3},{2,0},{3,1},{4,6},{5,7},{6,4},{7,5},{8,10},{9,11},{10,... | collective-permute-start | bytes 98312 | tf_op jit(solution)/shard_map/ppermute | solution.py:112
  24.8 0.0 collective-permute-start.4
  24.8 3.7 %collective-permute-done.1.refs_2_ = bf16[128,128]{1,0:T(8,128)(2,1)S(1)} collective-permute-done((bf16[128,128]{1,0:T(8,128)(2,1)S(1)}, bf16[128,128]{1,0:T(8,128)(2,1)S(1)}, u32[]{:S(2)}, u32[]{:S(2)}) %collective-permute-start.1) | collective-permute-done | bytes 32800 | tf_op jit(solution)/shard_map/ppermute | solution.py:112
  28.5 0.0 collective-permute-done.refs_1_
  28.5 0.0 collective-permute-done.2.refs_3_
  28.5 0.6 shard_map.93
  29.1 1.3 %collective-permute-start.3 = (bf16[2,96,256]{2,1,0:T(8,128)(2,1)S(1)}, bf16[2,96,256]{2,1,0:T(8,128)(2,1)S(1)}, u32[]{:S(2)}, u32[]{:S(2)}) collective-permute-start(bf16[2,96,256]{2,1,0:T(8,128)(2,1)S(1)} %get-tuple-element.23), channel_id=1, source_target_pairs={{4,0},{8,4},{12,8},{16,12},{20,16},{24,20},{28,24},{5,1},{9,5},{13... | collective-permute-start | bytes 294920 | tf_op jit(solution)/shard_map/ppermute | solution.py:18
  30.4 0.0 collective-permute-done.5.refs_2_
  30.4 0.1 collective-permute-start.6
  30.4 2.7 %collective-permute-start.12 = (bf16[4,2,64,128]{3,2,1,0:T(8,128)(2,1)S(1)}, bf16[4,2,64,128]{3,2,1,0:T(8,128)(2,1)S(1)}, u32[]{:S(2)}, u32[]{:S(2)}) collective-permute-start(bf16[4,2,64,128]{3,2,1,0:T(8,128)(2,1)S(1)} %get-tuple-element.27.refs_0_), channel_id=1, source_target_pairs={{0,24},{4,28},{8,16},{12,20},{16,8},{20,12},{24,0},{28,4},{1,25},{... | collective-permute-start | bytes 393224 | tf_op jit(solution)/shard_map/ppermute | solution.py:112
  33.1 2.3 %collective-permute-start.10 = (bf16[4,2,64,128]{3,2,1,0:T(8,128)(2,1)S(1)}, bf16[4,2,64,128]{3,2,1,0:T(8,128)(2,1)S(1)}, u32[]{:S(2)}, u32[]{:S(2)}) collective-permute-start(bf16[4,2,64,128]{3,2,1,0:T(8,128)(2,1)S(1)} %get-tuple-element.27.refs_0_), channel_id=1, source_target_pairs={{0,16},{4,20},{8,24},{12,28},{16,0},{20,4},{24,8},{28,12},{1,17},{... | collective-permute-start | bytes 393224 | tf_op jit(solution)/shard_map/ppermute | solution.py:112
  35.5 0.1 collective-permute-done.3.under
  35.6 4.0 %collective-permute-start.8 = (bf16[4,2,64,128]{3,2,1,0:T(8,128)(2,1)S(1)}, bf16[4,2,64,128]{3,2,1,0:T(8,128)(2,1)S(1)}, u32[]{:S(2)}, u32[]{:S(2)}) collective-permute-start(bf16[4,2,64,128]{3,2,1,0:T(8,128)(2,1)S(1)} %get-tuple-element.27.refs_0_), channel_id=1, source_target_pairs={{0,8},{4,12},{8,0},{12,4},{16,24},{20,28},{24,16},{28,20},{1,9},{5... | collective-permute-start | bytes 393224 | tf_op jit(solution)/shard_map/ppermute | solution.py:112
  39.6 0.0 collective-permute-done.12.refs_6_
  39.6 4.3 %collective-permute-start.7 = (bf16[4,2,64,128]{3,2,1,0:T(8,128)(2,1)S(1)}, bf16[4,2,64,128]{3,2,1,0:T(8,128)(2,1)S(1)}, u32[]{:S(2)}, u32[]{:S(2)}) collective-permute-start(bf16[4,2,64,128]{3,2,1,0:T(8,128)(2,1)S(1)} %get-tuple-element.27.refs_0_), channel_id=1, source_target_pairs={{0,4},{4,0},{8,12},{12,8},{16,20},{20,16},{24,28},{28,24},{1,5},{5... | collective-permute-start | bytes 393224 | tf_op jit(solution)/shard_map/ppermute | solution.py:112
  43.9 3.3 %collective-permute-done.10.refs_4_ = bf16[4,2,64,128]{3,2,1,0:T(8,128)(2,1)S(1)} collective-permute-done((bf16[4,2,64,128]{3,2,1,0:T(8,128)(2,1)S(1)}, bf16[4,2,64,128]{3,2,1,0:T(8,128)(2,1)S(1)}, u32[]{:S(2)}, u32[]{:S(2)}) %collective-permute-start.10) | collective-permute-done | bytes 131104 | tf_op jit(solution)/shard_map/ppermute | solution.py:112
  47.2 0.9 %collective-permute-start.13 = (bf16[4,2,64,128]{3,2,1,0:T(8,128)(2,1)S(1)}, bf16[4,2,64,128]{3,2,1,0:T(8,128)(2,1)S(1)}, u32[]{:S(2)}, u32[]{:S(2)}) collective-permute-start(bf16[4,2,64,128]{3,2,1,0:T(8,128)(2,1)S(1)} %collective-permute-done.12.refs_6_), channel_id=1, source_target_pairs={{0,4},{4,0},{8,12},{12,8},{16,20},{20,16},{24,28},{28,24},{1,5},{5... | collective-permute-start | bytes 393224 | tf_op jit(solution)/shard_map/ppermute | solution.py:112
  48.0 0.0 collective-permute-done.8.refs_2_
  48.0 1.2 %collective-permute-start.11 = (bf16[4,2,64,128]{3,2,1,0:T(8,128)(2,1)S(1)}, bf16[4,2,64,128]{3,2,1,0:T(8,128)(2,1)S(1)}, u32[]{:S(2)}, u32[]{:S(2)}) collective-permute-start(bf16[4,2,64,128]{3,2,1,0:T(8,128)(2,1)S(1)} %collective-permute-done.10.refs_4_), channel_id=1, source_target_pairs={{0,4},{4,0},{8,12},{12,8},{16,20},{20,16},{24,28},{28,24},{1,5},{5... | collective-permute-start | bytes 393224 | tf_op jit(solution)/shard_map/ppermute | solution.py:112
  49.3 0.0 collective-permute-done.4.refs_1_
  49.3 0.8 %collective-permute-start.9 = (bf16[4,2,64,128]{3,2,1,0:T(8,128)(2,1)S(1)}, bf16[4,2,64,128]{3,2,1,0:T(8,128)(2,1)S(1)}, u32[]{:S(2)}, u32[]{:S(2)}) collective-permute-start(bf16[4,2,64,128]{3,2,1,0:T(8,128)(2,1)S(1)} %collective-permute-done.8.refs_2_), channel_id=1, source_target_pairs={{0,4},{4,0},{8,12},{12,8},{16,20},{20,16},{24,28},{28,24},{1,5},{5... | collective-permute-start | bytes 393224 | tf_op jit(solution)/shard_map/ppermute | solution.py:112
  50.1 0.0 collective-permute-done.6.refs_3_
  50.1 0.0 copy-start.1
  50.1 0.9 %copy-done.1 = bf16[4,2,32,256]{3,2,1,0:T(8,128)(2,1)S(1)} copy-done((bf16[4,2,32,256]{3,2,1,0:T(8,128)(2,1)S(1)}, bf16[4,2,32,256]{3,2,1,0:T(8,128)(2,1)}, u32[]{:S(2)}) %copy-start.1) | copy-done | bytes 131096
  51.0 0.0 copy-start.3
  51.0 0.7 copy-done.3
  51.7 0.0 copy-start.4
  51.7 0.7 copy-done.4
  52.4 4.7 %shard_map.94 = (bf16[128,256]{1,0:T(8,128)(2,1)}, bf16[256,256]{1,0:T(8,128)(2,1)}, f32[1,256]{1,0:T(1,128)S(1)}, bf16[2,9,288,256]{3,2,1,0:T(8,128)(2,1)S(1)}) custom-call(s32[2]{0:T(128)S(1)} %pad_add_fusion.place, bf16[2,2,64,256]{3,2,1,0:T(8,128)(2,1)S(1)} %get-tuple-element.17.planes, bf16[2,2,32,256]{3,2,1,0:T(8,128)(2,1)S(1)} %get-tuple-element.22.cached, ...), custom_call_target="tpu_custom_call" | custom-call | flops 452984832 | bytes 3538944 | tf_op jit(solution)/shard_map/pallas_call | solution.py:425
  57.0 0.0 copy-start.5
  57.0 1.5 %copy-done.5 = bf16[2,9,288,256]{3,2,1,0:T(8,128)(2,1)} copy-done((bf16[2,9,288,256]{3,2,1,0:T(8,128)(2,1)}, bf16[2,9,288,256]{3,2,1,0:T(8,128)(2,1)S(1)}, u32[]{:S(2)}) %copy-start.5) | copy-done | bytes 2654232
  58.6 3.6 %all-to-all-start.1 = ((bf16[8,16,256]{2,1,0:T(8,128)(2,1)}), bf16[8,16,256]{2,1,0:T(8,128)(2,1)S(1)}, u32[]{:S(2)}, u32[]{:S(2)}) async-start(bf16[8,16,256]{2,1,0:T(8,128)(2,1)} %bitcast.6), calls=%async_computation.1 | async-start | bytes 131072 | tf_op jit(solution)/shard_map/all_to_all | solution.py:445
  62.1 0.0 collective-permute-done.7.refs_1_
  62.1 0.0 collective-permute-done.13.refs_7_
  62.1 0.0 collective-permute-done.11.refs_5_
  62.1 0.0 collective-permute-done.9.refs_3_
  62.2 0.0 copy-start.6
  62.2 1.7 %copy-done.6 = bf16[2,9,288,256]{3,2,1,0:T(8,128)(2,1)S(1)} copy-done((bf16[2,9,288,256]{3,2,1,0:T(8,128)(2,1)S(1)}, bf16[2,9,288,256]{3,2,1,0:T(8,128)(2,1)}, u32[]{:S(2)}) %copy-start.6) | copy-done | bytes 2654232
  63.9 4.1 %shard_map.95 = f32[27,64,256]{2,1,0:T(8,128)} custom-call(s32[2]{0:T(128)S(1)} %pad_add_fusion.place, bf16[2,9,288,256]{3,2,1,0:T(8,128)(2,1)S(1)} %copy-done.6, bf16[4,2,64,128]{3,2,1,0:T(8,128)(2,1)S(1)} %get-tuple-element.27.refs_0_, bf16[4,2,64,128]{3,2,1,0:T(8,128)(2,1)S(1)} %collective-permute-done.7.refs_1_, ...), custom_call_target="tpu_custom_call" | custom-call | flops 1811939328 | bytes 3538944 | tf_op jit(solution)/shard_map/pallas_call | solution.py:450
  68.0 1.1 %all-to-all-done.1 = bf16[8,16,256]{2,1,0:T(8,128)(2,1)S(1)} async-done(((bf16[8,16,256]{2,1,0:T(8,128)(2,1)}), bf16[8,16,256]{2,1,0:T(8,128)(2,1)S(1)}, u32[]{:S(2)}, u32[]{:S(2)}) %all-to-all-start.1) | async-done | bytes 65568 | tf_op jit(solution)/shard_map/all_to_all | solution.py:445
  69.1 0.1 collective-permute-start.16
  69.1 0.7 %collective-permute-start.15 = (f32[1,256]{1,0:T(1,128)S(1)}, f32[1,256]{1,0:T(1,128)S(1)}, u32[]{:S(2)}, u32[]{:S(2)}) collective-permute-start(f32[1,256]{1,0:T(1,128)S(1)} %bitcast.25), channel_id=1, source_target_pairs={{0,2},{1,3},{2,0},{3,1},{4,6},{5,7},{6,4},{7,5},{8,10},{9,11},{10,... | collective-permute-start | bytes 3080 | tf_op jit(solution)/shard_map/ppermute | solution.py:112
  69.9 1.1 %collective-permute-start.14 = (f32[1,256]{1,0:T(1,128)S(1)}, f32[1,256]{1,0:T(1,128)S(1)}, u32[]{:S(2)}, u32[]{:S(2)}) collective-permute-start(f32[1,256]{1,0:T(1,128)S(1)} %bitcast.26), channel_id=1, source_target_pairs={{0,1},{1,0},{2,3},{3,2},{4,5},{5,4},{6,7},{7,6},{8,9},{9,8},{10,11... | collective-permute-start | bytes 3080 | tf_op jit(solution)/shard_map/ppermute | solution.py:112
  71.0 0.6 fusion.2
  71.6 0.6 copy.13
  72.2 0.0 collective-permute-done.16
  72.2 0.5 collective-permute-done.15
  72.8 0.0 collective-permute-done.14
  72.8 0.6 fusion.1
  (3 shorter events, 0.0 us)
Async XLA Ops:
  2.1 16.2 %all-to-all-start = ((bf16[8,64,256]{2,1,0:T(8,128)(2,1)}), bf16[8,64,256]{2,1,0:T(8,128)(2,1)S(1)}, u32[]{:S(2)}, u32[]{:S(2)}) async-start(bf16[8,64,256]{2,1,0:T(8,128)(2,1)} %broadcast_in_dim.8), calls=%async_computation | async-start | bytes 524288 | tf_op jit(solution)/shard_map/all_to_all | solution.py:394
  18.3 12.1 %collective-permute-start.5 = (bf16[8,64,256]{2,1,0:T(8,128)(2,1)S(1)}, bf16[8,64,256]{2,1,0:T(8,128)(2,1)S(1)}, u32[]{:S(2)}, u32[]{:S(2)}) collective-permute-start(bf16[8,64,256]{2,1,0:T(8,128)(2,1)S(1)} %all-to-all-done.refs_0_), channel_id=1, source_target_pairs={{0,2},{1,3},{2,0},{3,1},{4,6},{5,7},{6,4},{7,5},{8,10},{9,11},{10,... | collective-permute-start | bytes 786440 | tf_op jit(solution)/shard_map/ppermute | solution.py:112
  19.9 0.9 %copy-start = (bf16[4,2,32,256]{3,2,1,0:T(8,128)(2,1)S(1)}, bf16[4,2,32,256]{3,2,1,0:T(8,128)(2,1)}, u32[]{:S(2)}) copy-start(bf16[4,2,32,256]{3,2,1,0:T(8,128)(2,1)} %param.5) | copy-start | bytes 393220
  20.8 0.7 copy-start.2
  22.5 5.9 %collective-permute-start = (bf16[384,128]{1,0:T(8,128)(2,1)S(1)}, bf16[384,128]{1,0:T(8,128)(2,1)S(1)}, u32[]{:S(2)}, u32[]{:S(2)}) collective-permute-start(bf16[384,128]{1,0:T(8,128)(2,1)S(1)} %get-tuple-element.19), channel_id=1, source_target_pairs={{0,1},{1,0},{2,3},{3,2},{4,5},{5,4},{6,7},{7,6},{8,9},{9,8},{10,11... | collective-permute-start | bytes 294920 | tf_op jit(solution)/shard_map/ppermute | solution.py:112
  22.6 5.9 %collective-permute-start.2 = (bf16[384,128]{1,0:T(8,128)(2,1)S(1)}, bf16[384,128]{1,0:T(8,128)(2,1)S(1)}, u32[]{:S(2)}, u32[]{:S(2)}) collective-permute-start(bf16[384,128]{1,0:T(8,128)(2,1)S(1)} %get-tuple-element.21), channel_id=1, source_target_pairs={{0,3},{1,2},{2,1},{3,0},{4,7},{5,6},{6,5},{7,4},{8,11},{9,10},{10,... | collective-permute-start | bytes 294920 | tf_op jit(solution)/shard_map/ppermute | solution.py:112
  23.2 5.2 %collective-permute-start.1 = (bf16[128,128]{1,0:T(8,128)(2,1)S(1)}, bf16[128,128]{1,0:T(8,128)(2,1)S(1)}, u32[]{:S(2)}, u32[]{:S(2)}) collective-permute-start(bf16[128,128]{1,0:T(8,128)(2,1)S(1)} %get-tuple-element.20), channel_id=1, source_target_pairs={{0,2},{1,3},{2,0},{3,1},{4,6},{5,7},{6,4},{7,5},{8,10},{9,11},{10,... | collective-permute-start | bytes 98312 | tf_op jit(solution)/shard_map/ppermute | solution.py:112
  24.8 24.5 %collective-permute-start.4 = (bf16[8,64,256]{2,1,0:T(8,128)(2,1)S(1)}, bf16[8,64,256]{2,1,0:T(8,128)(2,1)S(1)}, u32[]{:S(2)}, u32[]{:S(2)}) collective-permute-start(bf16[8,64,256]{2,1,0:T(8,128)(2,1)S(1)} %all-to-all-done.refs_0_), channel_id=1, source_target_pairs={{0,1},{1,0},{2,3},{3,2},{4,5},{5,4},{6,7},{7,6},{8,9},{9,8},{10,11... | collective-permute-start | bytes 786440 | tf_op jit(solution)/shard_map/ppermute | solution.py:112
  29.1 6.5 %collective-permute-start.3 = (bf16[2,96,256]{2,1,0:T(8,128)(2,1)S(1)}, bf16[2,96,256]{2,1,0:T(8,128)(2,1)S(1)}, u32[]{:S(2)}, u32[]{:S(2)}) collective-permute-start(bf16[2,96,256]{2,1,0:T(8,128)(2,1)S(1)} %get-tuple-element.23), channel_id=1, source_target_pairs={{4,0},{8,4},{12,8},{16,12},{20,16},{24,20},{28,24},{5,1},{9,5},{13... | collective-permute-start | bytes 294920 | tf_op jit(solution)/shard_map/ppermute | solution.py:18
  30.4 19.7 %collective-permute-start.6 = (bf16[8,64,256]{2,1,0:T(8,128)(2,1)S(1)}, bf16[8,64,256]{2,1,0:T(8,128)(2,1)S(1)}, u32[]{:S(2)}, u32[]{:S(2)}) collective-permute-start(bf16[8,64,256]{2,1,0:T(8,128)(2,1)S(1)} %collective-permute-done.5.refs_2_), channel_id=1, source_target_pairs={{0,1},{1,0},{2,3},{3,2},{4,5},{5,4},{6,7},{7,6},{8,9},{9,8},{10,11... | collective-permute-start | bytes 786440 | tf_op jit(solution)/shard_map/ppermute | solution.py:112
  30.4 9.2 %collective-permute-start.12 = (bf16[4,2,64,128]{3,2,1,0:T(8,128)(2,1)S(1)}, bf16[4,2,64,128]{3,2,1,0:T(8,128)(2,1)S(1)}, u32[]{:S(2)}, u32[]{:S(2)}) collective-permute-start(bf16[4,2,64,128]{3,2,1,0:T(8,128)(2,1)S(1)} %get-tuple-element.27.refs_0_), channel_id=1, source_target_pairs={{0,24},{4,28},{8,16},{12,20},{16,8},{20,12},{24,0},{28,4},{1,25},{... | collective-permute-start | bytes 393224 | tf_op jit(solution)/shard_map/ppermute | solution.py:112
  33.1 14.0 %collective-permute-start.10 = (bf16[4,2,64,128]{3,2,1,0:T(8,128)(2,1)S(1)}, bf16[4,2,64,128]{3,2,1,0:T(8,128)(2,1)S(1)}, u32[]{:S(2)}, u32[]{:S(2)}) collective-permute-start(bf16[4,2,64,128]{3,2,1,0:T(8,128)(2,1)S(1)} %get-tuple-element.27.refs_0_), channel_id=1, source_target_pairs={{0,16},{4,20},{8,24},{12,28},{16,0},{20,4},{24,8},{28,12},{1,17},{... | collective-permute-start | bytes 393224 | tf_op jit(solution)/shard_map/ppermute | solution.py:112
  35.6 12.5 %collective-permute-start.8 = (bf16[4,2,64,128]{3,2,1,0:T(8,128)(2,1)S(1)}, bf16[4,2,64,128]{3,2,1,0:T(8,128)(2,1)S(1)}, u32[]{:S(2)}, u32[]{:S(2)}) collective-permute-start(bf16[4,2,64,128]{3,2,1,0:T(8,128)(2,1)S(1)} %get-tuple-element.27.refs_0_), channel_id=1, source_target_pairs={{0,8},{4,12},{8,0},{12,4},{16,24},{20,28},{24,16},{28,20},{1,9},{5... | collective-permute-start | bytes 393224 | tf_op jit(solution)/shard_map/ppermute | solution.py:112
  39.6 22.5 %collective-permute-start.7 = (bf16[4,2,64,128]{3,2,1,0:T(8,128)(2,1)S(1)}, bf16[4,2,64,128]{3,2,1,0:T(8,128)(2,1)S(1)}, u32[]{:S(2)}, u32[]{:S(2)}) collective-permute-start(bf16[4,2,64,128]{3,2,1,0:T(8,128)(2,1)S(1)} %get-tuple-element.27.refs_0_), channel_id=1, source_target_pairs={{0,4},{4,0},{8,12},{12,8},{16,20},{20,16},{24,28},{28,24},{1,5},{5... | collective-permute-start | bytes 393224 | tf_op jit(solution)/shard_map/ppermute | solution.py:112
  47.2 15.0 %collective-permute-start.13 = (bf16[4,2,64,128]{3,2,1,0:T(8,128)(2,1)S(1)}, bf16[4,2,64,128]{3,2,1,0:T(8,128)(2,1)S(1)}, u32[]{:S(2)}, u32[]{:S(2)}) collective-permute-start(bf16[4,2,64,128]{3,2,1,0:T(8,128)(2,1)S(1)} %collective-permute-done.12.refs_6_), channel_id=1, source_target_pairs={{0,4},{4,0},{8,12},{12,8},{16,20},{20,16},{24,28},{28,24},{1,5},{5... | collective-permute-start | bytes 393224 | tf_op jit(solution)/shard_map/ppermute | solution.py:112
  48.0 14.1 %collective-permute-start.11 = (bf16[4,2,64,128]{3,2,1,0:T(8,128)(2,1)S(1)}, bf16[4,2,64,128]{3,2,1,0:T(8,128)(2,1)S(1)}, u32[]{:S(2)}, u32[]{:S(2)}) collective-permute-start(bf16[4,2,64,128]{3,2,1,0:T(8,128)(2,1)S(1)} %collective-permute-done.10.refs_4_), channel_id=1, source_target_pairs={{0,4},{4,0},{8,12},{12,8},{16,20},{20,16},{24,28},{28,24},{1,5},{5... | collective-permute-start | bytes 393224 | tf_op jit(solution)/shard_map/ppermute | solution.py:112
  49.3 12.9 %collective-permute-start.9 = (bf16[4,2,64,128]{3,2,1,0:T(8,128)(2,1)S(1)}, bf16[4,2,64,128]{3,2,1,0:T(8,128)(2,1)S(1)}, u32[]{:S(2)}, u32[]{:S(2)}) collective-permute-start(bf16[4,2,64,128]{3,2,1,0:T(8,128)(2,1)S(1)} %collective-permute-done.8.refs_2_), channel_id=1, source_target_pairs={{0,4},{4,0},{8,12},{12,8},{16,20},{20,16},{24,28},{28,24},{1,5},{5... | collective-permute-start | bytes 393224 | tf_op jit(solution)/shard_map/ppermute | solution.py:112
  50.1 0.9 %copy-start.1 = (bf16[4,2,32,256]{3,2,1,0:T(8,128)(2,1)S(1)}, bf16[4,2,32,256]{3,2,1,0:T(8,128)(2,1)}, u32[]{:S(2)}) copy-start(bf16[4,2,32,256]{3,2,1,0:T(8,128)(2,1)} %param.5) | copy-start | bytes 393220
  51.0 0.7 copy-start.3
  51.7 0.7 copy-start.4
  57.0 1.5 %copy-start.5 = (bf16[2,9,288,256]{3,2,1,0:T(8,128)(2,1)}, bf16[2,9,288,256]{3,2,1,0:T(8,128)(2,1)S(1)}, u32[]{:S(2)}) copy-start(bf16[2,9,288,256]{3,2,1,0:T(8,128)(2,1)S(1)} %get-tuple-element.26.grads) | copy-start | bytes 7962628
  58.6 10.5 %all-to-all-start.1 = ((bf16[8,16,256]{2,1,0:T(8,128)(2,1)}), bf16[8,16,256]{2,1,0:T(8,128)(2,1)S(1)}, u32[]{:S(2)}, u32[]{:S(2)}) async-start(bf16[8,16,256]{2,1,0:T(8,128)(2,1)} %bitcast.6), calls=%async_computation.1 | async-start | bytes 131072 | tf_op jit(solution)/shard_map/all_to_all | solution.py:445
  62.2 1.8 %copy-start.6 = (bf16[2,9,288,256]{3,2,1,0:T(8,128)(2,1)S(1)}, bf16[2,9,288,256]{3,2,1,0:T(8,128)(2,1)}, u32[]{:S(2)}) copy-start(bf16[2,9,288,256]{3,2,1,0:T(8,128)(2,1)} %copy-done.5) | copy-start | bytes 7962628
  69.1 3.2 %collective-permute-start.16 = (f32[1,256]{1,0:T(1,128)S(1)}, f32[1,256]{1,0:T(1,128)S(1)}, u32[]{:S(2)}, u32[]{:S(2)}) collective-permute-start(f32[1,256]{1,0:T(1,128)S(1)} %bitcast.24), channel_id=1, source_target_pairs={{0,3},{1,2},{2,1},{3,0},{4,7},{5,6},{6,5},{7,4},{8,11},{9,10},{10,... | collective-permute-start | bytes 3080 | tf_op jit(solution)/shard_map/ppermute | solution.py:112
  69.1 3.6 %collective-permute-start.15 = (f32[1,256]{1,0:T(1,128)S(1)}, f32[1,256]{1,0:T(1,128)S(1)}, u32[]{:S(2)}, u32[]{:S(2)}) collective-permute-start(f32[1,256]{1,0:T(1,128)S(1)} %bitcast.25), channel_id=1, source_target_pairs={{0,2},{1,3},{2,0},{3,1},{4,6},{5,7},{6,4},{7,5},{8,10},{9,11},{10,... | collective-permute-start | bytes 3080 | tf_op jit(solution)/shard_map/ppermute | solution.py:112
  69.9 2.9 %collective-permute-start.14 = (f32[1,256]{1,0:T(1,128)S(1)}, f32[1,256]{1,0:T(1,128)S(1)}, u32[]{:S(2)}, u32[]{:S(2)}) collective-permute-start(f32[1,256]{1,0:T(1,128)S(1)} %bitcast.26), channel_id=1, source_target_pairs={{0,1},{1,0},{2,3},{3,2},{4,5},{5,4},{6,7},{7,6},{8,9},{9,8},{10,11... | collective-permute-start | bytes 3080 | tf_op jit(solution)/shard_map/ppermute | solution.py:112

commit v2 on v1

--- a/solution.py
+++ b/solution.py
@@ -9,7 +9,9 @@
 
 EPS = 1e-06
 TAPS = [(a, b, c) for a in range(3) for b in range(3) for c in range(3)]
-VMEM_LIMIT = 48 * 1024 * 1024
+VMEM_LIMIT = 20 * 1024 * 1024
+VMEM_LIMIT_WIDE = 48 * 1024 * 1024
+WORK = 1200
 
 
 def shifted(value, axis, steps):
@@ -139,19 +141,13 @@
     return inv_rms, unit, unit * gain
 
 
-def hidden_kernel(F, J, T, place, frames_hbm, gain_hbm, planes, *rest):
-    sends, (frames, gain, tmp, sem) = rest[:T], rest[T:]
-    copies = [
-        pltpu.make_async_copy(frames_hbm, frames, sem.at[0]),
-        pltpu.make_async_copy(gain_hbm, gain, sem.at[1]),
-    ]
-    for copy in copies:
-        copy.start()
-    for copy in copies:
-        copy.wait()
+def hidden_kernel(F, J, T, place, frames, vectors, planes, frames_copy, vectors_copy, *rest):
+    sends, tmp = rest[:T], rest[T]
+    frames_copy[...] = frames[...]
+    vectors_copy[...] = vectors[...]
     channels = frames.shape[1]
     part = channels // T
-    _, _, normed = normalised(frames[...], gain[...])
+    _, _, normed = normalised(frames[...], vectors[0:1])
     value = normed / (1.0 + jnp.exp(-normed))
     tmp[0] = value[:, : channels // 2]
     tmp[1] = value[:, channels // 2 :]
@@ -190,13 +186,16 @@
             sends[k][rp * F * J : (rp + 1) * F * J] = chosen.astype(jnp.bfloat16)
 
 
-def join_kernel(F, J, T, place, planes, *refs):
-    messages, (joined, cached, under) = refs[:T], refs[T:]
+def join_kernel(F, J, T, place, grad_rows, planes, *refs):
+    messages, (joined, cached, under, _, blocks) = refs[:T], refs[T:]
     span = F * J
     block = place[1]
     for k in range(T):
+        at = pl.multiple_of((block ^ k) * span, 16)
         for rp in range(2):
-            joined[k, rp] = messages[k][rp * span : (rp + 1) * span, :]
+            blocks[rp, pl.ds(at, span), :] = messages[k][rp * span : (rp + 1) * span, :]
+    for rp in range(2):
+        joined[rp] = blocks[rp].T
     for rp in range(2):
         for cp in range(2):
             halves = []
@@ -220,6 +219,14 @@
     return jnp.where(meet(row, col), 1.0, 0.0).astype(jnp.bfloat16)
 
 
+def slice_of(value, block, k, T):
+    part = value.shape[1] // T
+    chosen = value[:, :part]
+    for d in range(1, T):
+        chosen = jnp.where(block == d ^ k, value[:, d * part : (d + 1) * part], chosen)
+    return chosen
+
+
 def shard_order(J, R, moved):
     jl = J // R
     return permutation(
@@ -231,25 +238,20 @@
 
 
 def slab_kernel(
-    F, J, R, T, slot, place, planes, cached, under, weight_hbm, bias_hbm, frames_hbm, gain_hbm, *refs
+    F, J, R, T, slot, place, planes, cached, under, weight_hbm, frames, vectors, *refs
 ):
     gathered = refs[:T]
     out, frames_grad, bias_sum, grads = refs[T : T + 4]
-    weight, bias, frames, gain, ext, tmp, sem = refs[T + 4 :]
+    weight, ext, tmp, sem = refs[T + 4 :]
     row, block = place[0], place[1]
     channels = frames.shape[1]
     span = F * J
+    gain, bias = vectors[0:1], vectors[1:2]
     taps_a = [
         pltpu.make_async_copy(weight_hbm.at[pl.ds(a * 9, 9)], weight.at[pl.ds(a * 9, 9)], sem.at[a])
         for a in range(3)
     ]
-    others = [
-        pltpu.make_async_copy(source, target, sem.at[3 + n])
-        for n, (source, target) in enumerate(
-            ((bias_hbm, bias), (frames_hbm, frames), (gain_hbm, gain))
-        )
-    ]
-    for copy in taps_a + others:
+    for copy in taps_a:
         copy.start()
 
     pair_rows = 2 * R * (J // R)
@@ -269,7 +271,7 @@
                 value = mm(orders[moved], source).astype(jnp.bfloat16)
                 for i in range(R):
                     grads[moved, i + 1, pl.ds(at, 2 * J), :] = value[i * 2 * J : (i + 1) * 2 * J]
-    bias_sum[...] = total
+    bias_sum[...] = slice_of(total, block, 0, T)
 
     rows = (F + 2) * J
     last = lax.broadcasted_iota(jnp.int32, (rows, 1), 0) % J == J - 1
@@ -302,14 +304,12 @@
                 tmp[half, pl.ds((t * 2 + rp) * 2 * J + cp, J, stride=2), :] = value[
                     t * J : (t + 1) * J, lanes
                 ]
-    for copy in others:
-        copy.wait()
     hidden_grad = jnp.concatenate([tmp[0], tmp[1]], axis=1)
-    inv_rms, unit, normed = normalised(frames[...], gain[...])
+    inv_rms, unit, normed = normalised(frames[...], gain)
     sigma = 1.0 / (1.0 + jnp.exp(-normed))
     normed_grad = hidden_grad * sigma * (1.0 + normed * (1.0 - sigma))
     gain_part = jnp.sum(normed_grad * unit, axis=0, keepdims=True)
-    unit_grad = normed_grad * gain[...]
+    unit_grad = normed_grad * gain
     mean = jnp.mean(unit_grad * unit, axis=-1, keepdims=True)
     frames_grad[...] = (inv_rms * (unit_grad - unit * mean)).astype(jnp.bfloat16)
 
@@ -321,9 +321,9 @@
         & (o % slot // jl == s // J)
         & (o // slot * jl + o % jl == s % J),
     )
-    value = mm(order, (latent + bias[...]).astype(jnp.bfloat16))
+    value = mm(order, (latent + bias).astype(jnp.bfloat16))
     line = lax.broadcasted_iota(jnp.int32, (R * slot, 1), 0) % slot
-    rest = gain_part
+    rest = jnp.concatenate([slice_of(gain_part, block, k, T) for k in range(T)], axis=1)
     for n in range(3):
         term = rest.astype(jnp.bfloat16).astype(jnp.float32)
         rest = rest - term
@@ -333,17 +333,17 @@
 
 def weight_kernel(F, J, R, T, part, place, grads, *refs):
     hidden = refs[:R]
-    out, even, odd = refs[R:]
+    out_hbm, out, even, odd, sem = refs[R:]
     channels = grads.shape[-1]
     depth = T * F * J
     lanes = 2 * part
-    row, block = place[0], place[1]
+    row = place[0]
     even[:, R * depth :] = jnp.zeros((lanes, depth), jnp.bfloat16)
     for k in range(R):
         at = pl.multiple_of((row ^ k) * depth, 128)
         for rp, turned in ((0, even), (1, odd)):
-            value = jnp.concatenate([hidden[k][block ^ t, rp] for t in range(T)], axis=0)
-            turned[:, pl.ds(at, depth)] = value.T
+            turned[:, pl.ds(at, depth)] = hidden[k][rp]
+    leaving = []
     for a in range(3):
         start = (2 - a) * J
         for moved in range(2):
@@ -360,17 +360,25 @@
                     for cp in range(2):
                         at = b * lanes + cp * part
                         out[(a * 3 + b) * 3 + cp] = value[at : at + part]
-
-
-def call(kernel, outs, scratch, flops, moved, places):
-    kinds = {"s": pltpu.SMEM, "v": pltpu.VMEM, "a": pl.ANY}
+        taps = pl.ds(a * 9, 9)
+        leaving.append(pltpu.make_async_copy(out.at[taps], out_hbm.at[taps], sem.at[a]))
+        leaving[a].start()
+    for copy in leaving:
+        copy.wait()
+
+
+def call(kernel, outs, scratch, flops, moved, places, aliases={}, limit=VMEM_LIMIT):
+    kinds = {"s": pltpu.SMEM, "v": pltpu.VMEM, "h": pltpu.HBM, "a": pl.ANY}
+    specs = [pl.BlockSpec(memory_space=kinds[p]) for p in places]
+    count = len(places) - len(outs)
     return pl.pallas_call(
         kernel,
         out_shape=[jax.ShapeDtypeStruct(s, d) for s, d in outs],
-        in_specs=[pl.BlockSpec(memory_space=kinds[p]) for p in places],
-        out_specs=[pl.BlockSpec(memory_space=pltpu.VMEM)] * len(outs),
+        in_specs=specs[:count],
+        out_specs=specs[count:],
         scratch_shapes=scratch,
-        compiler_params=pltpu.CompilerParams(vmem_limit_bytes=VMEM_LIMIT),
+        input_output_aliases=aliases,
+        compiler_params=pltpu.CompilerParams(vmem_limit_bytes=limit),
         cost_estimate=pl.CostEstimate(flops=flops, bytes_accessed=moved, transcendentals=0),
     )
 
@@ -384,8 +392,7 @@
     part = C // T
     used = span // R
     slot = -(-(used + 3) // 16) * 16
-    gain = norm_gain.reshape(1, C)
-    bias = conv_bias.reshape(1, C)
+    vectors = jnp.stack([norm_gain, conv_bias])
     flat = frames.reshape(-1, C)
     weight = conv_weight.reshape(27, C, C)
     place = jnp.stack([lax.axis_index("rows"), lax.axis_index("tm")]).astype(jnp.int32)
@@ -396,28 +403,25 @@
     )
 
     sizes = [(2 * span + (16 * J if k % 2 else 0), 2 * part) for k in range(T)]
-    planes, *sends = call(
+    planes, frames_copy, vectors, *sends = call(
         functools.partial(hidden_kernel, F, J, T),
-        [((2, 2, span, C), bf16)] + [(size, bf16) for size in sizes],
-        [
-            pltpu.VMEM((4 * span, C), bf16),
-            pltpu.VMEM((1, C), f32),
-            pltpu.VMEM((2, 4 * span, C // 2), f32),
-            pltpu.SemaphoreType.DMA((2,)),
-        ],
-        10 * 4 * span * C, 16 * span * C, "saa",
-    )(place, flat, gain)
+        [((2, 2, span, C), bf16), (flat.shape, bf16), ((2, C), f32)]
+        + [(size, bf16) for size in sizes],
+        [pltpu.VMEM((2, 4 * span, C // 2), f32)],
+        60 * WORK * span * C, 16 * span * C, "svv" + "v" * (T + 3),
+    )(place, flat, vectors)
     messages = [sends[0]] + [partners(sends[k], "tm", k) for k in range(1, T)]
-    joined, cached, under = call(
+    joined, cached, under, grad_rows = call(
         functools.partial(join_kernel, F, J, T),
         [
-            ((T, 2, span, 2 * part), bf16),
+            ((2, 2 * part, T * span), bf16),
             ((2, 2, 2 * J, C), bf16),
             ((2, 2 * J + span, C), bf16),
+            (grad_rows.shape, bf16),
         ],
-        [],
-        4 * span * C, 16 * span * C, "sv" + "v" * T,
-    )(place, planes, *messages)
+        [pltpu.VMEM((2, T * span, 2 * part), bf16)],
+        30 * WORK * span * C, 16 * span * C, "sav" + "v" * T + "vvva", {1: 3},
+    )(place, grad_rows, planes, *messages)
     under = shifted(under, "rows", -1)
     hidden_all = exchanged(joined, "rows")
     grad_all = exchanged(grad_rows, "tm")
@@ -427,45 +431,44 @@
         [
             ((R * slot, C), bf16),
             ((4 * span, C), bf16),
-            ((1, C), f32),
+            ((1, part), f32),
             ((2, R + 1, (F * T + 2) * J, C), bf16),
         ],
         [
             pltpu.VMEM((27, C, C), bf16),
-            pltpu.VMEM((1, C), f32),
-            pltpu.VMEM((4 * span, C), bf16),
-            pltpu.VMEM((1, C), f32),
             pltpu.VMEM((3, 3, (F + 2) * J, C), bf16),
             pltpu.VMEM((2, 4 * span, C // 2), f32),
-            pltpu.SemaphoreType.DMA((6,)),
+            pltpu.SemaphoreType.DMA((3,)),
         ],
-        4 * 27 * span * C * C, 2 * 27 * C * C, "svvvaaaa" + "v" * T,
-    )(place, planes, cached, under, weight, bias, flat, gain, *grad_all)
+        270 * WORK * span * C, 2 * 27 * C * C, "svvvhvv" + "v" * (T + 4),
+        limit=VMEM_LIMIT_WIDE,
+    )(place, planes, cached, under, weight, frames_copy, vectors, *grad_all)
 
     packed = lax.all_to_all(packed.reshape(R, slot, C), "rows", 0, 0, tiled=True)
     latent = packed[:, :used].reshape(R, F, J // R, C).transpose(1, 0, 2, 3)
     gain_sum = jnp.sum(packed[:, used : used + 3].astype(f32), axis=(0, 1)).reshape(1, C)
-    gain_sum = sum(partners(gain_sum, "tm", k) for k in range(1, T)) + gain_sum
+    gain_grad = gain_sum[:, :part]
+    for k in range(1, T):
+        gain_grad = gain_grad + partners(gain_sum[:, k * part : (k + 1) * part], "tm", k)
 
     (weight_grad,) = call(
         functools.partial(weight_kernel, F, J, R, T, part),
         [((27, part, C), f32)],
         [
+            pltpu.VMEM((27, part, C), f32),
             pltpu.VMEM((2 * part, (R + 1) * T * span), bf16),
             pltpu.VMEM((2 * part, R * T * span), bf16),
+            pltpu.SemaphoreType.DMA((3,)),
         ],
-        2 * 27 * R * T * span * part * C, 8 * 27 * part * C, "sv" + "v" * R,
+        220 * WORK * span * C, 8 * 27 * part * C, "sv" + "v" * R + "h",
     )(place, grads, *hidden_all)
 
-    start = lax.axis_index("tm") * part
-    gain_grad = lax.dynamic_slice(gain_sum.reshape(C), (start,), (part,))
-    bias_grad = lax.dynamic_slice(bias_sum.reshape(C), (start,), (part,))
     return (
         latent,
         frames_grad.reshape(frames.shape),
         weight_grad.reshape(3, 3, 3, part, C),
-        gain_grad,
-        bias_grad,
+        gain_grad.reshape(part),
+        bias_sum.reshape(part),
     )
 
 

time: 73.9 us -> 72.4 us (0.980)
  waiting for transfers between devices: 17.6 us -> 26 us
  starting transfers between devices: 34.1 us -> 27.2 us
  local copies, waits for them, and re-layouts: 9.84 us -> 6.39 us
    ppermute x16, waiting for transfers between devices: 7.57 us -> 23.6 us  [partners(): lax.ppermute(value, axis, [(source, source ^ bits) for source in range(co...]
    all_to_all x1, waiting for transfers between devices: 8.92 us -> 0.43 us  [gathered_form(): lax.all_to_all(jnp.broadcast_to(own, (R,) + own.shape[1:]), 'rows', 0, 0,...]
    ppermute x16, starting transfers between devices: 22 us -> 15.3 us  [partners(): lax.ppermute(value, axis, [(source, source ^ bits) for source in range(co...]
    unnamed x16 -> x8, local copies, waits for them, and re-layouts: 7.76 us -> 4.81 us
  transfers between devices with their start and end apart: 19 -> 19, of which waited for: 6 -> 9; matrix products, arithmetic and copies ran while one was open for 2% -> 2% of each run, Pallas kernels for 14% -> 13%
where the time goes in v2:
time: 72.4 us; the launch traced here: 71.9 us
  starting transfers between devices  27.2 us (38%)
  waiting for transfers between devices  26 us (36%)
  Pallas kernels  10.2 us (14%)
  local copies, waits for them, and re-layouts  6.39 us (9%)
  other arithmetic  1.32 us (2%)
  between operations  0.77 us (1%)
    ppermute x16, waiting for transfers between devices, partners(): lax.ppermute(value, axis, [(source, source ^ bits) for source in range(co...  23.6 us
    ppermute x16, starting transfers between devices, partners(): lax.ppermute(value, axis, [(source, source ^ bits) for source in range(co...  15.3 us
    all_to_all x1, starting transfers between devices, gathered_form(): lax.all_to_all(jnp.broadcast_to(own, (R,) + own.shape[1:]), 'rows', 0, 0,...  7.25 us
    pallas_call x1, Pallas kernels, gathered_form(): call(functools.partial(slab_kernel, F, J, R, T, slot), [((R * slot, C), b...  5.31 us
    unnamed x8, local copies, waits for them, and re-layouts  4.81 us
    pallas_call x1, Pallas kernels, gathered_form(): call(functools.partial(weight_kernel, F, J, R, T, part), [((27, part, C),...  3.43 us
    all_to_all x1, starting transfers between devices, gathered_form(): lax.all_to_all(packed.reshape(R, slot, C), 'rows', 0, 0, tiled=True)  3.35 us
    all_to_all x1, waiting for transfers between devices, gathered_form(): lax.all_to_all(packed.reshape(R, slot, C), 'rows', 0, 0, tiled=True)  1.62 us
  transfers between devices with their start and end apart: 19, of which 9 were waited for; matrix products, arithmetic and copies ran while one was open for 2% of the time, Pallas kernels for 13%

profile of v2, /device:TPU:0, one launch (start us, length us, event | category | flops | bytes accessed | tf_op | source)
XLA Modules:
  0.0 71.9 jit_solution(14864543789225376398)
XLA Ops:
  0.6 0.8 %broadcast_in_dim.7 = bf16[64,256]{1,0:T(8,128)(2,1)S(1)} reshape(bf16[4,8,2,256]{3,2,1,0:T(2,128)(2,1)} %param.9) | data formatting | bytes 65536 | tf_op jit(solution)/shard_map/broadcast_in_dim | solution.py:402
  1.4 0.7 %broadcast_in_dim.8 = bf16[8,64,256]{2,1,0:T(8,128)(2,1)} broadcast(bf16[64,256]{1,0:T(8,128)(2,1)S(1)} %broadcast_in_dim.7), dimensions={1,2} | broadcast | bytes 294912 | tf_op jit(solution)/shard_map/broadcast_in_dim | solution.py:402
  2.1 7.3 %all-to-all-start = ((bf16[8,64,256]{2,1,0:T(8,128)(2,1)}), bf16[8,64,256]{2,1,0:T(8,128)(2,1)S(1)}, u32[]{:S(2)}, u32[]{:S(2)}) async-start(bf16[8,64,256]{2,1,0:T(8,128)(2,1)} %broadcast_in_dim.8), calls=%async_computation | async-start | bytes 524288 | tf_op jit(solution)/shard_map/all_to_all | solution.py:401
  9.4 0.1 pad_add_fusion.place
  9.5 0.7 pad_maximum_fusion.vectors
  10.2 0.0 copy-start
  10.2 0.9 %copy-done = bf16[4,2,32,256]{3,2,1,0:T(8,128)(2,1)S(1)} copy-done((bf16[4,2,32,256]{3,2,1,0:T(8,128)(2,1)S(1)}, bf16[4,2,32,256]{3,2,1,0:T(8,128)(2,1)}, u32[]{:S(2)}) %copy-start) | copy-done | bytes 131096
  11.1 0.8 %shard_map.92 = (bf16[2,2,64,256]{3,2,1,0:T(8,128)(2,1)S(1)}, bf16[256,256]{1,0:T(8,128)(2,1)S(1)}, f32[2,256]{1,0:T(2,128)S(1)}, bf16[128,128]{1,0:T(8,128)(2,1...) custom-call(s32[2]{0:T(128)S(1)} %pad_add_fusion.place, ...), custom_call_target="tpu_custom_call" | custom-call | flops 1179648000 | bytes 262144 | tf_op jit(solution)/shard_map/pallas_call | solution.py:406
  11.9 0.1 collective-permute-start
  12.0 1.6 %collective-permute-start.2 = (bf16[384,128]{1,0:T(8,128)(2,1)S(1)}, bf16[384,128]{1,0:T(8,128)(2,1)S(1)}, u32[]{:S(2)}, u32[]{:S(2)}) collective-permute-start(bf16[384,128]{1,0:T(8,128)(2,1)S(1)} %get-tuple-element.24), channel_id=1, source_target_pairs={{0,3},{1,2},{2,1},{3,0},{4,7},{5,6},{6,5},{7,4},{8,11},{9,10},{10,... | collective-permute-start | bytes 294920 | tf_op jit(solution)/shard_map/ppermute | solution.py:114
  13.6 0.5 collective-permute-start.1
  14.1 3.7 %collective-permute-done.1.refs_2_ = bf16[128,128]{1,0:T(8,128)(2,1)S(1)} collective-permute-done((bf16[128,128]{1,0:T(8,128)(2,1)S(1)}, bf16[128,128]{1,0:T(8,128)(2,1)S(1)}, u32[]{:S(2)}, u32[]{:S(2)}) %collective-permute-start.1) | collective-permute-done | bytes 32800 | tf_op jit(solution)/shard_map/ppermute | solution.py:114
  17.9 0.0 collective-permute-done.refs_1_
  17.9 0.0 collective-permute-done.2.refs_3_
  17.9 0.4 all-to-all-done.grad_rows
  18.3 0.6 shard_map.93
  18.9 1.6 %collective-permute-start.5 = (bf16[8,64,256]{2,1,0:T(8,128)(2,1)S(1)}, bf16[8,64,256]{2,1,0:T(8,128)(2,1)S(1)}, u32[]{:S(2)}, u32[]{:S(2)}) collective-permute-start(bf16[8,64,256]{2,1,0:T(8,128)(2,1)S(1)} %get-tuple-element.29.refs_0_), channel_id=1, source_target_pairs={{0,2},{1,3},{2,0},{3,1},{4,6},{5,7},{6,4},{7,5},{8,10},{9,11},{10,... | collective-permute-start | bytes 786440 | tf_op jit(solution)/shard_map/ppermute | solution.py:114
  20.5 0.0 collective-permute-start.4
  20.5 6.0 %collective-permute-done.5.refs_2_ = bf16[8,64,256]{2,1,0:T(8,128)(2,1)S(1)} collective-permute-done((bf16[8,64,256]{2,1,0:T(8,128)(2,1)S(1)}, bf16[8,64,256]{2,1,0:T(8,128)(2,1)S(1)}, u32[]{:S(2)}, u32[]{:S(2)}) %collective-permute-start.5) | collective-permute-done | bytes 262176 | tf_op jit(solution)/shard_map/ppermute | solution.py:114
  26.6 0.0 collective-permute-start.6
  26.6 1.3 %collective-permute-start.3 = (bf16[2,96,256]{2,1,0:T(8,128)(2,1)S(1)}, bf16[2,96,256]{2,1,0:T(8,128)(2,1)S(1)}, u32[]{:S(2)}, u32[]{:S(2)}) collective-permute-start(bf16[2,96,256]{2,1,0:T(8,128)(2,1)S(1)} %get-tuple-element.26), channel_id=1, source_target_pairs={{4,0},{8,4},{12,8},{16,12},{20,16},{24,20},{28,24},{5,1},{9,5},{13... | collective-permute-start | bytes 294920 | tf_op jit(solution)/shard_map/ppermute | solution.py:20
  27.8 5.7 %collective-permute-start.12 = (bf16[2,128,256]{2,1,0:T(8,128)(2,1)S(1)}, bf16[2,128,256]{2,1,0:T(8,128)(2,1)S(1)}, u32[]{:S(2)}, u32[]{:S(2)}) collective-permute-start(bf16[2,128,256]{2,1,0:T(8,128)(2,1)S(1)} %get-tuple-element.33.refs_0_), channel_id=1, source_target_pairs={{0,24},{4,28},{8,16},{12,20},{16,8},{20,12},{24,0},{28,4},{1,25},{... | collective-permute-start | bytes 393224 | tf_op jit(solution)/shard_map/ppermute | solution.py:114
  33.5 0.0 collective-permute-start.10
  33.5 0.4 collective-permute-done.3.under
  33.9 1.6 %collective-permute-start.8 = (bf16[2,128,256]{2,1,0:T(8,128)(2,1)S(1)}, bf16[2,128,256]{2,1,0:T(8,128)(2,1)S(1)}, u32[]{:S(2)}, u32[]{:S(2)}) collective-permute-start(bf16[2,128,256]{2,1,0:T(8,128)(2,1)S(1)} %get-tuple-element.33.refs_0_), channel_id=1, source_target_pairs={{0,8},{4,12},{8,0},{12,4},{16,24},{20,28},{24,16},{28,20},{1,9},{5... | collective-permute-start | bytes 393224 | tf_op jit(solution)/shard_map/ppermute | solution.py:114
  35.5 4.4 %collective-permute-done.12.refs_6_ = bf16[2,128,256]{2,1,0:T(8,128)(2,1)S(1)} collective-permute-done((bf16[2,128,256]{2,1,0:T(8,128)(2,1)S(1)}, bf16[2,128,256]{2,1,0:T(8,128)(2,1)S(1)}, u32[]{:S(2)}, u32[]{:S(2)}) %collective-permute-start.12) | collective-permute-done | bytes 131104 | tf_op jit(solution)/shard_map/ppermute | solution.py:114
  39.9 0.0 collective-permute-start.7
  39.9 7.0 %collective-permute-done.10.refs_4_ = bf16[2,128,256]{2,1,0:T(8,128)(2,1)S(1)} collective-permute-done((bf16[2,128,256]{2,1,0:T(8,128)(2,1)S(1)}, bf16[2,128,256]{2,1,0:T(8,128)(2,1)S(1)}, u32[]{:S(2)}, u32[]{:S(2)}) %collective-permute-start.10) | collective-permute-done | bytes 131104 | tf_op jit(solution)/shard_map/ppermute | solution.py:114
  46.9 0.0 collective-permute-start.13
  47.0 0.0 collective-permute-done.8.refs_2_
  47.0 2.0 %collective-permute-start.11 = (bf16[2,128,256]{2,1,0:T(8,128)(2,1)S(1)}, bf16[2,128,256]{2,1,0:T(8,128)(2,1)S(1)}, u32[]{:S(2)}, u32[]{:S(2)}) collective-permute-start(bf16[2,128,256]{2,1,0:T(8,128)(2,1)S(1)} %collective-permute-done.10.refs_4_), channel_id=1, source_target_pairs={{0,4},{4,0},{8,12},{12,8},{16,20},{20,16},{24,28},{28,24},{1,5},{5... | collective-permute-start | bytes 393224 | tf_op jit(solution)/shard_map/ppermute | solution.py:114
  49.0 0.0 collective-permute-done.4.refs_1_
  49.0 0.1 collective-permute-start.9
  49.1 0.0 collective-permute-done.6.refs_3_
  49.1 5.3 %shard_map.94 = (bf16[128,256]{1,0:T(8,128)(2,1)}, bf16[256,256]{1,0:T(8,128)(2,1)}, f32[1,64]{1,0:T(1,128)}, bf16[2,9,288,256]{3,2,1,0:T(8,128)(2,1)S(1)}) custom-call(s32[2]{0:T(128)S(1)} %pad_add_fusion.place, bf16[2,2,64,256]{3,2,1,0:T(8,128)(2,1)S(1)} %get-tuple-element.20.planes, bf16[2,2,32,256]{3,2,1,0:T(8,128)(2,1)S(1)} %get-tuple-element.25.cached, ...), custom_call_target="tpu_custom_call" | custom-call | flops 5308416000 | bytes 3538944 | tf_op jit(solution)/shard_map/pallas_call | solution.py:429
  54.4 0.0 copy-start.1
  54.4 1.5 %copy-done.1 = bf16[2,9,288,256]{3,2,1,0:T(8,128)(2,1)} copy-done((bf16[2,9,288,256]{3,2,1,0:T(8,128)(2,1)}, bf16[2,9,288,256]{3,2,1,0:T(8,128)(2,1)S(1)}, u32[]{:S(2)}) %copy-start.1) | copy-done | bytes 2654232
  55.9 3.3 %all-to-all-start.1 = ((bf16[8,16,256]{2,1,0:T(8,128)(2,1)}), bf16[8,16,256]{2,1,0:T(8,128)(2,1)S(1)}, u32[]{:S(2)}, u32[]{:S(2)}) async-start(bf16[8,16,256]{2,1,0:T(8,128)(2,1)} %bitcast.6), calls=%async_computation.1 | async-start | bytes 131072 | tf_op jit(solution)/shard_map/all_to_all | solution.py:447
  59.3 0.0 collective-permute-done.7.refs_1_
  59.3 0.0 collective-permute-done.13.refs_7_
  59.3 0.0 collective-permute-done.11.refs_5_
  59.3 0.0 collective-permute-done.9.refs_3_
  59.3 0.0 copy-start.2
  59.3 1.7 %copy-done.2 = bf16[2,9,288,256]{3,2,1,0:T(8,128)(2,1)S(1)} copy-done((bf16[2,9,288,256]{3,2,1,0:T(8,128)(2,1)S(1)}, bf16[2,9,288,256]{3,2,1,0:T(8,128)(2,1)}, u32[]{:S(2)}) %copy-start.2) | copy-done | bytes 2654232
  61.0 3.4 %shard_map.95 = f32[27,64,256]{2,1,0:T(8,128)} custom-call(s32[2]{0:T(128)S(1)} %pad_add_fusion.place, bf16[2,9,288,256]{3,2,1,0:T(8,128)(2,1)S(1)} %copy-done.2, bf16[2,128,256]{2,1,0:T(8,128)(2,1)S(1)} %get-tuple-element.33.refs_0_, bf16[2,128,256]{2,1,0:T(8,128)(2,1)S(1)} %collective-permute-done.7.refs_1_, ...), custom_call_target="tpu_custom_call" | custom-call | flops 4325376000 | bytes 3538944 | tf_op jit(solution)/shard_map/pallas_call | solution.py:454
  64.5 1.6 %all-to-all-done.1 = bf16[8,16,256]{2,1,0:T(8,128)(2,1)S(1)} async-done(((bf16[8,16,256]{2,1,0:T(8,128)(2,1)}), bf16[8,16,256]{2,1,0:T(8,128)(2,1)S(1)}, u32[]{:S(2)}, u32[]{:S(2)}) %all-to-all-start.1) | async-done | bytes 65568 | tf_op jit(solution)/shard_map/all_to_all | solution.py:447
  66.1 0.1 fusion.3
  66.2 0.0 collective-permute-start.14
  66.2 1.6 %collective-permute-start.16 = (f32[1,64]{1,0:T(1,128)S(1)}, f32[1,64]{1,0:T(1,128)S(1)}, u32[]{:S(2)}, u32[]{:S(2)}) collective-permute-start(f32[1,64]{1,0:T(1,128)S(1)} %get-tuple-element.46), channel_id=1, source_target_pairs={{0,3},{1,2},{2,1},{3,0},{4,7},{5,6},{6,5},{7,4},{8,11},{9,10},{10,... | collective-permute-start | bytes 776 | tf_op jit(solution)/shard_map/ppermute | solution.py:114
  67.9 0.5 collective-permute-start.15
  68.4 0.6 copy.14
  69.0 0.0 collective-permute-done.14
  69.0 0.2 collective-permute-done.16
  69.3 2.1 %collective-permute-done.15 = f32[1,64]{1,0:T(1,128)S(1)} collective-permute-done((f32[1,64]{1,0:T(1,128)S(1)}, f32[1,64]{1,0:T(1,128)S(1)}, u32[]{:S(2)}, u32[]{:S(2)}) %collective-permute-start.15) | collective-permute-done | bytes 288 | tf_op jit(solution)/shard_map/ppermute | solution.py:114
  71.4 0.5 fusion.2
  (3 shorter events, 0.0 us)
Async XLA Ops:
  2.1 16.2 %all-to-all-start = ((bf16[8,64,256]{2,1,0:T(8,128)(2,1)}), bf16[8,64,256]{2,1,0:T(8,128)(2,1)S(1)}, u32[]{:S(2)}, u32[]{:S(2)}) async-start(bf16[8,64,256]{2,1,0:T(8,128)(2,1)} %broadcast_in_dim.8), calls=%async_computation | async-start | bytes 524288 | tf_op jit(solution)/shard_map/all_to_all | solution.py:401
  10.2 0.9 %copy-start = (bf16[4,2,32,256]{3,2,1,0:T(8,128)(2,1)S(1)}, bf16[4,2,32,256]{3,2,1,0:T(8,128)(2,1)}, u32[]{:S(2)}) copy-start(bf16[4,2,32,256]{3,2,1,0:T(8,128)(2,1)} %param.5) | copy-start | bytes 393220
  11.9 5.9 %collective-permute-start = (bf16[384,128]{1,0:T(8,128)(2,1)S(1)}, bf16[384,128]{1,0:T(8,128)(2,1)S(1)}, u32[]{:S(2)}, u32[]{:S(2)}) collective-permute-start(bf16[384,128]{1,0:T(8,128)(2,1)S(1)} %get-tuple-element.22), channel_id=1, source_target_pairs={{0,1},{1,0},{2,3},{3,2},{4,5},{5,4},{6,7},{7,6},{8,9},{9,8},{10,11... | collective-permute-start | bytes 294920 | tf_op jit(solution)/shard_map/ppermute | solution.py:114
  12.0 5.9 %collective-permute-start.2 = (bf16[384,128]{1,0:T(8,128)(2,1)S(1)}, bf16[384,128]{1,0:T(8,128)(2,1)S(1)}, u32[]{:S(2)}, u32[]{:S(2)}) collective-permute-start(bf16[384,128]{1,0:T(8,128)(2,1)S(1)} %get-tuple-element.24), channel_id=1, source_target_pairs={{0,3},{1,2},{2,1},{3,0},{4,7},{5,6},{6,5},{7,4},{8,11},{9,10},{10,... | collective-permute-start | bytes 294920 | tf_op jit(solution)/shard_map/ppermute | solution.py:114
  13.6 4.2 %collective-permute-start.1 = (bf16[128,128]{1,0:T(8,128)(2,1)S(1)}, bf16[128,128]{1,0:T(8,128)(2,1)S(1)}, u32[]{:S(2)}, u32[]{:S(2)}) collective-permute-start(bf16[128,128]{1,0:T(8,128)(2,1)S(1)} %get-tuple-element.23), channel_id=1, source_target_pairs={{0,2},{1,3},{2,0},{3,1},{4,6},{5,7},{6,4},{7,5},{8,10},{9,11},{10,... | collective-permute-start | bytes 98312 | tf_op jit(solution)/shard_map/ppermute | solution.py:114
  18.9 7.6 %collective-permute-start.5 = (bf16[8,64,256]{2,1,0:T(8,128)(2,1)S(1)}, bf16[8,64,256]{2,1,0:T(8,128)(2,1)S(1)}, u32[]{:S(2)}, u32[]{:S(2)}) collective-permute-start(bf16[8,64,256]{2,1,0:T(8,128)(2,1)S(1)} %get-tuple-element.29.refs_0_), channel_id=1, source_target_pairs={{0,2},{1,3},{2,0},{3,1},{4,6},{5,7},{6,4},{7,5},{8,10},{9,11},{10,... | collective-permute-start | bytes 786440 | tf_op jit(solution)/shard_map/ppermute | solution.py:114
  20.5 28.4 %collective-permute-start.4 = (bf16[8,64,256]{2,1,0:T(8,128)(2,1)S(1)}, bf16[8,64,256]{2,1,0:T(8,128)(2,1)S(1)}, u32[]{:S(2)}, u32[]{:S(2)}) collective-permute-start(bf16[8,64,256]{2,1,0:T(8,128)(2,1)S(1)} %get-tuple-element.29.refs_0_), channel_id=1, source_target_pairs={{0,1},{1,0},{2,3},{3,2},{4,5},{5,4},{6,7},{7,6},{8,9},{9,8},{10,11... | collective-permute-start | bytes 786440 | tf_op jit(solution)/shard_map/ppermute | solution.py:114
  26.6 22.5 %collective-permute-start.6 = (bf16[8,64,256]{2,1,0:T(8,128)(2,1)S(1)}, bf16[8,64,256]{2,1,0:T(8,128)(2,1)S(1)}, u32[]{:S(2)}, u32[]{:S(2)}) collective-permute-start(bf16[8,64,256]{2,1,0:T(8,128)(2,1)S(1)} %collective-permute-done.5.refs_2_), channel_id=1, source_target_pairs={{0,1},{1,0},{2,3},{3,2},{4,5},{5,4},{6,7},{7,6},{8,9},{9,8},{10,11... | collective-permute-start | bytes 786440 | tf_op jit(solution)/shard_map/ppermute | solution.py:114
  26.6 7.4 %collective-permute-start.3 = (bf16[2,96,256]{2,1,0:T(8,128)(2,1)S(1)}, bf16[2,96,256]{2,1,0:T(8,128)(2,1)S(1)}, u32[]{:S(2)}, u32[]{:S(2)}) collective-permute-start(bf16[2,96,256]{2,1,0:T(8,128)(2,1)S(1)} %get-tuple-element.26), channel_id=1, source_target_pairs={{4,0},{8,4},{12,8},{16,12},{20,16},{24,20},{28,24},{5,1},{9,5},{13... | collective-permute-start | bytes 294920 | tf_op jit(solution)/shard_map/ppermute | solution.py:20
  27.8 12.1 %collective-permute-start.12 = (bf16[2,128,256]{2,1,0:T(8,128)(2,1)S(1)}, bf16[2,128,256]{2,1,0:T(8,128)(2,1)S(1)}, u32[]{:S(2)}, u32[]{:S(2)}) collective-permute-start(bf16[2,128,256]{2,1,0:T(8,128)(2,1)S(1)} %get-tuple-element.33.refs_0_), channel_id=1, source_target_pairs={{0,24},{4,28},{8,16},{12,20},{16,8},{20,12},{24,0},{28,4},{1,25},{... | collective-permute-start | bytes 393224 | tf_op jit(solution)/shard_map/ppermute | solution.py:114
  33.5 13.4 %collective-permute-start.10 = (bf16[2,128,256]{2,1,0:T(8,128)(2,1)S(1)}, bf16[2,128,256]{2,1,0:T(8,128)(2,1)S(1)}, u32[]{:S(2)}, u32[]{:S(2)}) collective-permute-start(bf16[2,128,256]{2,1,0:T(8,128)(2,1)S(1)} %get-tuple-element.33.refs_0_), channel_id=1, source_target_pairs={{0,16},{4,20},{8,24},{12,28},{16,0},{20,4},{24,8},{28,12},{1,17},{... | collective-permute-start | bytes 393224 | tf_op jit(solution)/shard_map/ppermute | solution.py:114
  33.9 13.0 %collective-permute-start.8 = (bf16[2,128,256]{2,1,0:T(8,128)(2,1)S(1)}, bf16[2,128,256]{2,1,0:T(8,128)(2,1)S(1)}, u32[]{:S(2)}, u32[]{:S(2)}) collective-permute-start(bf16[2,128,256]{2,1,0:T(8,128)(2,1)S(1)} %get-tuple-element.33.refs_0_), channel_id=1, source_target_pairs={{0,8},{4,12},{8,0},{12,4},{16,24},{20,28},{24,16},{28,20},{1,9},{5... | collective-permute-start | bytes 393224 | tf_op jit(solution)/shard_map/ppermute | solution.py:114
  39.9 19.3 %collective-permute-start.7 = (bf16[2,128,256]{2,1,0:T(8,128)(2,1)S(1)}, bf16[2,128,256]{2,1,0:T(8,128)(2,1)S(1)}, u32[]{:S(2)}, u32[]{:S(2)}) collective-permute-start(bf16[2,128,256]{2,1,0:T(8,128)(2,1)S(1)} %get-tuple-element.33.refs_0_), channel_id=1, source_target_pairs={{0,4},{4,0},{8,12},{12,8},{16,20},{20,16},{24,28},{28,24},{1,5},{5... | collective-permute-start | bytes 393224 | tf_op jit(solution)/shard_map/ppermute | solution.py:114
  46.9 12.3 %collective-permute-start.13 = (bf16[2,128,256]{2,1,0:T(8,128)(2,1)S(1)}, bf16[2,128,256]{2,1,0:T(8,128)(2,1)S(1)}, u32[]{:S(2)}, u32[]{:S(2)}) collective-permute-start(bf16[2,128,256]{2,1,0:T(8,128)(2,1)S(1)} %collective-permute-done.12.refs_6_), channel_id=1, source_target_pairs={{0,4},{4,0},{8,12},{12,8},{16,20},{20,16},{24,28},{28,24},{1,5},{5... | collective-permute-start | bytes 393224 | tf_op jit(solution)/shard_map/ppermute | solution.py:114
  47.0 12.3 %collective-permute-start.11 = (bf16[2,128,256]{2,1,0:T(8,128)(2,1)S(1)}, bf16[2,128,256]{2,1,0:T(8,128)(2,1)S(1)}, u32[]{:S(2)}, u32[]{:S(2)}) collective-permute-start(bf16[2,128,256]{2,1,0:T(8,128)(2,1)S(1)} %collective-permute-done.10.refs_4_), channel_id=1, source_target_pairs={{0,4},{4,0},{8,12},{12,8},{16,20},{20,16},{24,28},{28,24},{1,5},{5... | collective-permute-start | bytes 393224 | tf_op jit(solution)/shard_map/ppermute | solution.py:114
  49.0 10.3 %collective-permute-start.9 = (bf16[2,128,256]{2,1,0:T(8,128)(2,1)S(1)}, bf16[2,128,256]{2,1,0:T(8,128)(2,1)S(1)}, u32[]{:S(2)}, u32[]{:S(2)}) collective-permute-start(bf16[2,128,256]{2,1,0:T(8,128)(2,1)S(1)} %collective-permute-done.8.refs_2_), channel_id=1, source_target_pairs={{0,4},{4,0},{8,12},{12,8},{16,20},{20,16},{24,28},{28,24},{1,5},{5... | collective-permute-start | bytes 393224 | tf_op jit(solution)/shard_map/ppermute | solution.py:114
  54.4 1.5 %copy-start.1 = (bf16[2,9,288,256]{3,2,1,0:T(8,128)(2,1)}, bf16[2,9,288,256]{3,2,1,0:T(8,128)(2,1)S(1)}, u32[]{:S(2)}) copy-start(bf16[2,9,288,256]{3,2,1,0:T(8,128)(2,1)S(1)} %get-tuple-element.32.grads) | copy-start | bytes 7962628
  55.9 10.2 %all-to-all-start.1 = ((bf16[8,16,256]{2,1,0:T(8,128)(2,1)}), bf16[8,16,256]{2,1,0:T(8,128)(2,1)S(1)}, u32[]{:S(2)}, u32[]{:S(2)}) async-start(bf16[8,16,256]{2,1,0:T(8,128)(2,1)} %bitcast.6), calls=%async_computation.1 | async-start | bytes 131072 | tf_op jit(solution)/shard_map/all_to_all | solution.py:447
  59.3 1.8 %copy-start.2 = (bf16[2,9,288,256]{3,2,1,0:T(8,128)(2,1)S(1)}, bf16[2,9,288,256]{3,2,1,0:T(8,128)(2,1)}, u32[]{:S(2)}) copy-start(bf16[2,9,288,256]{3,2,1,0:T(8,128)(2,1)} %copy-done.1) | copy-start | bytes 7962628
  66.2 2.8 %collective-permute-start.14 = (f32[1,64]{1,0:T(1,128)S(1)}, f32[1,64]{1,0:T(1,128)S(1)}, u32[]{:S(2)}, u32[]{:S(2)}) collective-permute-start(f32[1,64]{1,0:T(1,128)S(1)} %get-tuple-element.45), channel_id=1, source_target_pairs={{0,1},{1,0},{2,3},{3,2},{4,5},{5,4},{6,7},{7,6},{8,9},{9,8},{10,11... | collective-permute-start | bytes 776 | tf_op jit(solution)/shard_map/ppermute | solution.py:114
  66.2 3.0 %collective-permute-start.16 = (f32[1,64]{1,0:T(1,128)S(1)}, f32[1,64]{1,0:T(1,128)S(1)}, u32[]{:S(2)}, u32[]{:S(2)}) collective-permute-start(f32[1,64]{1,0:T(1,128)S(1)} %get-tuple-element.46), channel_id=1, source_target_pairs={{0,3},{1,2},{2,1},{3,0},{4,7},{5,6},{6,5},{7,4},{8,11},{9,10},{10,... | collective-permute-start | bytes 776 | tf_op jit(solution)/shard_map/ppermute | solution.py:114
  67.9 3.5 %collective-permute-start.15 = (f32[1,64]{1,0:T(1,128)S(1)}, f32[1,64]{1,0:T(1,128)S(1)}, u32[]{:S(2)}, u32[]{:S(2)}) collective-permute-start(f32[1,64]{1,0:T(1,128)S(1)} %get-tuple-element.47), channel_id=1, source_target_pairs={{0,2},{1,3},{2,0},{3,1},{4,6},{5,7},{6,4},{7,5},{8,10},{9,11},{10,... | collective-permute-start | bytes 776 | tf_op jit(solution)/shard_map/ppermute | solution.py:114

commit v3 on v2

--- a/solution.py
+++ b/solution.py
@@ -114,13 +114,12 @@
     return lax.ppermute(value, axis, [(source, source ^ bits) for source in range(count)])
 
 
-def exchanged(value, axis):
-    blocks = [value]
-    for k in range(1, lax.axis_size(axis)):
-        if k % 2 == 0:
-            blocks.append(partners(value, axis, k))
-        else:
-            blocks.append(partners(blocks[k - 1], axis, 1))
+def exchanged(value, axis, gate=None):
+    count = lax.axis_size(axis)
+    even = [value] + [partners(value, axis, k) for k in range(2, count, 2)]
+    blocks = []
+    for n, block in enumerate(even if gate is None else [value] + gate(even[1:])):
+        blocks += [block, partners(block, axis, 1)]
     return blocks
 
 
@@ -187,7 +186,7 @@
 
 
 def join_kernel(F, J, T, place, grad_rows, planes, *refs):
-    messages, (joined, cached, under, _, blocks) = refs[:T], refs[T:]
+    messages, (joined, cached, under, head, passed, blocks) = refs[:T], refs[T:]
     span = F * J
     block = place[1]
     for k in range(T):
@@ -196,6 +195,9 @@
             blocks[rp, pl.ds(at, span), :] = messages[k][rp * span : (rp + 1) * span, :]
     for rp in range(2):
         joined[rp] = blocks[rp].T
+    passed[...] = grad_rows[...]
+    for s in range(grad_rows.shape[0]):
+        head[s] = grad_rows[s, : 2 * J, :]
     for rp in range(2):
         for cp in range(2):
             halves = []
@@ -227,22 +229,30 @@
     return chosen
 
 
-def shard_order(J, R, moved):
+def shard_order(J, R, rows, first, moved):
     jl = J // R
     return permutation(
-        (R * 2 * J, R * 2 * J),
-        lambda o, s: (o // (2 * J) == s // jl % R)
+        (rows * 2 * J, R * 2 * J),
+        lambda o, s: (o // (2 * J) + first == s // jl % R)
         & (o // J % 2 == s // (jl * R) % 2)
         & (o % J == s // (2 * jl * R) * jl + s % jl + moved),
     )
 
 
+def shard_rows(source, start, count):
+    return jnp.concatenate(
+        [source[s, start : start + count, :] for s in range(source.shape[0])], axis=0
+    )
+
+
+def gate_kernel(*refs):
+    pass
+
+
 def slab_kernel(
-    F, J, R, T, slot, place, planes, cached, under, weight_hbm, frames, vectors, *refs
+    F, J, R, T, slot, place, planes, cached, under, weight_hbm, frames, vectors, gathered, following,
+    out, frames_grad, weight, near, ext, tmp, sem,
 ):
-    gathered = refs[:T]
-    out, frames_grad, bias_sum, grads = refs[T : T + 4]
-    weight, ext, tmp, sem = refs[T + 4 :]
     row, block = place[0], place[1]
     channels = frames.shape[1]
     span = F * J
@@ -254,24 +264,18 @@
     for copy in taps_a:
         copy.start()
 
-    pair_rows = 2 * R * (J // R)
-    grads[:, 0] = jnp.zeros((2,) + grads.shape[2:], jnp.bfloat16)
-    grads[:, :, T * span :, :] = jnp.zeros((2, R + 1, 2 * J, channels), jnp.bfloat16)
-    orders = [shard_order(J, R, moved) for moved in range(2)]
-    total = jnp.zeros((1, channels), jnp.float32)
-    for k in range(T):
-        for pair in range(F // 2):
-            start = pair * pair_rows
-            source = jnp.concatenate(
-                [gathered[k][s, start : start + pair_rows, :] for s in range(R)], axis=0
-            )
-            total = total + jnp.sum(source.astype(jnp.float32), axis=0, keepdims=True)
-            at = pl.multiple_of((block ^ k) * span + pair * 2 * J, 16)
-            for moved in range(2):
-                value = mm(orders[moved], source).astype(jnp.bfloat16)
-                for i in range(R):
-                    grads[moved, i + 1, pl.ds(at, 2 * J), :] = value[i * 2 * J : (i + 1) * 2 * J]
-    bias_sum[...] = slice_of(total, block, 0, T)
+    orders = [shard_order(J, R, 2, row - 1, moved) for moved in range(2)]
+    for pair in range(F // 2 + 1):
+        if pair < F // 2:
+            source = shard_rows(gathered, pair * 2 * J, 2 * J)
+        else:
+            source = shard_rows(following, 0, 2 * J)
+        for moved in range(2):
+            value = mm(orders[moved], source).astype(jnp.bfloat16)
+            for i in range(2):
+                near[moved, i, pair * 2 * J : (pair + 1) * 2 * J, :] = value[
+                    i * 2 * J : (i + 1) * 2 * J
+                ]
 
     rows = (F + 2) * J
     last = lax.broadcasted_iota(jnp.int32, (rows, 1), 0) % J == J - 1
@@ -292,8 +296,7 @@
         if n % 9 == 0:
             taps_a[a].wait()
         latent = latent + mm(ext[b, c, a * J : (a + F) * J, :], weight[n])
-        start = pl.multiple_of((block * F + 2 - a) * J, 16)
-        piece = grads[c // 2, row + 1 - b // 2, pl.ds(start, span), :]
+        piece = near[c // 2, 1 - b // 2, (2 - a) * J : (2 - a + F) * J, :]
         term = mm_t(piece, weight[n])
         key = (b % 2, c % 2)
         sums[key] = sums[key] + term if key in sums else term
@@ -331,13 +334,27 @@
     out[...] = value.astype(jnp.bfloat16)
 
 
-def weight_kernel(F, J, R, T, part, place, grads, *refs):
-    hidden = refs[:R]
-    out_hbm, out, even, odd, sem = refs[R:]
+def weight_kernel(F, J, R, T, part, place, _, *refs):
+    gathered, hidden = refs[:T], refs[T : T + R]
+    out_hbm, bias_sum, out, grads, even, odd, sem = refs[T + R :]
     channels = grads.shape[-1]
-    depth = T * F * J
+    span = F * J
+    depth = T * span
     lanes = 2 * part
-    row = place[0]
+    row, block = place[0], place[1]
+    grads[:, :, depth:, :] = jnp.zeros((2, R, 2 * J, channels), jnp.bfloat16)
+    orders = [shard_order(J, R, R, 0, moved) for moved in range(2)]
+    total = jnp.zeros((1, channels), jnp.float32)
+    for k in range(T):
+        for pair in range(F // 2):
+            source = shard_rows(gathered[k], pair * 2 * J, 2 * J)
+            total = total + jnp.sum(source.astype(jnp.float32), axis=0, keepdims=True)
+            at = pl.multiple_of((block ^ k) * span + pair * 2 * J, 16)
+            for moved in range(2):
+                value = mm(orders[moved], source).astype(jnp.bfloat16)
+                for i in range(R):
+                    grads[moved, i, pl.ds(at, 2 * J), :] = value[i * 2 * J : (i + 1) * 2 * J]
+    bias_sum[...] = slice_of(total, block, 0, T)
     even[:, R * depth :] = jnp.zeros((lanes, depth), jnp.bfloat16)
     for k in range(R):
         at = pl.multiple_of((row ^ k) * depth, 128)
@@ -347,7 +364,7 @@
     for a in range(3):
         start = (2 - a) * J
         for moved in range(2):
-            right = grads[moved, 1:, start : start + depth, :].reshape(R * depth, channels)
+            right = grads[moved, :, start : start + depth, :].reshape(R * depth, channels)
             size = part if moved else lanes
             left = jnp.concatenate(
                 [even[:size, : R * depth], odd[:size, :], even[:size, depth:]], axis=0
@@ -411,38 +428,44 @@
         60 * WORK * span * C, 16 * span * C, "svv" + "v" * (T + 3),
     )(place, flat, vectors)
     messages = [sends[0]] + [partners(sends[k], "tm", k) for k in range(1, T)]
-    joined, cached, under, grad_rows = call(
+    joined, cached, under, head, grad_rows = call(
         functools.partial(join_kernel, F, J, T),
         [
             ((2, 2 * part, T * span), bf16),
             ((2, 2, 2 * J, C), bf16),
             ((2, 2 * J + span, C), bf16),
+            ((R, 2 * J, C), bf16),
             (grad_rows.shape, bf16),
         ],
         [pltpu.VMEM((2, T * span, 2 * part), bf16)],
-        30 * WORK * span * C, 16 * span * C, "sav" + "v" * T + "vvva", {1: 3},
+        30 * WORK * span * C, 16 * span * C, "svv" + "v" * T + "vvvvv",
     )(place, grad_rows, planes, *messages)
     under = shifted(under, "rows", -1)
-    hidden_all = exchanged(joined, "rows")
-    grad_all = exchanged(grad_rows, "tm")
-
-    packed, frames_grad, bias_sum, grads = call(
+    following = shifted(head, "tm", -1)
+    packed, frames_grad = call(
         functools.partial(slab_kernel, F, J, R, T, slot),
-        [
-            ((R * slot, C), bf16),
-            ((4 * span, C), bf16),
-            ((1, part), f32),
-            ((2, R + 1, (F * T + 2) * J, C), bf16),
-        ],
+        [((R * slot, C), bf16), ((4 * span, C), bf16)],
         [
             pltpu.VMEM((27, C, C), bf16),
+            pltpu.VMEM((2, 2, (F + 2) * J, C), bf16),
             pltpu.VMEM((3, 3, (F + 2) * J, C), bf16),
             pltpu.VMEM((2, 4 * span, C // 2), f32),
             pltpu.SemaphoreType.DMA((3,)),
         ],
-        270 * WORK * span * C, 2 * 27 * C * C, "svvvhvv" + "v" * (T + 4),
+        2 * 54 * span * C * C, 2 * 27 * C * C, "svvvhvvvv" + "vv",
         limit=VMEM_LIMIT_WIDE,
-    )(place, planes, cached, under, weight, frames_copy, vectors, *grad_all)
+    )(place, planes, cached, under, weight, frames_copy, vectors, grad_rows, following)
+
+    def after_slab(blocks):
+        shapes = [(b.shape, bf16) for b in blocks]
+        count = len(blocks)
+        aliases = {n + 1: n for n in range(count)}
+        return list(
+            call(gate_kernel, shapes, [], 0, 0, "a" * (2 * count + 1), aliases)(packed, *blocks)
+        )
+
+    hidden_all = exchanged(joined, "rows", after_slab)
+    grad_all = exchanged(grad_rows, "tm")
 
     packed = lax.all_to_all(packed.reshape(R, slot, C), "rows", 0, 0, tiled=True)
     latent = packed[:, :used].reshape(R, F, J // R, C).transpose(1, 0, 2, 3)
@@ -451,17 +474,18 @@
     for k in range(1, T):
         gain_grad = gain_grad + partners(gain_sum[:, k * part : (k + 1) * part], "tm", k)
 
-    (weight_grad,) = call(
+    weight_grad, bias_sum = call(
         functools.partial(weight_kernel, F, J, R, T, part),
-        [((27, part, C), f32)],
+        [((27, part, C), f32), ((1, part), f32)],
         [
             pltpu.VMEM((27, part, C), f32),
+            pltpu.VMEM((2, R, (F * T + 2) * J, C), bf16),
             pltpu.VMEM((2 * part, (R + 1) * T * span), bf16),
             pltpu.VMEM((2 * part, R * T * span), bf16),
             pltpu.SemaphoreType.DMA((3,)),
         ],
-        220 * WORK * span * C, 8 * 27 * part * C, "sv" + "v" * R + "h",
-    )(place, grads, *hidden_all)
+        220 * WORK * span * C, 8 * 27 * part * C, "sa" + "v" * (T + R) + "hv",
+    )(place, gain_sum, *grad_all, *hidden_all)
 
     return (
         latent,

time: 72.4 us -> 80.6 us (1.11)
  waiting for transfers between devices: 26 us -> 17.3 us
  local copies, waits for them, and re-layouts: 6.39 us -> 14.4 us
  starting transfers between devices: 27.2 us -> 33.3 us
  Pallas kernels: 10.2 us -> 12.8 us
    ppermute x16, waiting for transfers between devices: 23.6 us -> 13.3 us  [partners(): lax.ppermute(value, axis, [(source, source ^ bits) for source in range(co...]
    unnamed x8 -> x36, local copies, waits for them, and re-layouts: 4.81 us -> 12.9 us
    all_to_all x1, waiting for transfers between devices: 1.62 us -> 3.96 us  [gathered_form(): lax.all_to_all(packed.reshape(R, slot, C), 'rows', 0, 0, tiled=True)]
    ppermute x16, starting transfers between devices: 15.3 us -> 17.6 us  [partners(): lax.ppermute(value, axis, [(source, source ^ bits) for source in range(co...]
    all_to_all x1, starting transfers between devices: 3.35 us -> 5.57 us  [gathered_form(): lax.all_to_all(packed.reshape(R, slot, C), 'rows', 0, 0, tiled=True)]
    pallas_call x1, Pallas kernels: 3.43 us -> 5.38 us  [gathered_form(): call(functools.partial(weight_kernel, F, J, R, T, part), [((27, part, C),...]
    ppermute x1 -> x2, starting transfers between devices: 1.28 us -> 2.57 us  [shifted(): lax.ppermute(value, axis, [(source, source + steps) for source in range(l...]
    pallas_call x1, Pallas kernels: 0.64 us -> 1.78 us  [gathered_form(): call(functools.partial(join_kernel, F, J, T), [((2, 2 * part, T * span),...]
  transfers between devices with their start and end apart: 19 -> 20, of which waited for: 9 -> 7; matrix products, arithmetic and copies ran while one was open for 2% -> 3% of each run, Pallas kernels for 13% -> 7%
where the time goes in v3:
time: 80.6 us; the launch traced here: 79.8 us
  starting transfers between devices  33.3 us (41%)
  waiting for transfers between devices  17.3 us (21%)
  local copies, waits for them, and re-layouts  14.4 us (18%)
  Pallas kernels  12.8 us (16%)
  other arithmetic  1.32 us (2%)
    ppermute x16, starting transfers between devices, partners(): lax.ppermute(value, axis, [(source, source ^ bits) for source in range(co...  17.6 us
    ppermute x16, waiting for transfers between devices, partners(): lax.ppermute(value, axis, [(source, source ^ bits) for source in range(co...  13.3 us
    unnamed x36, local copies, waits for them, and re-layouts  12.9 us
    all_to_all x1, starting transfers between devices, gathered_form(): lax.all_to_all(jnp.broadcast_to(own, (R,) + own.shape[1:]), 'rows', 0, 0,...  7.52 us
    all_to_all x1, starting transfers between devices, gathered_form(): lax.all_to_all(packed.reshape(R, slot, C), 'rows', 0, 0, tiled=True)  5.57 us
    pallas_call x1, Pallas kernels, gathered_form(): call(functools.partial(weight_kernel, F, J, R, T, part), [((27, part, C),...  5.38 us
    pallas_call x1, Pallas kernels, gathered_form(): call(functools.partial(slab_kernel, F, J, R, T, slot), [((R * slot, C), b...  4.78 us
    all_to_all x1, waiting for transfers between devices, gathered_form(): lax.all_to_all(packed.reshape(R, slot, C), 'rows', 0, 0, tiled=True)  3.96 us
  transfers between devices with their start and end apart: 20, of which 7 were waited for; matrix products, arithmetic and copies ran while one was open for 3% of the time, Pallas kernels for 7%

profile of v3, /device:TPU:0, one launch (start us, length us, event | category | flops | bytes accessed | tf_op | source)
XLA Modules:
  0.0 79.8 jit_solution(12296481861334400306)
XLA Ops:
  0.6 0.8 broadcast_in_dim.7
  1.4 0.7 broadcast_in_dim.8
  2.1 7.5 %all-to-all-start = ((bf16[8,64,256]{2,1,0:T(8,128)(2,1)}), bf16[8,64,256]{2,1,0:T(8,128)(2,1)}, u32[]{:S(2)}, u32[]{:S(2)}) async-start(bf16[8,64,256]{2,1,0:T(8,128)(2,1)} %broadcast_in_dim.8), calls=%async_computation | async-start | bytes 524288 | tf_op jit(solution)/shard_map/all_to_all | solution.py:418
  9.6 0.1 pad_add_fusion.place
  9.7 0.7 pad_maximum_fusion.vectors
  10.4 0.9 %copy-done.8 = bf16[4,2,32,256]{3,2,1,0:T(8,128)(2,1)S(1)} copy-done((bf16[4,2,32,256]{3,2,1,0:T(8,128)(2,1)S(1)}, bf16[4,2,32,256]{3,2,1,0:T(8,128)(2,1)}, u32[]{:S(2)}) %copy-start.8) | copy-done | bytes 131096
  11.3 0.8 %shard_map.92 = (bf16[2,2,64,256]{3,2,1,0:T(8,128)(2,1)S(1)}, bf16[256,256]{1,0:T(8,128)(2,1)S(1)}, f32[2,256]{1,0:T(2,128)S(1)}, bf16[128,128]{1,0:T(8,128)(2,1...) custom-call(s32[2]{0:T(128)S(1)} %pad_add_fusion.place, ...), custom_call_target="tpu_custom_call" | custom-call | flops 1179648000 | bytes 262144 | tf_op jit(solution)/shard_map/pallas_call | solution.py:423
  12.2 0.0 copy-start.3
  12.2 0.6 copy-done.3
  12.8 0.7 copy-done.6
  13.5 0.6 copy-done.15
  14.1 0.0 collective-permute-start
  14.1 1.6 %collective-permute-start.2 = (bf16[384,128]{1,0:T(8,128)(2,1)S(1)}, bf16[384,128]{1,0:T(8,128)(2,1)S(1)}, u32[]{:S(2)}, u32[]{:S(2)}) collective-permute-start(bf16[384,128]{1,0:T(8,128)(2,1)S(1)} %get-tuple-element.28), channel_id=1, source_target_pairs={{0,3},{1,2},{2,1},{3,0},{4,7},{5,6},{6,5},{7,4},{8,11},{9,10},{10,... | collective-permute-start | bytes 294920 | tf_op jit(solution)/shard_map/ppermute | solution.py:114
  15.8 0.5 collective-permute-start.1
  16.3 3.7 %collective-permute-done.1.refs_2_ = bf16[128,128]{1,0:T(8,128)(2,1)S(1)} collective-permute-done((bf16[128,128]{1,0:T(8,128)(2,1)S(1)}, bf16[128,128]{1,0:T(8,128)(2,1)S(1)}, u32[]{:S(2)}, u32[]{:S(2)}) %collective-permute-start.1) | collective-permute-done | bytes 32800 | tf_op jit(solution)/shard_map/ppermute | solution.py:114
  19.9 0.6 copy-done.13
  20.5 0.0 collective-permute-done.refs_1_
  20.5 0.7 copy-done.9
  21.2 0.0 collective-permute-done.2.refs_3_
  21.2 0.6 copy-done.11
  21.8 0.0 all-to-all-done.grad_rows
  21.8 0.9 %copy-done.4 = bf16[2,2,64,256]{3,2,1,0:T(8,128)(2,1)S(1)} copy-done((bf16[2,2,64,256]{3,2,1,0:T(8,128)(2,1)S(1)}, bf16[2,2,64,256]{3,2,1,0:T(8,128)(2,1)}, u32[]{:S(2)}) %copy-start.4) | copy-done | bytes 131096
  22.7 0.9 %copy-done.10 = bf16[384,128]{1,0:T(8,128)(2,1)S(1)} copy-done((bf16[384,128]{1,0:T(8,128)(2,1)S(1)}, bf16[384,128]{1,0:T(8,128)(2,1)}, u32[]{:S(2)}) %copy-start.10) | copy-done | bytes 98328
  23.6 0.9 %copy-done.12 = bf16[384,128]{1,0:T(8,128)(2,1)S(1)} copy-done((bf16[384,128]{1,0:T(8,128)(2,1)S(1)}, bf16[384,128]{1,0:T(8,128)(2,1)}, u32[]{:S(2)}) %copy-start.12) | copy-done | bytes 98328
  24.5 0.8 copy-done.14
  25.3 0.8 copy-done.16
  26.1 1.8 %shard_map.93 = (bf16[2,128,256]{2,1,0:T(8,128)(2,1)}, bf16[2,2,32,256]{3,2,1,0:T(8,128)(2,1)S(1)}, bf16[2,96,256]{2,1,0:T(8,128)(2,1)S(1)}, bf16[8,32,256]{2,1,0:T(8,128)(2,1)S(1)}, bf16[8,64,256]{2,1,0:T(8,128)(2,1)}) custom-call(s32[2]{0:T(128)S(1)} %pad_add_fusion.place, bf16[8,64,256]{2,1,0:T(8,128)(2,1)} %all-to-all-done.grad_rows, ...), custom_call_target="tpu_custom_call" | custom-call | flops 589824000 | bytes 262144 | tf_op jit(solution)/shard_map/pallas_call | solution.py:431
  27.8 1.3 %collective-permute-start.4 = (bf16[8,32,256]{2,1,0:T(8,128)(2,1)S(1)}, bf16[8,32,256]{2,1,0:T(8,128)(2,1)S(1)}, u32[]{:S(2)}, u32[]{:S(2)}) collective-permute-start(bf16[8,32,256]{2,1,0:T(8,128)(2,1)S(1)} %get-tuple-element.34), channel_id=1, source_target_pairs={{1,0},{2,1},{3,2},{5,4},{6,5},{7,6},{9,8},{10,9},{11,10},{13,12},{... | collective-permute-start | bytes 393224 | tf_op jit(solution)/shard_map/ppermute | solution.py:20
  29.1 1.3 %collective-permute-start.3 = (bf16[2,96,256]{2,1,0:T(8,128)(2,1)S(1)}, bf16[2,96,256]{2,1,0:T(8,128)(2,1)S(1)}, u32[]{:S(2)}, u32[]{:S(2)}) collective-permute-start(bf16[2,96,256]{2,1,0:T(8,128)(2,1)S(1)} %get-tuple-element.30), channel_id=1, source_target_pairs={{4,0},{8,4},{12,8},{16,12},{20,16},{24,20},{28,24},{5,1},{9,5},{13... | collective-permute-start | bytes 294920 | tf_op jit(solution)/shard_map/ppermute | solution.py:20
  30.4 4.2 %collective-permute-start.9 = (bf16[2,128,256]{2,1,0:T(8,128)(2,1)}, bf16[2,128,256]{2,1,0:T(8,128)(2,1)}, u32[]{:S(2)}, u32[]{:S(2)}) collective-permute-start(bf16[2,128,256]{2,1,0:T(8,128)(2,1)} %get-tuple-element.37.refs_4_), channel_id=1, source_target_pairs={{0,8},{4,12},{8,0},{12,4},{16,24},{20,28},{24,16},{28,20},{1,9},{5... | collective-permute-start | bytes 393224 | tf_op jit(solution)/shard_map/ppermute | solution.py:114
  34.6 2.4 %collective-permute-start.10 = (bf16[2,128,256]{2,1,0:T(8,128)(2,1)}, bf16[2,128,256]{2,1,0:T(8,128)(2,1)}, u32[]{:S(2)}, u32[]{:S(2)}) collective-permute-start(bf16[2,128,256]{2,1,0:T(8,128)(2,1)} %get-tuple-element.37.refs_4_), channel_id=1, source_target_pairs={{0,16},{4,20},{8,24},{12,28},{16,0},{20,4},{24,8},{28,12},{1,17},{... | collective-permute-start | bytes 393224 | tf_op jit(solution)/shard_map/ppermute | solution.py:114
  36.9 0.1 collective-permute-start.11
  37.0 0.0 collective-permute-done.3.under
  37.0 2.1 %collective-permute-start.6 = (bf16[8,64,256]{2,1,0:T(8,128)(2,1)}, bf16[8,64,256]{2,1,0:T(8,128)(2,1)}, u32[]{:S(2)}, u32[]{:S(2)}) collective-permute-start(bf16[8,64,256]{2,1,0:T(8,128)(2,1)} %get-tuple-element.33.gathered.refs_0_), channel_id=1, source_target_pairs={{0,2},{1,3},{2,0},{3,1},{4,6},{5,7},{6,4},{7,5},{8,10},{9,11},{10,... | collective-permute-start | bytes 786440 | tf_op jit(solution)/shard_map/ppermute | solution.py:114
  39.2 0.9 %copy-done.5 = bf16[2,2,64,256]{3,2,1,0:T(8,128)(2,1)S(1)} copy-done((bf16[2,2,64,256]{3,2,1,0:T(8,128)(2,1)S(1)}, bf16[2,2,64,256]{3,2,1,0:T(8,128)(2,1)}, u32[]{:S(2)}) %copy-start.5) | copy-done | bytes 131096
  40.1 0.9 %copy-done.7 = bf16[256,256]{1,0:T(8,128)(2,1)S(1)} copy-done((bf16[256,256]{1,0:T(8,128)(2,1)S(1)}, bf16[256,256]{1,0:T(8,128)(2,1)}, u32[]{:S(2)}) %copy-start.7) | copy-done | bytes 131096
  41.0 4.8 %shard_map.94 = (bf16[128,256]{1,0:T(8,128)(2,1)S(1)}, bf16[256,256]{1,0:T(8,128)(2,1)}) custom-call(s32[2]{0:T(128)S(1)} %pad_add_fusion.place, bf16[2,2,64,256]{3,2,1,0:T(8,128)(2,1)S(1)} %copy-done.5, bf16[2,2,32,256]{3,2,1,0:T(8,128)(2,1)S(1)} %get-tuple-element.29.cached, bf16[2,96,256]{2,1,0:T(8,128)(2,1)S(1)} %collective-permute-done.3.under, ...), custom_call_target="tpu_custom_call" | custom-call | flops 452984832 | bytes 3538944 | tf_op jit(solution)/shard_map/pallas_call | solution.py:445
  45.8 0.0 copy-start.1
  45.8 0.6 copy-done.1
  46.4 5.6 %all-to-all-start.1 = ((bf16[8,16,256]{2,1,0:T(8,128)(2,1)}), bf16[8,16,256]{2,1,0:T(8,128)(2,1)S(1)}, u32[]{:S(2)}, u32[]{:S(2)}) async-start(bf16[8,16,256]{2,1,0:T(8,128)(2,1)} %bitcast.17), calls=%async_computation.1 | async-start | bytes 131072 | tf_op jit(solution)/shard_map/all_to_all | solution.py:470
  52.0 0.0 collective-permute-start.5
  52.0 0.0 collective-permute-done.9.refs_1_
  52.0 2.1 %collective-permute-start.8 = (bf16[2,128,256]{2,1,0:T(8,128)(2,1)}, bf16[2,128,256]{2,1,0:T(8,128)(2,1)S(1)}, u32[]{:S(2)}, u32[]{:S(2)}) collective-permute-start(bf16[2,128,256]{2,1,0:T(8,128)(2,1)} %get-tuple-element.37.refs_4_), channel_id=1, source_target_pairs={{0,4},{4,0},{8,12},{12,8},{16,20},{20,16},{24,28},{28,24},{1,5},{5... | collective-permute-start | bytes 393224 | tf_op jit(solution)/shard_map/ppermute | solution.py:114
  54.1 0.8 %copy-done.2 = bf16[128,256]{1,0:T(8,128)(2,1)S(1)} copy-done((bf16[128,256]{1,0:T(8,128)(2,1)S(1)}, bf16[128,256]{1,0:T(8,128)(2,1)}, u32[]{:S(2)}) %copy-start.2) | copy-done | bytes 65560
  54.9 4.0 %all-to-all-done.1 = bf16[8,16,256]{2,1,0:T(8,128)(2,1)S(1)} async-done(((bf16[8,16,256]{2,1,0:T(8,128)(2,1)}), bf16[8,16,256]{2,1,0:T(8,128)(2,1)S(1)}, u32[]{:S(2)}, u32[]{:S(2)}) %all-to-all-start.1) | async-done | bytes 65568 | tf_op jit(solution)/shard_map/all_to_all | solution.py:470
  58.9 0.1 collective-permute-start.7
  59.0 0.1 fusion.3
  59.1 0.6 copy.16
  59.7 0.1 collective-permute-start.17
  59.9 2.0 %collective-permute-start.16 = (f32[1,64]{1,0:T(1,128)S(1)}, f32[1,64]{1,0:T(1,128)S(1)}, u32[]{:S(2)}, u32[]{:S(2)}) collective-permute-start(f32[1,64]{1,0:T(1,128)S(1)} %get-tuple-element.55), channel_id=1, source_target_pairs={{0,2},{1,3},{2,0},{3,1},{4,6},{5,7},{6,4},{7,5},{8,10},{9,11},{10,... | collective-permute-start | bytes 776 | tf_op jit(solution)/shard_map/ppermute | solution.py:114
  61.9 0.0 collective-permute-done.8.refs_5_
  61.9 0.0 collective-permute-start.15
  61.9 0.8 %collective-permute-done.17 = f32[1,64]{1,0:T(1,128)S(1)} collective-permute-done((f32[1,64]{1,0:T(1,128)S(1)}, f32[1,64]{1,0:T(1,128)S(1)}, u32[]{:S(2)}, u32[]{:S(2)}) %collective-permute-start.17) | collective-permute-done | bytes 288 | tf_op jit(solution)/shard_map/ppermute | solution.py:114
  62.7 0.4 collective-permute-start.12
  63.1 0.3 collective-permute-done.16
  63.4 1.3 %collective-permute-start.13 = (bf16[2,128,256]{2,1,0:T(8,128)(2,1)}, bf16[2,128,256]{2,1,0:T(8,128)(2,1)S(1)}, u32[]{:S(2)}, u32[]{:S(2)}) collective-permute-start(bf16[2,128,256]{2,1,0:T(8,128)(2,1)} %get-tuple-element.39.refs_8_), channel_id=1, source_target_pairs={{0,4},{4,0},{8,12},{12,8},{16,20},{20,16},{24,28},{28,24},{1,5},{5... | collective-permute-start | bytes 393224 | tf_op jit(solution)/shard_map/ppermute | solution.py:114
  64.7 0.0 collective-permute-done.15
  64.7 0.7 collective-permute-start.14
  65.5 0.5 fusion.2
  66.0 0.0 collective-permute-done.5.refs_1_
  66.0 3.2 %collective-permute-done.12.refs_7_ = bf16[2,128,256]{2,1,0:T(8,128)(2,1)S(1)} collective-permute-done((bf16[2,128,256]{2,1,0:T(8,128)(2,1)}, bf16[2,128,256]{2,1,0:T(8,128)(2,1)S(1)}, u32[]{:S(2)}, u32[]{:S(2)}) %collective-permute-start.12) | collective-permute-done | bytes 131104 | tf_op jit(solution)/shard_map/ppermute | solution.py:114
  69.2 2.8 %collective-permute-done.13.refs_9_ = bf16[2,128,256]{2,1,0:T(8,128)(2,1)S(1)} collective-permute-done((bf16[2,128,256]{2,1,0:T(8,128)(2,1)}, bf16[2,128,256]{2,1,0:T(8,128)(2,1)S(1)}, u32[]{:S(2)}, u32[]{:S(2)}) %collective-permute-start.13) | collective-permute-done | bytes 131104 | tf_op jit(solution)/shard_map/ppermute | solution.py:114
  72.0 2.4 %collective-permute-done.14.refs_11_ = bf16[2,128,256]{2,1,0:T(8,128)(2,1)S(1)} collective-permute-done((bf16[2,128,256]{2,1,0:T(8,128)(2,1)}, bf16[2,128,256]{2,1,0:T(8,128)(2,1)S(1)}, u32[]{:S(2)}, u32[]{:S(2)}) %collective-permute-start.14) | collective-permute-done | bytes 131104 | tf_op jit(solution)/shard_map/ppermute | solution.py:114
  74.4 5.4 %shard_map.96 = (f32[27,64,256]{2,1,0:T(8,128)}, f32[1,64]{1,0:T(1,128)}) custom-call(s32[2]{0:T(128)S(1)} %pad_add_fusion.place, f32[1,256]{1,0:T(1,128)S(1)} %bitcast.20, bf16[8,64,256]{2,1,0:T(8,128)(2,1)} %get-tuple-element.33.gathered.refs_0_, bf16[8,64,256]{2,1,0:T(8,128)(2,1)S(1)} %collective-permute-done.5.refs_1_, ...), custom_call_target="tpu_custom_call" | custom-call | flops 4325376000 | bytes 3538944 | tf_op jit(solution)/shard_map/pallas_call | solution.py:477
  (25 shorter events, 0.1 us)
Async XLA Ops:
  2.1 37.1 %copy-start = (bf16[3,3,3,256,256]{4,3,2,1,0:T(8,128)(2,1)S(1)}, bf16[3,3,3,256,256]{4,3,2,1,0:T(8,128)(2,1)}, u32[]{:S(2)}) copy-start(bf16[3,3,3,256,256]{4,3,2,1,0:T(8,128)(2,1)} %param.7) | copy-start | bytes 10616836
  2.1 19.7 %all-to-all-start = ((bf16[8,64,256]{2,1,0:T(8,128)(2,1)}), bf16[8,64,256]{2,1,0:T(8,128)(2,1)}, u32[]{:S(2)}, u32[]{:S(2)}) async-start(bf16[8,64,256]{2,1,0:T(8,128)(2,1)} %broadcast_in_dim.8), calls=%async_computation | async-start | bytes 524288 | tf_op jit(solution)/shard_map/all_to_all | solution.py:418
  10.4 0.9 %copy-start.8 = (bf16[4,2,32,256]{3,2,1,0:T(8,128)(2,1)S(1)}, bf16[4,2,32,256]{3,2,1,0:T(8,128)(2,1)}, u32[]{:S(2)}) copy-start(bf16[4,2,32,256]{3,2,1,0:T(8,128)(2,1)} %param.5) | copy-start | bytes 393220
  12.2 0.7 copy-start.3
  12.8 0.7 copy-start.6
  13.5 0.6 copy-start.15
  14.1 6.4 %collective-permute-start = (bf16[384,128]{1,0:T(8,128)(2,1)S(1)}, bf16[384,128]{1,0:T(8,128)(2,1)S(1)}, u32[]{:S(2)}, u32[]{:S(2)}) collective-permute-start(bf16[384,128]{1,0:T(8,128)(2,1)S(1)} %get-tuple-element.26), channel_id=1, source_target_pairs={{0,1},{1,0},{2,3},{3,2},{4,5},{5,4},{6,7},{7,6},{8,9},{9,8},{10,11... | collective-permute-start | bytes 294920 | tf_op jit(solution)/shard_map/ppermute | solution.py:114
  14.1 7.1 %collective-permute-start.2 = (bf16[384,128]{1,0:T(8,128)(2,1)S(1)}, bf16[384,128]{1,0:T(8,128)(2,1)S(1)}, u32[]{:S(2)}, u32[]{:S(2)}) collective-permute-start(bf16[384,128]{1,0:T(8,128)(2,1)S(1)} %get-tuple-element.28), channel_id=1, source_target_pairs={{0,3},{1,2},{2,1},{3,0},{4,7},{5,6},{6,5},{7,4},{8,11},{9,10},{10,... | collective-permute-start | bytes 294920 | tf_op jit(solution)/shard_map/ppermute | solution.py:114
  15.8 4.2 %collective-permute-start.1 = (bf16[128,128]{1,0:T(8,128)(2,1)S(1)}, bf16[128,128]{1,0:T(8,128)(2,1)S(1)}, u32[]{:S(2)}, u32[]{:S(2)}) collective-permute-start(bf16[128,128]{1,0:T(8,128)(2,1)S(1)} %get-tuple-element.27), channel_id=1, source_target_pairs={{0,2},{1,3},{2,0},{3,1},{4,6},{5,7},{6,4},{7,5},{8,10},{9,11},{10,... | collective-permute-start | bytes 98312 | tf_op jit(solution)/shard_map/ppermute | solution.py:114
  19.9 0.6 copy-start.13
  20.5 0.7 copy-start.9
  21.2 0.6 copy-start.11
  21.8 0.9 %copy-start.4 = (bf16[2,2,64,256]{3,2,1,0:T(8,128)(2,1)S(1)}, bf16[2,2,64,256]{3,2,1,0:T(8,128)(2,1)}, u32[]{:S(2)}) copy-start(bf16[2,2,64,256]{3,2,1,0:T(8,128)(2,1)} %copy-done.3) | copy-start | bytes 393220
  22.7 0.9 %copy-start.10 = (bf16[384,128]{1,0:T(8,128)(2,1)S(1)}, bf16[384,128]{1,0:T(8,128)(2,1)}, u32[]{:S(2)}) copy-start(bf16[384,128]{1,0:T(8,128)(2,1)} %copy-done.9) | copy-start | bytes 294916
  23.6 0.9 %copy-start.12 = (bf16[384,128]{1,0:T(8,128)(2,1)S(1)}, bf16[384,128]{1,0:T(8,128)(2,1)}, u32[]{:S(2)}) copy-start(bf16[384,128]{1,0:T(8,128)(2,1)} %copy-done.11) | copy-start | bytes 294916
  24.5 0.8 copy-start.14
  25.3 0.8 copy-start.16
  27.8 11.3 %collective-permute-start.4 = (bf16[8,32,256]{2,1,0:T(8,128)(2,1)S(1)}, bf16[8,32,256]{2,1,0:T(8,128)(2,1)S(1)}, u32[]{:S(2)}, u32[]{:S(2)}) collective-permute-start(bf16[8,32,256]{2,1,0:T(8,128)(2,1)S(1)} %get-tuple-element.34), channel_id=1, source_target_pairs={{1,0},{2,1},{3,2},{5,4},{6,5},{7,6},{9,8},{10,9},{11,10},{13,12},{... | collective-permute-start | bytes 393224 | tf_op jit(solution)/shard_map/ppermute | solution.py:20
  29.1 7.9 %collective-permute-start.3 = (bf16[2,96,256]{2,1,0:T(8,128)(2,1)S(1)}, bf16[2,96,256]{2,1,0:T(8,128)(2,1)S(1)}, u32[]{:S(2)}, u32[]{:S(2)}) collective-permute-start(bf16[2,96,256]{2,1,0:T(8,128)(2,1)S(1)} %get-tuple-element.30), channel_id=1, source_target_pairs={{4,0},{8,4},{12,8},{16,12},{20,16},{24,20},{28,24},{5,1},{9,5},{13... | collective-permute-start | bytes 294920 | tf_op jit(solution)/shard_map/ppermute | solution.py:20
  30.4 21.6 %collective-permute-start.9 = (bf16[2,128,256]{2,1,0:T(8,128)(2,1)}, bf16[2,128,256]{2,1,0:T(8,128)(2,1)}, u32[]{:S(2)}, u32[]{:S(2)}) collective-permute-start(bf16[2,128,256]{2,1,0:T(8,128)(2,1)} %get-tuple-element.37.refs_4_), channel_id=1, source_target_pairs={{0,8},{4,12},{8,0},{12,4},{16,24},{20,28},{24,16},{28,20},{1,9},{5... | collective-permute-start | bytes 393224 | tf_op jit(solution)/shard_map/ppermute | solution.py:114
  34.6 19.5 %collective-permute-start.10 = (bf16[2,128,256]{2,1,0:T(8,128)(2,1)}, bf16[2,128,256]{2,1,0:T(8,128)(2,1)}, u32[]{:S(2)}, u32[]{:S(2)}) collective-permute-start(bf16[2,128,256]{2,1,0:T(8,128)(2,1)} %get-tuple-element.37.refs_4_), channel_id=1, source_target_pairs={{0,16},{4,20},{8,24},{12,28},{16,0},{20,4},{24,8},{28,12},{1,17},{... | collective-permute-start | bytes 393224 | tf_op jit(solution)/shard_map/ppermute | solution.py:114
  36.9 17.1 %collective-permute-start.11 = (bf16[2,128,256]{2,1,0:T(8,128)(2,1)}, bf16[2,128,256]{2,1,0:T(8,128)(2,1)}, u32[]{:S(2)}, u32[]{:S(2)}) collective-permute-start(bf16[2,128,256]{2,1,0:T(8,128)(2,1)} %get-tuple-element.37.refs_4_), channel_id=1, source_target_pairs={{0,24},{4,28},{8,16},{12,20},{16,8},{20,12},{24,0},{28,4},{1,25},{... | collective-permute-start | bytes 393224 | tf_op jit(solution)/shard_map/ppermute | solution.py:114
  37.0 21.9 %collective-permute-start.6 = (bf16[8,64,256]{2,1,0:T(8,128)(2,1)}, bf16[8,64,256]{2,1,0:T(8,128)(2,1)}, u32[]{:S(2)}, u32[]{:S(2)}) collective-permute-start(bf16[8,64,256]{2,1,0:T(8,128)(2,1)} %get-tuple-element.33.gathered.refs_0_), channel_id=1, source_target_pairs={{0,2},{1,3},{2,0},{3,1},{4,6},{5,7},{6,4},{7,5},{8,10},{9,11},{10,... | collective-permute-start | bytes 786440 | tf_op jit(solution)/shard_map/ppermute | solution.py:114
  39.2 0.9 %copy-start.5 = (bf16[2,2,64,256]{3,2,1,0:T(8,128)(2,1)S(1)}, bf16[2,2,64,256]{3,2,1,0:T(8,128)(2,1)}, u32[]{:S(2)}) copy-start(bf16[2,2,64,256]{3,2,1,0:T(8,128)(2,1)} %copy-done.3) | copy-start | bytes 393220
  40.1 0.9 %copy-start.7 = (bf16[256,256]{1,0:T(8,128)(2,1)S(1)}, bf16[256,256]{1,0:T(8,128)(2,1)}, u32[]{:S(2)}) copy-start(bf16[256,256]{1,0:T(8,128)(2,1)} %copy-done.6) | copy-start | bytes 393220
  45.8 0.6 copy-start.1
  46.4 12.5 %all-to-all-start.1 = ((bf16[8,16,256]{2,1,0:T(8,128)(2,1)}), bf16[8,16,256]{2,1,0:T(8,128)(2,1)S(1)}, u32[]{:S(2)}, u32[]{:S(2)}) async-start(bf16[8,16,256]{2,1,0:T(8,128)(2,1)} %bitcast.17), calls=%async_computation.1 | async-start | bytes 131072 | tf_op jit(solution)/shard_map/all_to_all | solution.py:470
  52.0 14.0 %collective-permute-start.5 = (bf16[8,64,256]{2,1,0:T(8,128)(2,1)}, bf16[8,64,256]{2,1,0:T(8,128)(2,1)S(1)}, u32[]{:S(2)}, u32[]{:S(2)}) collective-permute-start(bf16[8,64,256]{2,1,0:T(8,128)(2,1)} %get-tuple-element.33.gathered.refs_0_), channel_id=1, source_target_pairs={{0,1},{1,0},{2,3},{3,2},{4,5},{5,4},{6,7},{7,6},{8,9},{9,8},{10,11... | collective-permute-start | bytes 786440 | tf_op jit(solution)/shard_map/ppermute | solution.py:114
  52.0 9.9 %collective-permute-start.8 = (bf16[2,128,256]{2,1,0:T(8,128)(2,1)}, bf16[2,128,256]{2,1,0:T(8,128)(2,1)S(1)}, u32[]{:S(2)}, u32[]{:S(2)}) collective-permute-start(bf16[2,128,256]{2,1,0:T(8,128)(2,1)} %get-tuple-element.37.refs_4_), channel_id=1, source_target_pairs={{0,4},{4,0},{8,12},{12,8},{16,20},{20,16},{24,28},{28,24},{1,5},{5... | collective-permute-start | bytes 393224 | tf_op jit(solution)/shard_map/ppermute | solution.py:114
  54.1 0.8 %copy-start.2 = (bf16[128,256]{1,0:T(8,128)(2,1)S(1)}, bf16[128,256]{1,0:T(8,128)(2,1)}, u32[]{:S(2)}) copy-start(bf16[128,256]{1,0:T(8,128)(2,1)} %copy-done.1) | copy-start | bytes 196612
  58.9 15.5 %collective-permute-start.7 = (bf16[8,64,256]{2,1,0:T(8,128)(2,1)}, bf16[8,64,256]{2,1,0:T(8,128)(2,1)S(1)}, u32[]{:S(2)}, u32[]{:S(2)}) collective-permute-start(bf16[8,64,256]{2,1,0:T(8,128)(2,1)} %collective-permute-done.6.refs_2_), channel_id=1, source_target_pairs={{0,1},{1,0},{2,3},{3,2},{4,5},{5,4},{6,7},{7,6},{8,9},{9,8},{10,11... | collective-permute-start | bytes 786440 | tf_op jit(solution)/shard_map/ppermute | solution.py:114
  59.7 3.0 %collective-permute-start.17 = (f32[1,64]{1,0:T(1,128)S(1)}, f32[1,64]{1,0:T(1,128)S(1)}, u32[]{:S(2)}, u32[]{:S(2)}) collective-permute-start(f32[1,64]{1,0:T(1,128)S(1)} %get-tuple-element.54), channel_id=1, source_target_pairs={{0,3},{1,2},{2,1},{3,0},{4,7},{5,6},{6,5},{7,4},{8,11},{9,10},{10,... | collective-permute-start | bytes 776 | tf_op jit(solution)/shard_map/ppermute | solution.py:114
  59.9 3.6 %collective-permute-start.16 = (f32[1,64]{1,0:T(1,128)S(1)}, f32[1,64]{1,0:T(1,128)S(1)}, u32[]{:S(2)}, u32[]{:S(2)}) collective-permute-start(f32[1,64]{1,0:T(1,128)S(1)} %get-tuple-element.55), channel_id=1, source_target_pairs={{0,2},{1,3},{2,0},{3,1},{4,6},{5,7},{6,4},{7,5},{8,10},{9,11},{10,... | collective-permute-start | bytes 776 | tf_op jit(solution)/shard_map/ppermute | solution.py:114
  61.9 2.9 %collective-permute-start.15 = (f32[1,64]{1,0:T(1,128)S(1)}, f32[1,64]{1,0:T(1,128)S(1)}, u32[]{:S(2)}, u32[]{:S(2)}) collective-permute-start(f32[1,64]{1,0:T(1,128)S(1)} %get-tuple-element.53), channel_id=1, source_target_pairs={{0,1},{1,0},{2,3},{3,2},{4,5},{5,4},{6,7},{7,6},{8,9},{9,8},{10,11... | collective-permute-start | bytes 776 | tf_op jit(solution)/shard_map/ppermute | solution.py:114
  62.7 6.5 %collective-permute-start.12 = (bf16[2,128,256]{2,1,0:T(8,128)(2,1)}, bf16[2,128,256]{2,1,0:T(8,128)(2,1)S(1)}, u32[]{:S(2)}, u32[]{:S(2)}) collective-permute-start(bf16[2,128,256]{2,1,0:T(8,128)(2,1)} %get-tuple-element.38.refs_6_), channel_id=1, source_target_pairs={{0,4},{4,0},{8,12},{12,8},{16,20},{20,16},{24,28},{28,24},{1,5},{5... | collective-permute-start | bytes 393224 | tf_op jit(solution)/shard_map/ppermute | solution.py:114
  63.4 8.6 %collective-permute-start.13 = (bf16[2,128,256]{2,1,0:T(8,128)(2,1)}, bf16[2,128,256]{2,1,0:T(8,128)(2,1)S(1)}, u32[]{:S(2)}, u32[]{:S(2)}) collective-permute-start(bf16[2,128,256]{2,1,0:T(8,128)(2,1)} %get-tuple-element.39.refs_8_), channel_id=1, source_target_pairs={{0,4},{4,0},{8,12},{12,8},{16,20},{20,16},{24,28},{28,24},{1,5},{5... | collective-permute-start | bytes 393224 | tf_op jit(solution)/shard_map/ppermute | solution.py:114
  64.7 9.7 %collective-permute-start.14 = (bf16[2,128,256]{2,1,0:T(8,128)(2,1)}, bf16[2,128,256]{2,1,0:T(8,128)(2,1)S(1)}, u32[]{:S(2)}, u32[]{:S(2)}) collective-permute-start(bf16[2,128,256]{2,1,0:T(8,128)(2,1)} %get-tuple-element.40.refs_10_), channel_id=1, source_target_pairs={{0,4},{4,0},{8,12},{12,8},{16,20},{20,16},{24,28},{28,24},{1,5},{5... | collective-permute-start | bytes 393224 | tf_op jit(solution)/shard_map/ppermute | solution.py:114

commit v4 on v3

--- a/solution.py
+++ b/solution.py
@@ -10,7 +10,6 @@
 EPS = 1e-06
 TAPS = [(a, b, c) for a in range(3) for b in range(3) for c in range(3)]
 VMEM_LIMIT = 20 * 1024 * 1024
-VMEM_LIMIT_WIDE = 48 * 1024 * 1024
 WORK = 1200
 
 
@@ -250,19 +249,13 @@
 
 
 def slab_kernel(
-    F, J, R, T, slot, place, planes, cached, under, weight_hbm, frames, vectors, gathered, following,
-    out, frames_grad, weight, near, ext, tmp, sem,
+    F, J, R, T, slot, place, planes, cached, under, weight, frames, vectors, gathered, following,
+    out, frames_grad, near, ext, tmp,
 ):
     row, block = place[0], place[1]
     channels = frames.shape[1]
     span = F * J
     gain, bias = vectors[0:1], vectors[1:2]
-    taps_a = [
-        pltpu.make_async_copy(weight_hbm.at[pl.ds(a * 9, 9)], weight.at[pl.ds(a * 9, 9)], sem.at[a])
-        for a in range(3)
-    ]
-    for copy in taps_a:
-        copy.start()
 
     orders = [shard_order(J, R, 2, row - 1, moved) for moved in range(2)]
     for pair in range(F // 2 + 1):
@@ -293,8 +286,6 @@
     latent = jnp.zeros((span, channels), jnp.float32)
     sums = {}
     for n, (a, b, c) in enumerate(TAPS):
-        if n % 9 == 0:
-            taps_a[a].wait()
         latent = latent + mm(ext[b, c, a * J : (a + F) * J, :], weight[n])
         piece = near[c // 2, 1 - b // 2, (2 - a) * J : (2 - a + F) * J, :]
         term = mm_t(piece, weight[n])
@@ -334,14 +325,24 @@
     out[...] = value.astype(jnp.bfloat16)
 
 
-def weight_kernel(F, J, R, T, part, place, _, *refs):
-    gathered, hidden = refs[:T], refs[T : T + R]
-    out_hbm, bias_sum, out, grads, even, odd, sem = refs[T + R :]
+def gain_kernel(T, used, received, _, *parts):
+    value = jnp.zeros(received.shape[1:], jnp.float32)
+    for s in range(received.shape[0]):
+        value = value + received[s].astype(jnp.float32)
+    line = lax.broadcasted_iota(jnp.int32, (received.shape[1], 1), 0)
+    value = jnp.where((line >= used) & (line < used + 3), value, 0.0)
+    value = jnp.sum(value, axis=0, keepdims=True)
+    part = received.shape[2] // T
+    for k in range(T):
+        parts[k][...] = value[:, k * part : (k + 1) * part]
+
+
+def order_kernel(F, J, R, T, place, *refs):
+    gathered, (grads, bias_sum) = refs[:T], refs[T:]
     channels = grads.shape[-1]
     span = F * J
     depth = T * span
-    lanes = 2 * part
-    row, block = place[0], place[1]
+    block = place[1]
     grads[:, :, depth:, :] = jnp.zeros((2, R, 2 * J, channels), jnp.bfloat16)
     orders = [shard_order(J, R, R, 0, moved) for moved in range(2)]
     total = jnp.zeros((1, channels), jnp.float32)
@@ -355,6 +356,15 @@
                 for i in range(R):
                     grads[moved, i, pl.ds(at, 2 * J), :] = value[i * 2 * J : (i + 1) * 2 * J]
     bias_sum[...] = slice_of(total, block, 0, T)
+
+
+def weight_kernel(F, J, R, T, part, place, _, grads, *refs):
+    hidden = refs[:R]
+    out_hbm, out, even, odd, sem = refs[R:]
+    channels = grads.shape[-1]
+    depth = T * F * J
+    lanes = 2 * part
+    row = place[0]
     even[:, R * depth :] = jnp.zeros((lanes, depth), jnp.bfloat16)
     for k in range(R):
         at = pl.multiple_of((row ^ k) * depth, 128)
@@ -384,7 +394,7 @@
         copy.wait()
 
 
-def call(kernel, outs, scratch, flops, moved, places, aliases={}, limit=VMEM_LIMIT):
+def call(kernel, outs, scratch, flops, moved, places, aliases={}):
     kinds = {"s": pltpu.SMEM, "v": pltpu.VMEM, "h": pltpu.HBM, "a": pl.ANY}
     specs = [pl.BlockSpec(memory_space=kinds[p]) for p in places]
     count = len(places) - len(outs)
@@ -395,7 +405,7 @@
         out_specs=specs[count:],
         scratch_shapes=scratch,
         input_output_aliases=aliases,
-        compiler_params=pltpu.CompilerParams(vmem_limit_bytes=limit),
+        compiler_params=pltpu.CompilerParams(vmem_limit_bytes=VMEM_LIMIT),
         cost_estimate=pl.CostEstimate(flops=flops, bytes_accessed=moved, transcendentals=0),
     )
 
@@ -446,14 +456,11 @@
         functools.partial(slab_kernel, F, J, R, T, slot),
         [((R * slot, C), bf16), ((4 * span, C), bf16)],
         [
-            pltpu.VMEM((27, C, C), bf16),
             pltpu.VMEM((2, 2, (F + 2) * J, C), bf16),
             pltpu.VMEM((3, 3, (F + 2) * J, C), bf16),
             pltpu.VMEM((2, 4 * span, C // 2), f32),
-            pltpu.SemaphoreType.DMA((3,)),
         ],
-        2 * 54 * span * C * C, 2 * 27 * C * C, "svvvhvvvv" + "vv",
-        limit=VMEM_LIMIT_WIDE,
+        2 * 54 * span * C * C, 2 * 27 * C * C, "svvvvvvvv" + "vv",
     )(place, planes, cached, under, weight, frames_copy, vectors, grad_rows, following)
 
     def after_slab(blocks):
@@ -469,23 +476,32 @@
 
     packed = lax.all_to_all(packed.reshape(R, slot, C), "rows", 0, 0, tiled=True)
     latent = packed[:, :used].reshape(R, F, J // R, C).transpose(1, 0, 2, 3)
-    gain_sum = jnp.sum(packed[:, used : used + 3].astype(f32), axis=(0, 1)).reshape(1, C)
-    gain_grad = gain_sum[:, :part]
+    gains = call(
+        functools.partial(gain_kernel, T, used),
+        [((1, part), f32)] * T,
+        [], R * slot * C, R * slot * C, "va" + "v" * T,
+    )(packed, hidden_all[2])
+    gain_grad = gains[0]
     for k in range(1, T):
-        gain_grad = gain_grad + partners(gain_sum[:, k * part : (k + 1) * part], "tm", k)
-
-    weight_grad, bias_sum = call(
+        gain_grad = gain_grad + partners(gains[k], "tm", k)
+
+    grads, bias_sum = call(
+        functools.partial(order_kernel, F, J, R, T),
+        [((2, R, (F * T + 2) * J, C), bf16), ((1, part), f32)],
+        [],
+        90 * WORK * span * C, 2 * R * T * span * C, "s" + "v" * (T + 2),
+    )(place, *grad_all)
+    (weight_grad,) = call(
         functools.partial(weight_kernel, F, J, R, T, part),
-        [((27, part, C), f32), ((1, part), f32)],
+        [((27, part, C), f32)],
         [
             pltpu.VMEM((27, part, C), f32),
-            pltpu.VMEM((2, R, (F * T + 2) * J, C), bf16),
             pltpu.VMEM((2 * part, (R + 1) * T * span), bf16),
             pltpu.VMEM((2 * part, R * T * span), bf16),
             pltpu.SemaphoreType.DMA((3,)),
         ],
-        220 * WORK * span * C, 8 * 27 * part * C, "sa" + "v" * (T + R) + "hv",
-    )(place, gain_sum, *grad_all, *hidden_all)
+        200 * WORK * span * C, 8 * 27 * part * C, "sav" + "v" * R + "h",
+    )(place, gains[0], grads, *hidden_all)
 
     return (
         latent,

time: 80.6 us -> 80.2 us (level)
  local copies, waits for them, and re-layouts: 14.4 us -> 17.7 us
  waiting for transfers between devices: 17.3 us -> 14.1 us
    ppermute x16, waiting for transfers between devices: 13.3 us -> 8.58 us  [partners(): lax.ppermute(value, axis, [(source, source ^ bits) for source in range(co...]
    unnamed x36 -> x42, local copies, waits for them, and re-layouts: 12.9 us -> 15.5 us
    pallas_call x0 -> x2, Pallas kernels: none -> 2.37 us  [the longest x1 2.28 us: gathered_form(): call(functools.partial(order_kernel, F, J, R, T), [((2, R, (F * T + 2) *...]
    all_to_all x1, waiting for transfers between devices: 3.96 us -> 5.54 us  [gathered_form(): lax.all_to_all(packed.reshape(R, slot, C), 'rows', 0, 0, tiled=True)]
    pallas_call x1, Pallas kernels: 5.38 us -> 4 us  [gathered_form(): call(functools.partial(weight_kernel, F, J, R, T, part), [((27, part, C),...]
    pallas_call x1, Pallas kernels: 4.78 us -> 3.72 us  [gathered_form(): call(functools.partial(slab_kernel, F, J, R, T, slot), [((R * slot, C), b...]
  transfers between devices with their start and end apart: 20 -> 20, of which waited for: 7 -> 5; matrix products, arithmetic and copies ran while one was open for 3% -> 2% of each run, Pallas kernels for 7% -> 9%
where the time goes in v4:
time: 80.2 us; the launch traced here: 79.3 us
  starting transfers between devices  32.8 us (41%)
  local copies, waits for them, and re-layouts  17.7 us (22%)
  waiting for transfers between devices  14.1 us (18%)
  Pallas kernels  12.7 us (16%)
  other arithmetic  1.29 us (2%)
    ppermute x16, starting transfers between devices, partners(): lax.ppermute(value, axis, [(source, source ^ bits) for source in range(co...  17.6 us
    unnamed x42, local copies, waits for them, and re-layouts  15.5 us
    ppermute x16, waiting for transfers between devices, partners(): lax.ppermute(value, axis, [(source, source ^ bits) for source in range(co...  8.58 us
    all_to_all x1, starting transfers between devices, gathered_form(): lax.all_to_all(jnp.broadcast_to(own, (R,) + own.shape[1:]), 'rows', 0, 0,...  7.25 us
    all_to_all x1, waiting for transfers between devices, gathered_form(): lax.all_to_all(packed.reshape(R, slot, C), 'rows', 0, 0, tiled=True)  5.54 us
    all_to_all x1, starting transfers between devices, gathered_form(): lax.all_to_all(packed.reshape(R, slot, C), 'rows', 0, 0, tiled=True)  5.44 us
    pallas_call x1, Pallas kernels, gathered_form(): call(functools.partial(weight_kernel, F, J, R, T, part), [((27, part, C),...  4 us
    pallas_call x1, Pallas kernels, gathered_form(): call(functools.partial(slab_kernel, F, J, R, T, slot), [((R * slot, C), b...  3.72 us
  transfers between devices with their start and end apart: 20, of which 5 were waited for; matrix products, arithmetic and copies ran while one was open for 2% of the time, Pallas kernels for 9%

profile of v4, /device:TPU:0, one launch (start us, length us, event | category | flops | bytes accessed | tf_op | source)
XLA Modules:
  0.0 79.3 jit_solution(15836365808845488187)
XLA Ops:
  0.6 0.8 broadcast_in_dim.7
  1.4 0.7 broadcast_in_dim.8
  2.1 7.3 %all-to-all-start = ((bf16[8,64,256]{2,1,0:T(8,128)(2,1)}), bf16[8,64,256]{2,1,0:T(8,128)(2,1)}, u32[]{:S(2)}, u32[]{:S(2)}) async-start(bf16[8,64,256]{2,1,0:T(8,128)(2,1)} %broadcast_in_dim.8), calls=%async_computation | async-start | bytes 524288 | tf_op jit(solution)/shard_map/all_to_all | solution.py:428
  9.4 0.1 pad_add_fusion.place
  9.5 0.7 pad_maximum_fusion.vectors
  10.2 0.9 %copy-done.12 = bf16[4,2,32,256]{3,2,1,0:T(8,128)(2,1)S(1)} copy-done((bf16[4,2,32,256]{3,2,1,0:T(8,128)(2,1)S(1)}, bf16[4,2,32,256]{3,2,1,0:T(8,128)(2,1)}, u32[]{:S(2)}) %copy-start.12) | copy-done | bytes 131096
  11.1 0.8 %shard_map.92 = (bf16[2,2,64,256]{3,2,1,0:T(8,128)(2,1)S(1)}, bf16[256,256]{1,0:T(8,128)(2,1)S(1)}, f32[2,256]{1,0:T(2,128)S(1)}, bf16[128,128]{1,0:T(8,128)(2,1...) custom-call(s32[2]{0:T(128)S(1)} %pad_add_fusion.place, ...), custom_call_target="tpu_custom_call" | custom-call | flops 1179648000 | bytes 262144 | tf_op jit(solution)/shard_map/pallas_call | solution.py:433
  11.9 0.0 copy-start.3
  11.9 0.6 copy-done.3
  12.6 0.6 copy-done.6
  13.2 0.6 copy-done.19
  13.8 0.0 collective-permute-start
  13.9 1.6 %collective-permute-start.2 = (bf16[384,128]{1,0:T(8,128)(2,1)S(1)}, bf16[384,128]{1,0:T(8,128)(2,1)S(1)}, u32[]{:S(2)}, u32[]{:S(2)}) collective-permute-start(bf16[384,128]{1,0:T(8,128)(2,1)S(1)} %get-tuple-element.32), channel_id=1, source_target_pairs={{0,3},{1,2},{2,1},{3,0},{4,7},{5,6},{6,5},{7,4},{8,11},{9,10},{10,... | collective-permute-start | bytes 294920 | tf_op jit(solution)/shard_map/ppermute | solution.py:113
  15.5 0.5 collective-permute-start.1
  16.0 3.7 %collective-permute-done.1.refs_2_ = bf16[128,128]{1,0:T(8,128)(2,1)S(1)} collective-permute-done((bf16[128,128]{1,0:T(8,128)(2,1)S(1)}, bf16[128,128]{1,0:T(8,128)(2,1)S(1)}, u32[]{:S(2)}, u32[]{:S(2)}) %collective-permute-start.1) | collective-permute-done | bytes 32800 | tf_op jit(solution)/shard_map/ppermute | solution.py:113
  19.7 0.6 copy-done.17
  20.3 0.0 collective-permute-done.refs_1_
  20.3 0.6 copy-done.13
  20.9 0.6 copy-done.15
  21.5 0.0 all-to-all-done.grad_rows
  21.5 0.9 %copy-done.4 = bf16[2,2,64,256]{3,2,1,0:T(8,128)(2,1)S(1)} copy-done((bf16[2,2,64,256]{3,2,1,0:T(8,128)(2,1)S(1)}, bf16[2,2,64,256]{3,2,1,0:T(8,128)(2,1)}, u32[]{:S(2)}) %copy-start.4) | copy-done | bytes 131096
  22.5 0.9 %copy-done.14 = bf16[384,128]{1,0:T(8,128)(2,1)S(1)} copy-done((bf16[384,128]{1,0:T(8,128)(2,1)S(1)}, bf16[384,128]{1,0:T(8,128)(2,1)}, u32[]{:S(2)}) %copy-start.14) | copy-done | bytes 98328
  23.3 0.9 %copy-done.16 = bf16[384,128]{1,0:T(8,128)(2,1)S(1)} copy-done((bf16[384,128]{1,0:T(8,128)(2,1)S(1)}, bf16[384,128]{1,0:T(8,128)(2,1)}, u32[]{:S(2)}) %copy-start.16) | copy-done | bytes 98328
  24.2 0.8 copy-done.18
  25.0 0.8 copy-done.20
  25.8 1.8 %shard_map.93 = (bf16[2,128,256]{2,1,0:T(8,128)(2,1)}, bf16[2,2,32,256]{3,2,1,0:T(8,128)(2,1)S(1)}, bf16[2,96,256]{2,1,0:T(8,128)(2,1)S(1)}, bf16[8,32,256]{2,1,0:T(8,128)(2,1)S(1)}, bf16[8,64,256]{2,1,0:T(8,128)(2,1)}) custom-call(s32[2]{0:T(128)S(1)} %pad_add_fusion.place, bf16[8,64,256]{2,1,0:T(8,128)(2,1)} %all-to-all-done.grad_rows, ...), custom_call_target="tpu_custom_call" | custom-call | flops 589824000 | bytes 262144 | tf_op jit(solution)/shard_map/pallas_call | solution.py:441
  27.5 1.5 %collective-permute-start.9 = (bf16[8,64,256]{2,1,0:T(8,128)(2,1)}, bf16[8,64,256]{2,1,0:T(8,128)(2,1)}, u32[]{:S(2)}, u32[]{:S(2)}) collective-permute-start(bf16[8,64,256]{2,1,0:T(8,128)(2,1)} %get-tuple-element.37.gathered.refs_0_), channel_id=1, source_target_pairs={{0,2},{1,3},{2,0},{3,1},{4,6},{5,7},{6,4},{7,5},{8,10},{9,11},{10,... | collective-permute-start | bytes 786440 | tf_op jit(solution)/shard_map/ppermute | solution.py:113
  29.0 1.3 %collective-permute-start.4 = (bf16[8,32,256]{2,1,0:T(8,128)(2,1)S(1)}, bf16[8,32,256]{2,1,0:T(8,128)(2,1)S(1)}, u32[]{:S(2)}, u32[]{:S(2)}) collective-permute-start(bf16[8,32,256]{2,1,0:T(8,128)(2,1)S(1)} %get-tuple-element.38), channel_id=1, source_target_pairs={{1,0},{2,1},{3,2},{5,4},{6,5},{7,6},{9,8},{10,9},{11,10},{13,12},{... | collective-permute-start | bytes 393224 | tf_op jit(solution)/shard_map/ppermute | solution.py:19
  30.3 1.3 %collective-permute-start.3 = (bf16[2,96,256]{2,1,0:T(8,128)(2,1)S(1)}, bf16[2,96,256]{2,1,0:T(8,128)(2,1)S(1)}, u32[]{:S(2)}, u32[]{:S(2)}) collective-permute-start(bf16[2,96,256]{2,1,0:T(8,128)(2,1)S(1)} %get-tuple-element.34), channel_id=1, source_target_pairs={{4,0},{8,4},{12,8},{16,12},{20,16},{24,20},{28,24},{5,1},{9,5},{13... | collective-permute-start | bytes 294920 | tf_op jit(solution)/shard_map/ppermute | solution.py:19
  31.6 6.0 %collective-permute-start.7 = (bf16[2,128,256]{2,1,0:T(8,128)(2,1)}, bf16[2,128,256]{2,1,0:T(8,128)(2,1)}, u32[]{:S(2)}, u32[]{:S(2)}) collective-permute-start(bf16[2,128,256]{2,1,0:T(8,128)(2,1)} %get-tuple-element.41.refs_0_), channel_id=1, source_target_pairs={{0,24},{4,28},{8,16},{12,20},{16,8},{20,12},{24,0},{28,4},{1,25},{... | collective-permute-start | bytes 393224 | tf_op jit(solution)/shard_map/ppermute | solution.py:113
  37.6 0.0 collective-permute-start.6
  37.6 0.0 collective-permute-done.3.under
  37.6 2.2 %collective-permute-start.5 = (bf16[2,128,256]{2,1,0:T(8,128)(2,1)}, bf16[2,128,256]{2,1,0:T(8,128)(2,1)}, u32[]{:S(2)}, u32[]{:S(2)}) collective-permute-start(bf16[2,128,256]{2,1,0:T(8,128)(2,1)} %get-tuple-element.41.refs_0_), channel_id=1, source_target_pairs={{0,8},{4,12},{8,0},{12,4},{16,24},{20,28},{24,16},{28,20},{1,9},{5... | collective-permute-start | bytes 393224 | tf_op jit(solution)/shard_map/ppermute | solution.py:113
  39.8 0.9 %copy-done.5 = bf16[2,2,64,256]{3,2,1,0:T(8,128)(2,1)S(1)} copy-done((bf16[2,2,64,256]{3,2,1,0:T(8,128)(2,1)S(1)}, bf16[2,2,64,256]{3,2,1,0:T(8,128)(2,1)}, u32[]{:S(2)}) %copy-start.5) | copy-done | bytes 131096
  40.7 0.9 %copy-done.7 = bf16[256,256]{1,0:T(8,128)(2,1)S(1)} copy-done((bf16[256,256]{1,0:T(8,128)(2,1)S(1)}, bf16[256,256]{1,0:T(8,128)(2,1)}, u32[]{:S(2)}) %copy-start.7) | copy-done | bytes 131096
  41.6 3.7 %shard_map.94 = (bf16[128,256]{1,0:T(8,128)(2,1)S(1)}, bf16[256,256]{1,0:T(8,128)(2,1)}) custom-call(s32[2]{0:T(128)S(1)} %pad_add_fusion.place, bf16[2,2,64,256]{3,2,1,0:T(8,128)(2,1)S(1)} %copy-done.5, bf16[2,2,32,256]{3,2,1,0:T(8,128)(2,1)S(1)} %get-tuple-element.33.cached, bf16[2,96,256]{2,1,0:T(8,128)(2,1)S(1)} %collective-permute-done.3.under, ...), custom_call_target="tpu_custom_call" | custom-call | flops 452984832 | bytes 3538944 | tf_op jit(solution)/shard_map/pallas_call | solution.py:455
  45.3 0.6 copy-done.1
  45.9 5.4 %all-to-all-start.1 = ((bf16[8,16,256]{2,1,0:T(8,128)(2,1)}), bf16[8,16,256]{2,1,0:T(8,128)(2,1)S(1)}, u32[]{:S(2)}, u32[]{:S(2)}) async-start(bf16[8,16,256]{2,1,0:T(8,128)(2,1)} %bitcast.16), calls=%async_computation.1 | async-start | bytes 131072 | tf_op jit(solution)/shard_map/all_to_all | solution.py:477
  51.4 0.0 collective-permute-done.9.refs_2_
  51.4 0.5 collective-permute-start.10
  51.9 0.8 %copy-done.2 = bf16[128,256]{1,0:T(8,128)(2,1)S(1)} copy-done((bf16[128,256]{1,0:T(8,128)(2,1)S(1)}, bf16[128,256]{1,0:T(8,128)(2,1)}, u32[]{:S(2)}) %copy-start.2) | copy-done | bytes 65560
  52.7 5.5 %all-to-all-done.1.received = bf16[8,16,256]{2,1,0:T(8,128)(2,1)S(1)} async-done(((bf16[8,16,256]{2,1,0:T(8,128)(2,1)}), bf16[8,16,256]{2,1,0:T(8,128)(2,1)S(1)}, u32[]{:S(2)}, u32[]{:S(2)}) %all-to-all-start.1) | async-done | bytes 65568 | tf_op jit(solution)/shard_map/all_to_all | solution.py:477
  58.3 0.1 shard_map.96
  58.4 0.1 collective-permute-start.15
  58.4 1.3 %collective-permute-start.16 = (f32[1,64]{1,0:T(1,128)S(1)}, f32[1,64]{1,0:T(1,128)S(1)}, u32[]{:S(2)}, u32[]{:S(2)}) collective-permute-start(f32[1,64]{1,0:T(1,128)S(1)} %get-tuple-element.48), channel_id=1, source_target_pairs={{0,2},{1,3},{2,0},{3,1},{4,6},{5,7},{6,4},{7,5},{8,10},{9,11},{10,... | collective-permute-start | bytes 776 | tf_op jit(solution)/shard_map/ppermute | solution.py:113
  59.7 0.6 collective-permute-start.17
  60.3 0.6 copy.15
  61.0 0.4 collective-permute-start.11
  61.3 0.7 collective-permute-done.16
  62.1 0.9 %collective-permute-start.12 = (bf16[2,128,256]{2,1,0:T(8,128)(2,1)}, bf16[2,128,256]{2,1,0:T(8,128)(2,1)S(1)}, u32[]{:S(2)}, u32[]{:S(2)}) collective-permute-start(bf16[2,128,256]{2,1,0:T(8,128)(2,1)} %get-tuple-element.42._.refs_2_), channel_id=1, source_target_pairs={{0,4},{4,0},{8,12},{12,8},{16,20},{20,16},{24,28},{28,24},{1,5},{5... | collective-permute-start | bytes 393224 | tf_op jit(solution)/shard_map/ppermute | solution.py:113
  63.0 0.0 collective-permute-done.17
  63.0 1.1 %collective-permute-start.13 = (bf16[2,128,256]{2,1,0:T(8,128)(2,1)}, bf16[2,128,256]{2,1,0:T(8,128)(2,1)S(1)}, u32[]{:S(2)}, u32[]{:S(2)}) collective-permute-start(bf16[2,128,256]{2,1,0:T(8,128)(2,1)} %get-tuple-element.45.refs_4_), channel_id=1, source_target_pairs={{0,4},{4,0},{8,12},{12,8},{16,20},{20,16},{24,28},{28,24},{1,5},{5... | collective-permute-start | bytes 393224 | tf_op jit(solution)/shard_map/ppermute | solution.py:113
  64.1 0.5 add_bitcast_fusion
  64.6 0.0 collective-permute-done.8.refs_1_
  64.6 0.7 copy-done.8
  65.3 0.9 %collective-permute-start.14 = (bf16[2,128,256]{2,1,0:T(8,128)(2,1)}, bf16[2,128,256]{2,1,0:T(8,128)(2,1)S(1)}, u32[]{:S(2)}, u32[]{:S(2)}) collective-permute-start(bf16[2,128,256]{2,1,0:T(8,128)(2,1)} %get-tuple-element.46.refs_6_), channel_id=1, source_target_pairs={{0,4},{4,0},{8,12},{12,8},{16,20},{20,16},{24,28},{28,24},{1,5},{5... | collective-permute-start | bytes 393224 | tf_op jit(solution)/shard_map/ppermute | solution.py:113
  66.2 0.7 copy-done.10
  67.0 0.9 %copy-done.9 = bf16[8,64,256]{2,1,0:T(8,128)(2,1)S(1)} copy-done((bf16[8,64,256]{2,1,0:T(8,128)(2,1)S(1)}, bf16[8,64,256]{2,1,0:T(8,128)(2,1)}, u32[]{:S(2)}) %copy-start.9) | copy-done | bytes 262168
  67.9 0.9 %copy-done.11 = bf16[8,64,256]{2,1,0:T(8,128)(2,1)S(1)} copy-done((bf16[8,64,256]{2,1,0:T(8,128)(2,1)S(1)}, bf16[8,64,256]{2,1,0:T(8,128)(2,1)}, u32[]{:S(2)}) %copy-start.11) | copy-done | bytes 262168
  68.9 2.3 %shard_map.97 = (bf16[2,8,288,256]{3,2,1,0:T(8,128)(2,1)S(1)}, f32[1,64]{1,0:T(1,128)}) custom-call(s32[2]{0:T(128)S(1)} %pad_add_fusion.place, bf16[8,64,256]{2,1,0:T(8,128)(2,1)} %get-tuple-element.37.gathered.refs_0_, bf16[8,64,256]{2,1,0:T(8,128)(2,1)S(1)} %copy-done.9, bf16[8,64,256]{2,1,0:T(8,128)(2,1)} %collective-permute-done.9.refs_2_, ...), custom_call_target="tpu_custom_call" | custom-call | flops 1769472000 | bytes 1048576 | tf_op jit(solution)/shard_map/pallas_call | solution.py:488
  71.2 0.0 collective-permute-done.11.refs_1_
  71.2 1.9 %collective-permute-done.13.refs_5_ = bf16[2,128,256]{2,1,0:T(8,128)(2,1)S(1)} collective-permute-done((bf16[2,128,256]{2,1,0:T(8,128)(2,1)}, bf16[2,128,256]{2,1,0:T(8,128)(2,1)S(1)}, u32[]{:S(2)}, u32[]{:S(2)}) %collective-permute-start.13) | collective-permute-done | bytes 131104 | tf_op jit(solution)/shard_map/ppermute | solution.py:113
  73.1 2.2 %collective-permute-done.14.refs_7_ = bf16[2,128,256]{2,1,0:T(8,128)(2,1)S(1)} collective-permute-done((bf16[2,128,256]{2,1,0:T(8,128)(2,1)}, bf16[2,128,256]{2,1,0:T(8,128)(2,1)S(1)}, u32[]{:S(2)}, u32[]{:S(2)}) %collective-permute-start.14) | collective-permute-done | bytes 131104 | tf_op jit(solution)/shard_map/ppermute | solution.py:113
  75.3 4.0 %shard_map.98 = f32[27,64,256]{2,1,0:T(8,128)} custom-call(s32[2]{0:T(128)S(1)} %pad_add_fusion.place, f32[1,64]{1,0:T(1,128)S(1)} %get-tuple-element.43._, bf16[2,8,288,256]{3,2,1,0:T(8,128)(2,1)S(1)} %get-tuple-element.44.grads, bf16[2,128,256]{2,1,0:T(8,128)(2,1)} %get-tuple-element.41.refs_0_, bf16[2,128,256]{2,1,0:T(8,128)(2,1)S(1)} %collective-permute-done.11.refs_1_, ...), custom_call_target="tpu_custom_call" | custom-call | flops 3932160000 | bytes 3538944 | tf_op jit(solution)/shard_map/pallas_call | solution.py:494
  (33 shorter events, 0.1 us)
Async XLA Ops:
  2.1 19.4 %all-to-all-start = ((bf16[8,64,256]{2,1,0:T(8,128)(2,1)}), bf16[8,64,256]{2,1,0:T(8,128)(2,1)}, u32[]{:S(2)}, u32[]{:S(2)}) async-start(bf16[8,64,256]{2,1,0:T(8,128)(2,1)} %broadcast_in_dim.8), calls=%async_computation | async-start | bytes 524288 | tf_op jit(solution)/shard_map/all_to_all | solution.py:428
  10.2 0.9 %copy-start.12 = (bf16[4,2,32,256]{3,2,1,0:T(8,128)(2,1)S(1)}, bf16[4,2,32,256]{3,2,1,0:T(8,128)(2,1)}, u32[]{:S(2)}) copy-start(bf16[4,2,32,256]{3,2,1,0:T(8,128)(2,1)} %param.5) | copy-start | bytes 393220
  11.1 28.7 %copy-start = (bf16[3,3,3,256,256]{4,3,2,1,0:T(8,128)(2,1)S(1)}, bf16[3,3,3,256,256]{4,3,2,1,0:T(8,128)(2,1)}, u32[]{:S(2)}) copy-start(bf16[3,3,3,256,256]{4,3,2,1,0:T(8,128)(2,1)} %param.7) | copy-start | bytes 10616836
  11.9 0.7 copy-start.3
  12.6 0.7 copy-start.6
  13.2 0.6 copy-start.19
  13.8 6.4 %collective-permute-start = (bf16[384,128]{1,0:T(8,128)(2,1)S(1)}, bf16[384,128]{1,0:T(8,128)(2,1)S(1)}, u32[]{:S(2)}, u32[]{:S(2)}) collective-permute-start(bf16[384,128]{1,0:T(8,128)(2,1)S(1)} %get-tuple-element.30), channel_id=1, source_target_pairs={{0,1},{1,0},{2,3},{3,2},{4,5},{5,4},{6,7},{7,6},{8,9},{9,8},{10,11... | collective-permute-start | bytes 294920 | tf_op jit(solution)/shard_map/ppermute | solution.py:113
  13.9 7.1 %collective-permute-start.2 = (bf16[384,128]{1,0:T(8,128)(2,1)S(1)}, bf16[384,128]{1,0:T(8,128)(2,1)S(1)}, u32[]{:S(2)}, u32[]{:S(2)}) collective-permute-start(bf16[384,128]{1,0:T(8,128)(2,1)S(1)} %get-tuple-element.32), channel_id=1, source_target_pairs={{0,3},{1,2},{2,1},{3,0},{4,7},{5,6},{6,5},{7,4},{8,11},{9,10},{10,... | collective-permute-start | bytes 294920 | tf_op jit(solution)/shard_map/ppermute | solution.py:113
  15.5 4.2 %collective-permute-start.1 = (bf16[128,128]{1,0:T(8,128)(2,1)S(1)}, bf16[128,128]{1,0:T(8,128)(2,1)S(1)}, u32[]{:S(2)}, u32[]{:S(2)}) collective-permute-start(bf16[128,128]{1,0:T(8,128)(2,1)S(1)} %get-tuple-element.31), channel_id=1, source_target_pairs={{0,2},{1,3},{2,0},{3,1},{4,6},{5,7},{6,4},{7,5},{8,10},{9,11},{10,... | collective-permute-start | bytes 98312 | tf_op jit(solution)/shard_map/ppermute | solution.py:113
  19.6 0.6 copy-start.17
  20.3 0.6 copy-start.13
  20.9 0.6 copy-start.15
  21.5 0.9 %copy-start.4 = (bf16[2,2,64,256]{3,2,1,0:T(8,128)(2,1)S(1)}, bf16[2,2,64,256]{3,2,1,0:T(8,128)(2,1)}, u32[]{:S(2)}) copy-start(bf16[2,2,64,256]{3,2,1,0:T(8,128)(2,1)} %copy-done.3) | copy-start | bytes 393220
  22.5 0.9 %copy-start.14 = (bf16[384,128]{1,0:T(8,128)(2,1)S(1)}, bf16[384,128]{1,0:T(8,128)(2,1)}, u32[]{:S(2)}) copy-start(bf16[384,128]{1,0:T(8,128)(2,1)} %copy-done.13) | copy-start | bytes 294916
  23.3 0.9 %copy-start.16 = (bf16[384,128]{1,0:T(8,128)(2,1)S(1)}, bf16[384,128]{1,0:T(8,128)(2,1)}, u32[]{:S(2)}) copy-start(bf16[384,128]{1,0:T(8,128)(2,1)} %copy-done.15) | copy-start | bytes 294916
  24.2 0.8 copy-start.18
  25.0 0.8 copy-start.20
  27.5 23.8 %collective-permute-start.9 = (bf16[8,64,256]{2,1,0:T(8,128)(2,1)}, bf16[8,64,256]{2,1,0:T(8,128)(2,1)}, u32[]{:S(2)}, u32[]{:S(2)}) collective-permute-start(bf16[8,64,256]{2,1,0:T(8,128)(2,1)} %get-tuple-element.37.gathered.refs_0_), channel_id=1, source_target_pairs={{0,2},{1,3},{2,0},{3,1},{4,6},{5,7},{6,4},{7,5},{8,10},{9,11},{10,... | collective-permute-start | bytes 786440 | tf_op jit(solution)/shard_map/ppermute | solution.py:113
  29.0 10.7 %collective-permute-start.4 = (bf16[8,32,256]{2,1,0:T(8,128)(2,1)S(1)}, bf16[8,32,256]{2,1,0:T(8,128)(2,1)S(1)}, u32[]{:S(2)}, u32[]{:S(2)}) collective-permute-start(bf16[8,32,256]{2,1,0:T(8,128)(2,1)S(1)} %get-tuple-element.38), channel_id=1, source_target_pairs={{1,0},{2,1},{3,2},{5,4},{6,5},{7,6},{9,8},{10,9},{11,10},{13,12},{... | collective-permute-start | bytes 393224 | tf_op jit(solution)/shard_map/ppermute | solution.py:19
  30.3 7.3 %collective-permute-start.3 = (bf16[2,96,256]{2,1,0:T(8,128)(2,1)S(1)}, bf16[2,96,256]{2,1,0:T(8,128)(2,1)S(1)}, u32[]{:S(2)}, u32[]{:S(2)}) collective-permute-start(bf16[2,96,256]{2,1,0:T(8,128)(2,1)S(1)} %get-tuple-element.34), channel_id=1, source_target_pairs={{4,0},{8,4},{12,8},{16,12},{20,16},{24,20},{28,24},{5,1},{9,5},{13... | collective-permute-start | bytes 294920 | tf_op jit(solution)/shard_map/ppermute | solution.py:19
  31.6 20.2 %collective-permute-start.7 = (bf16[2,128,256]{2,1,0:T(8,128)(2,1)}, bf16[2,128,256]{2,1,0:T(8,128)(2,1)}, u32[]{:S(2)}, u32[]{:S(2)}) collective-permute-start(bf16[2,128,256]{2,1,0:T(8,128)(2,1)} %get-tuple-element.41.refs_0_), channel_id=1, source_target_pairs={{0,24},{4,28},{8,16},{12,20},{16,8},{20,12},{24,0},{28,4},{1,25},{... | collective-permute-start | bytes 393224 | tf_op jit(solution)/shard_map/ppermute | solution.py:113
  37.6 14.3 %collective-permute-start.6 = (bf16[2,128,256]{2,1,0:T(8,128)(2,1)}, bf16[2,128,256]{2,1,0:T(8,128)(2,1)}, u32[]{:S(2)}, u32[]{:S(2)}) collective-permute-start(bf16[2,128,256]{2,1,0:T(8,128)(2,1)} %get-tuple-element.41.refs_0_), channel_id=1, source_target_pairs={{0,16},{4,20},{8,24},{12,28},{16,0},{20,4},{24,8},{28,12},{1,17},{... | collective-permute-start | bytes 393224 | tf_op jit(solution)/shard_map/ppermute | solution.py:113
  37.6 14.3 %collective-permute-start.5 = (bf16[2,128,256]{2,1,0:T(8,128)(2,1)}, bf16[2,128,256]{2,1,0:T(8,128)(2,1)}, u32[]{:S(2)}, u32[]{:S(2)}) collective-permute-start(bf16[2,128,256]{2,1,0:T(8,128)(2,1)} %get-tuple-element.41.refs_0_), channel_id=1, source_target_pairs={{0,8},{4,12},{8,0},{12,4},{16,24},{20,28},{24,16},{28,20},{1,9},{5... | collective-permute-start | bytes 393224 | tf_op jit(solution)/shard_map/ppermute | solution.py:113
  39.8 0.9 %copy-start.5 = (bf16[2,2,64,256]{3,2,1,0:T(8,128)(2,1)S(1)}, bf16[2,2,64,256]{3,2,1,0:T(8,128)(2,1)}, u32[]{:S(2)}) copy-start(bf16[2,2,64,256]{3,2,1,0:T(8,128)(2,1)} %copy-done.3) | copy-start | bytes 393220
  40.7 0.9 %copy-start.7 = (bf16[256,256]{1,0:T(8,128)(2,1)S(1)}, bf16[256,256]{1,0:T(8,128)(2,1)}, u32[]{:S(2)}) copy-start(bf16[256,256]{1,0:T(8,128)(2,1)} %copy-done.6) | copy-start | bytes 393220
  45.3 0.6 copy-start.1
  45.9 12.3 %all-to-all-start.1 = ((bf16[8,16,256]{2,1,0:T(8,128)(2,1)}), bf16[8,16,256]{2,1,0:T(8,128)(2,1)S(1)}, u32[]{:S(2)}, u32[]{:S(2)}) async-start(bf16[8,16,256]{2,1,0:T(8,128)(2,1)} %bitcast.16), calls=%async_computation.1 | async-start | bytes 131072 | tf_op jit(solution)/shard_map/all_to_all | solution.py:477
  51.3 13.3 %collective-permute-start.8 = (bf16[8,64,256]{2,1,0:T(8,128)(2,1)}, bf16[8,64,256]{2,1,0:T(8,128)(2,1)S(1)}, u32[]{:S(2)}, u32[]{:S(2)}) collective-permute-start(bf16[8,64,256]{2,1,0:T(8,128)(2,1)} %get-tuple-element.37.gathered.refs_0_), channel_id=1, source_target_pairs={{0,1},{1,0},{2,3},{3,2},{4,5},{5,4},{6,7},{7,6},{8,9},{9,8},{10,11... | collective-permute-start | bytes 786440 | tf_op jit(solution)/shard_map/ppermute | solution.py:113
  51.4 14.9 %collective-permute-start.10 = (bf16[8,64,256]{2,1,0:T(8,128)(2,1)}, bf16[8,64,256]{2,1,0:T(8,128)(2,1)S(1)}, u32[]{:S(2)}, u32[]{:S(2)}) collective-permute-start(bf16[8,64,256]{2,1,0:T(8,128)(2,1)} %collective-permute-done.9.refs_2_), channel_id=1, source_target_pairs={{0,1},{1,0},{2,3},{3,2},{4,5},{5,4},{6,7},{7,6},{8,9},{9,8},{10,11... | collective-permute-start | bytes 786440 | tf_op jit(solution)/shard_map/ppermute | solution.py:113
  51.9 0.8 %copy-start.2 = (bf16[128,256]{1,0:T(8,128)(2,1)S(1)}, bf16[128,256]{1,0:T(8,128)(2,1)}, u32[]{:S(2)}) copy-start(bf16[128,256]{1,0:T(8,128)(2,1)} %copy-done.1) | copy-start | bytes 196612
  58.4 2.6 %collective-permute-start.15 = (f32[1,64]{1,0:T(1,128)S(1)}, f32[1,64]{1,0:T(1,128)S(1)}, u32[]{:S(2)}, u32[]{:S(2)}) collective-permute-start(f32[1,64]{1,0:T(1,128)S(1)} %get-tuple-element.47), channel_id=1, source_target_pairs={{0,1},{1,0},{2,3},{3,2},{4,5},{5,4},{6,7},{7,6},{8,9},{9,8},{10,11... | collective-permute-start | bytes 776 | tf_op jit(solution)/shard_map/ppermute | solution.py:113
  58.4 3.6 %collective-permute-start.16 = (f32[1,64]{1,0:T(1,128)S(1)}, f32[1,64]{1,0:T(1,128)S(1)}, u32[]{:S(2)}, u32[]{:S(2)}) collective-permute-start(f32[1,64]{1,0:T(1,128)S(1)} %get-tuple-element.48), channel_id=1, source_target_pairs={{0,2},{1,3},{2,0},{3,1},{4,6},{5,7},{6,4},{7,5},{8,10},{9,11},{10,... | collective-permute-start | bytes 776 | tf_op jit(solution)/shard_map/ppermute | solution.py:113
  59.7 3.2 %collective-permute-start.17 = (f32[1,64]{1,0:T(1,128)S(1)}, f32[1,64]{1,0:T(1,128)S(1)}, u32[]{:S(2)}, u32[]{:S(2)}) collective-permute-start(f32[1,64]{1,0:T(1,128)S(1)} %get-tuple-element.49), channel_id=1, source_target_pairs={{0,3},{1,2},{2,1},{3,0},{4,7},{5,6},{6,5},{7,4},{8,11},{9,10},{10,... | collective-permute-start | bytes 776 | tf_op jit(solution)/shard_map/ppermute | solution.py:113
  61.0 10.2 %collective-permute-start.11 = (bf16[2,128,256]{2,1,0:T(8,128)(2,1)}, bf16[2,128,256]{2,1,0:T(8,128)(2,1)S(1)}, u32[]{:S(2)}, u32[]{:S(2)}) collective-permute-start(bf16[2,128,256]{2,1,0:T(8,128)(2,1)} %get-tuple-element.41.refs_0_), channel_id=1, source_target_pairs={{0,4},{4,0},{8,12},{12,8},{16,20},{20,16},{24,28},{28,24},{1,5},{5... | collective-permute-start | bytes 393224 | tf_op jit(solution)/shard_map/ppermute | solution.py:113
  62.1 13.3 %collective-permute-start.12 = (bf16[2,128,256]{2,1,0:T(8,128)(2,1)}, bf16[2,128,256]{2,1,0:T(8,128)(2,1)S(1)}, u32[]{:S(2)}, u32[]{:S(2)}) collective-permute-start(bf16[2,128,256]{2,1,0:T(8,128)(2,1)} %get-tuple-element.42._.refs_2_), channel_id=1, source_target_pairs={{0,4},{4,0},{8,12},{12,8},{16,20},{20,16},{24,28},{28,24},{1,5},{5... | collective-permute-start | bytes 393224 | tf_op jit(solution)/shard_map/ppermute | solution.py:113
  63.0 10.1 %collective-permute-start.13 = (bf16[2,128,256]{2,1,0:T(8,128)(2,1)}, bf16[2,128,256]{2,1,0:T(8,128)(2,1)S(1)}, u32[]{:S(2)}, u32[]{:S(2)}) collective-permute-start(bf16[2,128,256]{2,1,0:T(8,128)(2,1)} %get-tuple-element.45.refs_4_), channel_id=1, source_target_pairs={{0,4},{4,0},{8,12},{12,8},{16,20},{20,16},{24,28},{28,24},{1,5},{5... | collective-permute-start | bytes 393224 | tf_op jit(solution)/shard_map/ppermute | solution.py:113
  64.6 0.7 copy-start.8
  65.3 10.0 %collective-permute-start.14 = (bf16[2,128,256]{2,1,0:T(8,128)(2,1)}, bf16[2,128,256]{2,1,0:T(8,128)(2,1)S(1)}, u32[]{:S(2)}, u32[]{:S(2)}) collective-permute-start(bf16[2,128,256]{2,1,0:T(8,128)(2,1)} %get-tuple-element.46.refs_6_), channel_id=1, source_target_pairs={{0,4},{4,0},{8,12},{12,8},{16,20},{20,16},{24,28},{28,24},{1,5},{5... | collective-permute-start | bytes 393224 | tf_op jit(solution)/shard_map/ppermute | solution.py:113
  66.2 0.7 copy-start.10
  67.0 0.9 %copy-start.9 = (bf16[8,64,256]{2,1,0:T(8,128)(2,1)S(1)}, bf16[8,64,256]{2,1,0:T(8,128)(2,1)}, u32[]{:S(2)}) copy-start(bf16[8,64,256]{2,1,0:T(8,128)(2,1)} %copy-done.8) | copy-start | bytes 786436
  67.9 0.9 %copy-start.11 = (bf16[8,64,256]{2,1,0:T(8,128)(2,1)S(1)}, bf16[8,64,256]{2,1,0:T(8,128)(2,1)}, u32[]{:S(2)}) copy-start(bf16[8,64,256]{2,1,0:T(8,128)(2,1)} %copy-done.10) | copy-start | bytes 786436

commit v5 on v4

--- a/solution.py
+++ b/solution.py
@@ -10,6 +10,7 @@
 EPS = 1e-06
 TAPS = [(a, b, c) for a in range(3) for b in range(3) for c in range(3)]
 VMEM_LIMIT = 20 * 1024 * 1024
+VMEM_LIMIT_WIDE = 61 * 1024 * 1024
 WORK = 1200
 
 
@@ -249,13 +250,19 @@
 
 
 def slab_kernel(
-    F, J, R, T, slot, place, planes, cached, under, weight, frames, vectors, gathered, following,
-    out, frames_grad, near, ext, tmp,
+    F, J, R, T, slot, place, planes, cached, under, weight_hbm, frames, vectors, gathered, following,
+    out, frames_grad, weight, near, ext, tmp, sem,
 ):
     row, block = place[0], place[1]
     channels = frames.shape[1]
     span = F * J
     gain, bias = vectors[0:1], vectors[1:2]
+    fetches = [
+        pltpu.make_async_copy(weight_hbm.at[pl.ds(a * 9, 9)], weight.at[pl.ds(a * 9, 9)], sem.at[a])
+        for a in range(3)
+    ]
+    for copy in fetches:
+        copy.start()
 
     orders = [shard_order(J, R, 2, row - 1, moved) for moved in range(2)]
     for pair in range(F // 2 + 1):
@@ -286,6 +293,8 @@
     latent = jnp.zeros((span, channels), jnp.float32)
     sums = {}
     for n, (a, b, c) in enumerate(TAPS):
+        if n % 9 == 0:
+            fetches[a].wait()
         latent = latent + mm(ext[b, c, a * J : (a + F) * J, :], weight[n])
         piece = near[c // 2, 1 - b // 2, (2 - a) * J : (2 - a + F) * J, :]
         term = mm_t(piece, weight[n])
@@ -394,7 +403,7 @@
         copy.wait()
 
 
-def call(kernel, outs, scratch, flops, moved, places, aliases={}):
+def call(kernel, outs, scratch, flops, moved, places, aliases={}, limit=VMEM_LIMIT):
     kinds = {"s": pltpu.SMEM, "v": pltpu.VMEM, "h": pltpu.HBM, "a": pl.ANY}
     specs = [pl.BlockSpec(memory_space=kinds[p]) for p in places]
     count = len(places) - len(outs)
@@ -405,7 +414,7 @@
         out_specs=specs[count:],
         scratch_shapes=scratch,
         input_output_aliases=aliases,
-        compiler_params=pltpu.CompilerParams(vmem_limit_bytes=VMEM_LIMIT),
+        compiler_params=pltpu.CompilerParams(vmem_limit_bytes=limit),
         cost_estimate=pl.CostEstimate(flops=flops, bytes_accessed=moved, transcendentals=0),
     )
 
@@ -456,11 +465,14 @@
         functools.partial(slab_kernel, F, J, R, T, slot),
         [((R * slot, C), bf16), ((4 * span, C), bf16)],
         [
+            pltpu.VMEM((27, C, C), bf16),
             pltpu.VMEM((2, 2, (F + 2) * J, C), bf16),
             pltpu.VMEM((3, 3, (F + 2) * J, C), bf16),
             pltpu.VMEM((2, 4 * span, C // 2), f32),
+            pltpu.SemaphoreType.DMA((3,)),
         ],
-        2 * 54 * span * C * C, 2 * 27 * C * C, "svvvvvvvv" + "vv",
+        2 * 54 * span * C * C, 2 * 27 * C * C, "svvvhvvvv" + "vv",
+        limit=VMEM_LIMIT_WIDE,
     )(place, planes, cached, under, weight, frames_copy, vectors, grad_rows, following)
 
     def after_slab(blocks):
@@ -480,7 +492,7 @@
         functools.partial(gain_kernel, T, used),
         [((1, part), f32)] * T,
         [], R * slot * C, R * slot * C, "va" + "v" * T,
-    )(packed, hidden_all[2])
+    )(packed, hidden_all[-1])
     gain_grad = gains[0]
     for k in range(1, T):
         gain_grad = gain_grad + partners(gains[k], "tm", k)

time: 80.2 us -> 73.5 us (0.916)
  local copies, waits for them, and re-layouts: 17.7 us -> 7.35 us
  waiting for transfers between devices: 14.1 us -> 20.9 us
  starting transfers between devices: 32.8 us -> 30.5 us
    unnamed x42 -> x24, local copies, waits for them, and re-layouts: 15.5 us -> 5.19 us
    ppermute x16, waiting for transfers between devices: 8.58 us -> 14.5 us  [partners(): lax.ppermute(value, axis, [(source, source ^ bits) for source in range(co...]
    pallas_call x1, Pallas kernels: 3.72 us -> 5.33 us  [gathered_form(): call(functools.partial(slab_kernel, F, J, R, T, slot), [((R * slot, C), b...]
    ppermute x16, starting transfers between devices: 17.6 us -> 16.2 us  [partners(): lax.ppermute(value, axis, [(source, source ^ bits) for source in range(co...]
    pallas_call x1, Pallas kernels: 1.75 us -> 0.65 us  [gathered_form(): call(functools.partial(join_kernel, F, J, T), [((2, 2 * part, T * span),...]
    all_to_all x1, starting transfers between devices: 5.44 us -> 4.54 us  [gathered_form(): lax.all_to_all(packed.reshape(R, slot, C), 'rows', 0, 0, tiled=True)]
    all_to_all x1, waiting for transfers between devices: 5.54 us -> 6.39 us  [gathered_form(): lax.all_to_all(packed.reshape(R, slot, C), 'rows', 0, 0, tiled=True)]
  transfers between devices with their start and end apart: 20 -> 20, of which waited for: 5 -> 6; matrix products, arithmetic and copies ran while one was open for 2% -> 3% of each run, Pallas kernels for 9% -> 11%
where the time goes in v5:
time: 73.5 us; the launch traced here: 72.9 us
  starting transfers between devices  30.5 us (41%)
  waiting for transfers between devices  20.9 us (28%)
  Pallas kernels  12.1 us (16%)
  local copies, waits for them, and re-layouts  7.35 us (10%)
  other arithmetic  1.29 us (2%)
  between operations  0.78 us (1%)
    ppermute x16, starting transfers between devices, partners(): lax.ppermute(value, axis, [(source, source ^ bits) for source in range(co...  16.2 us
    ppermute x16, waiting for transfers between devices, partners(): lax.ppermute(value, axis, [(source, source ^ bits) for source in range(co...  14.5 us
    all_to_all x1, starting transfers between devices, gathered_form(): lax.all_to_all(jnp.broadcast_to(own, (R,) + own.shape[1:]), 'rows', 0, 0,...  7.25 us
    all_to_all x1, waiting for transfers between devices, gathered_form(): lax.all_to_all(packed.reshape(R, slot, C), 'rows', 0, 0, tiled=True)  6.39 us
    pallas_call x1, Pallas kernels, gathered_form(): call(functools.partial(slab_kernel, F, J, R, T, slot), [((R * slot, C), b...  5.33 us
    unnamed x24, local copies, waits for them, and re-layouts  5.19 us
    all_to_all x1, starting transfers between devices, gathered_form(): lax.all_to_all(packed.reshape(R, slot, C), 'rows', 0, 0, tiled=True)  4.54 us
    pallas_call x1, Pallas kernels, gathered_form(): call(functools.partial(weight_kernel, F, J, R, T, part), [((27, part, C),...  3.43 us
  transfers between devices with their start and end apart: 20, of which 6 were waited for; matrix products, arithmetic and copies ran while one was open for 3% of the time, Pallas kernels for 11%

profile of v5, /device:TPU:0, one launch (start us, length us, event | category | flops | bytes accessed | tf_op | source)
XLA Modules:
  0.0 72.9 jit_solution(3121199930087136252)
XLA Ops:
  0.6 0.8 %broadcast_in_dim.7 = bf16[64,256]{1,0:T(8,128)(2,1)S(1)} reshape(bf16[4,8,2,256]{3,2,1,0:T(2,128)(2,1)} %param.9) | data formatting | bytes 65536 | tf_op jit(solution)/shard_map/broadcast_in_dim | solution.py:438
  1.4 0.7 broadcast_in_dim.8
  2.1 7.3 %all-to-all-start = ((bf16[8,64,256]{2,1,0:T(8,128)(2,1)}), bf16[8,64,256]{2,1,0:T(8,128)(2,1)S(1)}, u32[]{:S(2)}, u32[]{:S(2)}) async-start(bf16[8,64,256]{2,1,0:T(8,128)(2,1)} %broadcast_in_dim.8), calls=%async_computation | async-start | bytes 524288 | tf_op jit(solution)/shard_map/all_to_all | solution.py:437
  9.4 0.1 pad_add_fusion.place
  9.5 0.7 pad_maximum_fusion.vectors
  10.2 0.9 %copy-done.9 = bf16[4,2,32,256]{3,2,1,0:T(8,128)(2,1)S(1)} copy-done((bf16[4,2,32,256]{3,2,1,0:T(8,128)(2,1)S(1)}, bf16[4,2,32,256]{3,2,1,0:T(8,128)(2,1)}, u32[]{:S(2)}) %copy-start.9) | copy-done | bytes 131096
  11.1 0.8 %shard_map.92 = (bf16[2,2,64,256]{3,2,1,0:T(8,128)(2,1)S(1)}, bf16[256,256]{1,0:T(8,128)(2,1)S(1)}, f32[2,256]{1,0:T(2,128)S(1)}, bf16[128,128]{1,0:T(8,128)(2,1...) custom-call(s32[2]{0:T(128)S(1)} %pad_add_fusion.place, ...), custom_call_target="tpu_custom_call" | custom-call | flops 1179648000 | bytes 262144 | tf_op jit(solution)/shard_map/pallas_call | solution.py:442
  11.9 0.0 copy-start.4
  11.9 0.6 copy-done.4
  12.6 0.6 copy-done.6
  13.2 0.0 collective-permute-start
  13.2 1.6 %collective-permute-start.2 = (bf16[384,128]{1,0:T(8,128)(2,1)S(1)}, bf16[384,128]{1,0:T(8,128)(2,1)S(1)}, u32[]{:S(2)}, u32[]{:S(2)}) collective-permute-start(bf16[384,128]{1,0:T(8,128)(2,1)S(1)} %get-tuple-element.32), channel_id=1, source_target_pairs={{0,3},{1,2},{2,1},{3,0},{4,7},{5,6},{6,5},{7,4},{8,11},{9,10},{10,... | collective-permute-start | bytes 294920 | tf_op jit(solution)/shard_map/ppermute | solution.py:114
  14.8 0.5 collective-permute-start.1
  15.3 3.7 %collective-permute-done.1.refs_2_ = bf16[128,128]{1,0:T(8,128)(2,1)S(1)} collective-permute-done((bf16[128,128]{1,0:T(8,128)(2,1)S(1)}, bf16[128,128]{1,0:T(8,128)(2,1)S(1)}, u32[]{:S(2)}, u32[]{:S(2)}) %collective-permute-start.1) | collective-permute-done | bytes 32800 | tf_op jit(solution)/shard_map/ppermute | solution.py:114
  19.0 0.0 collective-permute-done.refs_1_
  19.0 0.0 collective-permute-done.2.refs_3_
  19.0 0.0 all-to-all-done.grad_rows
  19.0 0.7 shard_map.93
  19.6 0.6 copy-done.5
  20.3 1.3 %collective-permute-start.3 = (bf16[2,96,256]{2,1,0:T(8,128)(2,1)S(1)}, bf16[2,96,256]{2,1,0:T(8,128)(2,1)S(1)}, u32[]{:S(2)}, u32[]{:S(2)}) collective-permute-start(bf16[2,96,256]{2,1,0:T(8,128)(2,1)S(1)} %get-tuple-element.34), channel_id=1, source_target_pairs={{4,0},{8,4},{12,8},{16,12},{20,16},{24,20},{28,24},{5,1},{9,5},{13... | collective-permute-start | bytes 294920 | tf_op jit(solution)/shard_map/ppermute | solution.py:20
  21.5 1.3 %collective-permute-start.4 = (bf16[8,32,256]{2,1,0:T(8,128)(2,1)S(1)}, bf16[8,32,256]{2,1,0:T(8,128)(2,1)S(1)}, u32[]{:S(2)}, u32[]{:S(2)}) collective-permute-start(bf16[8,32,256]{2,1,0:T(8,128)(2,1)S(1)} %get-tuple-element.38), channel_id=1, source_target_pairs={{1,0},{2,1},{3,2},{5,4},{6,5},{7,6},{9,8},{10,9},{11,10},{13,12},{... | collective-permute-start | bytes 393224 | tf_op jit(solution)/shard_map/ppermute | solution.py:20
  22.8 2.2 %collective-permute-start.10 = (bf16[8,64,256]{2,1,0:T(8,128)(2,1)S(1)}, bf16[8,64,256]{2,1,0:T(8,128)(2,1)S(1)}, u32[]{:S(2)}, u32[]{:S(2)}) collective-permute-start(bf16[8,64,256]{2,1,0:T(8,128)(2,1)S(1)} %get-tuple-element.37.gathered.refs_0_), channel_id=1, source_target_pairs={{0,2},{1,3},{2,0},{3,1},{4,6},{5,7},{6,4},{7,5},{8,10},{9,11},{10,... | collective-permute-start | bytes 786440 | tf_op jit(solution)/shard_map/ppermute | solution.py:114
  25.1 5.9 %collective-permute-start.7 = (bf16[2,128,256]{2,1,0:T(8,128)(2,1)S(1)}, bf16[2,128,256]{2,1,0:T(8,128)(2,1)S(1)}, u32[]{:S(2)}, u32[]{:S(2)}) collective-permute-start(bf16[2,128,256]{2,1,0:T(8,128)(2,1)S(1)} %get-tuple-element.41.refs_0_), channel_id=1, source_target_pairs={{0,24},{4,28},{8,16},{12,20},{16,8},{20,12},{24,0},{28,4},{1,25},{... | collective-permute-start | bytes 393224 | tf_op jit(solution)/shard_map/ppermute | solution.py:114
  31.0 0.0 collective-permute-start.6
  31.0 0.0 collective-permute-done.3.under
  31.0 0.6 collective-permute-start.5
  31.5 0.0 collective-permute-done.4.following
  31.5 0.0 copy-done.3
  31.5 0.1 copy-done.11
  31.6 0.6 copy-done.10
  32.2 5.3 %shard_map.94 = (bf16[128,256]{1,0:T(8,128)(2,1)}, bf16[256,256]{1,0:T(8,128)(2,1)}) custom-call(s32[2]{0:T(128)} %copy-done.7, bf16[2,2,64,256]{3,2,1,0:T(8,128)(2,1)} %copy-done.3, bf16[2,2,32,256]{3,2,1,0:T(8,128)(2,1)} %copy-done.5, bf16[2,96,256]{2,1,0:T(8,128)(2,1)} %copy-done.11, bf16[27,256,256]{2,1,0:T(8,128)(2,1)} %bitcast.17, ...), custom_call_target="tpu_custom_call" | custom-call | flops 452984832 | bytes 3538944 | tf_op jit(solution)/shard_map/pallas_call | solution.py:464
  37.5 0.0 collective-permute-done.7.refs_3_
  37.5 5.1 %collective-permute-done.6.refs_2_ = bf16[2,128,256]{2,1,0:T(8,128)(2,1)S(1)} collective-permute-done((bf16[2,128,256]{2,1,0:T(8,128)(2,1)S(1)}, bf16[2,128,256]{2,1,0:T(8,128)(2,1)S(1)}, u32[]{:S(2)}, u32[]{:S(2)}) %collective-permute-start.6) | collective-permute-done | bytes 131104 | tf_op jit(solution)/shard_map/ppermute | solution.py:114
  42.6 0.0 collective-permute-done.5.refs_1_
  42.6 0.8 %copy-done.2 = bf16[128,256]{1,0:T(8,128)(2,1)S(1)} copy-done((bf16[128,256]{1,0:T(8,128)(2,1)S(1)}, bf16[128,256]{1,0:T(8,128)(2,1)}, u32[]{:S(2)}) %copy-start.2) | copy-done | bytes 65560
  43.5 0.6 collective-permute-start.8
  44.1 4.5 %all-to-all-start.1 = ((bf16[8,16,256]{2,1,0:T(8,128)(2,1)}), bf16[8,16,256]{2,1,0:T(8,128)(2,1)S(1)}, u32[]{:S(2)}, u32[]{:S(2)}) async-start(bf16[8,16,256]{2,1,0:T(8,128)(2,1)} %bitcast.15), calls=%async_computation.1 | async-start | bytes 131072 | tf_op jit(solution)/shard_map/all_to_all | solution.py:489
  48.6 0.0 collective-permute-start.9
  48.6 0.0 collective-permute-done.10.refs_2_
  48.6 0.5 collective-permute-start.11
  49.1 6.4 %all-to-all-done.1.received = bf16[8,16,256]{2,1,0:T(8,128)(2,1)S(1)} async-done(((bf16[8,16,256]{2,1,0:T(8,128)(2,1)}), bf16[8,16,256]{2,1,0:T(8,128)(2,1)S(1)}, u32[]{:S(2)}, u32[]{:S(2)}) %all-to-all-start.1) | async-done | bytes 65568 | tf_op jit(solution)/shard_map/all_to_all | solution.py:489
  55.5 0.0 collective-permute-done.8._.refs_7_
  55.5 0.1 shard_map.96
  55.6 0.0 collective-permute-start.15
  55.6 0.6 collective-permute-start.16
  56.2 0.6 copy.15
  56.8 1.3 %collective-permute-start.17 = (f32[1,64]{1,0:T(1,128)S(1)}, f32[1,64]{1,0:T(1,128)S(1)}, u32[]{:S(2)}, u32[]{:S(2)}) collective-permute-start(f32[1,64]{1,0:T(1,128)S(1)} %get-tuple-element.49), channel_id=1, source_target_pairs={{0,3},{1,2},{2,1},{3,0},{4,7},{5,6},{6,5},{7,4},{8,11},{9,10},{10,... | collective-permute-start | bytes 776 | tf_op jit(solution)/shard_map/ppermute | solution.py:114
  58.1 0.0 collective-permute-done.15
  58.1 0.4 collective-permute-start.12
  58.5 0.7 collective-permute-done.16
  59.2 0.9 %collective-permute-start.13 = (bf16[2,128,256]{2,1,0:T(8,128)(2,1)S(1)}, bf16[2,128,256]{2,1,0:T(8,128)(2,1)S(1)}, u32[]{:S(2)}, u32[]{:S(2)}) collective-permute-start(bf16[2,128,256]{2,1,0:T(8,128)(2,1)S(1)} %get-tuple-element.45.refs_2_), channel_id=1, source_target_pairs={{0,4},{4,0},{8,12},{12,8},{16,20},{20,16},{24,28},{28,24},{1,5},{5... | collective-permute-start | bytes 393224 | tf_op jit(solution)/shard_map/ppermute | solution.py:114
  60.2 0.0 collective-permute-done.17
  60.2 1.1 %collective-permute-start.14 = (bf16[2,128,256]{2,1,0:T(8,128)(2,1)S(1)}, bf16[2,128,256]{2,1,0:T(8,128)(2,1)S(1)}, u32[]{:S(2)}, u32[]{:S(2)}) collective-permute-start(bf16[2,128,256]{2,1,0:T(8,128)(2,1)S(1)} %get-tuple-element.46.refs_4_), channel_id=1, source_target_pairs={{0,4},{4,0},{8,12},{12,8},{16,20},{20,16},{24,28},{28,24},{1,5},{5... | collective-permute-start | bytes 393224 | tf_op jit(solution)/shard_map/ppermute | solution.py:114
  61.3 0.5 add_bitcast_fusion
  61.8 0.0 collective-permute-done.9.refs_1_
  61.8 0.0 collective-permute-done.11.refs_3_
  61.8 0.0 copy-done.8
  61.8 0.0 copy-start.1
  61.8 0.9 %copy-done.1 = bf16[8,64,256]{2,1,0:T(8,128)(2,1)S(1)} copy-done((bf16[8,64,256]{2,1,0:T(8,128)(2,1)S(1)}, bf16[8,64,256]{2,1,0:T(8,128)(2,1)}, u32[]{:S(2)}) %copy-start.1) | copy-done | bytes 262168
  62.8 1.8 %shard_map.97 = (bf16[2,8,288,256]{3,2,1,0:T(8,128)(2,1)S(1)}, f32[1,64]{1,0:T(1,128)}) custom-call(s32[2]{0:T(128)S(1)} %copy-done.8, bf16[8,64,256]{2,1,0:T(8,128)(2,1)S(1)} %copy-done.1, bf16[8,64,256]{2,1,0:T(8,128)(2,1)S(1)} %collective-permute-done.9.refs_1_, bf16[8,64,256]{2,1,0:T(8,128)(2,1)S(1)} %collective-permute-done.10.refs_2_, ...), custom_call_target="tpu_custom_call" | custom-call | flops 1769472000 | bytes 1048576 | tf_op jit(solution)/shard_map/pallas_call | solution.py:500
  64.5 0.0 collective-permute-done.12.refs_1_
  64.5 2.7 %collective-permute-done.13.refs_3_ = bf16[2,128,256]{2,1,0:T(8,128)(2,1)S(1)} collective-permute-done((bf16[2,128,256]{2,1,0:T(8,128)(2,1)S(1)}, bf16[2,128,256]{2,1,0:T(8,128)(2,1)S(1)}, u32[]{:S(2)}, u32[]{:S(2)}) %collective-permute-start.13) | collective-permute-done | bytes 131104 | tf_op jit(solution)/shard_map/ppermute | solution.py:114
  67.3 2.2 %collective-permute-done.14.refs_5_ = bf16[2,128,256]{2,1,0:T(8,128)(2,1)S(1)} collective-permute-done((bf16[2,128,256]{2,1,0:T(8,128)(2,1)S(1)}, bf16[2,128,256]{2,1,0:T(8,128)(2,1)S(1)}, u32[]{:S(2)}, u32[]{:S(2)}) %collective-permute-start.14) | collective-permute-done | bytes 131104 | tf_op jit(solution)/shard_map/ppermute | solution.py:114
  69.5 3.4 %shard_map.98 = f32[27,64,256]{2,1,0:T(8,128)} custom-call(s32[2]{0:T(128)S(1)} %copy-done.8, f32[1,64]{1,0:T(1,128)S(1)} %get-tuple-element.43._, bf16[2,8,288,256]{3,2,1,0:T(8,128)(2,1)S(1)} %get-tuple-element.44.grads, bf16[2,128,256]{2,1,0:T(8,128)(2,1)S(1)} %get-tuple-element.41.refs_0_, bf16[2,128,256]{2,1,0:T(8,128)(2,1)S(1)} %collective-permute-done.12.refs_1_, ...), custom_call_target="tpu_custom_call" | custom-call | flops 3932160000 | bytes 3538944 | tf_op jit(solution)/shard_map/pallas_call | solution.py:506
  (15 shorter events, 0.0 us)
Async XLA Ops:
  2.1 16.8 %all-to-all-start = ((bf16[8,64,256]{2,1,0:T(8,128)(2,1)}), bf16[8,64,256]{2,1,0:T(8,128)(2,1)S(1)}, u32[]{:S(2)}, u32[]{:S(2)}) async-start(bf16[8,64,256]{2,1,0:T(8,128)(2,1)} %broadcast_in_dim.8), calls=%async_computation | async-start | bytes 524288 | tf_op jit(solution)/shard_map/all_to_all | solution.py:437
  9.5 10.2 %copy-start.7 = (s32[2]{0:T(128)}, s32[2]{0:T(128)S(1)}, u32[]{:S(2)}) copy-start(s32[2]{0:T(128)S(1)} %pad_add_fusion.place) | copy-start | bytes 28
  10.2 0.9 %copy-start.9 = (bf16[4,2,32,256]{3,2,1,0:T(8,128)(2,1)S(1)}, bf16[4,2,32,256]{3,2,1,0:T(8,128)(2,1)}, u32[]{:S(2)}) copy-start(bf16[4,2,32,256]{3,2,1,0:T(8,128)(2,1)} %param.5) | copy-start | bytes 393220
  11.9 0.7 copy-start.4
  12.6 0.6 copy-start.6
  13.2 18.4 %copy-start.3 = (bf16[2,2,64,256]{3,2,1,0:T(8,128)(2,1)}, bf16[2,2,64,256]{3,2,1,0:T(8,128)(2,1)S(1)}, u32[]{:S(2)}) copy-start(bf16[2,2,64,256]{3,2,1,0:T(8,128)(2,1)S(1)} %get-tuple-element.28.planes) | copy-start | bytes 393220
  13.2 5.8 %collective-permute-start = (bf16[384,128]{1,0:T(8,128)(2,1)S(1)}, bf16[384,128]{1,0:T(8,128)(2,1)S(1)}, u32[]{:S(2)}, u32[]{:S(2)}) collective-permute-start(bf16[384,128]{1,0:T(8,128)(2,1)S(1)} %get-tuple-element.30), channel_id=1, source_target_pairs={{0,1},{1,0},{2,3},{3,2},{4,5},{5,4},{6,7},{7,6},{8,9},{9,8},{10,11... | collective-permute-start | bytes 294920 | tf_op jit(solution)/shard_map/ppermute | solution.py:114
  13.2 5.8 %collective-permute-start.2 = (bf16[384,128]{1,0:T(8,128)(2,1)S(1)}, bf16[384,128]{1,0:T(8,128)(2,1)S(1)}, u32[]{:S(2)}, u32[]{:S(2)}) collective-permute-start(bf16[384,128]{1,0:T(8,128)(2,1)S(1)} %get-tuple-element.32), channel_id=1, source_target_pairs={{0,3},{1,2},{2,1},{3,0},{4,7},{5,6},{6,5},{7,4},{8,11},{9,10},{10,... | collective-permute-start | bytes 294920 | tf_op jit(solution)/shard_map/ppermute | solution.py:114
  14.8 4.2 %collective-permute-start.1 = (bf16[128,128]{1,0:T(8,128)(2,1)S(1)}, bf16[128,128]{1,0:T(8,128)(2,1)S(1)}, u32[]{:S(2)}, u32[]{:S(2)}) collective-permute-start(bf16[128,128]{1,0:T(8,128)(2,1)S(1)} %get-tuple-element.31), channel_id=1, source_target_pairs={{0,2},{1,3},{2,0},{3,1},{4,6},{5,7},{6,4},{7,5},{8,10},{9,11},{10,... | collective-permute-start | bytes 98312 | tf_op jit(solution)/shard_map/ppermute | solution.py:114
  19.6 0.6 copy-start.5
  20.3 11.3 %copy-start = (bf16[8,64,256]{2,1,0:T(8,128)(2,1)}, bf16[8,64,256]{2,1,0:T(8,128)(2,1)S(1)}, u32[]{:S(2)}) copy-start(bf16[8,64,256]{2,1,0:T(8,128)(2,1)S(1)} %get-tuple-element.37.gathered.refs_0_) | copy-start | bytes 786436
  20.3 10.7 %collective-permute-start.3 = (bf16[2,96,256]{2,1,0:T(8,128)(2,1)S(1)}, bf16[2,96,256]{2,1,0:T(8,128)(2,1)S(1)}, u32[]{:S(2)}, u32[]{:S(2)}) collective-permute-start(bf16[2,96,256]{2,1,0:T(8,128)(2,1)S(1)} %get-tuple-element.34), channel_id=1, source_target_pairs={{4,0},{8,4},{12,8},{16,12},{20,16},{24,20},{28,24},{5,1},{9,5},{13... | collective-permute-start | bytes 294920 | tf_op jit(solution)/shard_map/ppermute | solution.py:20
  21.5 10.0 %collective-permute-start.4 = (bf16[8,32,256]{2,1,0:T(8,128)(2,1)S(1)}, bf16[8,32,256]{2,1,0:T(8,128)(2,1)S(1)}, u32[]{:S(2)}, u32[]{:S(2)}) collective-permute-start(bf16[8,32,256]{2,1,0:T(8,128)(2,1)S(1)} %get-tuple-element.38), channel_id=1, source_target_pairs={{1,0},{2,1},{3,2},{5,4},{6,5},{7,6},{9,8},{10,9},{11,10},{13,12},{... | collective-permute-start | bytes 393224 | tf_op jit(solution)/shard_map/ppermute | solution.py:20
  22.8 25.8 %collective-permute-start.10 = (bf16[8,64,256]{2,1,0:T(8,128)(2,1)S(1)}, bf16[8,64,256]{2,1,0:T(8,128)(2,1)S(1)}, u32[]{:S(2)}, u32[]{:S(2)}) collective-permute-start(bf16[8,64,256]{2,1,0:T(8,128)(2,1)S(1)} %get-tuple-element.37.gathered.refs_0_), channel_id=1, source_target_pairs={{0,2},{1,3},{2,0},{3,1},{4,6},{5,7},{6,4},{7,5},{8,10},{9,11},{10,... | collective-permute-start | bytes 786440 | tf_op jit(solution)/shard_map/ppermute | solution.py:114
  25.1 12.5 %collective-permute-start.7 = (bf16[2,128,256]{2,1,0:T(8,128)(2,1)S(1)}, bf16[2,128,256]{2,1,0:T(8,128)(2,1)S(1)}, u32[]{:S(2)}, u32[]{:S(2)}) collective-permute-start(bf16[2,128,256]{2,1,0:T(8,128)(2,1)S(1)} %get-tuple-element.41.refs_0_), channel_id=1, source_target_pairs={{0,24},{4,28},{8,16},{12,20},{16,8},{20,12},{24,0},{28,4},{1,25},{... | collective-permute-start | bytes 393224 | tf_op jit(solution)/shard_map/ppermute | solution.py:114
  31.0 11.7 %collective-permute-start.6 = (bf16[2,128,256]{2,1,0:T(8,128)(2,1)S(1)}, bf16[2,128,256]{2,1,0:T(8,128)(2,1)S(1)}, u32[]{:S(2)}, u32[]{:S(2)}) collective-permute-start(bf16[2,128,256]{2,1,0:T(8,128)(2,1)S(1)} %get-tuple-element.41.refs_0_), channel_id=1, source_target_pairs={{0,16},{4,20},{8,24},{12,28},{16,0},{20,4},{24,8},{28,12},{1,17},{... | collective-permute-start | bytes 393224 | tf_op jit(solution)/shard_map/ppermute | solution.py:114
  31.0 0.6 copy-start.11
  31.0 11.7 %collective-permute-start.5 = (bf16[2,128,256]{2,1,0:T(8,128)(2,1)S(1)}, bf16[2,128,256]{2,1,0:T(8,128)(2,1)S(1)}, u32[]{:S(2)}, u32[]{:S(2)}) collective-permute-start(bf16[2,128,256]{2,1,0:T(8,128)(2,1)S(1)} %get-tuple-element.41.refs_0_), channel_id=1, source_target_pairs={{0,8},{4,12},{8,0},{12,4},{16,24},{20,28},{24,16},{28,20},{1,9},{5... | collective-permute-start | bytes 393224 | tf_op jit(solution)/shard_map/ppermute | solution.py:114
  31.5 0.7 copy-start.10
  32.2 29.6 %copy-start.8 = (s32[2]{0:T(128)S(1)}, s32[2]{0:T(128)}, u32[]{:S(2)}) copy-start(s32[2]{0:T(128)} %copy-done.7) | copy-start | bytes 28
  42.6 0.8 %copy-start.2 = (bf16[128,256]{1,0:T(8,128)(2,1)S(1)}, bf16[128,256]{1,0:T(8,128)(2,1)}, u32[]{:S(2)}) copy-start(bf16[128,256]{1,0:T(8,128)(2,1)} %get-tuple-element.39.refs_0_) | copy-start | bytes 196612
  43.5 12.0 %collective-permute-start.8 = (bf16[2,128,256]{2,1,0:T(8,128)(2,1)S(1)}, bf16[2,128,256]{2,1,0:T(8,128)(2,1)S(1)}, u32[]{:S(2)}, u32[]{:S(2)}) collective-permute-start(bf16[2,128,256]{2,1,0:T(8,128)(2,1)S(1)} %get-tuple-element.42.refs_6_), channel_id=1, source_target_pairs={{0,4},{4,0},{8,12},{12,8},{16,20},{20,16},{24,28},{28,24},{1,5},{5... | collective-permute-start | bytes 393224 | tf_op jit(solution)/shard_map/ppermute | solution.py:114
  44.1 11.4 %all-to-all-start.1 = ((bf16[8,16,256]{2,1,0:T(8,128)(2,1)}), bf16[8,16,256]{2,1,0:T(8,128)(2,1)S(1)}, u32[]{:S(2)}, u32[]{:S(2)}) async-start(bf16[8,16,256]{2,1,0:T(8,128)(2,1)} %bitcast.15), calls=%async_computation.1 | async-start | bytes 131072 | tf_op jit(solution)/shard_map/all_to_all | solution.py:489
  48.6 13.2 %collective-permute-start.9 = (bf16[8,64,256]{2,1,0:T(8,128)(2,1)}, bf16[8,64,256]{2,1,0:T(8,128)(2,1)S(1)}, u32[]{:S(2)}, u32[]{:S(2)}) collective-permute-start(bf16[8,64,256]{2,1,0:T(8,128)(2,1)} %copy-done), channel_id=1, source_target_pairs={{0,1},{1,0},{2,3},{3,2},{4,5},{5,4},{6,7},{7,6},{8,9},{9,8},{10,11... | collective-permute-start | bytes 786440 | tf_op jit(solution)/shard_map/ppermute | solution.py:114
  48.6 13.2 %collective-permute-start.11 = (bf16[8,64,256]{2,1,0:T(8,128)(2,1)S(1)}, bf16[8,64,256]{2,1,0:T(8,128)(2,1)S(1)}, u32[]{:S(2)}, u32[]{:S(2)}) collective-permute-start(bf16[8,64,256]{2,1,0:T(8,128)(2,1)S(1)} %collective-permute-done.10.refs_2_), channel_id=1, source_target_pairs={{0,1},{1,0},{2,3},{3,2},{4,5},{5,4},{6,7},{7,6},{8,9},{9,8},{10,11... | collective-permute-start | bytes 786440 | tf_op jit(solution)/shard_map/ppermute | solution.py:114
  55.6 2.5 %collective-permute-start.15 = (f32[1,64]{1,0:T(1,128)S(1)}, f32[1,64]{1,0:T(1,128)S(1)}, u32[]{:S(2)}, u32[]{:S(2)}) collective-permute-start(f32[1,64]{1,0:T(1,128)S(1)} %get-tuple-element.47), channel_id=1, source_target_pairs={{0,1},{1,0},{2,3},{3,2},{4,5},{5,4},{6,7},{7,6},{8,9},{9,8},{10,11... | collective-permute-start | bytes 776 | tf_op jit(solution)/shard_map/ppermute | solution.py:114
  55.6 3.6 %collective-permute-start.16 = (f32[1,64]{1,0:T(1,128)S(1)}, f32[1,64]{1,0:T(1,128)S(1)}, u32[]{:S(2)}, u32[]{:S(2)}) collective-permute-start(f32[1,64]{1,0:T(1,128)S(1)} %get-tuple-element.48), channel_id=1, source_target_pairs={{0,2},{1,3},{2,0},{3,1},{4,6},{5,7},{6,4},{7,5},{8,10},{9,11},{10,... | collective-permute-start | bytes 776 | tf_op jit(solution)/shard_map/ppermute | solution.py:114
  56.8 3.3 %collective-permute-start.17 = (f32[1,64]{1,0:T(1,128)S(1)}, f32[1,64]{1,0:T(1,128)S(1)}, u32[]{:S(2)}, u32[]{:S(2)}) collective-permute-start(f32[1,64]{1,0:T(1,128)S(1)} %get-tuple-element.49), channel_id=1, source_target_pairs={{0,3},{1,2},{2,1},{3,0},{4,7},{5,6},{6,5},{7,4},{8,11},{9,10},{10,... | collective-permute-start | bytes 776 | tf_op jit(solution)/shard_map/ppermute | solution.py:114
  58.1 6.4 %collective-permute-start.12 = (bf16[2,128,256]{2,1,0:T(8,128)(2,1)S(1)}, bf16[2,128,256]{2,1,0:T(8,128)(2,1)S(1)}, u32[]{:S(2)}, u32[]{:S(2)}) collective-permute-start(bf16[2,128,256]{2,1,0:T(8,128)(2,1)S(1)} %get-tuple-element.41.refs_0_), channel_id=1, source_target_pairs={{0,4},{4,0},{8,12},{12,8},{16,20},{20,16},{24,28},{28,24},{1,5},{5... | collective-permute-start | bytes 393224 | tf_op jit(solution)/shard_map/ppermute | solution.py:114
  59.2 8.0 %collective-permute-start.13 = (bf16[2,128,256]{2,1,0:T(8,128)(2,1)S(1)}, bf16[2,128,256]{2,1,0:T(8,128)(2,1)S(1)}, u32[]{:S(2)}, u32[]{:S(2)}) collective-permute-start(bf16[2,128,256]{2,1,0:T(8,128)(2,1)S(1)} %get-tuple-element.45.refs_2_), channel_id=1, source_target_pairs={{0,4},{4,0},{8,12},{12,8},{16,20},{20,16},{24,28},{28,24},{1,5},{5... | collective-permute-start | bytes 393224 | tf_op jit(solution)/shard_map/ppermute | solution.py:114
  60.2 9.3 %collective-permute-start.14 = (bf16[2,128,256]{2,1,0:T(8,128)(2,1)S(1)}, bf16[2,128,256]{2,1,0:T(8,128)(2,1)S(1)}, u32[]{:S(2)}, u32[]{:S(2)}) collective-permute-start(bf16[2,128,256]{2,1,0:T(8,128)(2,1)S(1)} %get-tuple-element.46.refs_4_), channel_id=1, source_target_pairs={{0,4},{4,0},{8,12},{12,8},{16,20},{20,16},{24,28},{28,24},{1,5},{5... | collective-permute-start | bytes 393224 | tf_op jit(solution)/shard_map/ppermute | solution.py:114
  61.8 1.0 %copy-start.1 = (bf16[8,64,256]{2,1,0:T(8,128)(2,1)S(1)}, bf16[8,64,256]{2,1,0:T(8,128)(2,1)}, u32[]{:S(2)}) copy-start(bf16[8,64,256]{2,1,0:T(8,128)(2,1)} %copy-done) | copy-start | bytes 786436

commit v6 on v5

--- a/solution.py
+++ b/solution.py
@@ -10,7 +10,7 @@
 EPS = 1e-06
 TAPS = [(a, b, c) for a in range(3) for b in range(3) for c in range(3)]
 VMEM_LIMIT = 20 * 1024 * 1024
-VMEM_LIMIT_WIDE = 61 * 1024 * 1024
+VMEM_LIMIT_WIDE = 60 * 1024 * 1024
 WORK = 1200
 
 
@@ -116,11 +116,18 @@
 
 def exchanged(value, axis, gate=None):
     count = lax.axis_size(axis)
-    even = [value] + [partners(value, axis, k) for k in range(2, count, 2)]
-    blocks = []
-    for n, block in enumerate(even if gate is None else [value] + gate(even[1:])):
-        blocks += [block, partners(block, axis, 1)]
-    return blocks
+    blocks = {0: value}
+    for k in range(1, count):
+        if k & (k - 1) == 0:
+            blocks[k] = partners(value, axis, k)
+    if gate is not None:
+        held = [k for k in blocks if k > 1]
+        blocks.update(zip(held, gate([blocks[k] for k in held])))
+    for k in range(1, count):
+        low = k & -k
+        if k != low:
+            blocks[k] = partners(blocks[k - low], axis, low)
+    return [blocks[k] for k in range(count)]
 
 
 def mm(left, right):
@@ -185,8 +192,14 @@
             sends[k][rp * F * J : (rp + 1) * F * J] = chosen.astype(jnp.bfloat16)
 
 
-def join_kernel(F, J, T, place, grad_rows, planes, *refs):
-    messages, (joined, cached, under, head, passed, blocks) = refs[:T], refs[T:]
+def head_kernel(rows, _, grad_rows, head, passed):
+    passed[...] = grad_rows[...]
+    for s in range(grad_rows.shape[0]):
+        head[s] = grad_rows[s, :rows, :]
+
+
+def join_kernel(F, J, T, place, planes, *refs):
+    messages, (joined, cached, under, blocks) = refs[:T], refs[T:]
     span = F * J
     block = place[1]
     for k in range(T):
@@ -195,9 +208,6 @@
             blocks[rp, pl.ds(at, span), :] = messages[k][rp * span : (rp + 1) * span, :]
     for rp in range(2):
         joined[rp] = blocks[rp].T
-    passed[...] = grad_rows[...]
-    for s in range(grad_rows.shape[0]):
-        head[s] = grad_rows[s, : 2 * J, :]
     for rp in range(2):
         for cp in range(2):
             halves = []
@@ -334,7 +344,8 @@
     out[...] = value.astype(jnp.bfloat16)
 
 
-def gain_kernel(T, used, received, _, *parts):
+def gain_kernel(T, used, received, *refs):
+    parts = refs[-T:]
     value = jnp.zeros(received.shape[1:], jnp.float32)
     for s in range(received.shape[0]):
         value = value + received[s].astype(jnp.float32)
@@ -446,19 +457,22 @@
         [pltpu.VMEM((2, 4 * span, C // 2), f32)],
         60 * WORK * span * C, 16 * span * C, "svv" + "v" * (T + 3),
     )(place, flat, vectors)
+    head, grad_rows = call(
+        functools.partial(head_kernel, 2 * J),
+        [((R, 2 * J, C), bf16), (grad_rows.shape, bf16)],
+        [], R * span * C, R * span * C, "avvv",
+    )(frames_copy, grad_rows)
     messages = [sends[0]] + [partners(sends[k], "tm", k) for k in range(1, T)]
-    joined, cached, under, head, grad_rows = call(
+    joined, cached, under = call(
         functools.partial(join_kernel, F, J, T),
         [
             ((2, 2 * part, T * span), bf16),
             ((2, 2, 2 * J, C), bf16),
             ((2, 2 * J + span, C), bf16),
-            ((R, 2 * J, C), bf16),
-            (grad_rows.shape, bf16),
         ],
         [pltpu.VMEM((2, T * span, 2 * part), bf16)],
-        30 * WORK * span * C, 16 * span * C, "svv" + "v" * T + "vvvvv",
-    )(place, grad_rows, planes, *messages)
+        30 * WORK * span * C, 16 * span * C, "sv" + "v" * T + "vvv",
+    )(place, planes, *messages)
     under = shifted(under, "rows", -1)
     following = shifted(head, "tm", -1)
     packed, frames_grad = call(
@@ -491,8 +505,8 @@
     gains = call(
         functools.partial(gain_kernel, T, used),
         [((1, part), f32)] * T,
-        [], R * slot * C, R * slot * C, "va" + "v" * T,
-    )(packed, hidden_all[-1])
+        [], R * slot * C, R * slot * C, "v" + "a" * (R // 2) + "v" * T,
+    )(packed, *hidden_all[1::2])
     gain_grad = gains[0]
     for k in range(1, T):
         gain_grad = gain_grad + partners(gains[k], "tm", k)

time: 73.5 us -> 65.2 us (0.89)
  waiting for transfers between devices: 20.9 us -> 12.5 us
  starting transfers between devices: 30.5 us -> 32 us
  local copies, waits for them, and re-layouts: 7.35 us -> 5.87 us
    ppermute x16, waiting for transfers between devices: 14.5 us -> 2.6 us  [partners(): lax.ppermute(value, axis, [(source, source ^ bits) for source in range(co...]
    all_to_all x1, waiting for transfers between devices: 0.01 us -> 3.65 us  [gathered_form(): lax.all_to_all(jnp.broadcast_to(own, (R,) + own.shape[1:]), 'rows', 0, 0,...]
    ppermute x16, starting transfers between devices: 16.2 us -> 18.8 us  [partners(): lax.ppermute(value, axis, [(source, source ^ bits) for source in range(co...]
    unnamed x24 -> x22, local copies, waits for them, and re-layouts: 5.19 us -> 3.7 us
    all_to_all x1, starting transfers between devices: 4.54 us -> 3.35 us  [gathered_form(): lax.all_to_all(packed.reshape(R, slot, C), 'rows', 0, 0, tiled=True)]
  transfers between devices with their start and end apart: 20 -> 20, of which waited for: 6 -> 5; matrix products, arithmetic and copies ran while one was open for 3% -> 3% of each run, Pallas kernels for 11% -> 11%
where the time goes in v6:
time: 65.2 us; the launch traced here: 64.7 us
  starting transfers between devices  32 us (49%)
  waiting for transfers between devices  12.5 us (19%)
  Pallas kernels  12.1 us (19%)
  local copies, waits for them, and re-layouts  5.87 us (9%)
  other arithmetic  1.29 us (2%)
  between operations  0.87 us (1%)
    ppermute x16, starting transfers between devices, partners(): lax.ppermute(value, axis, [(source, source ^ bits) for source in range(co...  18.8 us
    all_to_all x1, starting transfers between devices, gathered_form(): lax.all_to_all(jnp.broadcast_to(own, (R,) + own.shape[1:]), 'rows', 0, 0,...  7.25 us
    all_to_all x1, waiting for transfers between devices, gathered_form(): lax.all_to_all(packed.reshape(R, slot, C), 'rows', 0, 0, tiled=True)  6.25 us
    pallas_call x1, Pallas kernels, gathered_form(): call(functools.partial(slab_kernel, F, J, R, T, slot), [((R * slot, C), b...  5.33 us
    unnamed x22, local copies, waits for them, and re-layouts  3.7 us
    all_to_all x1, waiting for transfers between devices, gathered_form(): lax.all_to_all(jnp.broadcast_to(own, (R,) + own.shape[1:]), 'rows', 0, 0,...  3.65 us
    pallas_call x1, Pallas kernels, gathered_form(): call(functools.partial(weight_kernel, F, J, R, T, part), [((27, part, C),...  3.42 us
    all_to_all x1, starting transfers between devices, gathered_form(): lax.all_to_all(packed.reshape(R, slot, C), 'rows', 0, 0, tiled=True)  3.35 us
  transfers between devices with their start and end apart: 20, of which 5 were waited for; matrix products, arithmetic and copies ran while one was open for 3% of the time, Pallas kernels for 11%

profile of v6, /device:TPU:0, one launch (start us, length us, event | category | flops | bytes accessed | tf_op | source)
XLA Modules:
  0.0 64.7 jit_solution(4577122824405790587)
XLA Ops:
  0.6 0.8 %broadcast_in_dim.7 = bf16[64,256]{1,0:T(8,128)(2,1)S(1)} reshape(bf16[4,8,2,256]{3,2,1,0:T(2,128)(2,1)} %param.9) | data formatting | bytes 65536 | tf_op jit(solution)/shard_map/broadcast_in_dim | solution.py:449
  1.4 0.7 %broadcast_in_dim.8 = bf16[8,64,256]{2,1,0:T(8,128)(2,1)} broadcast(bf16[64,256]{1,0:T(8,128)(2,1)S(1)} %broadcast_in_dim.7), dimensions={1,2} | broadcast | bytes 294912 | tf_op jit(solution)/shard_map/broadcast_in_dim | solution.py:449
  2.1 7.3 %all-to-all-start = ((bf16[8,64,256]{2,1,0:T(8,128)(2,1)}), bf16[8,64,256]{2,1,0:T(8,128)(2,1)S(1)}, u32[]{:S(2)}, u32[]{:S(2)}) async-start(bf16[8,64,256]{2,1,0:T(8,128)(2,1)} %broadcast_in_dim.8), calls=%async_computation | async-start | bytes 524288 | tf_op jit(solution)/shard_map/all_to_all | solution.py:448
  9.4 0.1 pad_add_fusion.place
  9.5 0.7 %pad_maximum_fusion.vectors = f32[2,256]{1,0:T(2,128)S(1)} fusion(f32[1,256]{1,0:T(1,128)} %bitcast.18, f32[1,256]{1,0:T(1,128)} %bitcast.19), kind=kLoop, calls=%fused_computation.1 | loop fusion | flops 512 | bytes 4096 | tf_op jit(solution)/shard_map/stack | solution.py:442
  10.2 0.9 %copy-done.8 = bf16[4,2,32,256]{3,2,1,0:T(8,128)(2,1)S(1)} copy-done((bf16[4,2,32,256]{3,2,1,0:T(8,128)(2,1)S(1)}, bf16[4,2,32,256]{3,2,1,0:T(8,128)(2,1)}, u32[]{:S(2)}) %copy-start.8) | copy-done | bytes 131096
  11.1 0.8 %shard_map.92 = (bf16[2,2,64,256]{3,2,1,0:T(8,128)(2,1)S(1)}, bf16[256,256]{1,0:T(8,128)(2,1)S(1)}, f32[2,256]{1,0:T(2,128)S(1)}, bf16[128,128]{1,0:T(8,128)(2,1...) custom-call(s32[2]{0:T(128)S(1)} %pad_add_fusion.place, ...), custom_call_target="tpu_custom_call" | custom-call | flops 1179648000 | bytes 262144 | tf_op jit(solution)/shard_map/pallas_call | solution.py:453
  11.9 0.0 copy-start.5
  11.9 0.6 copy-done.5
  12.5 0.0 collective-permute-start
  12.5 1.6 %collective-permute-start.2 = (bf16[384,128]{1,0:T(8,128)(2,1)S(1)}, bf16[384,128]{1,0:T(8,128)(2,1)S(1)}, u32[]{:S(2)}, u32[]{:S(2)}) collective-permute-start(bf16[384,128]{1,0:T(8,128)(2,1)S(1)} %get-tuple-element.31), channel_id=1, source_target_pairs={{0,3},{1,2},{2,1},{3,0},{4,7},{5,6},{6,5},{7,4},{8,11},{9,10},{10,... | collective-permute-start | bytes 294920 | tf_op jit(solution)/shard_map/ppermute | solution.py:114
  14.1 0.5 collective-permute-start.1
  14.7 3.6 %all-to-all-done.grad_rows = bf16[8,64,256]{2,1,0:T(8,128)(2,1)S(1)} async-done(((bf16[8,64,256]{2,1,0:T(8,128)(2,1)}), bf16[8,64,256]{2,1,0:T(8,128)(2,1)S(1)}, u32[]{:S(2)}, u32[]{:S(2)}) %all-to-all-start) | async-done | bytes 262176 | tf_op jit(solution)/shard_map/all_to_all | solution.py:448
  18.3 0.0 copy-start.1
  18.3 1.3 %collective-permute-start.4 = (bf16[8,32,256]{2,1,0:T(8,128)(2,1)S(1)}, bf16[8,32,256]{2,1,0:T(8,128)(2,1)S(1)}, u32[]{:S(2)}, u32[]{:S(2)}) collective-permute-start(bf16[8,32,256]{2,1,0:T(8,128)(2,1)S(1)} %get-tuple-element.37), channel_id=1, source_target_pairs={{1,0},{2,1},{3,2},{5,4},{6,5},{7,6},{9,8},{10,9},{11,10},{13,12},{... | collective-permute-start | bytes 393224 | tf_op jit(solution)/shard_map/ppermute | solution.py:20
  19.6 0.0 collective-permute-done.1.refs_2_
  19.7 0.0 collective-permute-done.refs_1_
  19.7 0.0 collective-permute-done.2.refs_3_
  19.7 0.0 copy-done.6
  19.7 0.6 shard_map.93
  20.3 0.0 copy-start.4
  20.3 0.6 copy-done.4
  21.0 1.3 %collective-permute-start.3 = (bf16[2,96,256]{2,1,0:T(8,128)(2,1)S(1)}, bf16[2,96,256]{2,1,0:T(8,128)(2,1)S(1)}, u32[]{:S(2)}, u32[]{:S(2)}) collective-permute-start(bf16[2,96,256]{2,1,0:T(8,128)(2,1)S(1)} %get-tuple-element.33), channel_id=1, source_target_pairs={{4,0},{8,4},{12,8},{16,12},{20,16},{24,20},{28,24},{5,1},{9,5},{13... | collective-permute-start | bytes 294920 | tf_op jit(solution)/shard_map/ppermute | solution.py:20
  22.2 3.7 %collective-permute-start.7 = (bf16[2,128,256]{2,1,0:T(8,128)(2,1)S(1)}, bf16[2,128,256]{2,1,0:T(8,128)(2,1)S(1)}, u32[]{:S(2)}, u32[]{:S(2)}) collective-permute-start(bf16[2,128,256]{2,1,0:T(8,128)(2,1)S(1)} %get-tuple-element.40.refs_0_), channel_id=1, source_target_pairs={{0,16},{4,20},{8,24},{12,28},{16,0},{20,4},{24,8},{28,12},{1,17},{... | collective-permute-start | bytes 393224 | tf_op jit(solution)/shard_map/ppermute | solution.py:114
  25.9 1.5 %collective-permute-start.6 = (bf16[2,128,256]{2,1,0:T(8,128)(2,1)S(1)}, bf16[2,128,256]{2,1,0:T(8,128)(2,1)S(1)}, u32[]{:S(2)}, u32[]{:S(2)}) collective-permute-start(bf16[2,128,256]{2,1,0:T(8,128)(2,1)S(1)} %get-tuple-element.40.refs_0_), channel_id=1, source_target_pairs={{0,8},{4,12},{8,0},{12,4},{16,24},{20,28},{24,16},{28,20},{1,9},{5... | collective-permute-start | bytes 393224 | tf_op jit(solution)/shard_map/ppermute | solution.py:114
  27.4 1.5 %collective-permute-start.13 = (bf16[8,64,256]{2,1,0:T(8,128)(2,1)S(1)}, bf16[8,64,256]{2,1,0:T(8,128)(2,1)S(1)}, u32[]{:S(2)}, u32[]{:S(2)}) collective-permute-start(bf16[8,64,256]{2,1,0:T(8,128)(2,1)S(1)} %get-tuple-element.36.gathered.refs_0_), channel_id=1, source_target_pairs={{0,2},{1,3},{2,0},{3,1},{4,6},{5,7},{6,4},{7,5},{8,10},{9,11},{10,... | collective-permute-start | bytes 786440 | tf_op jit(solution)/shard_map/ppermute | solution.py:114
  28.9 0.0 collective-permute-done.3.under
  28.9 0.0 collective-permute-done.4.following
  28.9 0.0 copy-start.9
  29.0 0.6 copy-done.10
  29.6 0.0 copy-done.9
  29.6 5.3 %shard_map.95 = (bf16[128,256]{1,0:T(8,128)(2,1)}, bf16[256,256]{1,0:T(8,128)(2,1)}) custom-call(s32[2]{0:T(128)} %copy-done.6, bf16[2,2,64,256]{3,2,1,0:T(8,128)(2,1)} %copy-done.3, bf16[2,2,32,256]{3,2,1,0:T(8,128)(2,1)} %copy-done.4, bf16[2,96,256]{2,1,0:T(8,128)(2,1)} %copy-done.10, bf16[27,256,256]{2,1,0:T(8,128)(2,1)} %bitcast.16, ...), custom_call_target="tpu_custom_call" | custom-call | flops 452984832 | bytes 3538944 | tf_op jit(solution)/shard_map/pallas_call | solution.py:478
  35.0 0.0 collective-permute-done.7.refs_2_
  35.0 0.0 collective-permute-done.6.refs_1_
  35.0 0.6 collective-permute-start.10
  35.6 2.0 %collective-permute-start.5 = (bf16[2,128,256]{2,1,0:T(8,128)(2,1)S(1)}, bf16[2,128,256]{2,1,0:T(8,128)(2,1)S(1)}, u32[]{:S(2)}, u32[]{:S(2)}) collective-permute-start(bf16[2,128,256]{2,1,0:T(8,128)(2,1)S(1)} %get-tuple-element.40.refs_0_), channel_id=1, source_target_pairs={{0,4},{4,0},{8,12},{12,8},{16,20},{20,16},{24,28},{28,24},{1,5},{5... | collective-permute-start | bytes 393224 | tf_op jit(solution)/shard_map/ppermute | solution.py:114
  37.6 0.1 collective-permute-start.9
  37.7 1.9 %collective-permute-start.8 = (bf16[2,128,256]{2,1,0:T(8,128)(2,1)S(1)}, bf16[2,128,256]{2,1,0:T(8,128)(2,1)S(1)}, u32[]{:S(2)}, u32[]{:S(2)}) collective-permute-start(bf16[2,128,256]{2,1,0:T(8,128)(2,1)S(1)} %get-tuple-element.41.refs_2_), channel_id=1, source_target_pairs={{0,4},{4,0},{8,12},{12,8},{16,20},{20,16},{24,28},{28,24},{1,5},{5... | collective-permute-start | bytes 393224 | tf_op jit(solution)/shard_map/ppermute | solution.py:114
  39.6 0.7 %collective-permute-done.10.refs_6_ = bf16[2,128,256]{2,1,0:T(8,128)(2,1)S(1)} collective-permute-done((bf16[2,128,256]{2,1,0:T(8,128)(2,1)S(1)}, bf16[2,128,256]{2,1,0:T(8,128)(2,1)S(1)}, u32[]{:S(2)}, u32[]{:S(2)}) %collective-permute-start.10) | collective-permute-done | bytes 131104 | tf_op jit(solution)/shard_map/ppermute | solution.py:114
  40.3 3.0 %collective-permute-start.11 = (bf16[2,128,256]{2,1,0:T(8,128)(2,1)S(1)}, bf16[2,128,256]{2,1,0:T(8,128)(2,1)S(1)}, u32[]{:S(2)}, u32[]{:S(2)}) collective-permute-start(bf16[2,128,256]{2,1,0:T(8,128)(2,1)S(1)} %collective-permute-done.10.refs_6_), channel_id=1, source_target_pairs={{0,4},{4,0},{8,12},{12,8},{16,20},{20,16},{24,28},{28,24},{1,5},{5... | collective-permute-start | bytes 393224 | tf_op jit(solution)/shard_map/ppermute | solution.py:114
  43.3 3.3 %all-to-all-start.1 = ((bf16[8,16,256]{2,1,0:T(8,128)(2,1)}), bf16[8,16,256]{2,1,0:T(8,128)(2,1)S(1)}, u32[]{:S(2)}, u32[]{:S(2)}) async-start(bf16[8,16,256]{2,1,0:T(8,128)(2,1)} %bitcast.6), calls=%async_computation.1 | async-start | bytes 131072 | tf_op jit(solution)/shard_map/all_to_all | solution.py:503
  46.7 0.0 collective-permute-done.5.refs_0_.refs_1_
  46.7 0.1 collective-permute-start.12
  46.7 0.0 collective-permute-done.13.refs_2_
  46.8 0.5 collective-permute-start.14
  47.2 6.3 %all-to-all-done.1.received = bf16[8,16,256]{2,1,0:T(8,128)(2,1)S(1)} async-done(((bf16[8,16,256]{2,1,0:T(8,128)(2,1)}), bf16[8,16,256]{2,1,0:T(8,128)(2,1)S(1)}, u32[]{:S(2)}, u32[]{:S(2)}) %all-to-all-start.1) | async-done | bytes 65568 | tf_op jit(solution)/shard_map/all_to_all | solution.py:503
  53.5 0.0 collective-permute-done.8.refs_1_.refs_3_
  53.5 0.0 collective-permute-done.9.refs_2_.refs_5_
  53.5 0.0 collective-permute-done.11.refs_3_.refs_7_
  53.5 0.1 shard_map.97
  53.6 0.0 collective-permute-start.15
  53.6 1.4 %collective-permute-start.16 = (f32[1,64]{1,0:T(1,128)S(1)}, f32[1,64]{1,0:T(1,128)S(1)}, u32[]{:S(2)}, u32[]{:S(2)}) collective-permute-start(f32[1,64]{1,0:T(1,128)S(1)} %get-tuple-element.46), channel_id=1, source_target_pairs={{0,2},{1,3},{2,0},{3,1},{4,6},{5,7},{6,4},{7,5},{8,10},{9,11},{10,... | collective-permute-start | bytes 776 | tf_op jit(solution)/shard_map/ppermute | solution.py:114
  55.0 0.4 collective-permute-start.17
  55.5 0.6 copy.14
  56.1 0.0 collective-permute-done.15
  56.1 1.1 %collective-permute-done.16 = f32[1,64]{1,0:T(1,128)S(1)} collective-permute-done((f32[1,64]{1,0:T(1,128)S(1)}, f32[1,64]{1,0:T(1,128)S(1)}, u32[]{:S(2)}, u32[]{:S(2)}) %collective-permute-start.16) | collective-permute-done | bytes 288 | tf_op jit(solution)/shard_map/ppermute | solution.py:114
  57.2 0.8 %collective-permute-done.17 = f32[1,64]{1,0:T(1,128)S(1)} collective-permute-done((f32[1,64]{1,0:T(1,128)S(1)}, f32[1,64]{1,0:T(1,128)S(1)}, u32[]{:S(2)}, u32[]{:S(2)}) %collective-permute-start.17) | collective-permute-done | bytes 288 | tf_op jit(solution)/shard_map/ppermute | solution.py:114
  58.0 0.5 add_bitcast_fusion
  58.5 0.0 collective-permute-done.12.refs_1_
  58.5 0.0 collective-permute-done.14.refs_3_
  58.5 0.0 copy-start.2
  58.5 0.9 %copy-done.2 = bf16[8,64,256]{2,1,0:T(8,128)(2,1)S(1)} copy-done((bf16[8,64,256]{2,1,0:T(8,128)(2,1)S(1)}, bf16[8,64,256]{2,1,0:T(8,128)(2,1)}, u32[]{:S(2)}) %copy-start.2) | copy-done | bytes 262168
  59.5 1.8 %shard_map.98 = (bf16[2,8,288,256]{3,2,1,0:T(8,128)(2,1)S(1)}, f32[1,64]{1,0:T(1,128)}) custom-call(s32[2]{0:T(128)S(1)} %copy-done.7, bf16[8,64,256]{2,1,0:T(8,128)(2,1)S(1)} %copy-done.2, bf16[8,64,256]{2,1,0:T(8,128)(2,1)S(1)} %collective-permute-done.12.refs_1_, bf16[8,64,256]{2,1,0:T(8,128)(2,1)S(1)} %collective-permute-done.13.refs_2_, ...), custom_call_target="tpu_custom_call" | custom-call | flops 1769472000 | bytes 1048576 | tf_op jit(solution)/shard_map/pallas_call | solution.py:514
  61.2 3.4 %shard_map.99 = f32[27,64,256]{2,1,0:T(8,128)} custom-call(s32[2]{0:T(128)S(1)} %copy-done.7, f32[1,64]{1,0:T(1,128)S(1)} %get-tuple-element.43._, bf16[2,8,288,256]{3,2,1,0:T(8,128)(2,1)S(1)} %get-tuple-element.44.grads, bf16[2,128,256]{2,1,0:T(8,128)(2,1)S(1)} %get-tuple-element.40.refs_0_, ...), custom_call_target="tpu_custom_call" | custom-call | flops 3932160000 | bytes 3538944 | tf_op jit(solution)/shard_map/pallas_call | solution.py:520
  (14 shorter events, 0.1 us)
Async XLA Ops:
  2.1 16.2 %all-to-all-start = ((bf16[8,64,256]{2,1,0:T(8,128)(2,1)}), bf16[8,64,256]{2,1,0:T(8,128)(2,1)S(1)}, u32[]{:S(2)}, u32[]{:S(2)}) async-start(bf16[8,64,256]{2,1,0:T(8,128)(2,1)} %broadcast_in_dim.8), calls=%async_computation | async-start | bytes 524288 | tf_op jit(solution)/shard_map/all_to_all | solution.py:448
  9.5 10.2 %copy-start.6 = (s32[2]{0:T(128)}, s32[2]{0:T(128)S(1)}, u32[]{:S(2)}) copy-start(s32[2]{0:T(128)S(1)} %pad_add_fusion.place) | copy-start | bytes 28
  10.2 0.9 %copy-start.8 = (bf16[4,2,32,256]{3,2,1,0:T(8,128)(2,1)S(1)}, bf16[4,2,32,256]{3,2,1,0:T(8,128)(2,1)}, u32[]{:S(2)}) copy-start(bf16[4,2,32,256]{3,2,1,0:T(8,128)(2,1)} %param.5) | copy-start | bytes 393220
  11.9 0.6 copy-start.5
  12.5 16.4 %copy-start = (bf16[256,256]{1,0:T(8,128)(2,1)}, bf16[256,256]{1,0:T(8,128)(2,1)S(1)}, u32[]{:S(2)}) copy-start(bf16[256,256]{1,0:T(8,128)(2,1)S(1)} %get-tuple-element.34._.frames) | copy-start | bytes 393220
  12.5 16.5 %copy-start.3 = (bf16[2,2,64,256]{3,2,1,0:T(8,128)(2,1)}, bf16[2,2,64,256]{3,2,1,0:T(8,128)(2,1)S(1)}, u32[]{:S(2)}) copy-start(bf16[2,2,64,256]{3,2,1,0:T(8,128)(2,1)S(1)} %get-tuple-element.27.planes) | copy-start | bytes 393220
  12.5 7.1 %collective-permute-start = (bf16[384,128]{1,0:T(8,128)(2,1)S(1)}, bf16[384,128]{1,0:T(8,128)(2,1)S(1)}, u32[]{:S(2)}, u32[]{:S(2)}) collective-permute-start(bf16[384,128]{1,0:T(8,128)(2,1)S(1)} %get-tuple-element.29), channel_id=1, source_target_pairs={{0,1},{1,0},{2,3},{3,2},{4,5},{5,4},{6,7},{7,6},{8,9},{9,8},{10,11... | collective-permute-start | bytes 294920 | tf_op jit(solution)/shard_map/ppermute | solution.py:114
  12.5 7.2 %collective-permute-start.2 = (bf16[384,128]{1,0:T(8,128)(2,1)S(1)}, bf16[384,128]{1,0:T(8,128)(2,1)S(1)}, u32[]{:S(2)}, u32[]{:S(2)}) collective-permute-start(bf16[384,128]{1,0:T(8,128)(2,1)S(1)} %get-tuple-element.31), channel_id=1, source_target_pairs={{0,3},{1,2},{2,1},{3,0},{4,7},{5,6},{6,5},{7,4},{8,11},{9,10},{10,... | collective-permute-start | bytes 294920 | tf_op jit(solution)/shard_map/ppermute | solution.py:114
  14.1 5.5 %collective-permute-start.1 = (bf16[128,128]{1,0:T(8,128)(2,1)S(1)}, bf16[128,128]{1,0:T(8,128)(2,1)S(1)}, u32[]{:S(2)}, u32[]{:S(2)}) collective-permute-start(bf16[128,128]{1,0:T(8,128)(2,1)S(1)} %get-tuple-element.30), channel_id=1, source_target_pairs={{0,2},{1,3},{2,0},{3,1},{4,6},{5,7},{6,4},{7,5},{8,10},{9,11},{10,... | collective-permute-start | bytes 98312 | tf_op jit(solution)/shard_map/ppermute | solution.py:114
  18.3 10.6 %copy-start.1 = (bf16[8,64,256]{2,1,0:T(8,128)(2,1)}, bf16[8,64,256]{2,1,0:T(8,128)(2,1)S(1)}, u32[]{:S(2)}) copy-start(bf16[8,64,256]{2,1,0:T(8,128)(2,1)S(1)} %get-tuple-element.36.gathered.refs_0_) | copy-start | bytes 786436
  18.3 10.6 %collective-permute-start.4 = (bf16[8,32,256]{2,1,0:T(8,128)(2,1)S(1)}, bf16[8,32,256]{2,1,0:T(8,128)(2,1)S(1)}, u32[]{:S(2)}, u32[]{:S(2)}) collective-permute-start(bf16[8,32,256]{2,1,0:T(8,128)(2,1)S(1)} %get-tuple-element.37), channel_id=1, source_target_pairs={{1,0},{2,1},{3,2},{5,4},{6,5},{7,6},{9,8},{10,9},{11,10},{13,12},{... | collective-permute-start | bytes 393224 | tf_op jit(solution)/shard_map/ppermute | solution.py:20
  20.3 0.6 copy-start.4
  21.0 8.0 %collective-permute-start.3 = (bf16[2,96,256]{2,1,0:T(8,128)(2,1)S(1)}, bf16[2,96,256]{2,1,0:T(8,128)(2,1)S(1)}, u32[]{:S(2)}, u32[]{:S(2)}) collective-permute-start(bf16[2,96,256]{2,1,0:T(8,128)(2,1)S(1)} %get-tuple-element.33), channel_id=1, source_target_pairs={{4,0},{8,4},{12,8},{16,12},{20,16},{24,20},{28,24},{5,1},{9,5},{13... | collective-permute-start | bytes 294920 | tf_op jit(solution)/shard_map/ppermute | solution.py:20
  22.2 12.7 %collective-permute-start.7 = (bf16[2,128,256]{2,1,0:T(8,128)(2,1)S(1)}, bf16[2,128,256]{2,1,0:T(8,128)(2,1)S(1)}, u32[]{:S(2)}, u32[]{:S(2)}) collective-permute-start(bf16[2,128,256]{2,1,0:T(8,128)(2,1)S(1)} %get-tuple-element.40.refs_0_), channel_id=1, source_target_pairs={{0,16},{4,20},{8,24},{12,28},{16,0},{20,4},{24,8},{28,12},{1,17},{... | collective-permute-start | bytes 393224 | tf_op jit(solution)/shard_map/ppermute | solution.py:114
  25.9 9.0 %collective-permute-start.6 = (bf16[2,128,256]{2,1,0:T(8,128)(2,1)S(1)}, bf16[2,128,256]{2,1,0:T(8,128)(2,1)S(1)}, u32[]{:S(2)}, u32[]{:S(2)}) collective-permute-start(bf16[2,128,256]{2,1,0:T(8,128)(2,1)S(1)} %get-tuple-element.40.refs_0_), channel_id=1, source_target_pairs={{0,8},{4,12},{8,0},{12,4},{16,24},{20,28},{24,16},{28,20},{1,9},{5... | collective-permute-start | bytes 393224 | tf_op jit(solution)/shard_map/ppermute | solution.py:114
  27.4 19.3 %collective-permute-start.13 = (bf16[8,64,256]{2,1,0:T(8,128)(2,1)S(1)}, bf16[8,64,256]{2,1,0:T(8,128)(2,1)S(1)}, u32[]{:S(2)}, u32[]{:S(2)}) collective-permute-start(bf16[8,64,256]{2,1,0:T(8,128)(2,1)S(1)} %get-tuple-element.36.gathered.refs_0_), channel_id=1, source_target_pairs={{0,2},{1,3},{2,0},{3,1},{4,6},{5,7},{6,4},{7,5},{8,10},{9,11},{10,... | collective-permute-start | bytes 786440 | tf_op jit(solution)/shard_map/ppermute | solution.py:114
  28.9 0.6 copy-start.10
  28.9 0.7 %copy-start.9 = (bf16[8,32,256]{2,1,0:T(8,128)(2,1)}, bf16[8,32,256]{2,1,0:T(8,128)(2,1)S(1)}, u32[]{:S(2)}) copy-start(bf16[8,32,256]{2,1,0:T(8,128)(2,1)S(1)} %collective-permute-done.4.following) | copy-start | bytes 393220
  29.6 28.9 %copy-start.7 = (s32[2]{0:T(128)S(1)}, s32[2]{0:T(128)}, u32[]{:S(2)}) copy-start(s32[2]{0:T(128)} %copy-done.6) | copy-start | bytes 28
  35.0 5.3 %collective-permute-start.10 = (bf16[2,128,256]{2,1,0:T(8,128)(2,1)S(1)}, bf16[2,128,256]{2,1,0:T(8,128)(2,1)S(1)}, u32[]{:S(2)}, u32[]{:S(2)}) collective-permute-start(bf16[2,128,256]{2,1,0:T(8,128)(2,1)S(1)} %get-tuple-element.42.refs_4_), channel_id=1, source_target_pairs={{0,8},{4,12},{8,0},{12,4},{16,24},{20,28},{24,16},{28,20},{1,9},{5... | collective-permute-start | bytes 393224 | tf_op jit(solution)/shard_map/ppermute | solution.py:114
  35.6 11.0 %collective-permute-start.5 = (bf16[2,128,256]{2,1,0:T(8,128)(2,1)S(1)}, bf16[2,128,256]{2,1,0:T(8,128)(2,1)S(1)}, u32[]{:S(2)}, u32[]{:S(2)}) collective-permute-start(bf16[2,128,256]{2,1,0:T(8,128)(2,1)S(1)} %get-tuple-element.40.refs_0_), channel_id=1, source_target_pairs={{0,4},{4,0},{8,12},{12,8},{16,20},{20,16},{24,28},{28,24},{1,5},{5... | collective-permute-start | bytes 393224 | tf_op jit(solution)/shard_map/ppermute | solution.py:114
  37.6 15.9 %collective-permute-start.9 = (bf16[2,128,256]{2,1,0:T(8,128)(2,1)S(1)}, bf16[2,128,256]{2,1,0:T(8,128)(2,1)S(1)}, u32[]{:S(2)}, u32[]{:S(2)}) collective-permute-start(bf16[2,128,256]{2,1,0:T(8,128)(2,1)S(1)} %get-tuple-element.42.refs_4_), channel_id=1, source_target_pairs={{0,4},{4,0},{8,12},{12,8},{16,20},{20,16},{24,28},{28,24},{1,5},{5... | collective-permute-start | bytes 393224 | tf_op jit(solution)/shard_map/ppermute | solution.py:114
  37.7 15.8 %collective-permute-start.8 = (bf16[2,128,256]{2,1,0:T(8,128)(2,1)S(1)}, bf16[2,128,256]{2,1,0:T(8,128)(2,1)S(1)}, u32[]{:S(2)}, u32[]{:S(2)}) collective-permute-start(bf16[2,128,256]{2,1,0:T(8,128)(2,1)S(1)} %get-tuple-element.41.refs_2_), channel_id=1, source_target_pairs={{0,4},{4,0},{8,12},{12,8},{16,20},{20,16},{24,28},{28,24},{1,5},{5... | collective-permute-start | bytes 393224 | tf_op jit(solution)/shard_map/ppermute | solution.py:114
  40.3 13.2 %collective-permute-start.11 = (bf16[2,128,256]{2,1,0:T(8,128)(2,1)S(1)}, bf16[2,128,256]{2,1,0:T(8,128)(2,1)S(1)}, u32[]{:S(2)}, u32[]{:S(2)}) collective-permute-start(bf16[2,128,256]{2,1,0:T(8,128)(2,1)S(1)} %collective-permute-done.10.refs_6_), channel_id=1, source_target_pairs={{0,4},{4,0},{8,12},{12,8},{16,20},{20,16},{24,28},{28,24},{1,5},{5... | collective-permute-start | bytes 393224 | tf_op jit(solution)/shard_map/ppermute | solution.py:114
  43.3 10.2 %all-to-all-start.1 = ((bf16[8,16,256]{2,1,0:T(8,128)(2,1)}), bf16[8,16,256]{2,1,0:T(8,128)(2,1)S(1)}, u32[]{:S(2)}, u32[]{:S(2)}) async-start(bf16[8,16,256]{2,1,0:T(8,128)(2,1)} %bitcast.6), calls=%async_computation.1 | async-start | bytes 131072 | tf_op jit(solution)/shard_map/all_to_all | solution.py:503
  46.7 11.9 %collective-permute-start.12 = (bf16[8,64,256]{2,1,0:T(8,128)(2,1)}, bf16[8,64,256]{2,1,0:T(8,128)(2,1)S(1)}, u32[]{:S(2)}, u32[]{:S(2)}) collective-permute-start(bf16[8,64,256]{2,1,0:T(8,128)(2,1)} %copy-done.1), channel_id=1, source_target_pairs={{0,1},{1,0},{2,3},{3,2},{4,5},{5,4},{6,7},{7,6},{8,9},{9,8},{10,11... | collective-permute-start | bytes 786440 | tf_op jit(solution)/shard_map/ppermute | solution.py:114
  46.8 11.8 %collective-permute-start.14 = (bf16[8,64,256]{2,1,0:T(8,128)(2,1)S(1)}, bf16[8,64,256]{2,1,0:T(8,128)(2,1)S(1)}, u32[]{:S(2)}, u32[]{:S(2)}) collective-permute-start(bf16[8,64,256]{2,1,0:T(8,128)(2,1)S(1)} %collective-permute-done.13.refs_2_), channel_id=1, source_target_pairs={{0,1},{1,0},{2,3},{3,2},{4,5},{5,4},{6,7},{7,6},{8,9},{9,8},{10,11... | collective-permute-start | bytes 786440 | tf_op jit(solution)/shard_map/ppermute | solution.py:114
  53.6 2.5 %collective-permute-start.15 = (f32[1,64]{1,0:T(1,128)S(1)}, f32[1,64]{1,0:T(1,128)S(1)}, u32[]{:S(2)}, u32[]{:S(2)}) collective-permute-start(f32[1,64]{1,0:T(1,128)S(1)} %get-tuple-element.45), channel_id=1, source_target_pairs={{0,1},{1,0},{2,3},{3,2},{4,5},{5,4},{6,7},{7,6},{8,9},{9,8},{10,11... | collective-permute-start | bytes 776 | tf_op jit(solution)/shard_map/ppermute | solution.py:114
  53.6 3.6 %collective-permute-start.16 = (f32[1,64]{1,0:T(1,128)S(1)}, f32[1,64]{1,0:T(1,128)S(1)}, u32[]{:S(2)}, u32[]{:S(2)}) collective-permute-start(f32[1,64]{1,0:T(1,128)S(1)} %get-tuple-element.46), channel_id=1, source_target_pairs={{0,2},{1,3},{2,0},{3,1},{4,6},{5,7},{6,4},{7,5},{8,10},{9,11},{10,... | collective-permute-start | bytes 776 | tf_op jit(solution)/shard_map/ppermute | solution.py:114
  55.0 3.0 %collective-permute-start.17 = (f32[1,64]{1,0:T(1,128)S(1)}, f32[1,64]{1,0:T(1,128)S(1)}, u32[]{:S(2)}, u32[]{:S(2)}) collective-permute-start(f32[1,64]{1,0:T(1,128)S(1)} %get-tuple-element.47), channel_id=1, source_target_pairs={{0,3},{1,2},{2,1},{3,0},{4,7},{5,6},{6,5},{7,4},{8,11},{9,10},{10,... | collective-permute-start | bytes 776 | tf_op jit(solution)/shard_map/ppermute | solution.py:114
  58.5 1.0 %copy-start.2 = (bf16[8,64,256]{2,1,0:T(8,128)(2,1)S(1)}, bf16[8,64,256]{2,1,0:T(8,128)(2,1)}, u32[]{:S(2)}) copy-start(bf16[8,64,256]{2,1,0:T(8,128)(2,1)} %copy-done.1) | copy-start | bytes 786436

commit v7 on v6

--- a/solution.py
+++ b/solution.py
@@ -10,7 +10,7 @@
 EPS = 1e-06
 TAPS = [(a, b, c) for a in range(3) for b in range(3) for c in range(3)]
 VMEM_LIMIT = 20 * 1024 * 1024
-VMEM_LIMIT_WIDE = 60 * 1024 * 1024
+VMEM_LIMIT_WIDE = 59 * 1024 * 1024
 WORK = 1200
 
 
@@ -192,10 +192,23 @@
             sends[k][rp * F * J : (rp + 1) * F * J] = chosen.astype(jnp.bfloat16)
 
 
-def head_kernel(rows, _, grad_rows, head, passed):
-    passed[...] = grad_rows[...]
-    for s in range(grad_rows.shape[0]):
-        head[s] = grad_rows[s, :rows, :]
+def copies_kernel(own, ahead, out):
+    rows = own.shape[0]
+    for s in range(out.shape[0]):
+        out[s, :rows] = own[...]
+        out[s, rows:] = ahead[...]
+
+
+def own_kernel(_, both, own):
+    for s in range(both.shape[0]):
+        own[s] = both[s, : own.shape[1], :]
+
+
+def total_kernel(*refs):
+    total = refs[1][...]
+    for ref in refs[2:-1]:
+        total = total + ref[...]
+    refs[-1][...] = total
 
 
 def join_kernel(F, J, T, place, planes, *refs):
@@ -260,7 +273,7 @@
 
 
 def slab_kernel(
-    F, J, R, T, slot, place, planes, cached, under, weight_hbm, frames, vectors, gathered, following,
+    F, J, R, T, slot, place, planes, cached, under, weight_hbm, frames, vectors, gathered,
     out, frames_grad, weight, near, ext, tmp, sem,
 ):
     row, block = place[0], place[1]
@@ -276,10 +289,7 @@
 
     orders = [shard_order(J, R, 2, row - 1, moved) for moved in range(2)]
     for pair in range(F // 2 + 1):
-        if pair < F // 2:
-            source = shard_rows(gathered, pair * 2 * J, 2 * J)
-        else:
-            source = shard_rows(following, 0, 2 * J)
+        source = shard_rows(gathered, pair * 2 * J, 2 * J)
         for moved in range(2):
             value = mm(orders[moved], source).astype(jnp.bfloat16)
             for i in range(2):
@@ -444,10 +454,14 @@
     weight = conv_weight.reshape(27, C, C)
     place = jnp.stack([lax.axis_index("rows"), lax.axis_index("tm")]).astype(jnp.int32)
 
-    own = latent_grad.reshape(1, -1, C)
-    grad_rows = lax.all_to_all(
-        jnp.broadcast_to(own, (R,) + own.shape[1:]), "rows", 0, 0, tiled=True
-    )
+    own = latent_grad.reshape(span, C)
+    ahead = shifted(own[: 2 * J], "tm", -1)
+    (copies,) = call(
+        copies_kernel,
+        [((R, span + 2 * J, C), bf16)],
+        [], 2 * R * span * C, 2 * R * span * C, "vvv",
+    )(own, ahead)
+    grad_both = lax.all_to_all(copies, "rows", 0, 0, tiled=True)
 
     sizes = [(2 * span + (16 * J if k % 2 else 0), 2 * part) for k in range(T)]
     planes, frames_copy, vectors, *sends = call(
@@ -457,11 +471,11 @@
         [pltpu.VMEM((2, 4 * span, C // 2), f32)],
         60 * WORK * span * C, 16 * span * C, "svv" + "v" * (T + 3),
     )(place, flat, vectors)
-    head, grad_rows = call(
-        functools.partial(head_kernel, 2 * J),
-        [((R, 2 * J, C), bf16), (grad_rows.shape, bf16)],
-        [], R * span * C, R * span * C, "avvv",
-    )(frames_copy, grad_rows)
+    (grad_rows,) = call(
+        own_kernel,
+        [((R, span, C), bf16)],
+        [], R * span * C, R * span * C, "avv",
+    )(frames_copy, grad_both)
     messages = [sends[0]] + [partners(sends[k], "tm", k) for k in range(1, T)]
     joined, cached, under = call(
         functools.partial(join_kernel, F, J, T),
@@ -474,7 +488,6 @@
         30 * WORK * span * C, 16 * span * C, "sv" + "v" * T + "vvv",
     )(place, planes, *messages)
     under = shifted(under, "rows", -1)
-    following = shifted(head, "tm", -1)
     packed, frames_grad = call(
         functools.partial(slab_kernel, F, J, R, T, slot),
         [((R * slot, C), bf16), ((4 * span, C), bf16)],
@@ -485,9 +498,9 @@
             pltpu.VMEM((2, 4 * span, C // 2), f32),
             pltpu.SemaphoreType.DMA((3,)),
         ],
-        2 * 54 * span * C * C, 2 * 27 * C * C, "svvvhvvvv" + "vv",
+        2 * 54 * span * C * C, 2 * 27 * C * C, "svvvhvvv" + "vv",
         limit=VMEM_LIMIT_WIDE,
-    )(place, planes, cached, under, weight, frames_copy, vectors, grad_rows, following)
+    )(place, planes, cached, under, weight, frames_copy, vectors, grad_both)
 
     def after_slab(blocks):
         shapes = [(b.shape, bf16) for b in blocks]
@@ -502,21 +515,17 @@
 
     packed = lax.all_to_all(packed.reshape(R, slot, C), "rows", 0, 0, tiled=True)
     latent = packed[:, :used].reshape(R, F, J // R, C).transpose(1, 0, 2, 3)
-    gains = call(
-        functools.partial(gain_kernel, T, used),
-        [((1, part), f32)] * T,
-        [], R * slot * C, R * slot * C, "v" + "a" * (R // 2) + "v" * T,
-    )(packed, *hidden_all[1::2])
-    gain_grad = gains[0]
-    for k in range(1, T):
-        gain_grad = gain_grad + partners(gains[k], "tm", k)
-
     grads, bias_sum = call(
         functools.partial(order_kernel, F, J, R, T),
         [((2, R, (F * T + 2) * J, C), bf16), ((1, part), f32)],
         [],
         90 * WORK * span * C, 2 * R * T * span * C, "s" + "v" * (T + 2),
     )(place, *grad_all)
+    gains = call(
+        functools.partial(gain_kernel, T, used),
+        [((1, part), f32)] * T,
+        [], R * slot * C, R * slot * C, "v" + "a" * (R // 2 + 1) + "v" * T,
+    )(packed, bias_sum, *hidden_all[1::2])
     (weight_grad,) = call(
         functools.partial(weight_kernel, F, J, R, T, part),
         [((27, part, C), f32)],
@@ -529,6 +538,10 @@
         200 * WORK * span * C, 8 * 27 * part * C, "sav" + "v" * R + "h",
     )(place, gains[0], grads, *hidden_all)
 
+    terms = [gains[0]] + [partners(gains[k], "tm", k) for k in range(1, T)]
+    (gain_grad,) = call(
+        total_kernel, [((1, part), f32)], [], T * part, 4 * T * part, "a" + "v" * (T + 1)
+    )(weight_grad, *terms)
     return (
         latent,
         frames_grad.reshape(frames.shape),

time: 65.2 us -> 81 us (1.24)
  waiting for transfers between devices: 12.5 us -> 27.2 us
  local copies, waits for them, and re-layouts: 5.87 us -> 7.88 us
  starting transfers between devices: 32 us -> 30.3 us
  Pallas kernels: 12.1 us -> 13.4 us
    ppermute x16, waiting for transfers between devices: 2.6 us -> 10.9 us  [partners(): lax.ppermute(value, axis, [(source, source ^ bits) for source in range(co...]
    all_to_all x1, waiting for transfers between devices: 3.65 us -> 9.38 us  [gathered_form(): grad_both = lax.all_to_all(copies, 'rows', 0, 0, tiled=True)]
    ppermute x16, starting transfers between devices: 18.8 us -> 15.2 us  [partners(): lax.ppermute(value, axis, [(source, source ^ bits) for source in range(co...]
    ppermute x2, waiting for transfers between devices: 0.01 us -> 2.01 us  [shifted(): lax.ppermute(value, axis, [(source, source + steps) for source in range(l...]
    unnamed x22 -> x24, local copies, waits for them, and re-layouts: 3.7 us -> 5.69 us
    all_to_all x1, starting transfers between devices: 3.35 us -> 5.32 us  [gathered_form(): lax.all_to_all(packed.reshape(R, slot, C), 'rows', 0, 0, tiled=True)]
    broadcast_in_dim x2 -> x0, local copies, waits for them, and re-layouts: 1.5 us -> none  [gathered_form(): jnp.broadcast_to(own, (R,) + own.shape[1:])]
    all_to_all x1, waiting for transfers between devices: 6.25 us -> 4.95 us  [gathered_form(): lax.all_to_all(packed.reshape(R, slot, C), 'rows', 0, 0, tiled=True)]
  transfers between devices with their start and end apart: 20 -> 20, of which waited for: 5 -> 7; matrix products, arithmetic and copies ran while one was open for 3% -> 3% of each run, Pallas kernels for 11% -> 15%
where the time goes in v7:
time: 81 us; the launch traced here: 80.4 us
  starting transfers between devices  30.3 us (37%)
  waiting for transfers between devices  27.2 us (34%)
  Pallas kernels  13.4 us (17%)
  local copies, waits for them, and re-layouts  7.88 us (10%)
  between operations  0.81 us (1%)
    ppermute x16, starting transfers between devices, partners(): lax.ppermute(value, axis, [(source, source ^ bits) for source in range(co...  15.2 us
    ppermute x16, waiting for transfers between devices, partners(): lax.ppermute(value, axis, [(source, source ^ bits) for source in range(co...  10.9 us
    all_to_all x1, waiting for transfers between devices, gathered_form(): grad_both = lax.all_to_all(copies, 'rows', 0, 0, tiled=True)  9.38 us
    all_to_all x1, starting transfers between devices, gathered_form(): grad_both = lax.all_to_all(copies, 'rows', 0, 0, tiled=True)  7.25 us
    unnamed x24, local copies, waits for them, and re-layouts  5.69 us
    pallas_call x1, Pallas kernels, gathered_form(): call(functools.partial(slab_kernel, F, J, R, T, slot), [((R * slot, C), b...  5.36 us
    all_to_all x1, starting transfers between devices, gathered_form(): lax.all_to_all(packed.reshape(R, slot, C), 'rows', 0, 0, tiled=True)  5.32 us
    all_to_all x1, waiting for transfers between devices, gathered_form(): lax.all_to_all(packed.reshape(R, slot, C), 'rows', 0, 0, tiled=True)  4.95 us
  transfers between devices with their start and end apart: 20, of which 7 were waited for; matrix products, arithmetic and copies ran while one was open for 3% of the time, Pallas kernels for 15%

profile of v7, /device:TPU:0, one launch (start us, length us, event | category | flops | bytes accessed | tf_op | source)
XLA Modules:
  0.0 80.4 jit_solution(4610210584733170578)
XLA Ops:
  0.6 0.7 slice.9
  1.4 1.3 %collective-permute-start.4 = (bf16[32,256]{1,0:T(8,128)(2,1)S(1)}, bf16[32,256]{1,0:T(8,128)(2,1)S(1)}, u32[]{:S(2)}, u32[]{:S(2)}) collective-permute-start(bf16[32,256]{1,0:T(8,128)(2,1)S(1)} %slice.10), channel_id=1, source_target_pairs={{1,0},{2,1},{3,2},{5,4},{6,5},{7,6},{9,8},{10,9},{11,10},{13,12},{... | collective-permute-start | bytes 49160 | tf_op jit(solution)/shard_map/ppermute | solution.py:20
  2.7 0.8 reshape.40.own
  3.5 1.0 %collective-permute-done.4.ahead = bf16[32,256]{1,0:T(8,128)(2,1)S(1)} collective-permute-done((bf16[32,256]{1,0:T(8,128)(2,1)S(1)}, bf16[32,256]{1,0:T(8,128)(2,1)S(1)}, u32[]{:S(2)}, u32[]{:S(2)}) %collective-permute-start.4) | collective-permute-done | bytes 16416 | tf_op jit(solution)/shard_map/ppermute | solution.py:20
  4.5 0.8 shard_map.94
  5.2 7.3 %all-to-all-start = ((bf16[8,96,256]{2,1,0:T(8,128)(2,1)}), bf16[8,96,256]{2,1,0:T(8,128)(2,1)S(1)}, u32[]{:S(2)}, u32[]{:S(2)}) async-start(bf16[8,96,256]{2,1,0:T(8,128)(2,1)} %shard_map.94), calls=%async_computation | async-start | bytes 786432 | tf_op jit(solution)/shard_map/all_to_all | solution.py:464
  12.5 0.1 pad_add_fusion.place
  12.6 0.7 pad_maximum_fusion.vectors
  13.3 0.9 %copy-done.10 = bf16[4,2,32,256]{3,2,1,0:T(8,128)(2,1)S(1)} copy-done((bf16[4,2,32,256]{3,2,1,0:T(8,128)(2,1)S(1)}, bf16[4,2,32,256]{3,2,1,0:T(8,128)(2,1)}, u32[]{:S(2)}) %copy-start.10) | copy-done | bytes 131096
  14.2 0.8 %shard_map.92 = (bf16[2,2,64,256]{3,2,1,0:T(8,128)(2,1)S(1)}, bf16[256,256]{1,0:T(8,128)(2,1)S(1)}, f32[2,256]{1,0:T(2,128)S(1)}, bf16[128,128]{1,0:T(8,128)(2,1...) custom-call(s32[2]{0:T(128)S(1)} %pad_add_fusion.place, ...), custom_call_target="tpu_custom_call" | custom-call | flops 1179648000 | bytes 262144 | tf_op jit(solution)/shard_map/pallas_call | solution.py:467
  15.0 0.0 copy-start.6
  15.0 0.6 copy-done.6
  15.6 9.4 %all-to-all-done.gathered.both = bf16[8,96,256]{2,1,0:T(8,128)(2,1)S(1)} async-done(((bf16[8,96,256]{2,1,0:T(8,128)(2,1)}), bf16[8,96,256]{2,1,0:T(8,128)(2,1)S(1)}, u32[]{:S(2)}, u32[]{:S(2)}) %all-to-all-start) | async-done | bytes 393248 | tf_op jit(solution)/shard_map/all_to_all | solution.py:464
  25.0 1.1 %collective-permute-start.6 = (bf16[8,64,256]{2,1,0:T(8,128)(2,1)S(1)}, bf16[8,64,256]{2,1,0:T(8,128)(2,1)S(1)}, u32[]{:S(2)}, u32[]{:S(2)}) collective-permute-start(bf16[8,64,256]{2,1,0:T(8,128)(2,1)S(1)} %shard_map.96.refs_0_), channel_id=1, source_target_pairs={{0,2},{1,3},{2,0},{3,1},{4,6},{5,7},{6,4},{7,5},{8,10},{9,11},{10,... | collective-permute-start | bytes 786440 | tf_op jit(solution)/shard_map/ppermute | solution.py:114
  26.1 0.0 collective-permute-start
  26.1 1.1 %collective-permute-start.2 = (bf16[384,128]{1,0:T(8,128)(2,1)S(1)}, bf16[384,128]{1,0:T(8,128)(2,1)S(1)}, u32[]{:S(2)}, u32[]{:S(2)}) collective-permute-start(bf16[384,128]{1,0:T(8,128)(2,1)S(1)} %get-tuple-element.29), channel_id=1, source_target_pairs={{0,3},{1,2},{2,1},{3,0},{4,7},{5,6},{6,5},{7,4},{8,11},{9,10},{10,... | collective-permute-start | bytes 294920 | tf_op jit(solution)/shard_map/ppermute | solution.py:114
  27.2 1.0 %collective-permute-start.1 = (bf16[128,128]{1,0:T(8,128)(2,1)S(1)}, bf16[128,128]{1,0:T(8,128)(2,1)S(1)}, u32[]{:S(2)}, u32[]{:S(2)}) collective-permute-start(bf16[128,128]{1,0:T(8,128)(2,1)S(1)} %get-tuple-element.28), channel_id=1, source_target_pairs={{0,2},{1,3},{2,0},{3,1},{4,6},{5,7},{6,4},{7,5},{8,10},{9,11},{10,... | collective-permute-start | bytes 98312 | tf_op jit(solution)/shard_map/ppermute | solution.py:114
  28.2 8.3 %collective-permute-done.1.refs_2_ = bf16[128,128]{1,0:T(8,128)(2,1)S(1)} collective-permute-done((bf16[128,128]{1,0:T(8,128)(2,1)S(1)}, bf16[128,128]{1,0:T(8,128)(2,1)S(1)}, u32[]{:S(2)}, u32[]{:S(2)}) %collective-permute-start.1) | collective-permute-done | bytes 32800 | tf_op jit(solution)/shard_map/ppermute | solution.py:114
  36.5 0.0 collective-permute-done.refs_1_
  36.5 0.0 collective-permute-done.2.refs_3_
  36.6 0.6 shard_map.93
  37.2 0.6 copy-done.5
  37.8 1.3 %collective-permute-start.3 = (bf16[2,96,256]{2,1,0:T(8,128)(2,1)S(1)}, bf16[2,96,256]{2,1,0:T(8,128)(2,1)S(1)}, u32[]{:S(2)}, u32[]{:S(2)}) collective-permute-start(bf16[2,96,256]{2,1,0:T(8,128)(2,1)S(1)} %get-tuple-element.31), channel_id=1, source_target_pairs={{4,0},{8,4},{12,8},{16,12},{20,16},{24,20},{28,24},{5,1},{9,5},{13... | collective-permute-start | bytes 294920 | tf_op jit(solution)/shard_map/ppermute | solution.py:20
  39.1 2.4 %collective-permute-start.10 = (bf16[2,128,256]{2,1,0:T(8,128)(2,1)S(1)}, bf16[2,128,256]{2,1,0:T(8,128)(2,1)S(1)}, u32[]{:S(2)}, u32[]{:S(2)}) collective-permute-start(bf16[2,128,256]{2,1,0:T(8,128)(2,1)S(1)} %get-tuple-element.37.refs_0_), channel_id=1, source_target_pairs={{0,16},{4,20},{8,24},{12,28},{16,0},{20,4},{24,8},{28,12},{1,17},{... | collective-permute-start | bytes 393224 | tf_op jit(solution)/shard_map/ppermute | solution.py:114
  41.5 1.3 %collective-permute-start.9 = (bf16[2,128,256]{2,1,0:T(8,128)(2,1)S(1)}, bf16[2,128,256]{2,1,0:T(8,128)(2,1)S(1)}, u32[]{:S(2)}, u32[]{:S(2)}) collective-permute-start(bf16[2,128,256]{2,1,0:T(8,128)(2,1)S(1)} %get-tuple-element.37.refs_0_), channel_id=1, source_target_pairs={{0,8},{4,12},{8,0},{12,4},{16,24},{20,28},{24,16},{28,20},{1,9},{5... | collective-permute-start | bytes 393224 | tf_op jit(solution)/shard_map/ppermute | solution.py:114
  42.8 0.0 collective-permute-start.5
  42.8 0.0 collective-permute-done.6.refs_2_
  42.8 0.5 collective-permute-start.7
  43.3 1.0 %collective-permute-done.3.under = bf16[2,96,256]{2,1,0:T(8,128)(2,1)S(1)} collective-permute-done((bf16[2,96,256]{2,1,0:T(8,128)(2,1)S(1)}, bf16[2,96,256]{2,1,0:T(8,128)(2,1)S(1)}, u32[]{:S(2)}, u32[]{:S(2)}) %collective-permute-start.3) | collective-permute-done | bytes 98336 | tf_op jit(solution)/shard_map/ppermute | solution.py:20
  44.3 0.0 copy-done.2
  44.3 0.6 copy-done.11
  45.0 5.4 %shard_map.95 = (bf16[128,256]{1,0:T(8,128)(2,1)}, bf16[256,256]{1,0:T(8,128)(2,1)}) custom-call(s32[2]{0:T(128)} %copy-done.7, bf16[2,2,64,256]{3,2,1,0:T(8,128)(2,1)} %copy-done.4, bf16[2,2,32,256]{3,2,1,0:T(8,128)(2,1)} %copy-done.5, bf16[2,96,256]{2,1,0:T(8,128)(2,1)} %copy-done.11, bf16[27,256,256]{2,1,0:T(8,128)(2,1)} %bitcast.18, ...), custom_call_target="tpu_custom_call" | custom-call | flops 452984832 | bytes 3538944 | tf_op jit(solution)/shard_map/pallas_call | solution.py:491
  50.3 0.0 collective-permute-done.10.refs_2_
  50.3 0.0 collective-permute-done.9.refs_1_
  50.3 0.0 copy-start.3
  50.4 0.8 %copy-done.3 = bf16[128,256]{1,0:T(8,128)(2,1)S(1)} copy-done((bf16[128,256]{1,0:T(8,128)(2,1)S(1)}, bf16[128,256]{1,0:T(8,128)(2,1)}, u32[]{:S(2)}) %copy-start.3) | copy-done | bytes 65560
  51.2 1.8 %collective-permute-start.13 = (bf16[2,128,256]{2,1,0:T(8,128)(2,1)S(1)}, bf16[2,128,256]{2,1,0:T(8,128)(2,1)S(1)}, u32[]{:S(2)}, u32[]{:S(2)}) collective-permute-start(bf16[2,128,256]{2,1,0:T(8,128)(2,1)S(1)} %get-tuple-element.39.refs_4_), channel_id=1, source_target_pairs={{0,8},{4,12},{8,0},{12,4},{16,24},{20,28},{24,16},{28,20},{1,9},{5... | collective-permute-start | bytes 393224 | tf_op jit(solution)/shard_map/ppermute | solution.py:114
  53.0 5.3 %all-to-all-start.1 = ((bf16[8,16,256]{2,1,0:T(8,128)(2,1)}), bf16[8,16,256]{2,1,0:T(8,128)(2,1)S(1)}, u32[]{:S(2)}, u32[]{:S(2)}) async-start(bf16[8,16,256]{2,1,0:T(8,128)(2,1)} %bitcast.15), calls=%async_computation.1 | async-start | bytes 131072 | tf_op jit(solution)/shard_map/all_to_all | solution.py:516
  58.3 2.0 %collective-permute-start.8 = (bf16[2,128,256]{2,1,0:T(8,128)(2,1)S(1)}, bf16[2,128,256]{2,1,0:T(8,128)(2,1)S(1)}, u32[]{:S(2)}, u32[]{:S(2)}) collective-permute-start(bf16[2,128,256]{2,1,0:T(8,128)(2,1)S(1)} %get-tuple-element.37.refs_0_), channel_id=1, source_target_pairs={{0,4},{4,0},{8,12},{12,8},{16,20},{20,16},{24,28},{28,24},{1,5},{5... | collective-permute-start | bytes 393224 | tf_op jit(solution)/shard_map/ppermute | solution.py:114
  60.3 0.0 collective-permute-start.12
  60.4 4.9 %all-to-all-done.1.received = bf16[8,16,256]{2,1,0:T(8,128)(2,1)S(1)} async-done(((bf16[8,16,256]{2,1,0:T(8,128)(2,1)}), bf16[8,16,256]{2,1,0:T(8,128)(2,1)S(1)}, u32[]{:S(2)}, u32[]{:S(2)}) %all-to-all-start.1) | async-done | bytes 65568 | tf_op jit(solution)/shard_map/all_to_all | solution.py:516
  65.4 0.6 copy.14
  66.0 0.0 collective-permute-done.13.refs_6_
  66.0 0.3 collective-permute-start.11
  66.3 0.0 collective-permute-done.5.refs_1_
  66.3 1.7 %collective-permute-start.14 = (bf16[2,128,256]{2,1,0:T(8,128)(2,1)S(1)}, bf16[2,128,256]{2,1,0:T(8,128)(2,1)S(1)}, u32[]{:S(2)}, u32[]{:S(2)}) collective-permute-start(bf16[2,128,256]{2,1,0:T(8,128)(2,1)S(1)} %collective-permute-done.13.refs_6_), channel_id=1, source_target_pairs={{0,4},{4,0},{8,12},{12,8},{16,20},{20,16},{24,28},{28,24},{1,5},{5... | collective-permute-start | bytes 393224 | tf_op jit(solution)/shard_map/ppermute | solution.py:114
  68.0 0.0 collective-permute-done.7.refs_3_
  68.0 1.8 %shard_map.97 = (bf16[2,8,288,256]{3,2,1,0:T(8,128)(2,1)S(1)}, f32[1,64]{1,0:T(1,128)}) custom-call(s32[2]{0:T(128)S(1)} %copy-done.8, bf16[8,64,256]{2,1,0:T(8,128)(2,1)S(1)} %shard_map.96.refs_0_, bf16[8,64,256]{2,1,0:T(8,128)(2,1)S(1)} %collective-permute-done.5.refs_1_, bf16[8,64,256]{2,1,0:T(8,128)(2,1)S(1)} %collective-permute-done.6.refs_2_, ...), custom_call_target="tpu_custom_call" | custom-call | flops 1769472000 | bytes 1048576 | tf_op jit(solution)/shard_map/pallas_call | solution.py:518
  69.8 0.0 collective-permute-done.8.refs_1_
  69.8 1.2 %collective-permute-done.11.refs_2_.refs_3_ = bf16[2,128,256]{2,1,0:T(8,128)(2,1)S(1)} collective-permute-done((bf16[2,128,256]{2,1,0:T(8,128)(2,1)S(1)}, bf16[2,128,256]{2,1,0:T(8,128)(2,1)S(1)}, u32[]{:S(2)}, u32[]{:S(2)}) %collective-permute-start.11) | collective-permute-done | bytes 131104 | tf_op jit(solution)/shard_map/ppermute | solution.py:114
  71.0 0.0 collective-permute-done.12.refs_3_.refs_5_
  71.0 1.4 %collective-permute-done.14.refs_4_.refs_7_ = bf16[2,128,256]{2,1,0:T(8,128)(2,1)S(1)} collective-permute-done((bf16[2,128,256]{2,1,0:T(8,128)(2,1)S(1)}, bf16[2,128,256]{2,1,0:T(8,128)(2,1)S(1)}, u32[]{:S(2)}, u32[]{:S(2)}) %collective-permute-start.14) | collective-permute-done | bytes 131104 | tf_op jit(solution)/shard_map/ppermute | solution.py:114
  72.4 0.7 copy-done.9
  73.0 0.1 shard_map.99
  73.1 0.0 collective-permute-start.15
  73.1 0.3 collective-permute-start.16
  73.4 1.5 %collective-permute-start.17 = (f32[1,64]{1,0:T(1,128)S(1)}, f32[1,64]{1,0:T(1,128)S(1)}, u32[]{:S(2)}, u32[]{:S(2)}) collective-permute-start(f32[1,64]{1,0:T(1,128)S(1)} %get-tuple-element.44), channel_id=1, source_target_pairs={{0,3},{1,2},{2,1},{3,0},{4,7},{5,6},{6,5},{7,4},{8,11},{9,10},{10,... | collective-permute-start | bytes 776 | tf_op jit(solution)/shard_map/ppermute | solution.py:114
  75.0 3.4 %shard_map.100.refs_0_ = f32[27,64,256]{2,1,0:T(8,128)} custom-call(s32[2]{0:T(128)S(1)} %copy-done.8, f32[1,64]{1,0:T(1,128)S(1)} %get-tuple-element.40._.refs_1_, bf16[2,8,288,256]{3,2,1,0:T(8,128)(2,1)S(1)} %get-tuple-element.41.grads, bf16[2,128,256]{2,1,0:T(8,128)(2,1)S(1)} %get-tuple-element.37.refs_0_, ...), custom_call_target="tpu_custom_call" | custom-call | flops 3932160000 | bytes 3538944 | tf_op jit(solution)/shard_map/pallas_call | solution.py:529
  78.4 0.0 collective-permute-done.15.refs_2_
  78.4 0.0 collective-permute-done.16.refs_3_
  78.4 0.0 collective-permute-done.17.refs_4_
  78.4 0.0 copy-start.1
  78.5 1.5 %copy-done.1 = f32[27,64,256]{2,1,0:T(8,128)S(1)} copy-done((f32[27,64,256]{2,1,0:T(8,128)S(1)}, f32[27,64,256]{2,1,0:T(8,128)}, u32[]{:S(2)}) %copy-start.1) | copy-done | bytes 1769496
  79.9 0.5 shard_map.101
  (18 shorter events, 0.1 us)
Async XLA Ops:
  1.4 3.1 %collective-permute-start.4 = (bf16[32,256]{1,0:T(8,128)(2,1)S(1)}, bf16[32,256]{1,0:T(8,128)(2,1)S(1)}, u32[]{:S(2)}, u32[]{:S(2)}) collective-permute-start(bf16[32,256]{1,0:T(8,128)(2,1)S(1)} %slice.10), channel_id=1, source_target_pairs={{1,0},{2,1},{3,2},{5,4},{6,5},{7,6},{9,8},{10,9},{11,10},{13,12},{... | collective-permute-start | bytes 49160 | tf_op jit(solution)/shard_map/ppermute | solution.py:20
  5.2 19.8 %all-to-all-start = ((bf16[8,96,256]{2,1,0:T(8,128)(2,1)}), bf16[8,96,256]{2,1,0:T(8,128)(2,1)S(1)}, u32[]{:S(2)}, u32[]{:S(2)}) async-start(bf16[8,96,256]{2,1,0:T(8,128)(2,1)} %shard_map.94), calls=%async_computation | async-start | bytes 786432 | tf_op jit(solution)/shard_map/all_to_all | solution.py:464
  12.6 24.0 %copy-start.7 = (s32[2]{0:T(128)}, s32[2]{0:T(128)S(1)}, u32[]{:S(2)}) copy-start(s32[2]{0:T(128)S(1)} %pad_add_fusion.place) | copy-start | bytes 28
  13.3 0.9 %copy-start.10 = (bf16[4,2,32,256]{3,2,1,0:T(8,128)(2,1)S(1)}, bf16[4,2,32,256]{3,2,1,0:T(8,128)(2,1)}, u32[]{:S(2)}) copy-start(bf16[4,2,32,256]{3,2,1,0:T(8,128)(2,1)} %param.5) | copy-start | bytes 393220
  15.0 0.6 copy-start.6
  15.6 28.7 %copy-start.2 = (bf16[256,256]{1,0:T(8,128)(2,1)}, bf16[256,256]{1,0:T(8,128)(2,1)S(1)}, u32[]{:S(2)}) copy-start(bf16[256,256]{1,0:T(8,128)(2,1)S(1)} %get-tuple-element.32.frames._) | copy-start | bytes 393220
  15.6 28.7 %copy-start.4 = (bf16[2,2,64,256]{3,2,1,0:T(8,128)(2,1)}, bf16[2,2,64,256]{3,2,1,0:T(8,128)(2,1)S(1)}, u32[]{:S(2)}) copy-start(bf16[2,2,64,256]{3,2,1,0:T(8,128)(2,1)S(1)} %get-tuple-element.25.planes) | copy-start | bytes 393220
  25.0 19.3 %copy-start = (bf16[8,96,256]{2,1,0:T(8,128)(2,1)}, bf16[8,96,256]{2,1,0:T(8,128)(2,1)S(1)}, u32[]{:S(2)}) copy-start(bf16[8,96,256]{2,1,0:T(8,128)(2,1)S(1)} %all-to-all-done.gathered.both) | copy-start | bytes 1179652
  25.0 17.8 %collective-permute-start.6 = (bf16[8,64,256]{2,1,0:T(8,128)(2,1)S(1)}, bf16[8,64,256]{2,1,0:T(8,128)(2,1)S(1)}, u32[]{:S(2)}, u32[]{:S(2)}) collective-permute-start(bf16[8,64,256]{2,1,0:T(8,128)(2,1)S(1)} %shard_map.96.refs_0_), channel_id=1, source_target_pairs={{0,2},{1,3},{2,0},{3,1},{4,6},{5,7},{6,4},{7,5},{8,10},{9,11},{10,... | collective-permute-start | bytes 786440 | tf_op jit(solution)/shard_map/ppermute | solution.py:114
  26.1 10.4 %collective-permute-start = (bf16[384,128]{1,0:T(8,128)(2,1)S(1)}, bf16[384,128]{1,0:T(8,128)(2,1)S(1)}, u32[]{:S(2)}, u32[]{:S(2)}) collective-permute-start(bf16[384,128]{1,0:T(8,128)(2,1)S(1)} %get-tuple-element.27), channel_id=1, source_target_pairs={{0,1},{1,0},{2,3},{3,2},{4,5},{5,4},{6,7},{7,6},{8,9},{9,8},{10,11... | collective-permute-start | bytes 294920 | tf_op jit(solution)/shard_map/ppermute | solution.py:114
  26.1 10.4 %collective-permute-start.2 = (bf16[384,128]{1,0:T(8,128)(2,1)S(1)}, bf16[384,128]{1,0:T(8,128)(2,1)S(1)}, u32[]{:S(2)}, u32[]{:S(2)}) collective-permute-start(bf16[384,128]{1,0:T(8,128)(2,1)S(1)} %get-tuple-element.29), channel_id=1, source_target_pairs={{0,3},{1,2},{2,1},{3,0},{4,7},{5,6},{6,5},{7,4},{8,11},{9,10},{10,... | collective-permute-start | bytes 294920 | tf_op jit(solution)/shard_map/ppermute | solution.py:114
  27.2 9.3 %collective-permute-start.1 = (bf16[128,128]{1,0:T(8,128)(2,1)S(1)}, bf16[128,128]{1,0:T(8,128)(2,1)S(1)}, u32[]{:S(2)}, u32[]{:S(2)}) collective-permute-start(bf16[128,128]{1,0:T(8,128)(2,1)S(1)} %get-tuple-element.28), channel_id=1, source_target_pairs={{0,2},{1,3},{2,0},{3,1},{4,6},{5,7},{6,4},{7,5},{8,10},{9,11},{10,... | collective-permute-start | bytes 98312 | tf_op jit(solution)/shard_map/ppermute | solution.py:114
  37.2 0.6 copy-start.5
  37.8 6.5 %collective-permute-start.3 = (bf16[2,96,256]{2,1,0:T(8,128)(2,1)S(1)}, bf16[2,96,256]{2,1,0:T(8,128)(2,1)S(1)}, u32[]{:S(2)}, u32[]{:S(2)}) collective-permute-start(bf16[2,96,256]{2,1,0:T(8,128)(2,1)S(1)} %get-tuple-element.31), channel_id=1, source_target_pairs={{4,0},{8,4},{12,8},{16,12},{20,16},{24,20},{28,24},{5,1},{9,5},{13... | collective-permute-start | bytes 294920 | tf_op jit(solution)/shard_map/ppermute | solution.py:20
  39.1 11.2 %collective-permute-start.10 = (bf16[2,128,256]{2,1,0:T(8,128)(2,1)S(1)}, bf16[2,128,256]{2,1,0:T(8,128)(2,1)S(1)}, u32[]{:S(2)}, u32[]{:S(2)}) collective-permute-start(bf16[2,128,256]{2,1,0:T(8,128)(2,1)S(1)} %get-tuple-element.37.refs_0_), channel_id=1, source_target_pairs={{0,16},{4,20},{8,24},{12,28},{16,0},{20,4},{24,8},{28,12},{1,17},{... | collective-permute-start | bytes 393224 | tf_op jit(solution)/shard_map/ppermute | solution.py:114
  41.5 8.8 %collective-permute-start.9 = (bf16[2,128,256]{2,1,0:T(8,128)(2,1)S(1)}, bf16[2,128,256]{2,1,0:T(8,128)(2,1)S(1)}, u32[]{:S(2)}, u32[]{:S(2)}) collective-permute-start(bf16[2,128,256]{2,1,0:T(8,128)(2,1)S(1)} %get-tuple-element.37.refs_0_), channel_id=1, source_target_pairs={{0,8},{4,12},{8,0},{12,4},{16,24},{20,28},{24,16},{28,20},{1,9},{5... | collective-permute-start | bytes 393224 | tf_op jit(solution)/shard_map/ppermute | solution.py:114
  42.8 23.5 %collective-permute-start.5 = (bf16[8,64,256]{2,1,0:T(8,128)(2,1)S(1)}, bf16[8,64,256]{2,1,0:T(8,128)(2,1)S(1)}, u32[]{:S(2)}, u32[]{:S(2)}) collective-permute-start(bf16[8,64,256]{2,1,0:T(8,128)(2,1)S(1)} %shard_map.96.refs_0_), channel_id=1, source_target_pairs={{0,1},{1,0},{2,3},{3,2},{4,5},{5,4},{6,7},{7,6},{8,9},{9,8},{10,11... | collective-permute-start | bytes 786440 | tf_op jit(solution)/shard_map/ppermute | solution.py:114
  42.8 25.2 %collective-permute-start.7 = (bf16[8,64,256]{2,1,0:T(8,128)(2,1)S(1)}, bf16[8,64,256]{2,1,0:T(8,128)(2,1)S(1)}, u32[]{:S(2)}, u32[]{:S(2)}) collective-permute-start(bf16[8,64,256]{2,1,0:T(8,128)(2,1)S(1)} %collective-permute-done.6.refs_2_), channel_id=1, source_target_pairs={{0,1},{1,0},{2,3},{3,2},{4,5},{5,4},{6,7},{7,6},{8,9},{9,8},{10,11... | collective-permute-start | bytes 786440 | tf_op jit(solution)/shard_map/ppermute | solution.py:114
  44.3 0.6 copy-start.11
  45.0 23.1 %copy-start.8 = (s32[2]{0:T(128)S(1)}, s32[2]{0:T(128)}, u32[]{:S(2)}) copy-start(s32[2]{0:T(128)} %copy-done.7) | copy-start | bytes 28
  50.3 0.8 %copy-start.3 = (bf16[128,256]{1,0:T(8,128)(2,1)S(1)}, bf16[128,256]{1,0:T(8,128)(2,1)}, u32[]{:S(2)}) copy-start(bf16[128,256]{1,0:T(8,128)(2,1)} %get-tuple-element.34.refs_0_) | copy-start | bytes 196612
  51.2 14.8 %collective-permute-start.13 = (bf16[2,128,256]{2,1,0:T(8,128)(2,1)S(1)}, bf16[2,128,256]{2,1,0:T(8,128)(2,1)S(1)}, u32[]{:S(2)}, u32[]{:S(2)}) collective-permute-start(bf16[2,128,256]{2,1,0:T(8,128)(2,1)S(1)} %get-tuple-element.39.refs_4_), channel_id=1, source_target_pairs={{0,8},{4,12},{8,0},{12,4},{16,24},{20,28},{24,16},{28,20},{1,9},{5... | collective-permute-start | bytes 393224 | tf_op jit(solution)/shard_map/ppermute | solution.py:114
  53.0 12.3 %all-to-all-start.1 = ((bf16[8,16,256]{2,1,0:T(8,128)(2,1)}), bf16[8,16,256]{2,1,0:T(8,128)(2,1)S(1)}, u32[]{:S(2)}, u32[]{:S(2)}) async-start(bf16[8,16,256]{2,1,0:T(8,128)(2,1)} %bitcast.15), calls=%async_computation.1 | async-start | bytes 131072 | tf_op jit(solution)/shard_map/all_to_all | solution.py:516
  58.3 11.5 %collective-permute-start.8 = (bf16[2,128,256]{2,1,0:T(8,128)(2,1)S(1)}, bf16[2,128,256]{2,1,0:T(8,128)(2,1)S(1)}, u32[]{:S(2)}, u32[]{:S(2)}) collective-permute-start(bf16[2,128,256]{2,1,0:T(8,128)(2,1)S(1)} %get-tuple-element.37.refs_0_), channel_id=1, source_target_pairs={{0,4},{4,0},{8,12},{12,8},{16,20},{20,16},{24,28},{28,24},{1,5},{5... | collective-permute-start | bytes 393224 | tf_op jit(solution)/shard_map/ppermute | solution.py:114
  60.3 10.6 %collective-permute-start.12 = (bf16[2,128,256]{2,1,0:T(8,128)(2,1)S(1)}, bf16[2,128,256]{2,1,0:T(8,128)(2,1)S(1)}, u32[]{:S(2)}, u32[]{:S(2)}) collective-permute-start(bf16[2,128,256]{2,1,0:T(8,128)(2,1)S(1)} %get-tuple-element.39.refs_4_), channel_id=1, source_target_pairs={{0,4},{4,0},{8,12},{12,8},{16,20},{20,16},{24,28},{28,24},{1,5},{5... | collective-permute-start | bytes 393224 | tf_op jit(solution)/shard_map/ppermute | solution.py:114
  66.0 5.0 %collective-permute-start.11 = (bf16[2,128,256]{2,1,0:T(8,128)(2,1)S(1)}, bf16[2,128,256]{2,1,0:T(8,128)(2,1)S(1)}, u32[]{:S(2)}, u32[]{:S(2)}) collective-permute-start(bf16[2,128,256]{2,1,0:T(8,128)(2,1)S(1)} %get-tuple-element.38.refs_2_), channel_id=1, source_target_pairs={{0,4},{4,0},{8,12},{12,8},{16,20},{20,16},{24,28},{28,24},{1,5},{5... | collective-permute-start | bytes 393224 | tf_op jit(solution)/shard_map/ppermute | solution.py:114
  66.3 6.1 %collective-permute-start.14 = (bf16[2,128,256]{2,1,0:T(8,128)(2,1)S(1)}, bf16[2,128,256]{2,1,0:T(8,128)(2,1)S(1)}, u32[]{:S(2)}, u32[]{:S(2)}) collective-permute-start(bf16[2,128,256]{2,1,0:T(8,128)(2,1)S(1)} %collective-permute-done.13.refs_6_), channel_id=1, source_target_pairs={{0,4},{4,0},{8,12},{12,8},{16,20},{20,16},{24,28},{28,24},{1,5},{5... | collective-permute-start | bytes 393224 | tf_op jit(solution)/shard_map/ppermute | solution.py:114
  72.4 0.7 copy-start.9
  73.1 5.3 %collective-permute-start.15 = (f32[1,64]{1,0:T(1,128)S(1)}, f32[1,64]{1,0:T(1,128)S(1)}, u32[]{:S(2)}, u32[]{:S(2)}) collective-permute-start(f32[1,64]{1,0:T(1,128)S(1)} %get-tuple-element.42), channel_id=1, source_target_pairs={{0,1},{1,0},{2,3},{3,2},{4,5},{5,4},{6,7},{7,6},{8,9},{9,8},{10,11... | collective-permute-start | bytes 776 | tf_op jit(solution)/shard_map/ppermute | solution.py:114
  73.1 5.3 %collective-permute-start.16 = (f32[1,64]{1,0:T(1,128)S(1)}, f32[1,64]{1,0:T(1,128)S(1)}, u32[]{:S(2)}, u32[]{:S(2)}) collective-permute-start(f32[1,64]{1,0:T(1,128)S(1)} %get-tuple-element.43), channel_id=1, source_target_pairs={{0,2},{1,3},{2,0},{3,1},{4,6},{5,7},{6,4},{7,5},{8,10},{9,11},{10,... | collective-permute-start | bytes 776 | tf_op jit(solution)/shard_map/ppermute | solution.py:114
  73.4 5.0 %collective-permute-start.17 = (f32[1,64]{1,0:T(1,128)S(1)}, f32[1,64]{1,0:T(1,128)S(1)}, u32[]{:S(2)}, u32[]{:S(2)}) collective-permute-start(f32[1,64]{1,0:T(1,128)S(1)} %get-tuple-element.44), channel_id=1, source_target_pairs={{0,3},{1,2},{2,1},{3,0},{4,7},{5,6},{6,5},{7,4},{8,11},{9,10},{10,... | collective-permute-start | bytes 776 | tf_op jit(solution)/shard_map/ppermute | solution.py:114
  78.4 1.5 %copy-start.1 = (f32[27,64,256]{2,1,0:T(8,128)S(1)}, f32[27,64,256]{2,1,0:T(8,128)}, u32[]{:S(2)}) copy-start(f32[27,64,256]{2,1,0:T(8,128)} %shard_map.100.refs_0_) | copy-start | bytes 5308420

commit v8 on v6

--- a/solution.py
+++ b/solution.py
@@ -198,6 +198,13 @@
         head[s] = grad_rows[s, :rows, :]
 
 
+def total_kernel(*refs):
+    total = refs[0][...]
+    for ref in refs[1:-1]:
+        total = total + ref[...]
+    refs[-1][...] = total
+
+
 def join_kernel(F, J, T, place, planes, *refs):
     messages, (joined, cached, under, blocks) = refs[:T], refs[T:]
     span = F * J
@@ -378,9 +385,10 @@
     bias_sum[...] = slice_of(total, block, 0, T)
 
 
-def weight_kernel(F, J, R, T, part, place, _, grads, *refs):
+def weight_kernel(F, J, R, T, part, place, gain, grads, *refs):
     hidden = refs[:R]
-    out_hbm, out, even, odd, sem = refs[R:]
+    out_hbm, gain_out, out, even, odd, sem = refs[R:]
+    gain_out[...] = gain[...]
     channels = grads.shape[-1]
     depth = T * F * J
     lanes = 2 * part
@@ -500,35 +508,38 @@
     hidden_all = exchanged(joined, "rows", after_slab)
     grad_all = exchanged(grad_rows, "tm")
 
+    (packed,) = call(gate_kernel, [(packed.shape, bf16)], [], 0, 0, "aaa", {1: 0})(
+        hidden_all[R - 2], packed
+    )
     packed = lax.all_to_all(packed.reshape(R, slot, C), "rows", 0, 0, tiled=True)
     latent = packed[:, :used].reshape(R, F, J // R, C).transpose(1, 0, 2, 3)
-    gains = call(
-        functools.partial(gain_kernel, T, used),
-        [((1, part), f32)] * T,
-        [], R * slot * C, R * slot * C, "v" + "a" * (R // 2) + "v" * T,
-    )(packed, *hidden_all[1::2])
-    gain_grad = gains[0]
-    for k in range(1, T):
-        gain_grad = gain_grad + partners(gains[k], "tm", k)
-
     grads, bias_sum = call(
         functools.partial(order_kernel, F, J, R, T),
         [((2, R, (F * T + 2) * J, C), bf16), ((1, part), f32)],
         [],
         90 * WORK * span * C, 2 * R * T * span * C, "s" + "v" * (T + 2),
     )(place, *grad_all)
-    (weight_grad,) = call(
+    gains = call(
+        functools.partial(gain_kernel, T, used),
+        [((1, part), f32)] * T,
+        [], R * slot * C, R * slot * C, "v" + "a" * (R // 2 + 1) + "v" * T,
+    )(packed, bias_sum, *hidden_all[1::2])
+    weight_grad, own_gain = call(
         functools.partial(weight_kernel, F, J, R, T, part),
-        [((27, part, C), f32)],
+        [((27, part, C), f32), ((1, part), f32)],
         [
             pltpu.VMEM((27, part, C), f32),
             pltpu.VMEM((2 * part, (R + 1) * T * span), bf16),
             pltpu.VMEM((2 * part, R * T * span), bf16),
             pltpu.SemaphoreType.DMA((3,)),
         ],
-        200 * WORK * span * C, 8 * 27 * part * C, "sav" + "v" * R + "h",
+        200 * WORK * span * C, 8 * 27 * part * C, "svv" + "v" * R + "hv",
     )(place, gains[0], grads, *hidden_all)
 
+    terms = [own_gain] + [partners(gains[k], "tm", k) for k in range(1, T)]
+    (gain_grad,) = call(
+        total_kernel, [((1, part), f32)], [], T * part, 4 * T * part, "v" * (T + 1)
+    )(*terms)
     return (
         latent,
         frames_grad.reshape(frames.shape),

time: 65.2 us -> 75.9 us (1.16)
  waiting for transfers between devices: 12.5 us -> 21.3 us
  local copies, waits for them, and re-layouts: 5.87 us -> 7.96 us
    ppermute x16, waiting for transfers between devices: 2.6 us -> 11 us  [partners(): lax.ppermute(value, axis, [(source, source ^ bits) for source in range(co...]
    all_to_all x1, waiting for transfers between devices: 6.25 us -> 2.97 us  [gathered_form(): lax.all_to_all(packed.reshape(R, slot, C), 'rows', 0, 0, tiled=True)]
    ppermute x16, starting transfers between devices: 18.8 us -> 15.8 us  [partners(): lax.ppermute(value, axis, [(source, source ^ bits) for source in range(co...]
    all_to_all x1, starting transfers between devices: 3.35 us -> 6.18 us  [gathered_form(): lax.all_to_all(packed.reshape(R, slot, C), 'rows', 0, 0, tiled=True)]
    all_to_all x1, waiting for transfers between devices: 3.65 us -> 5.79 us  [gathered_form(): lax.all_to_all(jnp.broadcast_to(own, (R,) + own.shape[1:]), 'rows', 0, 0,...]
    unnamed x22 -> x28, local copies, waits for them, and re-layouts: 3.7 us -> 5.8 us
    ppermute x2, waiting for transfers between devices: 0.01 us -> 1.58 us  [shifted(): lax.ppermute(value, axis, [(source, source + steps) for source in range(l...]
  transfers between devices with their start and end apart: 20 -> 20, of which waited for: 5 -> 7; matrix products, arithmetic and copies ran while one was open for 3% -> 2% of each run, Pallas kernels for 11% -> 16%
where the time goes in v8:
time: 75.9 us; the launch traced here: 75.3 us
  starting transfers between devices  31.8 us (42%)
  waiting for transfers between devices  21.3 us (28%)
  Pallas kernels  12.6 us (17%)
  local copies, waits for them, and re-layouts  7.96 us (10%)
  between operations  0.81 us (1%)
  other arithmetic  0.78 us (1%)
    ppermute x16, starting transfers between devices, partners(): lax.ppermute(value, axis, [(source, source ^ bits) for source in range(co...  15.8 us
    ppermute x16, waiting for transfers between devices, partners(): lax.ppermute(value, axis, [(source, source ^ bits) for source in range(co...  11 us
    all_to_all x1, starting transfers between devices, gathered_form(): lax.all_to_all(jnp.broadcast_to(own, (R,) + own.shape[1:]), 'rows', 0, 0,...  7.25 us
    all_to_all x1, starting transfers between devices, gathered_form(): lax.all_to_all(packed.reshape(R, slot, C), 'rows', 0, 0, tiled=True)  6.18 us
    unnamed x28, local copies, waits for them, and re-layouts  5.8 us
    all_to_all x1, waiting for transfers between devices, gathered_form(): lax.all_to_all(jnp.broadcast_to(own, (R,) + own.shape[1:]), 'rows', 0, 0,...  5.79 us
    pallas_call x1, Pallas kernels, gathered_form(): call(functools.partial(slab_kernel, F, J, R, T, slot), [((R * slot, C), b...  5.33 us
    pallas_call x1, Pallas kernels, gathered_form(): call(functools.partial(weight_kernel, F, J, R, T, part), [((27, part, C),...  3.43 us
  transfers between devices with their start and end apart: 20, of which 7 were waited for; matrix products, arithmetic and copies ran while one was open for 2% of the time, Pallas kernels for 16%

profile of v8, /device:TPU:0, one launch (start us, length us, event | category | flops | bytes accessed | tf_op | source)
XLA Modules:
  0.0 75.3 jit_solution(12262295420435370316)
XLA Ops:
  0.6 0.8 %broadcast_in_dim.7 = bf16[64,256]{1,0:T(8,128)(2,1)S(1)} reshape(bf16[4,8,2,256]{3,2,1,0:T(2,128)(2,1)} %param.9) | data formatting | bytes 65536 | tf_op jit(solution)/shard_map/broadcast_in_dim | solution.py:457
  1.4 0.7 broadcast_in_dim.8
  2.1 7.3 %all-to-all-start = ((bf16[8,64,256]{2,1,0:T(8,128)(2,1)}), bf16[8,64,256]{2,1,0:T(8,128)(2,1)S(1)}, u32[]{:S(2)}, u32[]{:S(2)}) async-start(bf16[8,64,256]{2,1,0:T(8,128)(2,1)} %broadcast_in_dim.8), calls=%async_computation | async-start | bytes 524288 | tf_op jit(solution)/shard_map/all_to_all | solution.py:456
  9.4 0.1 pad_add_fusion.place
  9.5 0.7 pad_maximum_fusion.vectors
  10.2 0.9 %copy-done.11 = bf16[4,2,32,256]{3,2,1,0:T(8,128)(2,1)S(1)} copy-done((bf16[4,2,32,256]{3,2,1,0:T(8,128)(2,1)S(1)}, bf16[4,2,32,256]{3,2,1,0:T(8,128)(2,1)}, u32[]{:S(2)}) %copy-start.11) | copy-done | bytes 131096
  11.1 0.8 %shard_map.92 = (bf16[2,2,64,256]{3,2,1,0:T(8,128)(2,1)S(1)}, bf16[256,256]{1,0:T(8,128)(2,1)S(1)}, f32[2,256]{1,0:T(2,128)S(1)}, bf16[128,128]{1,0:T(8,128)(2,1...) custom-call(s32[2]{0:T(128)S(1)} %pad_add_fusion.place, ...), custom_call_target="tpu_custom_call" | custom-call | flops 1179648000 | bytes 262144 | tf_op jit(solution)/shard_map/pallas_call | solution.py:461
  11.9 0.0 copy-start.7
  11.9 0.6 copy-done.7
  12.5 5.8 %all-to-all-done.grad_rows = bf16[8,64,256]{2,1,0:T(8,128)(2,1)S(1)} async-done(((bf16[8,64,256]{2,1,0:T(8,128)(2,1)}), bf16[8,64,256]{2,1,0:T(8,128)(2,1)S(1)}, u32[]{:S(2)}, u32[]{:S(2)}) %all-to-all-start) | async-done | bytes 262176 | tf_op jit(solution)/shard_map/all_to_all | solution.py:456
  18.3 0.0 copy-start.3
  18.3 1.6 %collective-permute-start.9 = (bf16[8,64,256]{2,1,0:T(8,128)(2,1)S(1)}, bf16[8,64,256]{2,1,0:T(8,128)(2,1)S(1)}, u32[]{:S(2)}, u32[]{:S(2)}) collective-permute-start(bf16[8,64,256]{2,1,0:T(8,128)(2,1)S(1)} %get-tuple-element.38.gathered.refs_0_), channel_id=1, source_target_pairs={{0,2},{1,3},{2,0},{3,1},{4,6},{5,7},{6,4},{7,5},{8,10},{9,11},{10,... | collective-permute-start | bytes 786440 | tf_op jit(solution)/shard_map/ppermute | solution.py:114
  19.9 0.0 collective-permute-start
  19.9 0.6 collective-permute-start.2
  20.6 1.5 %collective-permute-start.1 = (bf16[128,128]{1,0:T(8,128)(2,1)S(1)}, bf16[128,128]{1,0:T(8,128)(2,1)S(1)}, u32[]{:S(2)}, u32[]{:S(2)}) collective-permute-start(bf16[128,128]{1,0:T(8,128)(2,1)S(1)} %get-tuple-element.32), channel_id=1, source_target_pairs={{0,2},{1,3},{2,0},{3,1},{4,6},{5,7},{6,4},{7,5},{8,10},{9,11},{10,... | collective-permute-start | bytes 98312 | tf_op jit(solution)/shard_map/ppermute | solution.py:114
  22.1 1.3 %collective-permute-start.4 = (bf16[8,32,256]{2,1,0:T(8,128)(2,1)S(1)}, bf16[8,32,256]{2,1,0:T(8,128)(2,1)S(1)}, u32[]{:S(2)}, u32[]{:S(2)}) collective-permute-start(bf16[8,32,256]{2,1,0:T(8,128)(2,1)S(1)} %get-tuple-element.39), channel_id=1, source_target_pairs={{1,0},{2,1},{3,2},{5,4},{6,5},{7,6},{9,8},{10,9},{11,10},{13,12},{... | collective-permute-start | bytes 393224 | tf_op jit(solution)/shard_map/ppermute | solution.py:20
  23.4 4.2 %collective-permute-done.1.refs_2_ = bf16[128,128]{1,0:T(8,128)(2,1)S(1)} collective-permute-done((bf16[128,128]{1,0:T(8,128)(2,1)S(1)}, bf16[128,128]{1,0:T(8,128)(2,1)S(1)}, u32[]{:S(2)}, u32[]{:S(2)}) %collective-permute-start.1) | collective-permute-done | bytes 32800 | tf_op jit(solution)/shard_map/ppermute | solution.py:114
  27.6 0.0 collective-permute-done.refs_1_
  27.6 0.0 collective-permute-done.2.refs_3_
  27.6 0.0 copy-done.8
  27.6 0.6 shard_map.93
  28.3 0.6 copy-done.6
  28.9 1.3 %collective-permute-start.3 = (bf16[2,96,256]{2,1,0:T(8,128)(2,1)S(1)}, bf16[2,96,256]{2,1,0:T(8,128)(2,1)S(1)}, u32[]{:S(2)}, u32[]{:S(2)}) collective-permute-start(bf16[2,96,256]{2,1,0:T(8,128)(2,1)S(1)} %get-tuple-element.35), channel_id=1, source_target_pairs={{4,0},{8,4},{12,8},{16,12},{20,16},{24,20},{28,24},{5,1},{9,5},{13... | collective-permute-start | bytes 294920 | tf_op jit(solution)/shard_map/ppermute | solution.py:20
  30.2 3.2 %collective-permute-start.6 = (bf16[2,128,256]{2,1,0:T(8,128)(2,1)S(1)}, bf16[2,128,256]{2,1,0:T(8,128)(2,1)S(1)}, u32[]{:S(2)}, u32[]{:S(2)}) collective-permute-start(bf16[2,128,256]{2,1,0:T(8,128)(2,1)S(1)} %get-tuple-element.41.refs_0_), channel_id=1, source_target_pairs={{0,16},{4,20},{8,24},{12,28},{16,0},{20,4},{24,8},{28,12},{1,17},{... | collective-permute-start | bytes 393224 | tf_op jit(solution)/shard_map/ppermute | solution.py:114
  33.4 0.4 collective-permute-start.5
  33.8 1.6 %collective-permute-done.3.under = bf16[2,96,256]{2,1,0:T(8,128)(2,1)S(1)} collective-permute-done((bf16[2,96,256]{2,1,0:T(8,128)(2,1)S(1)}, bf16[2,96,256]{2,1,0:T(8,128)(2,1)S(1)}, u32[]{:S(2)}, u32[]{:S(2)}) %collective-permute-start.3) | collective-permute-done | bytes 98336 | tf_op jit(solution)/shard_map/ppermute | solution.py:20
  35.4 0.0 collective-permute-start.8
  35.4 0.0 collective-permute-done.9.refs_2_
  35.4 0.5 collective-permute-start.10
  35.9 0.0 collective-permute-done.4.following
  35.9 0.1 copy-done.13
  36.0 0.5 copy-done.12
  36.5 5.3 %shard_map.95 = (bf16[128,256]{1,0:T(8,128)(2,1)}, bf16[256,256]{1,0:T(8,128)(2,1)}) custom-call(s32[2]{0:T(128)} %copy-done.8, bf16[2,2,64,256]{3,2,1,0:T(8,128)(2,1)} %copy-done.5, bf16[2,2,32,256]{3,2,1,0:T(8,128)(2,1)} %copy-done.6, bf16[2,96,256]{2,1,0:T(8,128)(2,1)} %copy-done.13, bf16[27,256,256]{2,1,0:T(8,128)(2,1)} %bitcast.17, ...), custom_call_target="tpu_custom_call" | custom-call | flops 452984832 | bytes 3538944 | tf_op jit(solution)/shard_map/pallas_call | solution.py:486
  41.9 0.0 collective-permute-done.6.refs_2_
  41.9 0.0 collective-permute-done.5.refs_1_
  41.9 0.8 %copy-done = bf16[128,256]{1,0:T(8,128)(2,1)S(1)} copy-done((bf16[128,256]{1,0:T(8,128)(2,1)S(1)}, bf16[128,256]{1,0:T(8,128)(2,1)}, u32[]{:S(2)}) %copy-start) | copy-done | bytes 65560
  42.7 1.8 %collective-permute-start.7 = (bf16[2,128,256]{2,1,0:T(8,128)(2,1)S(1)}, bf16[2,128,256]{2,1,0:T(8,128)(2,1)S(1)}, u32[]{:S(2)}, u32[]{:S(2)}) collective-permute-start(bf16[2,128,256]{2,1,0:T(8,128)(2,1)S(1)} %get-tuple-element.42.refs_4_), channel_id=1, source_target_pairs={{0,8},{4,12},{8,0},{12,4},{16,24},{20,28},{24,16},{28,20},{1,9},{5... | collective-permute-start | bytes 393224 | tf_op jit(solution)/shard_map/ppermute | solution.py:114
  44.5 3.7 %collective-permute-done.7.refs_0_.refs_6_ = bf16[2,128,256]{2,1,0:T(8,128)(2,1)S(1)} collective-permute-done((bf16[2,128,256]{2,1,0:T(8,128)(2,1)S(1)}, bf16[2,128,256]{2,1,0:T(8,128)(2,1)S(1)}, u32[]{:S(2)}, u32[]{:S(2)}) %collective-permute-start.7) | collective-permute-done | bytes 131104 | tf_op jit(solution)/shard_map/ppermute | solution.py:114
  48.2 0.6 copy-done.1
  48.9 6.2 %all-to-all-start.1 = ((bf16[8,16,256]{2,1,0:T(8,128)(2,1)}), bf16[8,16,256]{2,1,0:T(8,128)(2,1)S(1)}, u32[]{:S(2)}, u32[]{:S(2)}) async-start(bf16[8,16,256]{2,1,0:T(8,128)(2,1)} %bitcast.14), calls=%async_computation.1 | async-start | bytes 131072 | tf_op jit(solution)/shard_map/all_to_all | solution.py:514
  55.0 2.0 %collective-permute-start.11 = (bf16[2,128,256]{2,1,0:T(8,128)(2,1)S(1)}, bf16[2,128,256]{2,1,0:T(8,128)(2,1)S(1)}, u32[]{:S(2)}, u32[]{:S(2)}) collective-permute-start(bf16[2,128,256]{2,1,0:T(8,128)(2,1)S(1)} %get-tuple-element.41.refs_0_), channel_id=1, source_target_pairs={{0,4},{4,0},{8,12},{12,8},{16,20},{20,16},{24,28},{28,24},{1,5},{5... | collective-permute-start | bytes 393224 | tf_op jit(solution)/shard_map/ppermute | solution.py:114
  57.1 0.0 collective-permute-start.13
  57.1 2.0 %collective-permute-start.12 = (bf16[2,128,256]{2,1,0:T(8,128)(2,1)S(1)}, bf16[2,128,256]{2,1,0:T(8,128)(2,1)S(1)}, u32[]{:S(2)}, u32[]{:S(2)}) collective-permute-start(bf16[2,128,256]{2,1,0:T(8,128)(2,1)S(1)} %get-tuple-element.45.refs_2_), channel_id=1, source_target_pairs={{0,4},{4,0},{8,12},{12,8},{16,20},{20,16},{24,28},{28,24},{1,5},{5... | collective-permute-start | bytes 393224 | tf_op jit(solution)/shard_map/ppermute | solution.py:114
  59.1 3.0 %all-to-all-done.1.received = bf16[8,16,256]{2,1,0:T(8,128)(2,1)S(1)} async-done(((bf16[8,16,256]{2,1,0:T(8,128)(2,1)}), bf16[8,16,256]{2,1,0:T(8,128)(2,1)S(1)}, u32[]{:S(2)}, u32[]{:S(2)}) %all-to-all-start.1) | async-done | bytes 65568 | tf_op jit(solution)/shard_map/all_to_all | solution.py:514
  62.1 0.6 copy.15
  62.7 0.0 collective-permute-done.8.refs_1_
  62.7 0.3 collective-permute-start.14
  63.0 0.0 collective-permute-done.10.refs_3_
  63.0 0.9 %copy-done.4 = bf16[8,64,256]{2,1,0:T(8,128)(2,1)S(1)} copy-done((bf16[8,64,256]{2,1,0:T(8,128)(2,1)S(1)}, bf16[8,64,256]{2,1,0:T(8,128)(2,1)}, u32[]{:S(2)}) %copy-start.4) | copy-done | bytes 262168
  64.0 1.8 %shard_map.98 = (bf16[2,8,288,256]{3,2,1,0:T(8,128)(2,1)S(1)}, f32[1,64]{1,0:T(1,128)}) custom-call(s32[2]{0:T(128)S(1)} %copy-done.9, bf16[8,64,256]{2,1,0:T(8,128)(2,1)S(1)} %copy-done.4, bf16[8,64,256]{2,1,0:T(8,128)(2,1)S(1)} %collective-permute-done.8.refs_1_, bf16[8,64,256]{2,1,0:T(8,128)(2,1)S(1)} %collective-permute-done.9.refs_2_, ...), custom_call_target="tpu_custom_call" | custom-call | flops 1769472000 | bytes 1048576 | tf_op jit(solution)/shard_map/pallas_call | solution.py:516
  65.7 0.0 collective-permute-done.11.refs_1_
  65.7 1.6 %collective-permute-done.12.refs_2_.refs_3_ = bf16[2,128,256]{2,1,0:T(8,128)(2,1)S(1)} collective-permute-done((bf16[2,128,256]{2,1,0:T(8,128)(2,1)S(1)}, bf16[2,128,256]{2,1,0:T(8,128)(2,1)S(1)}, u32[]{:S(2)}, u32[]{:S(2)}) %collective-permute-start.12) | collective-permute-done | bytes 131104 | tf_op jit(solution)/shard_map/ppermute | solution.py:114
  67.3 0.0 collective-permute-done.13.refs_3_.refs_5_
  67.3 1.4 %collective-permute-done.14.refs_4_.refs_7_ = bf16[2,128,256]{2,1,0:T(8,128)(2,1)S(1)} collective-permute-done((bf16[2,128,256]{2,1,0:T(8,128)(2,1)S(1)}, bf16[2,128,256]{2,1,0:T(8,128)(2,1)S(1)}, u32[]{:S(2)}, u32[]{:S(2)}) %collective-permute-start.14) | collective-permute-done | bytes 131104 | tf_op jit(solution)/shard_map/ppermute | solution.py:114
  68.7 0.7 copy-done.10
  69.4 0.1 shard_map.99
  69.5 0.0 collective-permute-start.15
  69.5 1.7 %collective-permute-start.16 = (f32[1,64]{1,0:T(1,128)S(1)}, f32[1,64]{1,0:T(1,128)S(1)}, u32[]{:S(2)}, u32[]{:S(2)}) collective-permute-start(f32[1,64]{1,0:T(1,128)S(1)} %get-tuple-element.51), channel_id=1, source_target_pairs={{0,2},{1,3},{2,0},{3,1},{4,6},{5,7},{6,4},{7,5},{8,10},{9,11},{10,... | collective-permute-start | bytes 776 | tf_op jit(solution)/shard_map/ppermute | solution.py:114
  71.1 0.2 collective-permute-start.17
  71.3 3.4 %shard_map.100 = (f32[27,64,256]{2,1,0:T(8,128)}, f32[1,64]{1,0:T(1,128)S(1)}) custom-call(s32[2]{0:T(128)S(1)} %copy-done.9, f32[1,64]{1,0:T(1,128)S(1)} %get-tuple-element.46.gain, bf16[2,8,288,256]{3,2,1,0:T(8,128)(2,1)S(1)} %get-tuple-element.47.grads, bf16[2,128,256]{2,1,0:T(8,128)(2,1)S(1)} %get-tuple-element.41.refs_0_, ...), custom_call_target="tpu_custom_call" | custom-call | flops 3932160000 | bytes 3538944 | tf_op jit(solution)/shard_map/pallas_call | solution.py:527
  74.8 0.0 collective-permute-done.15.refs_1_
  74.8 0.0 collective-permute-done.16.refs_2_
  74.8 0.0 collective-permute-done.17.refs_3_
  74.8 0.5 shard_map.101
  (21 shorter events, 0.1 us)
Async XLA Ops:
  2.1 16.2 %all-to-all-start = ((bf16[8,64,256]{2,1,0:T(8,128)(2,1)}), bf16[8,64,256]{2,1,0:T(8,128)(2,1)S(1)}, u32[]{:S(2)}, u32[]{:S(2)}) async-start(bf16[8,64,256]{2,1,0:T(8,128)(2,1)} %broadcast_in_dim.8), calls=%async_computation | async-start | bytes 524288 | tf_op jit(solution)/shard_map/all_to_all | solution.py:456
  9.5 18.1 %copy-start.8 = (s32[2]{0:T(128)}, s32[2]{0:T(128)S(1)}, u32[]{:S(2)}) copy-start(s32[2]{0:T(128)S(1)} %pad_add_fusion.place) | copy-start | bytes 28
  10.2 0.9 %copy-start.11 = (bf16[4,2,32,256]{3,2,1,0:T(8,128)(2,1)S(1)}, bf16[4,2,32,256]{3,2,1,0:T(8,128)(2,1)}, u32[]{:S(2)}) copy-start(bf16[4,2,32,256]{3,2,1,0:T(8,128)(2,1)} %param.5) | copy-start | bytes 393220
  11.9 0.6 copy-start.7
  12.5 23.4 %copy-start.2 = (bf16[256,256]{1,0:T(8,128)(2,1)}, bf16[256,256]{1,0:T(8,128)(2,1)S(1)}, u32[]{:S(2)}) copy-start(bf16[256,256]{1,0:T(8,128)(2,1)S(1)} %get-tuple-element.36._.frames) | copy-start | bytes 393220
  12.5 23.4 %copy-start.5 = (bf16[2,2,64,256]{3,2,1,0:T(8,128)(2,1)}, bf16[2,2,64,256]{3,2,1,0:T(8,128)(2,1)S(1)}, u32[]{:S(2)}) copy-start(bf16[2,2,64,256]{3,2,1,0:T(8,128)(2,1)S(1)} %get-tuple-element.29.planes) | copy-start | bytes 393220
  18.3 17.6 %copy-start.3 = (bf16[8,64,256]{2,1,0:T(8,128)(2,1)}, bf16[8,64,256]{2,1,0:T(8,128)(2,1)S(1)}, u32[]{:S(2)}) copy-start(bf16[8,64,256]{2,1,0:T(8,128)(2,1)S(1)} %get-tuple-element.38.gathered.refs_0_) | copy-start | bytes 786436
  18.3 17.0 %collective-permute-start.9 = (bf16[8,64,256]{2,1,0:T(8,128)(2,1)S(1)}, bf16[8,64,256]{2,1,0:T(8,128)(2,1)S(1)}, u32[]{:S(2)}, u32[]{:S(2)}) collective-permute-start(bf16[8,64,256]{2,1,0:T(8,128)(2,1)S(1)} %get-tuple-element.38.gathered.refs_0_), channel_id=1, source_target_pairs={{0,2},{1,3},{2,0},{3,1},{4,6},{5,7},{6,4},{7,5},{8,10},{9,11},{10,... | collective-permute-start | bytes 786440 | tf_op jit(solution)/shard_map/ppermute | solution.py:114
  19.9 7.7 %collective-permute-start = (bf16[384,128]{1,0:T(8,128)(2,1)S(1)}, bf16[384,128]{1,0:T(8,128)(2,1)S(1)}, u32[]{:S(2)}, u32[]{:S(2)}) collective-permute-start(bf16[384,128]{1,0:T(8,128)(2,1)S(1)} %get-tuple-element.31), channel_id=1, source_target_pairs={{0,1},{1,0},{2,3},{3,2},{4,5},{5,4},{6,7},{7,6},{8,9},{9,8},{10,11... | collective-permute-start | bytes 294920 | tf_op jit(solution)/shard_map/ppermute | solution.py:114
  19.9 7.7 %collective-permute-start.2 = (bf16[384,128]{1,0:T(8,128)(2,1)S(1)}, bf16[384,128]{1,0:T(8,128)(2,1)S(1)}, u32[]{:S(2)}, u32[]{:S(2)}) collective-permute-start(bf16[384,128]{1,0:T(8,128)(2,1)S(1)} %get-tuple-element.33), channel_id=1, source_target_pairs={{0,3},{1,2},{2,1},{3,0},{4,7},{5,6},{6,5},{7,4},{8,11},{9,10},{10,... | collective-permute-start | bytes 294920 | tf_op jit(solution)/shard_map/ppermute | solution.py:114
  20.6 7.0 %collective-permute-start.1 = (bf16[128,128]{1,0:T(8,128)(2,1)S(1)}, bf16[128,128]{1,0:T(8,128)(2,1)S(1)}, u32[]{:S(2)}, u32[]{:S(2)}) collective-permute-start(bf16[128,128]{1,0:T(8,128)(2,1)S(1)} %get-tuple-element.32), channel_id=1, source_target_pairs={{0,2},{1,3},{2,0},{3,1},{4,6},{5,7},{6,4},{7,5},{8,10},{9,11},{10,... | collective-permute-start | bytes 98312 | tf_op jit(solution)/shard_map/ppermute | solution.py:114
  22.1 13.8 %collective-permute-start.4 = (bf16[8,32,256]{2,1,0:T(8,128)(2,1)S(1)}, bf16[8,32,256]{2,1,0:T(8,128)(2,1)S(1)}, u32[]{:S(2)}, u32[]{:S(2)}) collective-permute-start(bf16[8,32,256]{2,1,0:T(8,128)(2,1)S(1)} %get-tuple-element.39), channel_id=1, source_target_pairs={{1,0},{2,1},{3,2},{5,4},{6,5},{7,6},{9,8},{10,9},{11,10},{13,12},{... | collective-permute-start | bytes 393224 | tf_op jit(solution)/shard_map/ppermute | solution.py:20
  28.3 0.6 copy-start.6
  28.9 6.5 %collective-permute-start.3 = (bf16[2,96,256]{2,1,0:T(8,128)(2,1)S(1)}, bf16[2,96,256]{2,1,0:T(8,128)(2,1)S(1)}, u32[]{:S(2)}, u32[]{:S(2)}) collective-permute-start(bf16[2,96,256]{2,1,0:T(8,128)(2,1)S(1)} %get-tuple-element.35), channel_id=1, source_target_pairs={{4,0},{8,4},{12,8},{16,12},{20,16},{24,20},{28,24},{5,1},{9,5},{13... | collective-permute-start | bytes 294920 | tf_op jit(solution)/shard_map/ppermute | solution.py:20
  30.2 11.7 %collective-permute-start.6 = (bf16[2,128,256]{2,1,0:T(8,128)(2,1)S(1)}, bf16[2,128,256]{2,1,0:T(8,128)(2,1)S(1)}, u32[]{:S(2)}, u32[]{:S(2)}) collective-permute-start(bf16[2,128,256]{2,1,0:T(8,128)(2,1)S(1)} %get-tuple-element.41.refs_0_), channel_id=1, source_target_pairs={{0,16},{4,20},{8,24},{12,28},{16,0},{20,4},{24,8},{28,12},{1,17},{... | collective-permute-start | bytes 393224 | tf_op jit(solution)/shard_map/ppermute | solution.py:114
  33.4 8.5 %collective-permute-start.5 = (bf16[2,128,256]{2,1,0:T(8,128)(2,1)S(1)}, bf16[2,128,256]{2,1,0:T(8,128)(2,1)S(1)}, u32[]{:S(2)}, u32[]{:S(2)}) collective-permute-start(bf16[2,128,256]{2,1,0:T(8,128)(2,1)S(1)} %get-tuple-element.41.refs_0_), channel_id=1, source_target_pairs={{0,8},{4,12},{8,0},{12,4},{16,24},{20,28},{24,16},{28,20},{1,9},{5... | collective-permute-start | bytes 393224 | tf_op jit(solution)/shard_map/ppermute | solution.py:114
  35.4 0.6 copy-start.13
  35.4 27.4 %collective-permute-start.8 = (bf16[8,64,256]{2,1,0:T(8,128)(2,1)S(1)}, bf16[8,64,256]{2,1,0:T(8,128)(2,1)S(1)}, u32[]{:S(2)}, u32[]{:S(2)}) collective-permute-start(bf16[8,64,256]{2,1,0:T(8,128)(2,1)S(1)} %get-tuple-element.38.gathered.refs_0_), channel_id=1, source_target_pairs={{0,1},{1,0},{2,3},{3,2},{4,5},{5,4},{6,7},{7,6},{8,9},{9,8},{10,11... | collective-permute-start | bytes 786440 | tf_op jit(solution)/shard_map/ppermute | solution.py:114
  35.4 27.6 %collective-permute-start.10 = (bf16[8,64,256]{2,1,0:T(8,128)(2,1)S(1)}, bf16[8,64,256]{2,1,0:T(8,128)(2,1)S(1)}, u32[]{:S(2)}, u32[]{:S(2)}) collective-permute-start(bf16[8,64,256]{2,1,0:T(8,128)(2,1)S(1)} %collective-permute-done.9.refs_2_), channel_id=1, source_target_pairs={{0,1},{1,0},{2,3},{3,2},{4,5},{5,4},{6,7},{7,6},{8,9},{9,8},{10,11... | collective-permute-start | bytes 786440 | tf_op jit(solution)/shard_map/ppermute | solution.py:114
  35.9 0.7 copy-start.12
  36.5 26.5 %copy-start.9 = (s32[2]{0:T(128)S(1)}, s32[2]{0:T(128)}, u32[]{:S(2)}) copy-start(s32[2]{0:T(128)} %copy-done.8) | copy-start | bytes 28
  41.9 0.8 %copy-start = (bf16[128,256]{1,0:T(8,128)(2,1)S(1)}, bf16[128,256]{1,0:T(8,128)(2,1)}, u32[]{:S(2)}) copy-start(bf16[128,256]{1,0:T(8,128)(2,1)} %get-tuple-element.40.refs_0_.refs_1_) | copy-start | bytes 196612
  42.7 5.5 %collective-permute-start.7 = (bf16[2,128,256]{2,1,0:T(8,128)(2,1)S(1)}, bf16[2,128,256]{2,1,0:T(8,128)(2,1)S(1)}, u32[]{:S(2)}, u32[]{:S(2)}) collective-permute-start(bf16[2,128,256]{2,1,0:T(8,128)(2,1)S(1)} %get-tuple-element.42.refs_4_), channel_id=1, source_target_pairs={{0,8},{4,12},{8,0},{12,4},{16,24},{20,28},{24,16},{28,20},{1,9},{5... | collective-permute-start | bytes 393224 | tf_op jit(solution)/shard_map/ppermute | solution.py:114
  48.2 0.6 copy-start.1
  48.9 13.2 %all-to-all-start.1 = ((bf16[8,16,256]{2,1,0:T(8,128)(2,1)}), bf16[8,16,256]{2,1,0:T(8,128)(2,1)S(1)}, u32[]{:S(2)}, u32[]{:S(2)}) async-start(bf16[8,16,256]{2,1,0:T(8,128)(2,1)} %bitcast.14), calls=%async_computation.1 | async-start | bytes 131072 | tf_op jit(solution)/shard_map/all_to_all | solution.py:514
  55.0 10.7 %collective-permute-start.11 = (bf16[2,128,256]{2,1,0:T(8,128)(2,1)S(1)}, bf16[2,128,256]{2,1,0:T(8,128)(2,1)S(1)}, u32[]{:S(2)}, u32[]{:S(2)}) collective-permute-start(bf16[2,128,256]{2,1,0:T(8,128)(2,1)S(1)} %get-tuple-element.41.refs_0_), channel_id=1, source_target_pairs={{0,4},{4,0},{8,12},{12,8},{16,20},{20,16},{24,28},{28,24},{1,5},{5... | collective-permute-start | bytes 393224 | tf_op jit(solution)/shard_map/ppermute | solution.py:114
  57.1 10.3 %collective-permute-start.13 = (bf16[2,128,256]{2,1,0:T(8,128)(2,1)S(1)}, bf16[2,128,256]{2,1,0:T(8,128)(2,1)S(1)}, u32[]{:S(2)}, u32[]{:S(2)}) collective-permute-start(bf16[2,128,256]{2,1,0:T(8,128)(2,1)S(1)} %get-tuple-element.42.refs_4_), channel_id=1, source_target_pairs={{0,4},{4,0},{8,12},{12,8},{16,20},{20,16},{24,28},{28,24},{1,5},{5... | collective-permute-start | bytes 393224 | tf_op jit(solution)/shard_map/ppermute | solution.py:114
  57.1 10.2 %collective-permute-start.12 = (bf16[2,128,256]{2,1,0:T(8,128)(2,1)S(1)}, bf16[2,128,256]{2,1,0:T(8,128)(2,1)S(1)}, u32[]{:S(2)}, u32[]{:S(2)}) collective-permute-start(bf16[2,128,256]{2,1,0:T(8,128)(2,1)S(1)} %get-tuple-element.45.refs_2_), channel_id=1, source_target_pairs={{0,4},{4,0},{8,12},{12,8},{16,20},{20,16},{24,28},{28,24},{1,5},{5... | collective-permute-start | bytes 393224 | tf_op jit(solution)/shard_map/ppermute | solution.py:114
  62.7 6.0 %collective-permute-start.14 = (bf16[2,128,256]{2,1,0:T(8,128)(2,1)S(1)}, bf16[2,128,256]{2,1,0:T(8,128)(2,1)S(1)}, u32[]{:S(2)}, u32[]{:S(2)}) collective-permute-start(bf16[2,128,256]{2,1,0:T(8,128)(2,1)S(1)} %collective-permute-done.7.refs_0_.refs_6_), channel_id=1, source_target_pairs={{0,4},{4,0},{8,12},{12,8},{16,20},{20,16},{24,28},{28,24},{1,5},{5... | collective-permute-start | bytes 393224 | tf_op jit(solution)/shard_map/ppermute | solution.py:114
  63.0 1.0 %copy-start.4 = (bf16[8,64,256]{2,1,0:T(8,128)(2,1)S(1)}, bf16[8,64,256]{2,1,0:T(8,128)(2,1)}, u32[]{:S(2)}) copy-start(bf16[8,64,256]{2,1,0:T(8,128)(2,1)} %copy-done.3) | copy-start | bytes 786436
  68.7 0.7 copy-start.10
  69.5 5.3 %collective-permute-start.15 = (f32[1,64]{1,0:T(1,128)S(1)}, f32[1,64]{1,0:T(1,128)S(1)}, u32[]{:S(2)}, u32[]{:S(2)}) collective-permute-start(f32[1,64]{1,0:T(1,128)S(1)} %get-tuple-element.50), channel_id=1, source_target_pairs={{0,1},{1,0},{2,3},{3,2},{4,5},{5,4},{6,7},{7,6},{8,9},{9,8},{10,11... | collective-permute-start | bytes 776 | tf_op jit(solution)/shard_map/ppermute | solution.py:114
  69.5 5.3 %collective-permute-start.16 = (f32[1,64]{1,0:T(1,128)S(1)}, f32[1,64]{1,0:T(1,128)S(1)}, u32[]{:S(2)}, u32[]{:S(2)}) collective-permute-start(f32[1,64]{1,0:T(1,128)S(1)} %get-tuple-element.51), channel_id=1, source_target_pairs={{0,2},{1,3},{2,0},{3,1},{4,6},{5,7},{6,4},{7,5},{8,10},{9,11},{10,... | collective-permute-start | bytes 776 | tf_op jit(solution)/shard_map/ppermute | solution.py:114
  71.1 3.7 %collective-permute-start.17 = (f32[1,64]{1,0:T(1,128)S(1)}, f32[1,64]{1,0:T(1,128)S(1)}, u32[]{:S(2)}, u32[]{:S(2)}) collective-permute-start(f32[1,64]{1,0:T(1,128)S(1)} %get-tuple-element.52), channel_id=1, source_target_pairs={{0,3},{1,2},{2,1},{3,0},{4,7},{5,6},{6,5},{7,4},{8,11},{9,10},{10,... | collective-permute-start | bytes 776 | tf_op jit(solution)/shard_map/ppermute | solution.py:114

commit v9 on v8

--- a/solution.py
+++ b/solution.py
@@ -508,22 +508,19 @@
     hidden_all = exchanged(joined, "rows", after_slab)
     grad_all = exchanged(grad_rows, "tm")
 
-    (packed,) = call(gate_kernel, [(packed.shape, bf16)], [], 0, 0, "aaa", {1: 0})(
-        hidden_all[R - 2], packed
-    )
     packed = lax.all_to_all(packed.reshape(R, slot, C), "rows", 0, 0, tiled=True)
     latent = packed[:, :used].reshape(R, F, J // R, C).transpose(1, 0, 2, 3)
+    gains = call(
+        functools.partial(gain_kernel, T, used),
+        [((1, part), f32)] * T,
+        [], R * slot * C, R * slot * C, "v" + "a" * (R // 2) + "v" * T,
+    )(packed, *hidden_all[1::2])
     grads, bias_sum = call(
         functools.partial(order_kernel, F, J, R, T),
         [((2, R, (F * T + 2) * J, C), bf16), ((1, part), f32)],
         [],
         90 * WORK * span * C, 2 * R * T * span * C, "s" + "v" * (T + 2),
     )(place, *grad_all)
-    gains = call(
-        functools.partial(gain_kernel, T, used),
-        [((1, part), f32)] * T,
-        [], R * slot * C, R * slot * C, "v" + "a" * (R // 2 + 1) + "v" * T,
-    )(packed, bias_sum, *hidden_all[1::2])
     weight_grad, own_gain = call(
         functools.partial(weight_kernel, F, J, R, T, part),
         [((27, part, C), f32), ((1, part), f32)],

time: 75.9 us -> 69.3 us (0.913)
  waiting for transfers between devices: 21.3 us -> 8.99 us
  blocking collectives: 0 us -> 11.2 us
  starting transfers between devices: 31.8 us -> 27.6 us
  local copies, waits for them, and re-layouts: 7.96 us -> 6.69 us
    all_to_all x0 -> x1, blocking collectives: none -> 11.2 us  [gathered_form(): lax.all_to_all(packed.reshape(R, slot, C), 'rows', 0, 0, tiled=True)]
    ppermute x16, waiting for transfers between devices: 11 us -> 4.76 us  [partners(): lax.ppermute(value, axis, [(source, source ^ bits) for source in range(co...]
    all_to_all x1 -> x0, starting transfers between devices: 6.18 us -> none  [gathered_form(): lax.all_to_all(packed.reshape(R, slot, C), 'rows', 0, 0, tiled=True)]
    all_to_all x1 -> x0, waiting for transfers between devices: 2.97 us -> none  [gathered_form(): lax.all_to_all(packed.reshape(R, slot, C), 'rows', 0, 0, tiled=True)]
    ppermute x16, starting transfers between devices: 15.8 us -> 17.8 us  [partners(): lax.ppermute(value, axis, [(source, source ^ bits) for source in range(co...]
    all_to_all x1, waiting for transfers between devices: 5.79 us -> 4.15 us  [gathered_form(): lax.all_to_all(jnp.broadcast_to(own, (R,) + own.shape[1:]), 'rows', 0, 0,...]
    ppermute x2, waiting for transfers between devices: 1.58 us -> 0.07 us  [shifted(): lax.ppermute(value, axis, [(source, source + steps) for source in range(l...]
    unnamed x28 -> x24, local copies, waits for them, and re-layouts: 5.8 us -> 4.53 us
  transfers between devices with their start and end apart: 20 -> 19, of which waited for: 7 -> 4; matrix products, arithmetic and copies ran while one was open for 2% -> 2% of each run, Pallas kernels for 16% -> 18%
where the time goes in v9:
time: 69.3 us; the launch traced here: 68.8 us
  starting transfers between devices  27.6 us (40%)
  Pallas kernels  12.7 us (18%)
  blocking collectives  11.2 us (16%)
  waiting for transfers between devices  8.99 us (13%)
  local copies, waits for them, and re-layouts  6.69 us (10%)
  between operations  0.83 us (1%)
  other arithmetic  0.78 us (1%)
    ppermute x16, starting transfers between devices, partners(): lax.ppermute(value, axis, [(source, source ^ bits) for source in range(co...  17.8 us
    all_to_all x1, blocking collectives, gathered_form(): lax.all_to_all(packed.reshape(R, slot, C), 'rows', 0, 0, tiled=True)  11.2 us
    all_to_all x1, starting transfers between devices, gathered_form(): lax.all_to_all(jnp.broadcast_to(own, (R,) + own.shape[1:]), 'rows', 0, 0,...  7.25 us
    pallas_call x1, Pallas kernels, gathered_form(): call(functools.partial(slab_kernel, F, J, R, T, slot), [((R * slot, C), b...  5.33 us
    ppermute x16, waiting for transfers between devices, partners(): lax.ppermute(value, axis, [(source, source ^ bits) for source in range(co...  4.76 us
    unnamed x24, local copies, waits for them, and re-layouts  4.53 us
    all_to_all x1, waiting for transfers between devices, gathered_form(): lax.all_to_all(jnp.broadcast_to(own, (R,) + own.shape[1:]), 'rows', 0, 0,...  4.15 us
    pallas_call x1, Pallas kernels, gathered_form(): call(functools.partial(weight_kernel, F, J, R, T, part), [((27, part, C),...  3.47 us
  transfers between devices with their start and end apart: 19, of which 4 were waited for; matrix products, arithmetic and copies ran while one was open for 2% of the time, Pallas kernels for 18%

profile of v9, /device:TPU:0, one launch (start us, length us, event | category | flops | bytes accessed | tf_op | source)
XLA Modules:
  0.0 68.8 jit_solution(15098655274699161323)
XLA Ops:
  0.6 0.8 %broadcast_in_dim.7 = bf16[64,256]{1,0:T(8,128)(2,1)S(1)} reshape(bf16[4,8,2,256]{3,2,1,0:T(2,128)(2,1)} %param.9) | data formatting | bytes 65536 | tf_op jit(solution)/shard_map/broadcast_in_dim | solution.py:457
  1.4 0.7 %broadcast_in_dim.8 = bf16[8,64,256]{2,1,0:T(8,128)(2,1)} broadcast(bf16[64,256]{1,0:T(8,128)(2,1)S(1)} %broadcast_in_dim.7), dimensions={1,2} | broadcast | bytes 294912 | tf_op jit(solution)/shard_map/broadcast_in_dim | solution.py:457
  2.1 7.3 %all-to-all-start = ((bf16[8,64,256]{2,1,0:T(8,128)(2,1)}), bf16[8,64,256]{2,1,0:T(8,128)(2,1)S(1)}, u32[]{:S(2)}, u32[]{:S(2)}) async-start(bf16[8,64,256]{2,1,0:T(8,128)(2,1)} %broadcast_in_dim.8), calls=%async_computation | async-start | bytes 524288 | tf_op jit(solution)/shard_map/all_to_all | solution.py:456
  9.4 0.1 pad_add_fusion.place
  9.5 0.7 %pad_maximum_fusion.vectors = f32[2,256]{1,0:T(2,128)S(1)} fusion(f32[1,256]{1,0:T(1,128)} %bitcast.18, f32[1,256]{1,0:T(1,128)} %bitcast.19), kind=kLoop, calls=%fused_computation.1 | loop fusion | flops 512 | bytes 4096 | tf_op jit(solution)/shard_map/stack | solution.py:450
  10.2 0.9 %copy-done.9 = bf16[4,2,32,256]{3,2,1,0:T(8,128)(2,1)S(1)} copy-done((bf16[4,2,32,256]{3,2,1,0:T(8,128)(2,1)S(1)}, bf16[4,2,32,256]{3,2,1,0:T(8,128)(2,1)}, u32[]{:S(2)}) %copy-start.9) | copy-done | bytes 131096
  11.1 0.8 %shard_map.92 = (bf16[2,2,64,256]{3,2,1,0:T(8,128)(2,1)S(1)}, bf16[256,256]{1,0:T(8,128)(2,1)S(1)}, f32[2,256]{1,0:T(2,128)S(1)}, bf16[128,128]{1,0:T(8,128)(2,1...) custom-call(s32[2]{0:T(128)S(1)} %pad_add_fusion.place, ...), custom_call_target="tpu_custom_call" | custom-call | flops 1179648000 | bytes 262144 | tf_op jit(solution)/shard_map/pallas_call | solution.py:461
  11.9 0.0 copy-start.6
  11.9 0.6 copy-done.6
  12.5 0.0 collective-permute-start
  12.5 1.6 %collective-permute-start.2 = (bf16[384,128]{1,0:T(8,128)(2,1)S(1)}, bf16[384,128]{1,0:T(8,128)(2,1)S(1)}, u32[]{:S(2)}, u32[]{:S(2)}) collective-permute-start(bf16[384,128]{1,0:T(8,128)(2,1)S(1)} %get-tuple-element.33), channel_id=1, source_target_pairs={{0,3},{1,2},{2,1},{3,0},{4,7},{5,6},{6,5},{7,4},{8,11},{9,10},{10,... | collective-permute-start | bytes 294920 | tf_op jit(solution)/shard_map/ppermute | solution.py:114
  14.1 4.2 %all-to-all-done.grad_rows = bf16[8,64,256]{2,1,0:T(8,128)(2,1)S(1)} async-done(((bf16[8,64,256]{2,1,0:T(8,128)(2,1)}), bf16[8,64,256]{2,1,0:T(8,128)(2,1)S(1)}, u32[]{:S(2)}, u32[]{:S(2)}) %all-to-all-start) | async-done | bytes 262176 | tf_op jit(solution)/shard_map/all_to_all | solution.py:456
  18.3 0.0 copy-start.1
  18.3 1.6 %collective-permute-start.13 = (bf16[8,64,256]{2,1,0:T(8,128)(2,1)S(1)}, bf16[8,64,256]{2,1,0:T(8,128)(2,1)S(1)}, u32[]{:S(2)}, u32[]{:S(2)}) collective-permute-start(bf16[8,64,256]{2,1,0:T(8,128)(2,1)S(1)} %get-tuple-element.38.gathered.refs_0_), channel_id=1, source_target_pairs={{0,2},{1,3},{2,0},{3,1},{4,6},{5,7},{6,4},{7,5},{8,10},{9,11},{10,... | collective-permute-start | bytes 786440 | tf_op jit(solution)/shard_map/ppermute | solution.py:114
  19.9 0.5 collective-permute-start.1
  20.4 1.3 %collective-permute-start.4 = (bf16[8,32,256]{2,1,0:T(8,128)(2,1)S(1)}, bf16[8,32,256]{2,1,0:T(8,128)(2,1)S(1)}, u32[]{:S(2)}, u32[]{:S(2)}) collective-permute-start(bf16[8,32,256]{2,1,0:T(8,128)(2,1)S(1)} %get-tuple-element.39), channel_id=1, source_target_pairs={{1,0},{2,1},{3,2},{5,4},{6,5},{7,6},{9,8},{10,9},{11,10},{13,12},{... | collective-permute-start | bytes 393224 | tf_op jit(solution)/shard_map/ppermute | solution.py:20
  21.7 3.6 %collective-permute-done.1.refs_2_ = bf16[128,128]{1,0:T(8,128)(2,1)S(1)} collective-permute-done((bf16[128,128]{1,0:T(8,128)(2,1)S(1)}, bf16[128,128]{1,0:T(8,128)(2,1)S(1)}, u32[]{:S(2)}, u32[]{:S(2)}) %collective-permute-start.1) | collective-permute-done | bytes 32800 | tf_op jit(solution)/shard_map/ppermute | solution.py:114
  25.3 0.0 collective-permute-done.refs_1_
  25.3 0.0 collective-permute-done.2.refs_3_
  25.3 0.0 copy-done.7
  25.3 0.6 shard_map.93
  26.0 0.0 copy-start.5
  26.0 0.6 copy-done.5
  26.6 1.3 %collective-permute-start.3 = (bf16[2,96,256]{2,1,0:T(8,128)(2,1)S(1)}, bf16[2,96,256]{2,1,0:T(8,128)(2,1)S(1)}, u32[]{:S(2)}, u32[]{:S(2)}) collective-permute-start(bf16[2,96,256]{2,1,0:T(8,128)(2,1)S(1)} %get-tuple-element.35), channel_id=1, source_target_pairs={{4,0},{8,4},{12,8},{16,12},{20,16},{24,20},{28,24},{5,1},{9,5},{13... | collective-permute-start | bytes 294920 | tf_op jit(solution)/shard_map/ppermute | solution.py:20
  27.9 3.7 %collective-permute-start.7 = (bf16[2,128,256]{2,1,0:T(8,128)(2,1)S(1)}, bf16[2,128,256]{2,1,0:T(8,128)(2,1)S(1)}, u32[]{:S(2)}, u32[]{:S(2)}) collective-permute-start(bf16[2,128,256]{2,1,0:T(8,128)(2,1)S(1)} %get-tuple-element.42.refs_0_), channel_id=1, source_target_pairs={{0,16},{4,20},{8,24},{12,28},{16,0},{20,4},{24,8},{28,12},{1,17},{... | collective-permute-start | bytes 393224 | tf_op jit(solution)/shard_map/ppermute | solution.py:114
  31.6 1.5 %collective-permute-start.6 = (bf16[2,128,256]{2,1,0:T(8,128)(2,1)S(1)}, bf16[2,128,256]{2,1,0:T(8,128)(2,1)S(1)}, u32[]{:S(2)}, u32[]{:S(2)}) collective-permute-start(bf16[2,128,256]{2,1,0:T(8,128)(2,1)S(1)} %get-tuple-element.42.refs_0_), channel_id=1, source_target_pairs={{0,8},{4,12},{8,0},{12,4},{16,24},{20,28},{24,16},{28,20},{1,9},{5... | collective-permute-start | bytes 393224 | tf_op jit(solution)/shard_map/ppermute | solution.py:114
  33.0 0.1 collective-permute-done.3.under
  33.1 3.2 %collective-permute-start.5 = (bf16[2,128,256]{2,1,0:T(8,128)(2,1)S(1)}, bf16[2,128,256]{2,1,0:T(8,128)(2,1)S(1)}, u32[]{:S(2)}, u32[]{:S(2)}) collective-permute-start(bf16[2,128,256]{2,1,0:T(8,128)(2,1)S(1)} %get-tuple-element.42.refs_0_), channel_id=1, source_target_pairs={{0,4},{4,0},{8,12},{12,8},{16,20},{20,16},{24,28},{28,24},{1,5},{5... | collective-permute-start | bytes 393224 | tf_op jit(solution)/shard_map/ppermute | solution.py:114
  36.3 0.0 collective-permute-done.4.following
  36.3 0.0 copy-done
  36.3 0.6 copy-done.10
  37.0 5.3 %shard_map.95 = (bf16[128,256]{1,0:T(8,128)(2,1)}, bf16[256,256]{1,0:T(8,128)(2,1)}) custom-call(s32[2]{0:T(128)} %copy-done.7, bf16[2,2,64,256]{3,2,1,0:T(8,128)(2,1)} %copy-done.4, bf16[2,2,32,256]{3,2,1,0:T(8,128)(2,1)} %copy-done.5, bf16[2,96,256]{2,1,0:T(8,128)(2,1)} %copy-done.11, bf16[27,256,256]{2,1,0:T(8,128)(2,1)} %bitcast.16, ...), custom_call_target="tpu_custom_call" | custom-call | flops 452984832 | bytes 3538944 | tf_op jit(solution)/shard_map/pallas_call | solution.py:486
  42.3 0.0 collective-permute-done.7.refs_2_
  42.3 0.0 collective-permute-done.6.refs_1_
  42.3 0.8 %copy-done.3 = bf16[128,256]{1,0:T(8,128)(2,1)S(1)} copy-done((bf16[128,256]{1,0:T(8,128)(2,1)S(1)}, bf16[128,256]{1,0:T(8,128)(2,1)}, u32[]{:S(2)}) %copy-start.3) | copy-done | bytes 65560
  43.1 1.3 %collective-permute-start.10 = (bf16[2,128,256]{2,1,0:T(8,128)(2,1)S(1)}, bf16[2,128,256]{2,1,0:T(8,128)(2,1)S(1)}, u32[]{:S(2)}, u32[]{:S(2)}) collective-permute-start(bf16[2,128,256]{2,1,0:T(8,128)(2,1)S(1)} %get-tuple-element.44.refs_4_), channel_id=1, source_target_pairs={{0,8},{4,12},{8,0},{12,4},{16,24},{20,28},{24,16},{28,20},{1,9},{5... | collective-permute-start | bytes 393224 | tf_op jit(solution)/shard_map/ppermute | solution.py:114
  44.4 0.0 collective-permute-start.12
  44.4 0.0 collective-permute-done.13.refs_2_
  44.5 0.5 collective-permute-start.14
  45.0 0.0 collective-permute-start.9
  45.0 0.0 collective-permute-done.5.refs_0_.refs_1_
  45.0 2.0 %collective-permute-start.8 = (bf16[2,128,256]{2,1,0:T(8,128)(2,1)S(1)}, bf16[2,128,256]{2,1,0:T(8,128)(2,1)S(1)}, u32[]{:S(2)}, u32[]{:S(2)}) collective-permute-start(bf16[2,128,256]{2,1,0:T(8,128)(2,1)S(1)} %get-tuple-element.43.refs_2_), channel_id=1, source_target_pairs={{0,4},{4,0},{8,12},{12,8},{16,20},{20,16},{24,28},{28,24},{1,5},{5... | collective-permute-start | bytes 393224 | tf_op jit(solution)/shard_map/ppermute | solution.py:114
  47.0 1.1 %collective-permute-done.10.refs_6_ = bf16[2,128,256]{2,1,0:T(8,128)(2,1)S(1)} collective-permute-done((bf16[2,128,256]{2,1,0:T(8,128)(2,1)S(1)}, bf16[2,128,256]{2,1,0:T(8,128)(2,1)S(1)}, u32[]{:S(2)}, u32[]{:S(2)}) %collective-permute-start.10) | collective-permute-done | bytes 131104 | tf_op jit(solution)/shard_map/ppermute | solution.py:114
  48.1 0.0 collective-permute-start.11
  48.1 11.2 %all_to_all.10.received = bf16[8,16,256]{2,1,0:T(8,128)(2,1)S(1)} all-to-all(bf16[8,16,256]{2,1,0:T(8,128)(2,1)S(1)} %bitcast.14), channel_id=1, replica_groups=mesh['rows'=8,'tm'=4] {'rows'}, dimensions={0} | all-to-all | bytes 131072 | tf_op jit(solution)/shard_map/all_to_all | solution.py:511
  59.4 0.6 copy.14
  60.1 0.0 collective-permute-done.8.refs_1_.refs_3_
  60.1 0.0 collective-permute-done.9.refs_2_.refs_5_
  60.1 0.0 collective-permute-done.11.refs_3_.refs_7_
  60.1 0.1 shard_map.97
  60.2 0.0 collective-permute-start.15
  60.2 1.6 %collective-permute-start.16 = (f32[1,64]{1,0:T(1,128)S(1)}, f32[1,64]{1,0:T(1,128)S(1)}, u32[]{:S(2)}, u32[]{:S(2)}) collective-permute-start(f32[1,64]{1,0:T(1,128)S(1)} %get-tuple-element.50), channel_id=1, source_target_pairs={{0,2},{1,3},{2,0},{3,1},{4,6},{5,7},{6,4},{7,5},{8,10},{9,11},{10,... | collective-permute-start | bytes 776 | tf_op jit(solution)/shard_map/ppermute | solution.py:114
  61.8 0.3 collective-permute-start.17
  62.0 0.0 collective-permute-done.12.refs_1_
  62.0 0.0 collective-permute-done.14.refs_3_
  62.0 0.0 copy-done.8
  62.0 0.0 copy-start.2
  62.1 0.9 %copy-done.2 = bf16[8,64,256]{2,1,0:T(8,128)(2,1)S(1)} copy-done((bf16[8,64,256]{2,1,0:T(8,128)(2,1)S(1)}, bf16[8,64,256]{2,1,0:T(8,128)(2,1)}, u32[]{:S(2)}) %copy-start.2) | copy-done | bytes 262168
  63.0 1.8 %shard_map.98 = (bf16[2,8,288,256]{3,2,1,0:T(8,128)(2,1)S(1)}, f32[1,64]{1,0:T(1,128)}) custom-call(s32[2]{0:T(128)S(1)} %copy-done.8, bf16[8,64,256]{2,1,0:T(8,128)(2,1)S(1)} %copy-done.2, bf16[8,64,256]{2,1,0:T(8,128)(2,1)S(1)} %collective-permute-done.12.refs_1_, bf16[8,64,256]{2,1,0:T(8,128)(2,1)S(1)} %collective-permute-done.13.refs_2_, ...), custom_call_target="tpu_custom_call" | custom-call | flops 1769472000 | bytes 1048576 | tf_op jit(solution)/shard_map/pallas_call | solution.py:518
  64.8 3.5 %shard_map.99 = (f32[27,64,256]{2,1,0:T(8,128)}, f32[1,64]{1,0:T(1,128)S(1)}) custom-call(s32[2]{0:T(128)S(1)} %copy-done.8, f32[1,64]{1,0:T(1,128)S(1)} %get-tuple-element.45.gain, bf16[2,8,288,256]{3,2,1,0:T(8,128)(2,1)S(1)} %get-tuple-element.46.grads, bf16[2,128,256]{2,1,0:T(8,128)(2,1)S(1)} %get-tuple-element.42.refs_0_, ...), custom_call_target="tpu_custom_call" | custom-call | flops 3932160000 | bytes 3538944 | tf_op jit(solution)/shard_map/pallas_call | solution.py:524
  68.2 0.0 collective-permute-done.15.refs_1_
  68.2 0.0 collective-permute-done.16.refs_2_
  68.3 0.0 collective-permute-done.17.refs_3_
  68.3 0.5 shard_map.100
  (15 shorter events, 0.1 us)
Async XLA Ops:
  2.1 16.2 %all-to-all-start = ((bf16[8,64,256]{2,1,0:T(8,128)(2,1)}), bf16[8,64,256]{2,1,0:T(8,128)(2,1)S(1)}, u32[]{:S(2)}, u32[]{:S(2)}) async-start(bf16[8,64,256]{2,1,0:T(8,128)(2,1)} %broadcast_in_dim.8), calls=%async_computation | async-start | bytes 524288 | tf_op jit(solution)/shard_map/all_to_all | solution.py:456
  9.5 15.9 %copy-start.7 = (s32[2]{0:T(128)}, s32[2]{0:T(128)S(1)}, u32[]{:S(2)}) copy-start(s32[2]{0:T(128)S(1)} %pad_add_fusion.place) | copy-start | bytes 28
  10.2 0.9 %copy-start.9 = (bf16[4,2,32,256]{3,2,1,0:T(8,128)(2,1)S(1)}, bf16[4,2,32,256]{3,2,1,0:T(8,128)(2,1)}, u32[]{:S(2)}) copy-start(bf16[4,2,32,256]{3,2,1,0:T(8,128)(2,1)} %param.5) | copy-start | bytes 393220
  11.9 0.6 copy-start.6
  12.5 23.8 %copy-start = (bf16[256,256]{1,0:T(8,128)(2,1)}, bf16[256,256]{1,0:T(8,128)(2,1)S(1)}, u32[]{:S(2)}) copy-start(bf16[256,256]{1,0:T(8,128)(2,1)S(1)} %get-tuple-element.36._.frames) | copy-start | bytes 393220
  12.5 23.8 %copy-start.4 = (bf16[2,2,64,256]{3,2,1,0:T(8,128)(2,1)}, bf16[2,2,64,256]{3,2,1,0:T(8,128)(2,1)S(1)}, u32[]{:S(2)}) copy-start(bf16[2,2,64,256]{3,2,1,0:T(8,128)(2,1)S(1)} %get-tuple-element.29.planes) | copy-start | bytes 393220
  12.5 12.8 %collective-permute-start = (bf16[384,128]{1,0:T(8,128)(2,1)S(1)}, bf16[384,128]{1,0:T(8,128)(2,1)S(1)}, u32[]{:S(2)}, u32[]{:S(2)}) collective-permute-start(bf16[384,128]{1,0:T(8,128)(2,1)S(1)} %get-tuple-element.31), channel_id=1, source_target_pairs={{0,1},{1,0},{2,3},{3,2},{4,5},{5,4},{6,7},{7,6},{8,9},{9,8},{10,11... | collective-permute-start | bytes 294920 | tf_op jit(solution)/shard_map/ppermute | solution.py:114
  12.5 12.8 %collective-permute-start.2 = (bf16[384,128]{1,0:T(8,128)(2,1)S(1)}, bf16[384,128]{1,0:T(8,128)(2,1)S(1)}, u32[]{:S(2)}, u32[]{:S(2)}) collective-permute-start(bf16[384,128]{1,0:T(8,128)(2,1)S(1)} %get-tuple-element.33), channel_id=1, source_target_pairs={{0,3},{1,2},{2,1},{3,0},{4,7},{5,6},{6,5},{7,4},{8,11},{9,10},{10,... | collective-permute-start | bytes 294920 | tf_op jit(solution)/shard_map/ppermute | solution.py:114
  18.3 18.0 %copy-start.1 = (bf16[8,64,256]{2,1,0:T(8,128)(2,1)}, bf16[8,64,256]{2,1,0:T(8,128)(2,1)S(1)}, u32[]{:S(2)}) copy-start(bf16[8,64,256]{2,1,0:T(8,128)(2,1)S(1)} %get-tuple-element.38.gathered.refs_0_) | copy-start | bytes 786436
  18.3 26.1 %collective-permute-start.13 = (bf16[8,64,256]{2,1,0:T(8,128)(2,1)S(1)}, bf16[8,64,256]{2,1,0:T(8,128)(2,1)S(1)}, u32[]{:S(2)}, u32[]{:S(2)}) collective-permute-start(bf16[8,64,256]{2,1,0:T(8,128)(2,1)S(1)} %get-tuple-element.38.gathered.refs_0_), channel_id=1, source_target_pairs={{0,2},{1,3},{2,0},{3,1},{4,6},{5,7},{6,4},{7,5},{8,10},{9,11},{10,... | collective-permute-start | bytes 786440 | tf_op jit(solution)/shard_map/ppermute | solution.py:114
  19.9 5.4 %collective-permute-start.1 = (bf16[128,128]{1,0:T(8,128)(2,1)S(1)}, bf16[128,128]{1,0:T(8,128)(2,1)S(1)}, u32[]{:S(2)}, u32[]{:S(2)}) collective-permute-start(bf16[128,128]{1,0:T(8,128)(2,1)S(1)} %get-tuple-element.32), channel_id=1, source_target_pairs={{0,2},{1,3},{2,0},{3,1},{4,6},{5,7},{6,4},{7,5},{8,10},{9,11},{10,... | collective-permute-start | bytes 98312 | tf_op jit(solution)/shard_map/ppermute | solution.py:114
  20.4 15.9 %collective-permute-start.4 = (bf16[8,32,256]{2,1,0:T(8,128)(2,1)S(1)}, bf16[8,32,256]{2,1,0:T(8,128)(2,1)S(1)}, u32[]{:S(2)}, u32[]{:S(2)}) collective-permute-start(bf16[8,32,256]{2,1,0:T(8,128)(2,1)S(1)} %get-tuple-element.39), channel_id=1, source_target_pairs={{1,0},{2,1},{3,2},{5,4},{6,5},{7,6},{9,8},{10,9},{11,10},{13,12},{... | collective-permute-start | bytes 393224 | tf_op jit(solution)/shard_map/ppermute | solution.py:20
  26.0 0.6 copy-start.5
  26.6 6.5 %collective-permute-start.3 = (bf16[2,96,256]{2,1,0:T(8,128)(2,1)S(1)}, bf16[2,96,256]{2,1,0:T(8,128)(2,1)S(1)}, u32[]{:S(2)}, u32[]{:S(2)}) collective-permute-start(bf16[2,96,256]{2,1,0:T(8,128)(2,1)S(1)} %get-tuple-element.35), channel_id=1, source_target_pairs={{4,0},{8,4},{12,8},{16,12},{20,16},{24,20},{28,24},{5,1},{9,5},{13... | collective-permute-start | bytes 294920 | tf_op jit(solution)/shard_map/ppermute | solution.py:20
  27.9 14.4 %collective-permute-start.7 = (bf16[2,128,256]{2,1,0:T(8,128)(2,1)S(1)}, bf16[2,128,256]{2,1,0:T(8,128)(2,1)S(1)}, u32[]{:S(2)}, u32[]{:S(2)}) collective-permute-start(bf16[2,128,256]{2,1,0:T(8,128)(2,1)S(1)} %get-tuple-element.42.refs_0_), channel_id=1, source_target_pairs={{0,16},{4,20},{8,24},{12,28},{16,0},{20,4},{24,8},{28,12},{1,17},{... | collective-permute-start | bytes 393224 | tf_op jit(solution)/shard_map/ppermute | solution.py:114
  31.6 10.7 %collective-permute-start.6 = (bf16[2,128,256]{2,1,0:T(8,128)(2,1)S(1)}, bf16[2,128,256]{2,1,0:T(8,128)(2,1)S(1)}, u32[]{:S(2)}, u32[]{:S(2)}) collective-permute-start(bf16[2,128,256]{2,1,0:T(8,128)(2,1)S(1)} %get-tuple-element.42.refs_0_), channel_id=1, source_target_pairs={{0,8},{4,12},{8,0},{12,4},{16,24},{20,28},{24,16},{28,20},{1,9},{5... | collective-permute-start | bytes 393224 | tf_op jit(solution)/shard_map/ppermute | solution.py:114
  33.1 3.2 %copy-start.11 = (bf16[2,96,256]{2,1,0:T(8,128)(2,1)}, bf16[2,96,256]{2,1,0:T(8,128)(2,1)S(1)}, u32[]{:S(2)}) copy-start(bf16[2,96,256]{2,1,0:T(8,128)(2,1)S(1)} %collective-permute-done.3.under) | copy-start | bytes 294916
  33.1 11.9 %collective-permute-start.5 = (bf16[2,128,256]{2,1,0:T(8,128)(2,1)S(1)}, bf16[2,128,256]{2,1,0:T(8,128)(2,1)S(1)}, u32[]{:S(2)}, u32[]{:S(2)}) collective-permute-start(bf16[2,128,256]{2,1,0:T(8,128)(2,1)S(1)} %get-tuple-element.42.refs_0_), channel_id=1, source_target_pairs={{0,4},{4,0},{8,12},{12,8},{16,20},{20,16},{24,28},{28,24},{1,5},{5... | collective-permute-start | bytes 393224 | tf_op jit(solution)/shard_map/ppermute | solution.py:114
  36.3 0.7 copy-start.10
  37.0 25.1 %copy-start.8 = (s32[2]{0:T(128)S(1)}, s32[2]{0:T(128)}, u32[]{:S(2)}) copy-start(s32[2]{0:T(128)} %copy-done.7) | copy-start | bytes 28
  42.3 0.8 %copy-start.3 = (bf16[128,256]{1,0:T(8,128)(2,1)S(1)}, bf16[128,256]{1,0:T(8,128)(2,1)}, u32[]{:S(2)}) copy-start(bf16[128,256]{1,0:T(8,128)(2,1)} %get-tuple-element.40.refs_0_) | copy-start | bytes 196612
  43.1 5.0 %collective-permute-start.10 = (bf16[2,128,256]{2,1,0:T(8,128)(2,1)S(1)}, bf16[2,128,256]{2,1,0:T(8,128)(2,1)S(1)}, u32[]{:S(2)}, u32[]{:S(2)}) collective-permute-start(bf16[2,128,256]{2,1,0:T(8,128)(2,1)S(1)} %get-tuple-element.44.refs_4_), channel_id=1, source_target_pairs={{0,8},{4,12},{8,0},{12,4},{16,24},{20,28},{24,16},{28,20},{1,9},{5... | collective-permute-start | bytes 393224 | tf_op jit(solution)/shard_map/ppermute | solution.py:114
  44.4 17.6 %collective-permute-start.12 = (bf16[8,64,256]{2,1,0:T(8,128)(2,1)}, bf16[8,64,256]{2,1,0:T(8,128)(2,1)S(1)}, u32[]{:S(2)}, u32[]{:S(2)}) collective-permute-start(bf16[8,64,256]{2,1,0:T(8,128)(2,1)} %copy-done.1), channel_id=1, source_target_pairs={{0,1},{1,0},{2,3},{3,2},{4,5},{5,4},{6,7},{7,6},{8,9},{9,8},{10,11... | collective-permute-start | bytes 786440 | tf_op jit(solution)/shard_map/ppermute | solution.py:114
  44.5 17.6 %collective-permute-start.14 = (bf16[8,64,256]{2,1,0:T(8,128)(2,1)S(1)}, bf16[8,64,256]{2,1,0:T(8,128)(2,1)S(1)}, u32[]{:S(2)}, u32[]{:S(2)}) collective-permute-start(bf16[8,64,256]{2,1,0:T(8,128)(2,1)S(1)} %collective-permute-done.13.refs_2_), channel_id=1, source_target_pairs={{0,1},{1,0},{2,3},{3,2},{4,5},{5,4},{6,7},{7,6},{8,9},{9,8},{10,11... | collective-permute-start | bytes 786440 | tf_op jit(solution)/shard_map/ppermute | solution.py:114
  45.0 15.1 %collective-permute-start.9 = (bf16[2,128,256]{2,1,0:T(8,128)(2,1)S(1)}, bf16[2,128,256]{2,1,0:T(8,128)(2,1)S(1)}, u32[]{:S(2)}, u32[]{:S(2)}) collective-permute-start(bf16[2,128,256]{2,1,0:T(8,128)(2,1)S(1)} %get-tuple-element.44.refs_4_), channel_id=1, source_target_pairs={{0,4},{4,0},{8,12},{12,8},{16,20},{20,16},{24,28},{28,24},{1,5},{5... | collective-permute-start | bytes 393224 | tf_op jit(solution)/shard_map/ppermute | solution.py:114
  45.0 15.1 %collective-permute-start.8 = (bf16[2,128,256]{2,1,0:T(8,128)(2,1)S(1)}, bf16[2,128,256]{2,1,0:T(8,128)(2,1)S(1)}, u32[]{:S(2)}, u32[]{:S(2)}) collective-permute-start(bf16[2,128,256]{2,1,0:T(8,128)(2,1)S(1)} %get-tuple-element.43.refs_2_), channel_id=1, source_target_pairs={{0,4},{4,0},{8,12},{12,8},{16,20},{20,16},{24,28},{28,24},{1,5},{5... | collective-permute-start | bytes 393224 | tf_op jit(solution)/shard_map/ppermute | solution.py:114
  48.1 11.9 %collective-permute-start.11 = (bf16[2,128,256]{2,1,0:T(8,128)(2,1)S(1)}, bf16[2,128,256]{2,1,0:T(8,128)(2,1)S(1)}, u32[]{:S(2)}, u32[]{:S(2)}) collective-permute-start(bf16[2,128,256]{2,1,0:T(8,128)(2,1)S(1)} %collective-permute-done.10.refs_6_), channel_id=1, source_target_pairs={{0,4},{4,0},{8,12},{12,8},{16,20},{20,16},{24,28},{28,24},{1,5},{5... | collective-permute-start | bytes 393224 | tf_op jit(solution)/shard_map/ppermute | solution.py:114
  60.2 8.1 %collective-permute-start.15 = (f32[1,64]{1,0:T(1,128)S(1)}, f32[1,64]{1,0:T(1,128)S(1)}, u32[]{:S(2)}, u32[]{:S(2)}) collective-permute-start(f32[1,64]{1,0:T(1,128)S(1)} %get-tuple-element.49), channel_id=1, source_target_pairs={{0,1},{1,0},{2,3},{3,2},{4,5},{5,4},{6,7},{7,6},{8,9},{9,8},{10,11... | collective-permute-start | bytes 776 | tf_op jit(solution)/shard_map/ppermute | solution.py:114
  60.2 8.1 %collective-permute-start.16 = (f32[1,64]{1,0:T(1,128)S(1)}, f32[1,64]{1,0:T(1,128)S(1)}, u32[]{:S(2)}, u32[]{:S(2)}) collective-permute-start(f32[1,64]{1,0:T(1,128)S(1)} %get-tuple-element.50), channel_id=1, source_target_pairs={{0,2},{1,3},{2,0},{3,1},{4,6},{5,7},{6,4},{7,5},{8,10},{9,11},{10,... | collective-permute-start | bytes 776 | tf_op jit(solution)/shard_map/ppermute | solution.py:114
  61.8 6.5 %collective-permute-start.17 = (f32[1,64]{1,0:T(1,128)S(1)}, f32[1,64]{1,0:T(1,128)S(1)}, u32[]{:S(2)}, u32[]{:S(2)}) collective-permute-start(f32[1,64]{1,0:T(1,128)S(1)} %get-tuple-element.51), channel_id=1, source_target_pairs={{0,3},{1,2},{2,1},{3,0},{4,7},{5,6},{6,5},{7,4},{8,11},{9,10},{10,... | collective-permute-start | bytes 776 | tf_op jit(solution)/shard_map/ppermute | solution.py:114
  62.0 1.0 %copy-start.2 = (bf16[8,64,256]{2,1,0:T(8,128)(2,1)S(1)}, bf16[8,64,256]{2,1,0:T(8,128)(2,1)}, u32[]{:S(2)}) copy-start(bf16[8,64,256]{2,1,0:T(8,128)(2,1)} %copy-done.1) | copy-start | bytes 786436

commit v10 on v9

--- a/solution.py
+++ b/solution.py
@@ -10,7 +10,7 @@
 EPS = 1e-06
 TAPS = [(a, b, c) for a in range(3) for b in range(3) for c in range(3)]
 VMEM_LIMIT = 20 * 1024 * 1024
-VMEM_LIMIT_WIDE = 60 * 1024 * 1024
+VMEM_LIMIT_WIDE = 57 * 1024 * 1024
 WORK = 1200
 
 
@@ -465,12 +465,12 @@
         [pltpu.VMEM((2, 4 * span, C // 2), f32)],
         60 * WORK * span * C, 16 * span * C, "svv" + "v" * (T + 3),
     )(place, flat, vectors)
+    messages = [sends[0]] + [partners(sends[k], "tm", k) for k in range(1, T)]
     head, grad_rows = call(
         functools.partial(head_kernel, 2 * J),
         [((R, 2 * J, C), bf16), (grad_rows.shape, bf16)],
         [], R * span * C, R * span * C, "avvv",
-    )(frames_copy, grad_rows)
-    messages = [sends[0]] + [partners(sends[k], "tm", k) for k in range(1, T)]
+    )(messages[1], grad_rows)
     joined, cached, under = call(
         functools.partial(join_kernel, F, J, T),
         [
@@ -505,8 +505,14 @@
             call(gate_kernel, shapes, [], 0, 0, "a" * (2 * count + 1), aliases)(packed, *blocks)
         )
 
-    hidden_all = exchanged(joined, "rows", after_slab)
-    grad_all = exchanged(grad_rows, "tm")
+    later = {}
+
+    def gate(blocks):
+        *blocks, later["grads"] = after_slab(blocks + [grad_rows])
+        return blocks
+
+    hidden_all = exchanged(joined, "rows", gate)
+    grad_all = exchanged(later["grads"], "tm")
 
     packed = lax.all_to_all(packed.reshape(R, slot, C), "rows", 0, 0, tiled=True)
     latent = packed[:, :used].reshape(R, F, J // R, C).transpose(1, 0, 2, 3)

time: 69.3 us -> 67.9 us (0.980)
  blocking collectives: 11.2 us -> 9.27 us
  starting transfers between devices: 27.6 us -> 28.8 us
  waiting for transfers between devices: 8.99 us -> 7.96 us
    all_to_all x1, blocking collectives: 11.2 us -> 9.27 us  [gathered_form(): lax.all_to_all(packed.reshape(R, slot, C), 'rows', 0, 0, tiled=True)]
    all_to_all x1, waiting for transfers between devices: 4.15 us -> 3 us  [gathered_form(): lax.all_to_all(jnp.broadcast_to(own, (R,) + own.shape[1:]), 'rows', 0, 0,...]
    ppermute x16, starting transfers between devices: 17.8 us -> 18.9 us  [partners(): lax.ppermute(value, axis, [(source, source ^ bits) for source in range(co...]
    ppermute x2, waiting for transfers between devices: 0.07 us -> 0.97 us  [shifted(): lax.ppermute(value, axis, [(source, source + steps) for source in range(l...]
    ppermute x16, waiting for transfers between devices: 4.76 us -> 3.99 us  [partners(): lax.ppermute(value, axis, [(source, source ^ bits) for source in range(co...]
  transfers between devices with their start and end apart: 19 -> 19, of which waited for: 4 -> 5; matrix products, arithmetic and copies ran while one was open for 2% -> 2% of each run, Pallas kernels for 18% -> 18%
where the time goes in v10:
time: 67.9 us; the launch traced here: 67.5 us
  starting transfers between devices  28.8 us (42%)
  Pallas kernels  12.7 us (19%)
  blocking collectives  9.27 us (14%)
  waiting for transfers between devices  7.96 us (12%)
  local copies, waits for them, and re-layouts  7.13 us (11%)
  between operations  0.8 us (1%)
  other arithmetic  0.78 us (1%)
    ppermute x16, starting transfers between devices, partners(): lax.ppermute(value, axis, [(source, source ^ bits) for source in range(co...  18.9 us
    all_to_all x1, blocking collectives, gathered_form(): lax.all_to_all(packed.reshape(R, slot, C), 'rows', 0, 0, tiled=True)  9.27 us
    all_to_all x1, starting transfers between devices, gathered_form(): lax.all_to_all(jnp.broadcast_to(own, (R,) + own.shape[1:]), 'rows', 0, 0,...  7.25 us
    pallas_call x1, Pallas kernels, gathered_form(): call(functools.partial(slab_kernel, F, J, R, T, slot), [((R * slot, C), b...  5.33 us
    unnamed x24, local copies, waits for them, and re-layouts  4.97 us
    ppermute x16, waiting for transfers between devices, partners(): lax.ppermute(value, axis, [(source, source ^ bits) for source in range(co...  3.99 us
    pallas_call x1, Pallas kernels, gathered_form(): call(functools.partial(weight_kernel, F, J, R, T, part), [((27, part, C),...  3.47 us
    all_to_all x1, waiting for transfers between devices, gathered_form(): lax.all_to_all(jnp.broadcast_to(own, (R,) + own.shape[1:]), 'rows', 0, 0,...  3 us
  transfers between devices with their start and end apart: 19, of which 5 were waited for; matrix products, arithmetic and copies ran while one was open for 2% of the time, Pallas kernels for 18%

profile of v10, /device:TPU:0, one launch (start us, length us, event | category | flops | bytes accessed | tf_op | source)
XLA Modules:
  0.0 67.5 jit_solution(8781218765207747940)
XLA Ops:
  0.6 0.8 %broadcast_in_dim.7 = bf16[64,256]{1,0:T(8,128)(2,1)S(1)} reshape(bf16[4,8,2,256]{3,2,1,0:T(2,128)(2,1)} %param.9) | data formatting | bytes 65536 | tf_op jit(solution)/shard_map/broadcast_in_dim | solution.py:457
  1.4 0.7 %broadcast_in_dim.8 = bf16[8,64,256]{2,1,0:T(8,128)(2,1)} broadcast(bf16[64,256]{1,0:T(8,128)(2,1)S(1)} %broadcast_in_dim.7), dimensions={1,2} | broadcast | bytes 294912 | tf_op jit(solution)/shard_map/broadcast_in_dim | solution.py:457
  2.1 7.3 %all-to-all-start = ((bf16[8,64,256]{2,1,0:T(8,128)(2,1)}), bf16[8,64,256]{2,1,0:T(8,128)(2,1)S(1)}, u32[]{:S(2)}, u32[]{:S(2)}) async-start(bf16[8,64,256]{2,1,0:T(8,128)(2,1)} %broadcast_in_dim.8), calls=%async_computation | async-start | bytes 524288 | tf_op jit(solution)/shard_map/all_to_all | solution.py:456
  9.4 0.1 pad_add_fusion.place
  9.5 0.7 %pad_maximum_fusion.vectors = f32[2,256]{1,0:T(2,128)S(1)} fusion(f32[1,256]{1,0:T(1,128)} %bitcast.18, f32[1,256]{1,0:T(1,128)} %bitcast.19), kind=kLoop, calls=%fused_computation.1 | loop fusion | flops 512 | bytes 4096 | tf_op jit(solution)/shard_map/stack | solution.py:450
  10.2 0.9 %copy-done.9 = bf16[4,2,32,256]{3,2,1,0:T(8,128)(2,1)S(1)} copy-done((bf16[4,2,32,256]{3,2,1,0:T(8,128)(2,1)S(1)}, bf16[4,2,32,256]{3,2,1,0:T(8,128)(2,1)}, u32[]{:S(2)}) %copy-start.9) | copy-done | bytes 131096
  11.1 0.8 %shard_map.92 = (bf16[2,2,64,256]{3,2,1,0:T(8,128)(2,1)S(1)}, bf16[256,256]{1,0:T(8,128)(2,1)S(1)}, f32[2,256]{1,0:T(2,128)S(1)}, bf16[128,128]{1,0:T(8,128)(2,1...) custom-call(s32[2]{0:T(128)S(1)} %pad_add_fusion.place, ...), custom_call_target="tpu_custom_call" | custom-call | flops 1179648000 | bytes 262144 | tf_op jit(solution)/shard_map/pallas_call | solution.py:461
  11.9 0.0 copy-start.4
  11.9 0.6 copy-done.4
  12.6 0.6 copy-done.6
  13.2 0.0 collective-permute-start
  13.2 1.6 %collective-permute-start.2 = (bf16[384,128]{1,0:T(8,128)(2,1)S(1)}, bf16[384,128]{1,0:T(8,128)(2,1)S(1)}, u32[]{:S(2)}, u32[]{:S(2)}) collective-permute-start(bf16[384,128]{1,0:T(8,128)(2,1)S(1)} %get-tuple-element.34), channel_id=1, source_target_pairs={{0,3},{1,2},{2,1},{3,0},{4,7},{5,6},{6,5},{7,4},{8,11},{9,10},{10,... | collective-permute-start | bytes 294920 | tf_op jit(solution)/shard_map/ppermute | solution.py:114
  14.8 0.5 collective-permute-start.1
  15.3 0.0 collective-permute-done.refs_1_._
  15.3 3.0 %all-to-all-done.grad_rows = bf16[8,64,256]{2,1,0:T(8,128)(2,1)S(1)} async-done(((bf16[8,64,256]{2,1,0:T(8,128)(2,1)}), bf16[8,64,256]{2,1,0:T(8,128)(2,1)S(1)}, u32[]{:S(2)}, u32[]{:S(2)}) %all-to-all-start) | async-done | bytes 262176 | tf_op jit(solution)/shard_map/all_to_all | solution.py:456
  18.3 0.0 copy-start
  18.3 0.7 %copy-done = bf16[8,64,256]{2,1,0:T(8,128)(2,1)} copy-done((bf16[8,64,256]{2,1,0:T(8,128)(2,1)}, bf16[8,64,256]{2,1,0:T(8,128)(2,1)S(1)}, u32[]{:S(2)}) %copy-start) | copy-done | bytes 262168
  19.0 1.3 %collective-permute-start.4 = (bf16[8,32,256]{2,1,0:T(8,128)(2,1)S(1)}, bf16[8,32,256]{2,1,0:T(8,128)(2,1)S(1)}, u32[]{:S(2)}, u32[]{:S(2)}) collective-permute-start(bf16[8,32,256]{2,1,0:T(8,128)(2,1)S(1)} %get-tuple-element.40), channel_id=1, source_target_pairs={{1,0},{2,1},{3,2},{5,4},{6,5},{7,6},{9,8},{10,9},{11,10},{13,12},{... | collective-permute-start | bytes 393224 | tf_op jit(solution)/shard_map/ppermute | solution.py:20
  20.3 0.0 collective-permute-done.1.refs_2_
  20.3 0.0 collective-permute-done.2.refs_3_
  20.3 0.0 copy-done.7
  20.4 0.6 shard_map.93
  21.0 0.0 copy-start.5
  21.0 0.6 copy-done.5
  21.6 1.4 %collective-permute-start.3 = (bf16[2,96,256]{2,1,0:T(8,128)(2,1)S(1)}, bf16[2,96,256]{2,1,0:T(8,128)(2,1)S(1)}, u32[]{:S(2)}, u32[]{:S(2)}) collective-permute-start(bf16[2,96,256]{2,1,0:T(8,128)(2,1)S(1)} %get-tuple-element.36), channel_id=1, source_target_pairs={{4,0},{8,4},{12,8},{16,12},{20,16},{24,20},{28,24},{5,1},{9,5},{13... | collective-permute-start | bytes 294920 | tf_op jit(solution)/shard_map/ppermute | solution.py:20
  23.0 3.7 %collective-permute-start.7 = (bf16[2,128,256]{2,1,0:T(8,128)(2,1)S(1)}, bf16[2,128,256]{2,1,0:T(8,128)(2,1)S(1)}, u32[]{:S(2)}, u32[]{:S(2)}) collective-permute-start(bf16[2,128,256]{2,1,0:T(8,128)(2,1)S(1)} %get-tuple-element.43.refs_0_), channel_id=1, source_target_pairs={{0,16},{4,20},{8,24},{12,28},{16,0},{20,4},{24,8},{28,12},{1,17},{... | collective-permute-start | bytes 393224 | tf_op jit(solution)/shard_map/ppermute | solution.py:114
  26.7 1.5 %collective-permute-start.6 = (bf16[2,128,256]{2,1,0:T(8,128)(2,1)S(1)}, bf16[2,128,256]{2,1,0:T(8,128)(2,1)S(1)}, u32[]{:S(2)}, u32[]{:S(2)}) collective-permute-start(bf16[2,128,256]{2,1,0:T(8,128)(2,1)S(1)} %get-tuple-element.43.refs_0_), channel_id=1, source_target_pairs={{0,8},{4,12},{8,0},{12,4},{16,24},{20,28},{24,16},{28,20},{1,9},{5... | collective-permute-start | bytes 393224 | tf_op jit(solution)/shard_map/ppermute | solution.py:114
  28.2 1.0 %collective-permute-done.3.under = bf16[2,96,256]{2,1,0:T(8,128)(2,1)S(1)} collective-permute-done((bf16[2,96,256]{2,1,0:T(8,128)(2,1)S(1)}, bf16[2,96,256]{2,1,0:T(8,128)(2,1)S(1)}, u32[]{:S(2)}, u32[]{:S(2)}) %collective-permute-start.3) | collective-permute-done | bytes 98336 | tf_op jit(solution)/shard_map/ppermute | solution.py:20
  29.2 0.0 collective-permute-done.4.following
  29.2 0.0 copy-done.3
  29.2 0.6 copy-done.11
  29.8 0.0 copy-done.10
  29.8 5.3 %shard_map.95 = (bf16[128,256]{1,0:T(8,128)(2,1)}, bf16[256,256]{1,0:T(8,128)(2,1)}) custom-call(s32[2]{0:T(128)} %copy-done.7, bf16[2,2,64,256]{3,2,1,0:T(8,128)(2,1)} %copy-done.3, bf16[2,2,32,256]{3,2,1,0:T(8,128)(2,1)} %copy-done.5, bf16[2,96,256]{2,1,0:T(8,128)(2,1)} %copy-done.11, bf16[27,256,256]{2,1,0:T(8,128)(2,1)} %bitcast.16, ...), custom_call_target="tpu_custom_call" | custom-call | flops 452984832 | bytes 3538944 | tf_op jit(solution)/shard_map/pallas_call | solution.py:486
  35.2 0.4 collective-permute-done.7.refs_2_
  35.5 0.1 collective-permute-done.6.refs_1_
  35.6 0.8 %copy-done.2 = bf16[128,256]{1,0:T(8,128)(2,1)S(1)} copy-done((bf16[128,256]{1,0:T(8,128)(2,1)S(1)}, bf16[128,256]{1,0:T(8,128)(2,1)}, u32[]{:S(2)}) %copy-start.2) | copy-done | bytes 65560
  36.5 1.8 %collective-permute-start.13 = (bf16[8,64,256]{2,1,0:T(8,128)(2,1)S(1)}, bf16[8,64,256]{2,1,0:T(8,128)(2,1)S(1)}, u32[]{:S(2)}, u32[]{:S(2)}) collective-permute-start(bf16[8,64,256]{2,1,0:T(8,128)(2,1)S(1)} %get-tuple-element.47.refs_0_), channel_id=1, source_target_pairs={{0,2},{1,3},{2,0},{3,1},{4,6},{5,7},{6,4},{7,5},{8,10},{9,11},{10,... | collective-permute-start | bytes 786440 | tf_op jit(solution)/shard_map/ppermute | solution.py:114
  38.3 3.0 %collective-permute-start.5 = (bf16[2,128,256]{2,1,0:T(8,128)(2,1)S(1)}, bf16[2,128,256]{2,1,0:T(8,128)(2,1)S(1)}, u32[]{:S(2)}, u32[]{:S(2)}) collective-permute-start(bf16[2,128,256]{2,1,0:T(8,128)(2,1)S(1)} %get-tuple-element.43.refs_0_), channel_id=1, source_target_pairs={{0,4},{4,0},{8,12},{12,8},{16,20},{20,16},{24,28},{28,24},{1,5},{5... | collective-permute-start | bytes 393224 | tf_op jit(solution)/shard_map/ppermute | solution.py:114
  41.3 0.0 collective-permute-start.10
  41.3 0.0 collective-permute-start.12
  41.3 3.5 %collective-permute-done.13.refs_2_ = bf16[8,64,256]{2,1,0:T(8,128)(2,1)S(1)} collective-permute-done((bf16[8,64,256]{2,1,0:T(8,128)(2,1)S(1)}, bf16[8,64,256]{2,1,0:T(8,128)(2,1)S(1)}, u32[]{:S(2)}, u32[]{:S(2)}) %collective-permute-start.13) | collective-permute-done | bytes 262176 | tf_op jit(solution)/shard_map/ppermute | solution.py:114
  44.8 0.0 collective-permute-start.14
  44.8 2.9 %collective-permute-start.9 = (bf16[2,128,256]{2,1,0:T(8,128)(2,1)S(1)}, bf16[2,128,256]{2,1,0:T(8,128)(2,1)S(1)}, u32[]{:S(2)}, u32[]{:S(2)}) collective-permute-start(bf16[2,128,256]{2,1,0:T(8,128)(2,1)S(1)} %get-tuple-element.45.refs_4_), channel_id=1, source_target_pairs={{0,4},{4,0},{8,12},{12,8},{16,20},{20,16},{24,28},{28,24},{1,5},{5... | collective-permute-start | bytes 393224 | tf_op jit(solution)/shard_map/ppermute | solution.py:114
  47.7 0.0 collective-permute-done.5.refs_0_.refs_1_
  47.7 0.1 collective-permute-start.8
  47.8 0.0 collective-permute-done.10.refs_6_
  47.8 2.0 %collective-permute-start.11 = (bf16[2,128,256]{2,1,0:T(8,128)(2,1)S(1)}, bf16[2,128,256]{2,1,0:T(8,128)(2,1)S(1)}, u32[]{:S(2)}, u32[]{:S(2)}) collective-permute-start(bf16[2,128,256]{2,1,0:T(8,128)(2,1)S(1)} %collective-permute-done.10.refs_6_), channel_id=1, source_target_pairs={{0,4},{4,0},{8,12},{12,8},{16,20},{20,16},{24,28},{28,24},{1,5},{5... | collective-permute-start | bytes 393224 | tf_op jit(solution)/shard_map/ppermute | solution.py:114
  49.7 9.3 %all_to_all.10.received = bf16[8,16,256]{2,1,0:T(8,128)(2,1)S(1)} all-to-all(bf16[8,16,256]{2,1,0:T(8,128)(2,1)S(1)} %bitcast.14), channel_id=1, replica_groups=mesh['rows'=8,'tm'=4] {'rows'}, dimensions={0} | all-to-all | bytes 131072 | tf_op jit(solution)/shard_map/all_to_all | solution.py:517
  59.0 0.6 copy.15
  59.7 0.0 collective-permute-done.8.refs_1_.refs_3_
  59.7 0.0 collective-permute-done.9.refs_2_.refs_5_
  59.7 0.0 collective-permute-done.11.refs_3_.refs_7_
  59.7 0.1 shard_map.97
  59.8 0.0 collective-permute-start.15
  59.8 0.9 %collective-permute-start.16 = (f32[1,64]{1,0:T(1,128)S(1)}, f32[1,64]{1,0:T(1,128)S(1)}, u32[]{:S(2)}, u32[]{:S(2)}) collective-permute-start(f32[1,64]{1,0:T(1,128)S(1)} %get-tuple-element.52), channel_id=1, source_target_pairs={{0,2},{1,3},{2,0},{3,1},{4,6},{5,7},{6,4},{7,5},{8,10},{9,11},{10,... | collective-permute-start | bytes 776 | tf_op jit(solution)/shard_map/ppermute | solution.py:114
  60.7 0.9 %collective-permute-start.17 = (f32[1,64]{1,0:T(1,128)S(1)}, f32[1,64]{1,0:T(1,128)S(1)}, u32[]{:S(2)}, u32[]{:S(2)}) collective-permute-start(f32[1,64]{1,0:T(1,128)S(1)} %get-tuple-element.53), channel_id=1, source_target_pairs={{0,3},{1,2},{2,1},{3,0},{4,7},{5,6},{6,5},{7,4},{8,11},{9,10},{10,... | collective-permute-start | bytes 776 | tf_op jit(solution)/shard_map/ppermute | solution.py:114
  61.6 0.0 collective-permute-done.12.refs_1_
  61.7 0.0 collective-permute-done.14.refs_3_
  61.7 1.8 %shard_map.98 = (bf16[2,8,288,256]{3,2,1,0:T(8,128)(2,1)S(1)}, f32[1,64]{1,0:T(1,128)}) custom-call(s32[2]{0:T(128)S(1)} %copy-done.8, bf16[8,64,256]{2,1,0:T(8,128)(2,1)S(1)} %get-tuple-element.47.refs_0_, bf16[8,64,256]{2,1,0:T(8,128)(2,1)S(1)} %collective-permute-done.12.refs_1_, bf16[8,64,256]{2,1,0:T(8,128)(2,1)S(1)} %collective-permute-done.13.refs_2_, ...), custom_call_target="tpu_custom_call" | custom-call | flops 1769472000 | bytes 1048576 | tf_op jit(solution)/shard_map/pallas_call | solution.py:524
  63.4 3.5 %shard_map.99 = (f32[27,64,256]{2,1,0:T(8,128)}, f32[1,64]{1,0:T(1,128)S(1)}) custom-call(s32[2]{0:T(128)S(1)} %copy-done.8, f32[1,64]{1,0:T(1,128)S(1)} %get-tuple-element.46.gain, bf16[2,8,288,256]{3,2,1,0:T(8,128)(2,1)S(1)} %get-tuple-element.48.grads, bf16[2,128,256]{2,1,0:T(8,128)(2,1)S(1)} %get-tuple-element.43.refs_0_, ...), custom_call_target="tpu_custom_call" | custom-call | flops 3932160000 | bytes 3538944 | tf_op jit(solution)/shard_map/pallas_call | solution.py:530
  66.9 0.0 collective-permute-done.15.refs_1_
  66.9 0.0 collective-permute-done.16.refs_2_
  66.9 0.0 collective-permute-done.17.refs_3_
  66.9 0.5 shard_map.100
  (15 shorter events, 0.1 us)
Async XLA Ops:
  2.1 16.2 %all-to-all-start = ((bf16[8,64,256]{2,1,0:T(8,128)(2,1)}), bf16[8,64,256]{2,1,0:T(8,128)(2,1)S(1)}, u32[]{:S(2)}, u32[]{:S(2)}) async-start(bf16[8,64,256]{2,1,0:T(8,128)(2,1)} %broadcast_in_dim.8), calls=%async_computation | async-start | bytes 524288 | tf_op jit(solution)/shard_map/all_to_all | solution.py:456
  9.5 10.9 %copy-start.7 = (s32[2]{0:T(128)}, s32[2]{0:T(128)S(1)}, u32[]{:S(2)}) copy-start(s32[2]{0:T(128)S(1)} %pad_add_fusion.place) | copy-start | bytes 28
  10.2 0.9 %copy-start.9 = (bf16[4,2,32,256]{3,2,1,0:T(8,128)(2,1)S(1)}, bf16[4,2,32,256]{3,2,1,0:T(8,128)(2,1)}, u32[]{:S(2)}) copy-start(bf16[4,2,32,256]{3,2,1,0:T(8,128)(2,1)} %param.5) | copy-start | bytes 393220
  11.9 0.7 copy-start.4
  12.6 0.6 copy-start.6
  13.2 16.0 %copy-start.3 = (bf16[2,2,64,256]{3,2,1,0:T(8,128)(2,1)}, bf16[2,2,64,256]{3,2,1,0:T(8,128)(2,1)S(1)}, u32[]{:S(2)}) copy-start(bf16[2,2,64,256]{3,2,1,0:T(8,128)(2,1)S(1)} %get-tuple-element.30.planes) | copy-start | bytes 393220
  13.2 2.1 %collective-permute-start = (bf16[384,128]{1,0:T(8,128)(2,1)S(1)}, bf16[384,128]{1,0:T(8,128)(2,1)S(1)}, u32[]{:S(2)}, u32[]{:S(2)}) collective-permute-start(bf16[384,128]{1,0:T(8,128)(2,1)S(1)} %get-tuple-element.32), channel_id=1, source_target_pairs={{0,1},{1,0},{2,3},{3,2},{4,5},{5,4},{6,7},{7,6},{8,9},{9,8},{10,11... | collective-permute-start | bytes 294920 | tf_op jit(solution)/shard_map/ppermute | solution.py:114
  13.2 7.2 %collective-permute-start.2 = (bf16[384,128]{1,0:T(8,128)(2,1)S(1)}, bf16[384,128]{1,0:T(8,128)(2,1)S(1)}, u32[]{:S(2)}, u32[]{:S(2)}) collective-permute-start(bf16[384,128]{1,0:T(8,128)(2,1)S(1)} %get-tuple-element.34), channel_id=1, source_target_pairs={{0,3},{1,2},{2,1},{3,0},{4,7},{5,6},{6,5},{7,4},{8,11},{9,10},{10,... | collective-permute-start | bytes 294920 | tf_op jit(solution)/shard_map/ppermute | solution.py:114
  14.8 5.5 %collective-permute-start.1 = (bf16[128,128]{1,0:T(8,128)(2,1)S(1)}, bf16[128,128]{1,0:T(8,128)(2,1)S(1)}, u32[]{:S(2)}, u32[]{:S(2)}) collective-permute-start(bf16[128,128]{1,0:T(8,128)(2,1)S(1)} %get-tuple-element.33), channel_id=1, source_target_pairs={{0,2},{1,3},{2,0},{3,1},{4,6},{5,7},{6,4},{7,5},{8,10},{9,11},{10,... | collective-permute-start | bytes 98312 | tf_op jit(solution)/shard_map/ppermute | solution.py:114
  18.3 0.7 %copy-start = (bf16[8,64,256]{2,1,0:T(8,128)(2,1)}, bf16[8,64,256]{2,1,0:T(8,128)(2,1)S(1)}, u32[]{:S(2)}) copy-start(bf16[8,64,256]{2,1,0:T(8,128)(2,1)S(1)} %get-tuple-element.39.gathered.refs_3_) | copy-start | bytes 786436
  19.0 10.1 %collective-permute-start.4 = (bf16[8,32,256]{2,1,0:T(8,128)(2,1)S(1)}, bf16[8,32,256]{2,1,0:T(8,128)(2,1)S(1)}, u32[]{:S(2)}, u32[]{:S(2)}) collective-permute-start(bf16[8,32,256]{2,1,0:T(8,128)(2,1)S(1)} %get-tuple-element.40), channel_id=1, source_target_pairs={{1,0},{2,1},{3,2},{5,4},{6,5},{7,6},{9,8},{10,9},{11,10},{13,12},{... | collective-permute-start | bytes 393224 | tf_op jit(solution)/shard_map/ppermute | solution.py:20
  21.0 0.6 copy-start.5
  21.6 14.0 %copy-start.1 = (bf16[8,64,256]{2,1,0:T(8,128)(2,1)S(1)}, bf16[8,64,256]{2,1,0:T(8,128)(2,1)}, u32[]{:S(2)}) copy-start(bf16[8,64,256]{2,1,0:T(8,128)(2,1)} %copy-done) | copy-start | bytes 786436
  21.6 7.5 %collective-permute-start.3 = (bf16[2,96,256]{2,1,0:T(8,128)(2,1)S(1)}, bf16[2,96,256]{2,1,0:T(8,128)(2,1)S(1)}, u32[]{:S(2)}, u32[]{:S(2)}) collective-permute-start(bf16[2,96,256]{2,1,0:T(8,128)(2,1)S(1)} %get-tuple-element.36), channel_id=1, source_target_pairs={{4,0},{8,4},{12,8},{16,12},{20,16},{24,20},{28,24},{5,1},{9,5},{13... | collective-permute-start | bytes 294920 | tf_op jit(solution)/shard_map/ppermute | solution.py:20
  23.0 12.5 %collective-permute-start.7 = (bf16[2,128,256]{2,1,0:T(8,128)(2,1)S(1)}, bf16[2,128,256]{2,1,0:T(8,128)(2,1)S(1)}, u32[]{:S(2)}, u32[]{:S(2)}) collective-permute-start(bf16[2,128,256]{2,1,0:T(8,128)(2,1)S(1)} %get-tuple-element.43.refs_0_), channel_id=1, source_target_pairs={{0,16},{4,20},{8,24},{12,28},{16,0},{20,4},{24,8},{28,12},{1,17},{... | collective-permute-start | bytes 393224 | tf_op jit(solution)/shard_map/ppermute | solution.py:114
  26.7 8.9 %collective-permute-start.6 = (bf16[2,128,256]{2,1,0:T(8,128)(2,1)S(1)}, bf16[2,128,256]{2,1,0:T(8,128)(2,1)S(1)}, u32[]{:S(2)}, u32[]{:S(2)}) collective-permute-start(bf16[2,128,256]{2,1,0:T(8,128)(2,1)S(1)} %get-tuple-element.43.refs_0_), channel_id=1, source_target_pairs={{0,8},{4,12},{8,0},{12,4},{16,24},{20,28},{24,16},{28,20},{1,9},{5... | collective-permute-start | bytes 393224 | tf_op jit(solution)/shard_map/ppermute | solution.py:114
  29.2 0.6 copy-start.11
  29.2 0.7 %copy-start.10 = (bf16[8,32,256]{2,1,0:T(8,128)(2,1)}, bf16[8,32,256]{2,1,0:T(8,128)(2,1)S(1)}, u32[]{:S(2)}) copy-start(bf16[8,32,256]{2,1,0:T(8,128)(2,1)S(1)} %collective-permute-done.4.following) | copy-start | bytes 393220
  29.8 31.8 %copy-start.8 = (s32[2]{0:T(128)S(1)}, s32[2]{0:T(128)}, u32[]{:S(2)}) copy-start(s32[2]{0:T(128)} %copy-done.7) | copy-start | bytes 28
  35.6 0.8 %copy-start.2 = (bf16[128,256]{1,0:T(8,128)(2,1)S(1)}, bf16[128,256]{1,0:T(8,128)(2,1)}, u32[]{:S(2)}) copy-start(bf16[128,256]{1,0:T(8,128)(2,1)} %get-tuple-element.41.refs_0_) | copy-start | bytes 196612
  36.5 8.3 %collective-permute-start.13 = (bf16[8,64,256]{2,1,0:T(8,128)(2,1)S(1)}, bf16[8,64,256]{2,1,0:T(8,128)(2,1)S(1)}, u32[]{:S(2)}, u32[]{:S(2)}) collective-permute-start(bf16[8,64,256]{2,1,0:T(8,128)(2,1)S(1)} %get-tuple-element.47.refs_0_), channel_id=1, source_target_pairs={{0,2},{1,3},{2,0},{3,1},{4,6},{5,7},{6,4},{7,5},{8,10},{9,11},{10,... | collective-permute-start | bytes 786440 | tf_op jit(solution)/shard_map/ppermute | solution.py:114
  38.3 9.4 %collective-permute-start.5 = (bf16[2,128,256]{2,1,0:T(8,128)(2,1)S(1)}, bf16[2,128,256]{2,1,0:T(8,128)(2,1)S(1)}, u32[]{:S(2)}, u32[]{:S(2)}) collective-permute-start(bf16[2,128,256]{2,1,0:T(8,128)(2,1)S(1)} %get-tuple-element.43.refs_0_), channel_id=1, source_target_pairs={{0,4},{4,0},{8,12},{12,8},{16,20},{20,16},{24,28},{28,24},{1,5},{5... | collective-permute-start | bytes 393224 | tf_op jit(solution)/shard_map/ppermute | solution.py:114
  41.3 6.5 %collective-permute-start.10 = (bf16[2,128,256]{2,1,0:T(8,128)(2,1)S(1)}, bf16[2,128,256]{2,1,0:T(8,128)(2,1)S(1)}, u32[]{:S(2)}, u32[]{:S(2)}) collective-permute-start(bf16[2,128,256]{2,1,0:T(8,128)(2,1)S(1)} %get-tuple-element.45.refs_4_), channel_id=1, source_target_pairs={{0,8},{4,12},{8,0},{12,4},{16,24},{20,28},{24,16},{28,20},{1,9},{5... | collective-permute-start | bytes 393224 | tf_op jit(solution)/shard_map/ppermute | solution.py:114
  41.3 20.4 %collective-permute-start.12 = (bf16[8,64,256]{2,1,0:T(8,128)(2,1)S(1)}, bf16[8,64,256]{2,1,0:T(8,128)(2,1)S(1)}, u32[]{:S(2)}, u32[]{:S(2)}) collective-permute-start(bf16[8,64,256]{2,1,0:T(8,128)(2,1)S(1)} %get-tuple-element.47.refs_0_), channel_id=1, source_target_pairs={{0,1},{1,0},{2,3},{3,2},{4,5},{5,4},{6,7},{7,6},{8,9},{9,8},{10,11... | collective-permute-start | bytes 786440 | tf_op jit(solution)/shard_map/ppermute | solution.py:114
  44.8 16.9 %collective-permute-start.14 = (bf16[8,64,256]{2,1,0:T(8,128)(2,1)S(1)}, bf16[8,64,256]{2,1,0:T(8,128)(2,1)S(1)}, u32[]{:S(2)}, u32[]{:S(2)}) collective-permute-start(bf16[8,64,256]{2,1,0:T(8,128)(2,1)S(1)} %collective-permute-done.13.refs_2_), channel_id=1, source_target_pairs={{0,1},{1,0},{2,3},{3,2},{4,5},{5,4},{6,7},{7,6},{8,9},{9,8},{10,11... | collective-permute-start | bytes 786440 | tf_op jit(solution)/shard_map/ppermute | solution.py:114
  44.8 14.9 %collective-permute-start.9 = (bf16[2,128,256]{2,1,0:T(8,128)(2,1)S(1)}, bf16[2,128,256]{2,1,0:T(8,128)(2,1)S(1)}, u32[]{:S(2)}, u32[]{:S(2)}) collective-permute-start(bf16[2,128,256]{2,1,0:T(8,128)(2,1)S(1)} %get-tuple-element.45.refs_4_), channel_id=1, source_target_pairs={{0,4},{4,0},{8,12},{12,8},{16,20},{20,16},{24,28},{28,24},{1,5},{5... | collective-permute-start | bytes 393224 | tf_op jit(solution)/shard_map/ppermute | solution.py:114
  47.7 12.0 %collective-permute-start.8 = (bf16[2,128,256]{2,1,0:T(8,128)(2,1)S(1)}, bf16[2,128,256]{2,1,0:T(8,128)(2,1)S(1)}, u32[]{:S(2)}, u32[]{:S(2)}) collective-permute-start(bf16[2,128,256]{2,1,0:T(8,128)(2,1)S(1)} %get-tuple-element.44.refs_2_), channel_id=1, source_target_pairs={{0,4},{4,0},{8,12},{12,8},{16,20},{20,16},{24,28},{28,24},{1,5},{5... | collective-permute-start | bytes 393224 | tf_op jit(solution)/shard_map/ppermute | solution.py:114
  47.8 11.9 %collective-permute-start.11 = (bf16[2,128,256]{2,1,0:T(8,128)(2,1)S(1)}, bf16[2,128,256]{2,1,0:T(8,128)(2,1)S(1)}, u32[]{:S(2)}, u32[]{:S(2)}) collective-permute-start(bf16[2,128,256]{2,1,0:T(8,128)(2,1)S(1)} %collective-permute-done.10.refs_6_), channel_id=1, source_target_pairs={{0,4},{4,0},{8,12},{12,8},{16,20},{20,16},{24,28},{28,24},{1,5},{5... | collective-permute-start | bytes 393224 | tf_op jit(solution)/shard_map/ppermute | solution.py:114
  59.8 7.1 %collective-permute-start.15 = (f32[1,64]{1,0:T(1,128)S(1)}, f32[1,64]{1,0:T(1,128)S(1)}, u32[]{:S(2)}, u32[]{:S(2)}) collective-permute-start(f32[1,64]{1,0:T(1,128)S(1)} %get-tuple-element.51), channel_id=1, source_target_pairs={{0,1},{1,0},{2,3},{3,2},{4,5},{5,4},{6,7},{7,6},{8,9},{9,8},{10,11... | collective-permute-start | bytes 776 | tf_op jit(solution)/shard_map/ppermute | solution.py:114
  59.8 7.1 %collective-permute-start.16 = (f32[1,64]{1,0:T(1,128)S(1)}, f32[1,64]{1,0:T(1,128)S(1)}, u32[]{:S(2)}, u32[]{:S(2)}) collective-permute-start(f32[1,64]{1,0:T(1,128)S(1)} %get-tuple-element.52), channel_id=1, source_target_pairs={{0,2},{1,3},{2,0},{3,1},{4,6},{5,7},{6,4},{7,5},{8,10},{9,11},{10,... | collective-permute-start | bytes 776 | tf_op jit(solution)/shard_map/ppermute | solution.py:114
  60.7 6.2 %collective-permute-start.17 = (f32[1,64]{1,0:T(1,128)S(1)}, f32[1,64]{1,0:T(1,128)S(1)}, u32[]{:S(2)}, u32[]{:S(2)}) collective-permute-start(f32[1,64]{1,0:T(1,128)S(1)} %get-tuple-element.53), channel_id=1, source_target_pairs={{0,3},{1,2},{2,1},{3,0},{4,7},{5,6},{6,5},{7,4},{8,11},{9,10},{10,... | collective-permute-start | bytes 776 | tf_op jit(solution)/shard_map/ppermute | solution.py:114

commit v11 on v6

--- a/solution.py
+++ b/solution.py
@@ -121,7 +121,7 @@
         if k & (k - 1) == 0:
             blocks[k] = partners(value, axis, k)
     if gate is not None:
-        held = [k for k in blocks if k > 1]
+        held = [k for k in blocks if k > 0]
         blocks.update(zip(held, gate([blocks[k] for k in held])))
     for k in range(1, count):
         low = k & -k

time: 65.2 us -> 65.7 us (level)
  no operation moved by 1% of the time
where the time goes in v11:
time: 65.7 us; the launch traced here: 65.2 us
  starting transfers between devices  32.3 us (49%)
  waiting for transfers between devices  12.8 us (19%)
  Pallas kernels  12.1 us (18%)
  local copies, waits for them, and re-layouts  5.86 us (9%)
  other arithmetic  1.3 us (2%)
  between operations  0.85 us (1%)
    ppermute x16, starting transfers between devices, partners(): lax.ppermute(value, axis, [(source, source ^ bits) for source in range(co...  19.1 us
    all_to_all x1, starting transfers between devices, gathered_form(): lax.all_to_all(jnp.broadcast_to(own, (R,) + own.shape[1:]), 'rows', 0, 0,...  7.25 us
    all_to_all x1, waiting for transfers between devices, gathered_form(): lax.all_to_all(packed.reshape(R, slot, C), 'rows', 0, 0, tiled=True)  6.26 us
    pallas_call x1, Pallas kernels, gathered_form(): call(functools.partial(slab_kernel, F, J, R, T, slot), [((R * slot, C), b...  5.33 us
    unnamed x22, local copies, waits for them, and re-layouts  3.7 us
    all_to_all x1, waiting for transfers between devices, gathered_form(): lax.all_to_all(jnp.broadcast_to(own, (R,) + own.shape[1:]), 'rows', 0, 0,...  3.65 us
    pallas_call x1, Pallas kernels, gathered_form(): call(functools.partial(weight_kernel, F, J, R, T, part), [((27, part, C),...  3.43 us
    all_to_all x1, starting transfers between devices, gathered_form(): lax.all_to_all(packed.reshape(R, slot, C), 'rows', 0, 0, tiled=True)  3.35 us
  transfers between devices with their start and end apart: 20, of which 5 were waited for; matrix products, arithmetic and copies ran while one was open for 3% of the time, Pallas kernels for 11%

profile of v11, /device:TPU:0, one launch (start us, length us, event | category | flops | bytes accessed | tf_op | source)
XLA Modules:
  0.0 65.2 jit_solution(1965943851241139991)
XLA Ops:
  0.6 0.8 %broadcast_in_dim.7 = bf16[64,256]{1,0:T(8,128)(2,1)S(1)} reshape(bf16[4,8,2,256]{3,2,1,0:T(2,128)(2,1)} %param.9) | data formatting | bytes 65536 | tf_op jit(solution)/shard_map/broadcast_in_dim | solution.py:449
  1.4 0.7 %broadcast_in_dim.8 = bf16[8,64,256]{2,1,0:T(8,128)(2,1)} broadcast(bf16[64,256]{1,0:T(8,128)(2,1)S(1)} %broadcast_in_dim.7), dimensions={1,2} | broadcast | bytes 294912 | tf_op jit(solution)/shard_map/broadcast_in_dim | solution.py:449
  2.1 7.3 %all-to-all-start = ((bf16[8,64,256]{2,1,0:T(8,128)(2,1)}), bf16[8,64,256]{2,1,0:T(8,128)(2,1)S(1)}, u32[]{:S(2)}, u32[]{:S(2)}) async-start(bf16[8,64,256]{2,1,0:T(8,128)(2,1)} %broadcast_in_dim.8), calls=%async_computation | async-start | bytes 524288 | tf_op jit(solution)/shard_map/all_to_all | solution.py:448
  9.4 0.1 pad_add_fusion.place
  9.5 0.7 %pad_maximum_fusion.vectors = f32[2,256]{1,0:T(2,128)S(1)} fusion(f32[1,256]{1,0:T(1,128)} %bitcast.18, f32[1,256]{1,0:T(1,128)} %bitcast.19), kind=kLoop, calls=%fused_computation.1 | loop fusion | flops 512 | bytes 4096 | tf_op jit(solution)/shard_map/stack | solution.py:442
  10.2 0.9 %copy-done.8 = bf16[4,2,32,256]{3,2,1,0:T(8,128)(2,1)S(1)} copy-done((bf16[4,2,32,256]{3,2,1,0:T(8,128)(2,1)S(1)}, bf16[4,2,32,256]{3,2,1,0:T(8,128)(2,1)}, u32[]{:S(2)}) %copy-start.8) | copy-done | bytes 131096
  11.1 0.8 %shard_map.92 = (bf16[2,2,64,256]{3,2,1,0:T(8,128)(2,1)S(1)}, bf16[256,256]{1,0:T(8,128)(2,1)S(1)}, f32[2,256]{1,0:T(2,128)S(1)}, bf16[128,128]{1,0:T(8,128)(2,1...) custom-call(s32[2]{0:T(128)S(1)} %pad_add_fusion.place, ...), custom_call_target="tpu_custom_call" | custom-call | flops 1179648000 | bytes 262144 | tf_op jit(solution)/shard_map/pallas_call | solution.py:453
  11.9 0.0 copy-start.5
  11.9 0.6 copy-done.5
  12.5 0.0 collective-permute-start
  12.5 1.6 %collective-permute-start.2 = (bf16[384,128]{1,0:T(8,128)(2,1)S(1)}, bf16[384,128]{1,0:T(8,128)(2,1)S(1)}, u32[]{:S(2)}, u32[]{:S(2)}) collective-permute-start(bf16[384,128]{1,0:T(8,128)(2,1)S(1)} %get-tuple-element.32), channel_id=1, source_target_pairs={{0,3},{1,2},{2,1},{3,0},{4,7},{5,6},{6,5},{7,4},{8,11},{9,10},{10,... | collective-permute-start | bytes 294920 | tf_op jit(solution)/shard_map/ppermute | solution.py:114
  14.1 0.5 collective-permute-start.1
  14.7 3.6 %all-to-all-done.grad_rows = bf16[8,64,256]{2,1,0:T(8,128)(2,1)S(1)} async-done(((bf16[8,64,256]{2,1,0:T(8,128)(2,1)}), bf16[8,64,256]{2,1,0:T(8,128)(2,1)S(1)}, u32[]{:S(2)}, u32[]{:S(2)}) %all-to-all-start) | async-done | bytes 262176 | tf_op jit(solution)/shard_map/all_to_all | solution.py:448
  18.3 0.0 copy-start.1
  18.3 1.3 %collective-permute-start.4 = (bf16[8,32,256]{2,1,0:T(8,128)(2,1)S(1)}, bf16[8,32,256]{2,1,0:T(8,128)(2,1)S(1)}, u32[]{:S(2)}, u32[]{:S(2)}) collective-permute-start(bf16[8,32,256]{2,1,0:T(8,128)(2,1)S(1)} %get-tuple-element.38), channel_id=1, source_target_pairs={{1,0},{2,1},{3,2},{5,4},{6,5},{7,6},{9,8},{10,9},{11,10},{13,12},{... | collective-permute-start | bytes 393224 | tf_op jit(solution)/shard_map/ppermute | solution.py:20
  19.6 0.0 collective-permute-done.1.refs_2_
  19.7 0.0 collective-permute-done.refs_1_
  19.7 0.0 collective-permute-done.2.refs_3_
  19.7 0.0 copy-done.6
  19.7 0.6 shard_map.93
  20.3 0.0 copy-start.4
  20.3 0.6 copy-done.4
  21.0 1.3 %collective-permute-start.3 = (bf16[2,96,256]{2,1,0:T(8,128)(2,1)S(1)}, bf16[2,96,256]{2,1,0:T(8,128)(2,1)S(1)}, u32[]{:S(2)}, u32[]{:S(2)}) collective-permute-start(bf16[2,96,256]{2,1,0:T(8,128)(2,1)S(1)} %get-tuple-element.34), channel_id=1, source_target_pairs={{4,0},{8,4},{12,8},{16,12},{20,16},{24,20},{28,24},{5,1},{9,5},{13... | collective-permute-start | bytes 294920 | tf_op jit(solution)/shard_map/ppermute | solution.py:20
  22.2 3.7 %collective-permute-start.7 = (bf16[2,128,256]{2,1,0:T(8,128)(2,1)S(1)}, bf16[2,128,256]{2,1,0:T(8,128)(2,1)S(1)}, u32[]{:S(2)}, u32[]{:S(2)}) collective-permute-start(bf16[2,128,256]{2,1,0:T(8,128)(2,1)S(1)} %get-tuple-element.41.refs_0_), channel_id=1, source_target_pairs={{0,16},{4,20},{8,24},{12,28},{16,0},{20,4},{24,8},{28,12},{1,17},{... | collective-permute-start | bytes 393224 | tf_op jit(solution)/shard_map/ppermute | solution.py:114
  25.9 1.5 %collective-permute-start.6 = (bf16[2,128,256]{2,1,0:T(8,128)(2,1)S(1)}, bf16[2,128,256]{2,1,0:T(8,128)(2,1)S(1)}, u32[]{:S(2)}, u32[]{:S(2)}) collective-permute-start(bf16[2,128,256]{2,1,0:T(8,128)(2,1)S(1)} %get-tuple-element.41.refs_0_), channel_id=1, source_target_pairs={{0,8},{4,12},{8,0},{12,4},{16,24},{20,28},{24,16},{28,20},{1,9},{5... | collective-permute-start | bytes 393224 | tf_op jit(solution)/shard_map/ppermute | solution.py:114
  27.4 0.6 collective-permute-start.5
  28.0 0.4 collective-permute-done.3.under
  28.4 1.8 %collective-permute-start.13 = (bf16[8,64,256]{2,1,0:T(8,128)(2,1)S(1)}, bf16[8,64,256]{2,1,0:T(8,128)(2,1)S(1)}, u32[]{:S(2)}, u32[]{:S(2)}) collective-permute-start(bf16[8,64,256]{2,1,0:T(8,128)(2,1)S(1)} %get-tuple-element.37.gathered.refs_0_), channel_id=1, source_target_pairs={{0,2},{1,3},{2,0},{3,1},{4,6},{5,7},{6,4},{7,5},{8,10},{9,11},{10,... | collective-permute-start | bytes 786440 | tf_op jit(solution)/shard_map/ppermute | solution.py:114
  30.2 0.0 collective-permute-done.4.following
  30.2 0.0 copy-done.3
  30.2 0.0 copy-done.1
  30.2 0.6 copy-done.9
  30.9 5.3 %shard_map.95 = (bf16[128,256]{1,0:T(8,128)(2,1)}, bf16[256,256]{1,0:T(8,128)(2,1)}) custom-call(s32[2]{0:T(128)} %copy-done.6, bf16[2,2,64,256]{3,2,1,0:T(8,128)(2,1)} %copy-done.3, bf16[2,2,32,256]{3,2,1,0:T(8,128)(2,1)} %copy-done.4, bf16[2,96,256]{2,1,0:T(8,128)(2,1)} %copy-done.10, bf16[27,256,256]{2,1,0:T(8,128)(2,1)} %bitcast.16, ...), custom_call_target="tpu_custom_call" | custom-call | flops 452984832 | bytes 3538944 | tf_op jit(solution)/shard_map/pallas_call | solution.py:478
  36.2 0.0 collective-permute-done.7.refs_3_
  36.2 0.0 collective-permute-done.6.refs_2_
  36.2 0.0 collective-permute-done.5.refs_1_
  36.2 1.4 %collective-permute-start.10 = (bf16[2,128,256]{2,1,0:T(8,128)(2,1)S(1)}, bf16[2,128,256]{2,1,0:T(8,128)(2,1)S(1)}, u32[]{:S(2)}, u32[]{:S(2)}) collective-permute-start(bf16[2,128,256]{2,1,0:T(8,128)(2,1)S(1)} %get-tuple-element.44.refs_4_), channel_id=1, source_target_pairs={{0,8},{4,12},{8,0},{12,4},{16,24},{20,28},{24,16},{28,20},{1,9},{5... | collective-permute-start | bytes 393224 | tf_op jit(solution)/shard_map/ppermute | solution.py:114
  37.6 2.1 %collective-permute-start.9 = (bf16[2,128,256]{2,1,0:T(8,128)(2,1)S(1)}, bf16[2,128,256]{2,1,0:T(8,128)(2,1)S(1)}, u32[]{:S(2)}, u32[]{:S(2)}) collective-permute-start(bf16[2,128,256]{2,1,0:T(8,128)(2,1)S(1)} %get-tuple-element.44.refs_4_), channel_id=1, source_target_pairs={{0,4},{4,0},{8,12},{12,8},{16,20},{20,16},{24,28},{28,24},{1,5},{5... | collective-permute-start | bytes 393224 | tf_op jit(solution)/shard_map/ppermute | solution.py:114
  39.8 0.1 collective-permute-start.8
  39.8 1.4 %collective-permute-done.10.refs_6_ = bf16[2,128,256]{2,1,0:T(8,128)(2,1)S(1)} collective-permute-done((bf16[2,128,256]{2,1,0:T(8,128)(2,1)S(1)}, bf16[2,128,256]{2,1,0:T(8,128)(2,1)S(1)}, u32[]{:S(2)}, u32[]{:S(2)}) %collective-permute-start.10) | collective-permute-done | bytes 131104 | tf_op jit(solution)/shard_map/ppermute | solution.py:114
  41.3 3.4 %collective-permute-start.11 = (bf16[2,128,256]{2,1,0:T(8,128)(2,1)S(1)}, bf16[2,128,256]{2,1,0:T(8,128)(2,1)S(1)}, u32[]{:S(2)}, u32[]{:S(2)}) collective-permute-start(bf16[2,128,256]{2,1,0:T(8,128)(2,1)S(1)} %collective-permute-done.10.refs_6_), channel_id=1, source_target_pairs={{0,4},{4,0},{8,12},{12,8},{16,20},{20,16},{24,28},{28,24},{1,5},{5... | collective-permute-start | bytes 393224 | tf_op jit(solution)/shard_map/ppermute | solution.py:114
  44.6 3.3 %all-to-all-start.1 = ((bf16[8,16,256]{2,1,0:T(8,128)(2,1)}), bf16[8,16,256]{2,1,0:T(8,128)(2,1)S(1)}, u32[]{:S(2)}, u32[]{:S(2)}) async-start(bf16[8,16,256]{2,1,0:T(8,128)(2,1)} %bitcast.6), calls=%async_computation.1 | async-start | bytes 131072 | tf_op jit(solution)/shard_map/all_to_all | solution.py:503
  48.0 0.1 collective-permute-start.12
  48.1 0.0 collective-permute-done.13.refs_2_
  48.1 0.5 collective-permute-start.14
  48.6 6.3 %all-to-all-done.1.received = bf16[8,16,256]{2,1,0:T(8,128)(2,1)S(1)} async-done(((bf16[8,16,256]{2,1,0:T(8,128)(2,1)}), bf16[8,16,256]{2,1,0:T(8,128)(2,1)S(1)}, u32[]{:S(2)}, u32[]{:S(2)}) %all-to-all-start.1) | async-done | bytes 65568 | tf_op jit(solution)/shard_map/all_to_all | solution.py:503
  54.8 0.0 collective-permute-done.8.refs_1_.refs_3_
  54.8 0.0 collective-permute-done.9.refs_2_.refs_5_
  54.8 0.0 collective-permute-done.11.refs_3_.refs_7_
  54.9 0.1 shard_map.97
  54.9 0.0 collective-permute-start.15
  55.0 0.5 collective-permute-start.16
  55.4 1.4 %collective-permute-start.17 = (f32[1,64]{1,0:T(1,128)S(1)}, f32[1,64]{1,0:T(1,128)S(1)}, u32[]{:S(2)}, u32[]{:S(2)}) collective-permute-start(f32[1,64]{1,0:T(1,128)S(1)} %get-tuple-element.49), channel_id=1, source_target_pairs={{0,3},{1,2},{2,1},{3,0},{4,7},{5,6},{6,5},{7,4},{8,11},{9,10},{10,... | collective-permute-start | bytes 776 | tf_op jit(solution)/shard_map/ppermute | solution.py:114
  56.8 0.6 copy.15
  57.5 0.0 collective-permute-done.15
  57.5 1.1 %collective-permute-done.16 = f32[1,64]{1,0:T(1,128)S(1)} collective-permute-done((f32[1,64]{1,0:T(1,128)S(1)}, f32[1,64]{1,0:T(1,128)S(1)}, u32[]{:S(2)}, u32[]{:S(2)}) %collective-permute-start.16) | collective-permute-done | bytes 288 | tf_op jit(solution)/shard_map/ppermute | solution.py:114
  58.6 0.0 collective-permute-done.17
  58.6 0.5 add_bitcast_fusion
  59.1 0.0 collective-permute-done.12.refs_1_
  59.1 0.0 collective-permute-done.14.refs_3_
  59.1 0.0 copy-start.2
  59.1 0.9 %copy-done.2 = bf16[8,64,256]{2,1,0:T(8,128)(2,1)S(1)} copy-done((bf16[8,64,256]{2,1,0:T(8,128)(2,1)S(1)}, bf16[8,64,256]{2,1,0:T(8,128)(2,1)}, u32[]{:S(2)}) %copy-start.2) | copy-done | bytes 262168
  60.0 1.8 %shard_map.98 = (bf16[2,8,288,256]{3,2,1,0:T(8,128)(2,1)S(1)}, f32[1,64]{1,0:T(1,128)}) custom-call(s32[2]{0:T(128)S(1)} %copy-done.7, bf16[8,64,256]{2,1,0:T(8,128)(2,1)S(1)} %copy-done.2, bf16[8,64,256]{2,1,0:T(8,128)(2,1)S(1)} %collective-permute-done.12.refs_1_, bf16[8,64,256]{2,1,0:T(8,128)(2,1)S(1)} %collective-permute-done.13.refs_2_, ...), custom_call_target="tpu_custom_call" | custom-call | flops 1769472000 | bytes 1048576 | tf_op jit(solution)/shard_map/pallas_call | solution.py:514
  61.8 3.4 %shard_map.99 = f32[27,64,256]{2,1,0:T(8,128)} custom-call(s32[2]{0:T(128)S(1)} %copy-done.7, f32[1,64]{1,0:T(1,128)S(1)} %get-tuple-element.45._, bf16[2,8,288,256]{3,2,1,0:T(8,128)(2,1)S(1)} %get-tuple-element.46.grads, bf16[2,128,256]{2,1,0:T(8,128)(2,1)S(1)} %get-tuple-element.41.refs_0_, bf16[2,128,256]{2,1,0:T(8,128)(2,1)S(1)} %get-tuple-element.42.refs_0_.refs_1_, ...), custom_call_target="tpu_custom_call" | custom-call | flops 3932160000 | bytes 3538944 | tf_op jit(solution)/shard_map/pallas_call | solution.py:520
  (14 shorter events, 0.1 us)
Async XLA Ops:
  2.1 16.2 %all-to-all-start = ((bf16[8,64,256]{2,1,0:T(8,128)(2,1)}), bf16[8,64,256]{2,1,0:T(8,128)(2,1)S(1)}, u32[]{:S(2)}, u32[]{:S(2)}) async-start(bf16[8,64,256]{2,1,0:T(8,128)(2,1)} %broadcast_in_dim.8), calls=%async_computation | async-start | bytes 524288 | tf_op jit(solution)/shard_map/all_to_all | solution.py:448
  9.5 10.2 %copy-start.6 = (s32[2]{0:T(128)}, s32[2]{0:T(128)S(1)}, u32[]{:S(2)}) copy-start(s32[2]{0:T(128)S(1)} %pad_add_fusion.place) | copy-start | bytes 28
  10.2 0.9 %copy-start.8 = (bf16[4,2,32,256]{3,2,1,0:T(8,128)(2,1)S(1)}, bf16[4,2,32,256]{3,2,1,0:T(8,128)(2,1)}, u32[]{:S(2)}) copy-start(bf16[4,2,32,256]{3,2,1,0:T(8,128)(2,1)} %param.5) | copy-start | bytes 393220
  11.9 0.6 copy-start.5
  12.5 17.7 %copy-start = (bf16[256,256]{1,0:T(8,128)(2,1)}, bf16[256,256]{1,0:T(8,128)(2,1)S(1)}, u32[]{:S(2)}) copy-start(bf16[256,256]{1,0:T(8,128)(2,1)S(1)} %get-tuple-element.35._.frames) | copy-start | bytes 393220
  12.5 17.7 %copy-start.3 = (bf16[2,2,64,256]{3,2,1,0:T(8,128)(2,1)}, bf16[2,2,64,256]{3,2,1,0:T(8,128)(2,1)S(1)}, u32[]{:S(2)}) copy-start(bf16[2,2,64,256]{3,2,1,0:T(8,128)(2,1)S(1)} %get-tuple-element.28.planes) | copy-start | bytes 393220
  12.5 7.1 %collective-permute-start = (bf16[384,128]{1,0:T(8,128)(2,1)S(1)}, bf16[384,128]{1,0:T(8,128)(2,1)S(1)}, u32[]{:S(2)}, u32[]{:S(2)}) collective-permute-start(bf16[384,128]{1,0:T(8,128)(2,1)S(1)} %get-tuple-element.30), channel_id=1, source_target_pairs={{0,1},{1,0},{2,3},{3,2},{4,5},{5,4},{6,7},{7,6},{8,9},{9,8},{10,11... | collective-permute-start | bytes 294920 | tf_op jit(solution)/shard_map/ppermute | solution.py:114
  12.5 7.2 %collective-permute-start.2 = (bf16[384,128]{1,0:T(8,128)(2,1)S(1)}, bf16[384,128]{1,0:T(8,128)(2,1)S(1)}, u32[]{:S(2)}, u32[]{:S(2)}) collective-permute-start(bf16[384,128]{1,0:T(8,128)(2,1)S(1)} %get-tuple-element.32), channel_id=1, source_target_pairs={{0,3},{1,2},{2,1},{3,0},{4,7},{5,6},{6,5},{7,4},{8,11},{9,10},{10,... | collective-permute-start | bytes 294920 | tf_op jit(solution)/shard_map/ppermute | solution.py:114
  14.1 5.5 %collective-permute-start.1 = (bf16[128,128]{1,0:T(8,128)(2,1)S(1)}, bf16[128,128]{1,0:T(8,128)(2,1)S(1)}, u32[]{:S(2)}, u32[]{:S(2)}) collective-permute-start(bf16[128,128]{1,0:T(8,128)(2,1)S(1)} %get-tuple-element.31), channel_id=1, source_target_pairs={{0,2},{1,3},{2,0},{3,1},{4,6},{5,7},{6,4},{7,5},{8,10},{9,11},{10,... | collective-permute-start | bytes 98312 | tf_op jit(solution)/shard_map/ppermute | solution.py:114
  18.3 11.9 %copy-start.1 = (bf16[8,64,256]{2,1,0:T(8,128)(2,1)}, bf16[8,64,256]{2,1,0:T(8,128)(2,1)S(1)}, u32[]{:S(2)}) copy-start(bf16[8,64,256]{2,1,0:T(8,128)(2,1)S(1)} %get-tuple-element.37.gathered.refs_0_) | copy-start | bytes 786436
  18.3 11.8 %collective-permute-start.4 = (bf16[8,32,256]{2,1,0:T(8,128)(2,1)S(1)}, bf16[8,32,256]{2,1,0:T(8,128)(2,1)S(1)}, u32[]{:S(2)}, u32[]{:S(2)}) collective-permute-start(bf16[8,32,256]{2,1,0:T(8,128)(2,1)S(1)} %get-tuple-element.38), channel_id=1, source_target_pairs={{1,0},{2,1},{3,2},{5,4},{6,5},{7,6},{9,8},{10,9},{11,10},{13,12},{... | collective-permute-start | bytes 393224 | tf_op jit(solution)/shard_map/ppermute | solution.py:20
  20.3 0.6 copy-start.4
  21.0 7.4 %collective-permute-start.3 = (bf16[2,96,256]{2,1,0:T(8,128)(2,1)S(1)}, bf16[2,96,256]{2,1,0:T(8,128)(2,1)S(1)}, u32[]{:S(2)}, u32[]{:S(2)}) collective-permute-start(bf16[2,96,256]{2,1,0:T(8,128)(2,1)S(1)} %get-tuple-element.34), channel_id=1, source_target_pairs={{4,0},{8,4},{12,8},{16,12},{20,16},{24,20},{28,24},{5,1},{9,5},{13... | collective-permute-start | bytes 294920 | tf_op jit(solution)/shard_map/ppermute | solution.py:20
  22.2 14.0 %collective-permute-start.7 = (bf16[2,128,256]{2,1,0:T(8,128)(2,1)S(1)}, bf16[2,128,256]{2,1,0:T(8,128)(2,1)S(1)}, u32[]{:S(2)}, u32[]{:S(2)}) collective-permute-start(bf16[2,128,256]{2,1,0:T(8,128)(2,1)S(1)} %get-tuple-element.41.refs_0_), channel_id=1, source_target_pairs={{0,16},{4,20},{8,24},{12,28},{16,0},{20,4},{24,8},{28,12},{1,17},{... | collective-permute-start | bytes 393224 | tf_op jit(solution)/shard_map/ppermute | solution.py:114
  25.9 10.3 %collective-permute-start.6 = (bf16[2,128,256]{2,1,0:T(8,128)(2,1)S(1)}, bf16[2,128,256]{2,1,0:T(8,128)(2,1)S(1)}, u32[]{:S(2)}, u32[]{:S(2)}) collective-permute-start(bf16[2,128,256]{2,1,0:T(8,128)(2,1)S(1)} %get-tuple-element.41.refs_0_), channel_id=1, source_target_pairs={{0,8},{4,12},{8,0},{12,4},{16,24},{20,28},{24,16},{28,20},{1,9},{5... | collective-permute-start | bytes 393224 | tf_op jit(solution)/shard_map/ppermute | solution.py:114
  27.4 8.8 %collective-permute-start.5 = (bf16[2,128,256]{2,1,0:T(8,128)(2,1)S(1)}, bf16[2,128,256]{2,1,0:T(8,128)(2,1)S(1)}, u32[]{:S(2)}, u32[]{:S(2)}) collective-permute-start(bf16[2,128,256]{2,1,0:T(8,128)(2,1)S(1)} %get-tuple-element.41.refs_0_), channel_id=1, source_target_pairs={{0,4},{4,0},{8,12},{12,8},{16,20},{20,16},{24,28},{28,24},{1,5},{5... | collective-permute-start | bytes 393224 | tf_op jit(solution)/shard_map/ppermute | solution.py:114
  28.4 1.9 %copy-start.10 = (bf16[2,96,256]{2,1,0:T(8,128)(2,1)}, bf16[2,96,256]{2,1,0:T(8,128)(2,1)S(1)}, u32[]{:S(2)}) copy-start(bf16[2,96,256]{2,1,0:T(8,128)(2,1)S(1)} %collective-permute-done.3.under) | copy-start | bytes 294916
  28.4 19.7 %collective-permute-start.13 = (bf16[8,64,256]{2,1,0:T(8,128)(2,1)S(1)}, bf16[8,64,256]{2,1,0:T(8,128)(2,1)S(1)}, u32[]{:S(2)}, u32[]{:S(2)}) collective-permute-start(bf16[8,64,256]{2,1,0:T(8,128)(2,1)S(1)} %get-tuple-element.37.gathered.refs_0_), channel_id=1, source_target_pairs={{0,2},{1,3},{2,0},{3,1},{4,6},{5,7},{6,4},{7,5},{8,10},{9,11},{10,... | collective-permute-start | bytes 786440 | tf_op jit(solution)/shard_map/ppermute | solution.py:114
  30.2 0.7 %copy-start.9 = (bf16[8,32,256]{2,1,0:T(8,128)(2,1)}, bf16[8,32,256]{2,1,0:T(8,128)(2,1)S(1)}, u32[]{:S(2)}) copy-start(bf16[8,32,256]{2,1,0:T(8,128)(2,1)S(1)} %collective-permute-done.4.following) | copy-start | bytes 393220
  30.9 28.2 %copy-start.7 = (s32[2]{0:T(128)S(1)}, s32[2]{0:T(128)}, u32[]{:S(2)}) copy-start(s32[2]{0:T(128)} %copy-done.6) | copy-start | bytes 28
  36.2 5.0 %collective-permute-start.10 = (bf16[2,128,256]{2,1,0:T(8,128)(2,1)S(1)}, bf16[2,128,256]{2,1,0:T(8,128)(2,1)S(1)}, u32[]{:S(2)}, u32[]{:S(2)}) collective-permute-start(bf16[2,128,256]{2,1,0:T(8,128)(2,1)S(1)} %get-tuple-element.44.refs_4_), channel_id=1, source_target_pairs={{0,8},{4,12},{8,0},{12,4},{16,24},{20,28},{24,16},{28,20},{1,9},{5... | collective-permute-start | bytes 393224 | tf_op jit(solution)/shard_map/ppermute | solution.py:114
  37.6 17.2 %collective-permute-start.9 = (bf16[2,128,256]{2,1,0:T(8,128)(2,1)S(1)}, bf16[2,128,256]{2,1,0:T(8,128)(2,1)S(1)}, u32[]{:S(2)}, u32[]{:S(2)}) collective-permute-start(bf16[2,128,256]{2,1,0:T(8,128)(2,1)S(1)} %get-tuple-element.44.refs_4_), channel_id=1, source_target_pairs={{0,4},{4,0},{8,12},{12,8},{16,20},{20,16},{24,28},{28,24},{1,5},{5... | collective-permute-start | bytes 393224 | tf_op jit(solution)/shard_map/ppermute | solution.py:114
  39.8 15.1 %collective-permute-start.8 = (bf16[2,128,256]{2,1,0:T(8,128)(2,1)S(1)}, bf16[2,128,256]{2,1,0:T(8,128)(2,1)S(1)}, u32[]{:S(2)}, u32[]{:S(2)}) collective-permute-start(bf16[2,128,256]{2,1,0:T(8,128)(2,1)S(1)} %get-tuple-element.43.refs_2_), channel_id=1, source_target_pairs={{0,4},{4,0},{8,12},{12,8},{16,20},{20,16},{24,28},{28,24},{1,5},{5... | collective-permute-start | bytes 393224 | tf_op jit(solution)/shard_map/ppermute | solution.py:114
  41.3 13.6 %collective-permute-start.11 = (bf16[2,128,256]{2,1,0:T(8,128)(2,1)S(1)}, bf16[2,128,256]{2,1,0:T(8,128)(2,1)S(1)}, u32[]{:S(2)}, u32[]{:S(2)}) collective-permute-start(bf16[2,128,256]{2,1,0:T(8,128)(2,1)S(1)} %collective-permute-done.10.refs_6_), channel_id=1, source_target_pairs={{0,4},{4,0},{8,12},{12,8},{16,20},{20,16},{24,28},{28,24},{1,5},{5... | collective-permute-start | bytes 393224 | tf_op jit(solution)/shard_map/ppermute | solution.py:114
  44.6 10.2 %all-to-all-start.1 = ((bf16[8,16,256]{2,1,0:T(8,128)(2,1)}), bf16[8,16,256]{2,1,0:T(8,128)(2,1)S(1)}, u32[]{:S(2)}, u32[]{:S(2)}) async-start(bf16[8,16,256]{2,1,0:T(8,128)(2,1)} %bitcast.6), calls=%async_computation.1 | async-start | bytes 131072 | tf_op jit(solution)/shard_map/all_to_all | solution.py:503
  48.0 11.1 %collective-permute-start.12 = (bf16[8,64,256]{2,1,0:T(8,128)(2,1)}, bf16[8,64,256]{2,1,0:T(8,128)(2,1)S(1)}, u32[]{:S(2)}, u32[]{:S(2)}) collective-permute-start(bf16[8,64,256]{2,1,0:T(8,128)(2,1)} %copy-done.1), channel_id=1, source_target_pairs={{0,1},{1,0},{2,3},{3,2},{4,5},{5,4},{6,7},{7,6},{8,9},{9,8},{10,11... | collective-permute-start | bytes 786440 | tf_op jit(solution)/shard_map/ppermute | solution.py:114
  48.1 11.0 %collective-permute-start.14 = (bf16[8,64,256]{2,1,0:T(8,128)(2,1)S(1)}, bf16[8,64,256]{2,1,0:T(8,128)(2,1)S(1)}, u32[]{:S(2)}, u32[]{:S(2)}) collective-permute-start(bf16[8,64,256]{2,1,0:T(8,128)(2,1)S(1)} %collective-permute-done.13.refs_2_), channel_id=1, source_target_pairs={{0,1},{1,0},{2,3},{3,2},{4,5},{5,4},{6,7},{7,6},{8,9},{9,8},{10,11... | collective-permute-start | bytes 786440 | tf_op jit(solution)/shard_map/ppermute | solution.py:114
  54.9 2.5 %collective-permute-start.15 = (f32[1,64]{1,0:T(1,128)S(1)}, f32[1,64]{1,0:T(1,128)S(1)}, u32[]{:S(2)}, u32[]{:S(2)}) collective-permute-start(f32[1,64]{1,0:T(1,128)S(1)} %get-tuple-element.47), channel_id=1, source_target_pairs={{0,1},{1,0},{2,3},{3,2},{4,5},{5,4},{6,7},{7,6},{8,9},{9,8},{10,11... | collective-permute-start | bytes 776 | tf_op jit(solution)/shard_map/ppermute | solution.py:114
  55.0 3.6 %collective-permute-start.16 = (f32[1,64]{1,0:T(1,128)S(1)}, f32[1,64]{1,0:T(1,128)S(1)}, u32[]{:S(2)}, u32[]{:S(2)}) collective-permute-start(f32[1,64]{1,0:T(1,128)S(1)} %get-tuple-element.48), channel_id=1, source_target_pairs={{0,2},{1,3},{2,0},{3,1},{4,6},{5,7},{6,4},{7,5},{8,10},{9,11},{10,... | collective-permute-start | bytes 776 | tf_op jit(solution)/shard_map/ppermute | solution.py:114
  55.4 3.2 %collective-permute-start.17 = (f32[1,64]{1,0:T(1,128)S(1)}, f32[1,64]{1,0:T(1,128)S(1)}, u32[]{:S(2)}, u32[]{:S(2)}) collective-permute-start(f32[1,64]{1,0:T(1,128)S(1)} %get-tuple-element.49), channel_id=1, source_target_pairs={{0,3},{1,2},{2,1},{3,0},{4,7},{5,6},{6,5},{7,4},{8,11},{9,10},{10,... | collective-permute-start | bytes 776 | tf_op jit(solution)/shard_map/ppermute | solution.py:114
  59.1 1.0 %copy-start.2 = (bf16[8,64,256]{2,1,0:T(8,128)(2,1)S(1)}, bf16[8,64,256]{2,1,0:T(8,128)(2,1)}, u32[]{:S(2)}) copy-start(bf16[8,64,256]{2,1,0:T(8,128)(2,1)} %copy-done.1) | copy-start | bytes 786436

commit v12 on v9

--- a/solution.py
+++ b/solution.py
@@ -121,7 +121,7 @@
         if k & (k - 1) == 0:
             blocks[k] = partners(value, axis, k)
     if gate is not None:
-        held = [k for k in blocks if k > 1]
+        held = [k for k in blocks if k > 0]
         blocks.update(zip(held, gate([blocks[k] for k in held])))
     for k in range(1, count):
         low = k & -k
@@ -465,12 +465,12 @@
         [pltpu.VMEM((2, 4 * span, C // 2), f32)],
         60 * WORK * span * C, 16 * span * C, "svv" + "v" * (T + 3),
     )(place, flat, vectors)
+    messages = [sends[0]] + [partners(sends[k], "tm", k) for k in range(1, T)]
     head, grad_rows = call(
         functools.partial(head_kernel, 2 * J),
         [((R, 2 * J, C), bf16), (grad_rows.shape, bf16)],
         [], R * span * C, R * span * C, "avvv",
-    )(frames_copy, grad_rows)
-    messages = [sends[0]] + [partners(sends[k], "tm", k) for k in range(1, T)]
+    )(messages[1], grad_rows)
     joined, cached, under = call(
         functools.partial(join_kernel, F, J, T),
         [

time: 69.3 us -> 65.9 us (0.951)
  waiting for transfers between devices: 8.99 us -> 4.95 us
    ppermute x16, waiting for transfers between devices: 4.76 us -> 1.94 us  [partners(): lax.ppermute(value, axis, [(source, source ^ bits) for source in range(co...]
    all_to_all x1, waiting for transfers between devices: 4.15 us -> 3 us  [gathered_form(): lax.all_to_all(jnp.broadcast_to(own, (R,) + own.shape[1:]), 'rows', 0, 0,...]
  transfers between devices with their start and end apart: 19 -> 19, of which waited for: 4 -> 2; matrix products, arithmetic and copies ran while one was open for 2% -> 2% of each run, Pallas kernels for 18% -> 19%
where the time goes in v12:
time: 65.9 us; the launch traced here: 65.4 us
  starting transfers between devices  27.4 us (42%)
  Pallas kernels  12.6 us (19%)
  blocking collectives  11.4 us (17%)
  local copies, waits for them, and re-layouts  7.35 us (11%)
  waiting for transfers between devices  4.95 us (8%)
  between operations  0.82 us (1%)
  other arithmetic  0.78 us (1%)
    ppermute x16, starting transfers between devices, partners(): lax.ppermute(value, axis, [(source, source ^ bits) for source in range(co...  17.6 us
    all_to_all x1, blocking collectives, gathered_form(): lax.all_to_all(packed.reshape(R, slot, C), 'rows', 0, 0, tiled=True)  11.4 us
    all_to_all x1, starting transfers between devices, gathered_form(): lax.all_to_all(jnp.broadcast_to(own, (R,) + own.shape[1:]), 'rows', 0, 0,...  7.25 us
    pallas_call x1, Pallas kernels, gathered_form(): call(functools.partial(slab_kernel, F, J, R, T, slot), [((R * slot, C), b...  5.33 us
    unnamed x24, local copies, waits for them, and re-layouts  5.19 us
    pallas_call x1, Pallas kernels, gathered_form(): call(functools.partial(weight_kernel, F, J, R, T, part), [((27, part, C),...  3.43 us
    all_to_all x1, waiting for transfers between devices, gathered_form(): lax.all_to_all(jnp.broadcast_to(own, (R,) + own.shape[1:]), 'rows', 0, 0,...  3 us
    ppermute x2, starting transfers between devices, shifted(): lax.ppermute(value, axis, [(source, source + steps) for source in range(l...  2.57 us
  transfers between devices with their start and end apart: 19, of which 2 were waited for; matrix products, arithmetic and copies ran while one was open for 2% of the time, Pallas kernels for 19%

profile of v12, /device:TPU:0, one launch (start us, length us, event | category | flops | bytes accessed | tf_op | source)
XLA Modules:
  0.0 65.4 jit_solution(2176082611666805735)
XLA Ops:
  0.6 0.8 %broadcast_in_dim.7 = bf16[64,256]{1,0:T(8,128)(2,1)S(1)} reshape(bf16[4,8,2,256]{3,2,1,0:T(2,128)(2,1)} %param.9) | data formatting | bytes 65536 | tf_op jit(solution)/shard_map/broadcast_in_dim | solution.py:457
  1.4 0.7 %broadcast_in_dim.8 = bf16[8,64,256]{2,1,0:T(8,128)(2,1)} broadcast(bf16[64,256]{1,0:T(8,128)(2,1)S(1)} %broadcast_in_dim.7), dimensions={1,2} | broadcast | bytes 294912 | tf_op jit(solution)/shard_map/broadcast_in_dim | solution.py:457
  2.1 7.3 %all-to-all-start = ((bf16[8,64,256]{2,1,0:T(8,128)(2,1)}), bf16[8,64,256]{2,1,0:T(8,128)(2,1)S(1)}, u32[]{:S(2)}, u32[]{:S(2)}) async-start(bf16[8,64,256]{2,1,0:T(8,128)(2,1)} %broadcast_in_dim.8), calls=%async_computation | async-start | bytes 524288 | tf_op jit(solution)/shard_map/all_to_all | solution.py:456
  9.4 0.1 pad_add_fusion.place
  9.5 0.7 %pad_maximum_fusion.vectors = f32[2,256]{1,0:T(2,128)S(1)} fusion(f32[1,256]{1,0:T(1,128)} %bitcast.18, f32[1,256]{1,0:T(1,128)} %bitcast.19), kind=kLoop, calls=%fused_computation.1 | loop fusion | flops 512 | bytes 4096 | tf_op jit(solution)/shard_map/stack | solution.py:450
  10.2 0.9 %copy-done.9 = bf16[4,2,32,256]{3,2,1,0:T(8,128)(2,1)S(1)} copy-done((bf16[4,2,32,256]{3,2,1,0:T(8,128)(2,1)S(1)}, bf16[4,2,32,256]{3,2,1,0:T(8,128)(2,1)}, u32[]{:S(2)}) %copy-start.9) | copy-done | bytes 131096
  11.1 0.8 %shard_map.92 = (bf16[2,2,64,256]{3,2,1,0:T(8,128)(2,1)S(1)}, bf16[256,256]{1,0:T(8,128)(2,1)S(1)}, f32[2,256]{1,0:T(2,128)S(1)}, bf16[128,128]{1,0:T(8,128)(2,1...) custom-call(s32[2]{0:T(128)S(1)} %pad_add_fusion.place, ...), custom_call_target="tpu_custom_call" | custom-call | flops 1179648000 | bytes 262144 | tf_op jit(solution)/shard_map/pallas_call | solution.py:461
  11.9 0.6 copy-done.4
  12.6 0.6 copy-done.6
  13.2 0.0 collective-permute-start
  13.2 1.6 %collective-permute-start.2 = (bf16[384,128]{1,0:T(8,128)(2,1)S(1)}, bf16[384,128]{1,0:T(8,128)(2,1)S(1)}, u32[]{:S(2)}, u32[]{:S(2)}) collective-permute-start(bf16[384,128]{1,0:T(8,128)(2,1)S(1)} %get-tuple-element.34), channel_id=1, source_target_pairs={{0,3},{1,2},{2,1},{3,0},{4,7},{5,6},{6,5},{7,4},{8,11},{9,10},{10,... | collective-permute-start | bytes 294920 | tf_op jit(solution)/shard_map/ppermute | solution.py:114
  14.8 0.5 collective-permute-start.1
  15.3 0.0 collective-permute-done.refs_1_._
  15.3 3.0 %all-to-all-done.grad_rows = bf16[8,64,256]{2,1,0:T(8,128)(2,1)S(1)} async-done(((bf16[8,64,256]{2,1,0:T(8,128)(2,1)}), bf16[8,64,256]{2,1,0:T(8,128)(2,1)S(1)}, u32[]{:S(2)}, u32[]{:S(2)}) %all-to-all-start) | async-done | bytes 262176 | tf_op jit(solution)/shard_map/all_to_all | solution.py:456
  18.3 0.0 copy-start
  18.3 1.6 %collective-permute-start.13 = (bf16[8,64,256]{2,1,0:T(8,128)(2,1)S(1)}, bf16[8,64,256]{2,1,0:T(8,128)(2,1)S(1)}, u32[]{:S(2)}, u32[]{:S(2)}) collective-permute-start(bf16[8,64,256]{2,1,0:T(8,128)(2,1)S(1)} %get-tuple-element.39.gathered.refs_0_), channel_id=1, source_target_pairs={{0,2},{1,3},{2,0},{3,1},{4,6},{5,7},{6,4},{7,5},{8,10},{9,11},{10,... | collective-permute-start | bytes 786440 | tf_op jit(solution)/shard_map/ppermute | solution.py:114
  19.9 0.0 collective-permute-done.1.refs_2_
  19.9 0.0 collective-permute-done.2.refs_3_
  19.9 0.6 shard_map.93
  20.6 0.0 copy-start.5
  20.6 0.6 copy-done.5
  21.2 1.3 %collective-permute-start.3 = (bf16[2,96,256]{2,1,0:T(8,128)(2,1)S(1)}, bf16[2,96,256]{2,1,0:T(8,128)(2,1)S(1)}, u32[]{:S(2)}, u32[]{:S(2)}) collective-permute-start(bf16[2,96,256]{2,1,0:T(8,128)(2,1)S(1)} %get-tuple-element.36), channel_id=1, source_target_pairs={{4,0},{8,4},{12,8},{16,12},{20,16},{24,20},{28,24},{5,1},{9,5},{13... | collective-permute-start | bytes 294920 | tf_op jit(solution)/shard_map/ppermute | solution.py:20
  22.5 1.3 %collective-permute-start.4 = (bf16[8,32,256]{2,1,0:T(8,128)(2,1)S(1)}, bf16[8,32,256]{2,1,0:T(8,128)(2,1)S(1)}, u32[]{:S(2)}, u32[]{:S(2)}) collective-permute-start(bf16[8,32,256]{2,1,0:T(8,128)(2,1)S(1)} %get-tuple-element.40), channel_id=1, source_target_pairs={{1,0},{2,1},{3,2},{5,4},{6,5},{7,6},{9,8},{10,9},{11,10},{13,12},{... | collective-permute-start | bytes 393224 | tf_op jit(solution)/shard_map/ppermute | solution.py:20
  23.8 4.7 %collective-permute-start.7 = (bf16[2,128,256]{2,1,0:T(8,128)(2,1)S(1)}, bf16[2,128,256]{2,1,0:T(8,128)(2,1)S(1)}, u32[]{:S(2)}, u32[]{:S(2)}) collective-permute-start(bf16[2,128,256]{2,1,0:T(8,128)(2,1)S(1)} %get-tuple-element.43.refs_0_), channel_id=1, source_target_pairs={{0,16},{4,20},{8,24},{12,28},{16,0},{20,4},{24,8},{28,12},{1,17},{... | collective-permute-start | bytes 393224 | tf_op jit(solution)/shard_map/ppermute | solution.py:114
  28.5 1.5 %collective-permute-start.6 = (bf16[2,128,256]{2,1,0:T(8,128)(2,1)S(1)}, bf16[2,128,256]{2,1,0:T(8,128)(2,1)S(1)}, u32[]{:S(2)}, u32[]{:S(2)}) collective-permute-start(bf16[2,128,256]{2,1,0:T(8,128)(2,1)S(1)} %get-tuple-element.43.refs_0_), channel_id=1, source_target_pairs={{0,8},{4,12},{8,0},{12,4},{16,24},{20,28},{24,16},{28,20},{1,9},{5... | collective-permute-start | bytes 393224 | tf_op jit(solution)/shard_map/ppermute | solution.py:114
  30.0 0.0 collective-permute-done.3.under
  30.0 0.6 collective-permute-start.5
  30.6 0.0 collective-permute-done.4.following
  30.6 0.0 copy-done.3
  30.6 0.1 copy-done.11
  30.6 0.6 copy-done.10
  31.2 5.3 %shard_map.95 = (bf16[128,256]{1,0:T(8,128)(2,1)}, bf16[256,256]{1,0:T(8,128)(2,1)}) custom-call(s32[2]{0:T(128)} %copy-done.7, bf16[2,2,64,256]{3,2,1,0:T(8,128)(2,1)} %copy-done.3, bf16[2,2,32,256]{3,2,1,0:T(8,128)(2,1)} %copy-done.5, bf16[2,96,256]{2,1,0:T(8,128)(2,1)} %copy-done.11, bf16[27,256,256]{2,1,0:T(8,128)(2,1)} %bitcast.16, ...), custom_call_target="tpu_custom_call" | custom-call | flops 452984832 | bytes 3538944 | tf_op jit(solution)/shard_map/pallas_call | solution.py:486
  36.6 0.0 collective-permute-done.7.refs_3_
  36.6 0.0 collective-permute-done.6.refs_2_
  36.6 0.0 collective-permute-done.5.refs_1_
  36.6 0.0 copy-start.2
  36.6 0.8 %copy-done.2 = bf16[128,256]{1,0:T(8,128)(2,1)S(1)} copy-done((bf16[128,256]{1,0:T(8,128)(2,1)S(1)}, bf16[128,256]{1,0:T(8,128)(2,1)}, u32[]{:S(2)}) %copy-start.2) | copy-done | bytes 65560
  37.4 1.2 %collective-permute-start.10 = (bf16[2,128,256]{2,1,0:T(8,128)(2,1)S(1)}, bf16[2,128,256]{2,1,0:T(8,128)(2,1)S(1)}, u32[]{:S(2)}, u32[]{:S(2)}) collective-permute-start(bf16[2,128,256]{2,1,0:T(8,128)(2,1)S(1)} %get-tuple-element.46.refs_4_), channel_id=1, source_target_pairs={{0,8},{4,12},{8,0},{12,4},{16,24},{20,28},{24,16},{28,20},{1,9},{5... | collective-permute-start | bytes 393224 | tf_op jit(solution)/shard_map/ppermute | solution.py:114
  38.6 0.7 %collective-permute-start.12 = (bf16[8,64,256]{2,1,0:T(8,128)(2,1)}, bf16[8,64,256]{2,1,0:T(8,128)(2,1)S(1)}, u32[]{:S(2)}, u32[]{:S(2)}) collective-permute-start(bf16[8,64,256]{2,1,0:T(8,128)(2,1)} %copy-done), channel_id=1, source_target_pairs={{0,1},{1,0},{2,3},{3,2},{4,5},{5,4},{6,7},{7,6},{8,9},{9,8},{10,11... | collective-permute-start | bytes 786440 | tf_op jit(solution)/shard_map/ppermute | solution.py:114
  39.3 0.0 collective-permute-done.13.refs_2_
  39.3 0.0 collective-permute-start.14
  39.3 0.6 collective-permute-start.9
  40.0 1.4 %collective-permute-start.8 = (bf16[2,128,256]{2,1,0:T(8,128)(2,1)S(1)}, bf16[2,128,256]{2,1,0:T(8,128)(2,1)S(1)}, u32[]{:S(2)}, u32[]{:S(2)}) collective-permute-start(bf16[2,128,256]{2,1,0:T(8,128)(2,1)S(1)} %get-tuple-element.45.refs_2_), channel_id=1, source_target_pairs={{0,4},{4,0},{8,12},{12,8},{16,20},{20,16},{24,28},{28,24},{1,5},{5... | collective-permute-start | bytes 393224 | tf_op jit(solution)/shard_map/ppermute | solution.py:114
  41.4 1.9 %collective-permute-done.10.refs_6_ = bf16[2,128,256]{2,1,0:T(8,128)(2,1)S(1)} collective-permute-done((bf16[2,128,256]{2,1,0:T(8,128)(2,1)S(1)}, bf16[2,128,256]{2,1,0:T(8,128)(2,1)S(1)}, u32[]{:S(2)}, u32[]{:S(2)}) %collective-permute-start.10) | collective-permute-done | bytes 131104 | tf_op jit(solution)/shard_map/ppermute | solution.py:114
  43.3 1.3 %collective-permute-start.11 = (bf16[2,128,256]{2,1,0:T(8,128)(2,1)S(1)}, bf16[2,128,256]{2,1,0:T(8,128)(2,1)S(1)}, u32[]{:S(2)}, u32[]{:S(2)}) collective-permute-start(bf16[2,128,256]{2,1,0:T(8,128)(2,1)S(1)} %collective-permute-done.10.refs_6_), channel_id=1, source_target_pairs={{0,4},{4,0},{8,12},{12,8},{16,20},{20,16},{24,28},{28,24},{1,5},{5... | collective-permute-start | bytes 393224 | tf_op jit(solution)/shard_map/ppermute | solution.py:114
  44.6 11.4 %all_to_all.10.received = bf16[8,16,256]{2,1,0:T(8,128)(2,1)S(1)} all-to-all(bf16[8,16,256]{2,1,0:T(8,128)(2,1)S(1)} %bitcast.14), channel_id=1, replica_groups=mesh['rows'=8,'tm'=4] {'rows'}, dimensions={0} | all-to-all | bytes 131072 | tf_op jit(solution)/shard_map/all_to_all | solution.py:511
  56.1 0.6 copy.15
  56.7 0.0 collective-permute-done.8.refs_1_.refs_3_
  56.7 0.0 collective-permute-done.9.refs_2_.refs_5_
  56.7 0.0 collective-permute-done.11.refs_3_.refs_7_
  56.7 0.1 shard_map.97
  56.8 0.0 collective-permute-start.15
  56.8 1.0 %collective-permute-start.16 = (f32[1,64]{1,0:T(1,128)S(1)}, f32[1,64]{1,0:T(1,128)S(1)}, u32[]{:S(2)}, u32[]{:S(2)}) collective-permute-start(f32[1,64]{1,0:T(1,128)S(1)} %get-tuple-element.52), channel_id=1, source_target_pairs={{0,2},{1,3},{2,0},{3,1},{4,6},{5,7},{6,4},{7,5},{8,10},{9,11},{10,... | collective-permute-start | bytes 776 | tf_op jit(solution)/shard_map/ppermute | solution.py:114
  57.8 0.9 %collective-permute-start.17 = (f32[1,64]{1,0:T(1,128)S(1)}, f32[1,64]{1,0:T(1,128)S(1)}, u32[]{:S(2)}, u32[]{:S(2)}) collective-permute-start(f32[1,64]{1,0:T(1,128)S(1)} %get-tuple-element.53), channel_id=1, source_target_pairs={{0,3},{1,2},{2,1},{3,0},{4,7},{5,6},{6,5},{7,4},{8,11},{9,10},{10,... | collective-permute-start | bytes 776 | tf_op jit(solution)/shard_map/ppermute | solution.py:114
  58.7 0.0 collective-permute-done.12.refs_1_
  58.7 0.0 collective-permute-done.14.refs_3_
  58.7 0.0 copy-start.1
  58.7 0.9 %copy-done.1 = bf16[8,64,256]{2,1,0:T(8,128)(2,1)S(1)} copy-done((bf16[8,64,256]{2,1,0:T(8,128)(2,1)S(1)}, bf16[8,64,256]{2,1,0:T(8,128)(2,1)}, u32[]{:S(2)}) %copy-start.1) | copy-done | bytes 262168
  59.6 1.8 %shard_map.98 = (bf16[2,8,288,256]{3,2,1,0:T(8,128)(2,1)S(1)}, f32[1,64]{1,0:T(1,128)}) custom-call(s32[2]{0:T(128)S(1)} %copy-done.8, bf16[8,64,256]{2,1,0:T(8,128)(2,1)S(1)} %copy-done.1, bf16[8,64,256]{2,1,0:T(8,128)(2,1)S(1)} %collective-permute-done.12.refs_1_, bf16[8,64,256]{2,1,0:T(8,128)(2,1)S(1)} %collective-permute-done.13.refs_2_, ...), custom_call_target="tpu_custom_call" | custom-call | flops 1769472000 | bytes 1048576 | tf_op jit(solution)/shard_map/pallas_call | solution.py:518
  61.4 3.4 %shard_map.99 = (f32[27,64,256]{2,1,0:T(8,128)}, f32[1,64]{1,0:T(1,128)S(1)}) custom-call(s32[2]{0:T(128)S(1)} %copy-done.8, f32[1,64]{1,0:T(1,128)S(1)} %get-tuple-element.47.gain, bf16[2,8,288,256]{3,2,1,0:T(8,128)(2,1)S(1)} %get-tuple-element.48.grads, bf16[2,128,256]{2,1,0:T(8,128)(2,1)S(1)} %get-tuple-element.43.refs_0_, ...), custom_call_target="tpu_custom_call" | custom-call | flops 3932160000 | bytes 3538944 | tf_op jit(solution)/shard_map/pallas_call | solution.py:524
  64.8 0.0 collective-permute-done.15.refs_1_
  64.9 0.0 collective-permute-done.16.refs_2_
  64.9 0.0 collective-permute-done.17.refs_3_
  64.9 0.5 shard_map.100
  (15 shorter events, 0.1 us)
Async XLA Ops:
  2.1 16.2 %all-to-all-start = ((bf16[8,64,256]{2,1,0:T(8,128)(2,1)}), bf16[8,64,256]{2,1,0:T(8,128)(2,1)S(1)}, u32[]{:S(2)}, u32[]{:S(2)}) async-start(bf16[8,64,256]{2,1,0:T(8,128)(2,1)} %broadcast_in_dim.8), calls=%async_computation | async-start | bytes 524288 | tf_op jit(solution)/shard_map/all_to_all | solution.py:456
  9.5 10.5 %copy-start.7 = (s32[2]{0:T(128)}, s32[2]{0:T(128)S(1)}, u32[]{:S(2)}) copy-start(s32[2]{0:T(128)S(1)} %pad_add_fusion.place) | copy-start | bytes 28
  10.2 0.9 %copy-start.9 = (bf16[4,2,32,256]{3,2,1,0:T(8,128)(2,1)S(1)}, bf16[4,2,32,256]{3,2,1,0:T(8,128)(2,1)}, u32[]{:S(2)}) copy-start(bf16[4,2,32,256]{3,2,1,0:T(8,128)(2,1)} %param.5) | copy-start | bytes 393220
  11.9 0.7 copy-start.4
  12.6 0.6 copy-start.6
  13.2 17.4 %copy-start.3 = (bf16[2,2,64,256]{3,2,1,0:T(8,128)(2,1)}, bf16[2,2,64,256]{3,2,1,0:T(8,128)(2,1)S(1)}, u32[]{:S(2)}) copy-start(bf16[2,2,64,256]{3,2,1,0:T(8,128)(2,1)S(1)} %get-tuple-element.30.planes) | copy-start | bytes 393220
  13.2 2.1 %collective-permute-start = (bf16[384,128]{1,0:T(8,128)(2,1)S(1)}, bf16[384,128]{1,0:T(8,128)(2,1)S(1)}, u32[]{:S(2)}, u32[]{:S(2)}) collective-permute-start(bf16[384,128]{1,0:T(8,128)(2,1)S(1)} %get-tuple-element.32), channel_id=1, source_target_pairs={{0,1},{1,0},{2,3},{3,2},{4,5},{5,4},{6,7},{7,6},{8,9},{9,8},{10,11... | collective-permute-start | bytes 294920 | tf_op jit(solution)/shard_map/ppermute | solution.py:114
  13.2 6.8 %collective-permute-start.2 = (bf16[384,128]{1,0:T(8,128)(2,1)S(1)}, bf16[384,128]{1,0:T(8,128)(2,1)S(1)}, u32[]{:S(2)}, u32[]{:S(2)}) collective-permute-start(bf16[384,128]{1,0:T(8,128)(2,1)S(1)} %get-tuple-element.34), channel_id=1, source_target_pairs={{0,3},{1,2},{2,1},{3,0},{4,7},{5,6},{6,5},{7,4},{8,11},{9,10},{10,... | collective-permute-start | bytes 294920 | tf_op jit(solution)/shard_map/ppermute | solution.py:114
  14.8 5.1 %collective-permute-start.1 = (bf16[128,128]{1,0:T(8,128)(2,1)S(1)}, bf16[128,128]{1,0:T(8,128)(2,1)S(1)}, u32[]{:S(2)}, u32[]{:S(2)}) collective-permute-start(bf16[128,128]{1,0:T(8,128)(2,1)S(1)} %get-tuple-element.33), channel_id=1, source_target_pairs={{0,2},{1,3},{2,0},{3,1},{4,6},{5,7},{6,4},{7,5},{8,10},{9,11},{10,... | collective-permute-start | bytes 98312 | tf_op jit(solution)/shard_map/ppermute | solution.py:114
  18.3 12.2 %copy-start = (bf16[8,64,256]{2,1,0:T(8,128)(2,1)}, bf16[8,64,256]{2,1,0:T(8,128)(2,1)S(1)}, u32[]{:S(2)}) copy-start(bf16[8,64,256]{2,1,0:T(8,128)(2,1)S(1)} %get-tuple-element.39.gathered.refs_0_) | copy-start | bytes 786436
  18.3 21.0 %collective-permute-start.13 = (bf16[8,64,256]{2,1,0:T(8,128)(2,1)S(1)}, bf16[8,64,256]{2,1,0:T(8,128)(2,1)S(1)}, u32[]{:S(2)}, u32[]{:S(2)}) collective-permute-start(bf16[8,64,256]{2,1,0:T(8,128)(2,1)S(1)} %get-tuple-element.39.gathered.refs_0_), channel_id=1, source_target_pairs={{0,2},{1,3},{2,0},{3,1},{4,6},{5,7},{6,4},{7,5},{8,10},{9,11},{10,... | collective-permute-start | bytes 786440 | tf_op jit(solution)/shard_map/ppermute | solution.py:114
  20.6 0.6 copy-start.5
  21.2 8.8 %collective-permute-start.3 = (bf16[2,96,256]{2,1,0:T(8,128)(2,1)S(1)}, bf16[2,96,256]{2,1,0:T(8,128)(2,1)S(1)}, u32[]{:S(2)}, u32[]{:S(2)}) collective-permute-start(bf16[2,96,256]{2,1,0:T(8,128)(2,1)S(1)} %get-tuple-element.36), channel_id=1, source_target_pairs={{4,0},{8,4},{12,8},{16,12},{20,16},{24,20},{28,24},{5,1},{9,5},{13... | collective-permute-start | bytes 294920 | tf_op jit(solution)/shard_map/ppermute | solution.py:20
  22.5 8.1 %collective-permute-start.4 = (bf16[8,32,256]{2,1,0:T(8,128)(2,1)S(1)}, bf16[8,32,256]{2,1,0:T(8,128)(2,1)S(1)}, u32[]{:S(2)}, u32[]{:S(2)}) collective-permute-start(bf16[8,32,256]{2,1,0:T(8,128)(2,1)S(1)} %get-tuple-element.40), channel_id=1, source_target_pairs={{1,0},{2,1},{3,2},{5,4},{6,5},{7,6},{9,8},{10,9},{11,10},{13,12},{... | collective-permute-start | bytes 393224 | tf_op jit(solution)/shard_map/ppermute | solution.py:20
  23.8 12.8 %collective-permute-start.7 = (bf16[2,128,256]{2,1,0:T(8,128)(2,1)S(1)}, bf16[2,128,256]{2,1,0:T(8,128)(2,1)S(1)}, u32[]{:S(2)}, u32[]{:S(2)}) collective-permute-start(bf16[2,128,256]{2,1,0:T(8,128)(2,1)S(1)} %get-tuple-element.43.refs_0_), channel_id=1, source_target_pairs={{0,16},{4,20},{8,24},{12,28},{16,0},{20,4},{24,8},{28,12},{1,17},{... | collective-permute-start | bytes 393224 | tf_op jit(solution)/shard_map/ppermute | solution.py:114
  28.5 8.1 %collective-permute-start.6 = (bf16[2,128,256]{2,1,0:T(8,128)(2,1)S(1)}, bf16[2,128,256]{2,1,0:T(8,128)(2,1)S(1)}, u32[]{:S(2)}, u32[]{:S(2)}) collective-permute-start(bf16[2,128,256]{2,1,0:T(8,128)(2,1)S(1)} %get-tuple-element.43.refs_0_), channel_id=1, source_target_pairs={{0,8},{4,12},{8,0},{12,4},{16,24},{20,28},{24,16},{28,20},{1,9},{5... | collective-permute-start | bytes 393224 | tf_op jit(solution)/shard_map/ppermute | solution.py:114
  30.0 0.6 copy-start.11
  30.0 6.6 %collective-permute-start.5 = (bf16[2,128,256]{2,1,0:T(8,128)(2,1)S(1)}, bf16[2,128,256]{2,1,0:T(8,128)(2,1)S(1)}, u32[]{:S(2)}, u32[]{:S(2)}) collective-permute-start(bf16[2,128,256]{2,1,0:T(8,128)(2,1)S(1)} %get-tuple-element.43.refs_0_), channel_id=1, source_target_pairs={{0,4},{4,0},{8,12},{12,8},{16,20},{20,16},{24,28},{28,24},{1,5},{5... | collective-permute-start | bytes 393224 | tf_op jit(solution)/shard_map/ppermute | solution.py:114
  30.6 0.7 %copy-start.10 = (bf16[8,32,256]{2,1,0:T(8,128)(2,1)}, bf16[8,32,256]{2,1,0:T(8,128)(2,1)S(1)}, u32[]{:S(2)}) copy-start(bf16[8,32,256]{2,1,0:T(8,128)(2,1)S(1)} %collective-permute-done.4.following) | copy-start | bytes 393220
  31.2 27.5 %copy-start.8 = (s32[2]{0:T(128)S(1)}, s32[2]{0:T(128)}, u32[]{:S(2)}) copy-start(s32[2]{0:T(128)} %copy-done.7) | copy-start | bytes 28
  36.6 0.8 %copy-start.2 = (bf16[128,256]{1,0:T(8,128)(2,1)S(1)}, bf16[128,256]{1,0:T(8,128)(2,1)}, u32[]{:S(2)}) copy-start(bf16[128,256]{1,0:T(8,128)(2,1)} %get-tuple-element.41.refs_0_) | copy-start | bytes 196612
  37.4 5.8 %collective-permute-start.10 = (bf16[2,128,256]{2,1,0:T(8,128)(2,1)S(1)}, bf16[2,128,256]{2,1,0:T(8,128)(2,1)S(1)}, u32[]{:S(2)}, u32[]{:S(2)}) collective-permute-start(bf16[2,128,256]{2,1,0:T(8,128)(2,1)S(1)} %get-tuple-element.46.refs_4_), channel_id=1, source_target_pairs={{0,8},{4,12},{8,0},{12,4},{16,24},{20,28},{24,16},{28,20},{1,9},{5... | collective-permute-start | bytes 393224 | tf_op jit(solution)/shard_map/ppermute | solution.py:114
  38.6 20.0 %collective-permute-start.12 = (bf16[8,64,256]{2,1,0:T(8,128)(2,1)}, bf16[8,64,256]{2,1,0:T(8,128)(2,1)S(1)}, u32[]{:S(2)}, u32[]{:S(2)}) collective-permute-start(bf16[8,64,256]{2,1,0:T(8,128)(2,1)} %copy-done), channel_id=1, source_target_pairs={{0,1},{1,0},{2,3},{3,2},{4,5},{5,4},{6,7},{7,6},{8,9},{9,8},{10,11... | collective-permute-start | bytes 786440 | tf_op jit(solution)/shard_map/ppermute | solution.py:114
  39.3 19.3 %collective-permute-start.14 = (bf16[8,64,256]{2,1,0:T(8,128)(2,1)S(1)}, bf16[8,64,256]{2,1,0:T(8,128)(2,1)S(1)}, u32[]{:S(2)}, u32[]{:S(2)}) collective-permute-start(bf16[8,64,256]{2,1,0:T(8,128)(2,1)S(1)} %collective-permute-done.13.refs_2_), channel_id=1, source_target_pairs={{0,1},{1,0},{2,3},{3,2},{4,5},{5,4},{6,7},{7,6},{8,9},{9,8},{10,11... | collective-permute-start | bytes 786440 | tf_op jit(solution)/shard_map/ppermute | solution.py:114
  39.3 17.4 %collective-permute-start.9 = (bf16[2,128,256]{2,1,0:T(8,128)(2,1)S(1)}, bf16[2,128,256]{2,1,0:T(8,128)(2,1)S(1)}, u32[]{:S(2)}, u32[]{:S(2)}) collective-permute-start(bf16[2,128,256]{2,1,0:T(8,128)(2,1)S(1)} %get-tuple-element.46.refs_4_), channel_id=1, source_target_pairs={{0,4},{4,0},{8,12},{12,8},{16,20},{20,16},{24,28},{28,24},{1,5},{5... | collective-permute-start | bytes 393224 | tf_op jit(solution)/shard_map/ppermute | solution.py:114
  40.0 16.7 %collective-permute-start.8 = (bf16[2,128,256]{2,1,0:T(8,128)(2,1)S(1)}, bf16[2,128,256]{2,1,0:T(8,128)(2,1)S(1)}, u32[]{:S(2)}, u32[]{:S(2)}) collective-permute-start(bf16[2,128,256]{2,1,0:T(8,128)(2,1)S(1)} %get-tuple-element.45.refs_2_), channel_id=1, source_target_pairs={{0,4},{4,0},{8,12},{12,8},{16,20},{20,16},{24,28},{28,24},{1,5},{5... | collective-permute-start | bytes 393224 | tf_op jit(solution)/shard_map/ppermute | solution.py:114
  43.3 13.4 %collective-permute-start.11 = (bf16[2,128,256]{2,1,0:T(8,128)(2,1)S(1)}, bf16[2,128,256]{2,1,0:T(8,128)(2,1)S(1)}, u32[]{:S(2)}, u32[]{:S(2)}) collective-permute-start(bf16[2,128,256]{2,1,0:T(8,128)(2,1)S(1)} %collective-permute-done.10.refs_6_), channel_id=1, source_target_pairs={{0,4},{4,0},{8,12},{12,8},{16,20},{20,16},{24,28},{28,24},{1,5},{5... | collective-permute-start | bytes 393224 | tf_op jit(solution)/shard_map/ppermute | solution.py:114
  56.8 8.0 %collective-permute-start.15 = (f32[1,64]{1,0:T(1,128)S(1)}, f32[1,64]{1,0:T(1,128)S(1)}, u32[]{:S(2)}, u32[]{:S(2)}) collective-permute-start(f32[1,64]{1,0:T(1,128)S(1)} %get-tuple-element.51), channel_id=1, source_target_pairs={{0,1},{1,0},{2,3},{3,2},{4,5},{5,4},{6,7},{7,6},{8,9},{9,8},{10,11... | collective-permute-start | bytes 776 | tf_op jit(solution)/shard_map/ppermute | solution.py:114
  56.8 8.0 %collective-permute-start.16 = (f32[1,64]{1,0:T(1,128)S(1)}, f32[1,64]{1,0:T(1,128)S(1)}, u32[]{:S(2)}, u32[]{:S(2)}) collective-permute-start(f32[1,64]{1,0:T(1,128)S(1)} %get-tuple-element.52), channel_id=1, source_target_pairs={{0,2},{1,3},{2,0},{3,1},{4,6},{5,7},{6,4},{7,5},{8,10},{9,11},{10,... | collective-permute-start | bytes 776 | tf_op jit(solution)/shard_map/ppermute | solution.py:114
  57.8 7.1 %collective-permute-start.17 = (f32[1,64]{1,0:T(1,128)S(1)}, f32[1,64]{1,0:T(1,128)S(1)}, u32[]{:S(2)}, u32[]{:S(2)}) collective-permute-start(f32[1,64]{1,0:T(1,128)S(1)} %get-tuple-element.53), channel_id=1, source_target_pairs={{0,3},{1,2},{2,1},{3,0},{4,7},{5,6},{6,5},{7,4},{8,11},{9,10},{10,... | collective-permute-start | bytes 776 | tf_op jit(solution)/shard_map/ppermute | solution.py:114
  58.7 1.0 %copy-start.1 = (bf16[8,64,256]{2,1,0:T(8,128)(2,1)S(1)}, bf16[8,64,256]{2,1,0:T(8,128)(2,1)}, u32[]{:S(2)}) copy-start(bf16[8,64,256]{2,1,0:T(8,128)(2,1)} %copy-done) | copy-start | bytes 786436

commit v13 on v6

--- a/solution.py
+++ b/solution.py
@@ -147,10 +147,12 @@
     return inv_rms, unit, unit * gain
 
 
-def hidden_kernel(F, J, T, place, frames, vectors, planes, frames_copy, vectors_copy, *rest):
+def hidden_kernel(F, J, T, place, frames, vectors, planes, kept, *rest):
     sends, tmp = rest[:T], rest[T]
-    frames_copy[...] = frames[...]
-    vectors_copy[...] = vectors[...]
+    count = frames.shape[0]
+    kept[:count] = frames[...].astype(jnp.float32)
+    kept[count:] = jnp.zeros((kept.shape[0] - count, kept.shape[1]), jnp.float32)
+    kept[count : count + 2] = vectors[...]
     channels = frames.shape[1]
     part = channels // T
     _, _, normed = normalised(frames[...], vectors[0:1])
@@ -260,13 +262,13 @@
 
 
 def slab_kernel(
-    F, J, R, T, slot, place, planes, cached, under, weight_hbm, frames, vectors, gathered, following,
+    F, J, R, T, slot, place, planes, cached, under, weight_hbm, kept, gathered, following,
     out, frames_grad, weight, near, ext, tmp, sem,
 ):
     row, block = place[0], place[1]
-    channels = frames.shape[1]
+    channels = kept.shape[1]
     span = F * J
-    gain, bias = vectors[0:1], vectors[1:2]
+    gain, bias = kept[4 * span : 4 * span + 1], kept[4 * span + 1 : 4 * span + 2]
     fetches = [
         pltpu.make_async_copy(weight_hbm.at[pl.ds(a * 9, 9)], weight.at[pl.ds(a * 9, 9)], sem.at[a])
         for a in range(3)
@@ -318,7 +320,7 @@
                     t * J : (t + 1) * J, lanes
                 ]
     hidden_grad = jnp.concatenate([tmp[0], tmp[1]], axis=1)
-    inv_rms, unit, normed = normalised(frames[...], gain)
+    inv_rms, unit, normed = normalised(kept[: 4 * span], gain)
     sigma = 1.0 / (1.0 + jnp.exp(-normed))
     normed_grad = hidden_grad * sigma * (1.0 + normed * (1.0 - sigma))
     gain_part = jnp.sum(normed_grad * unit, axis=0, keepdims=True)
@@ -450,18 +452,18 @@
     )
 
     sizes = [(2 * span + (16 * J if k % 2 else 0), 2 * part) for k in range(T)]
-    planes, frames_copy, vectors, *sends = call(
+    planes, kept, *sends = call(
         functools.partial(hidden_kernel, F, J, T),
-        [((2, 2, span, C), bf16), (flat.shape, bf16), ((2, C), f32)]
+        [((2, 2, span, C), bf16), ((4 * span + 8, C), f32)]
         + [(size, bf16) for size in sizes],
         [pltpu.VMEM((2, 4 * span, C // 2), f32)],
-        60 * WORK * span * C, 16 * span * C, "svv" + "v" * (T + 3),
+        60 * WORK * span * C, 16 * span * C, "svv" + "v" * (T + 2),
     )(place, flat, vectors)
     head, grad_rows = call(
         functools.partial(head_kernel, 2 * J),
         [((R, 2 * J, C), bf16), (grad_rows.shape, bf16)],
         [], R * span * C, R * span * C, "avvv",
-    )(frames_copy, grad_rows)
+    )(kept, grad_rows)
     messages = [sends[0]] + [partners(sends[k], "tm", k) for k in range(1, T)]
     joined, cached, under = call(
         functools.partial(join_kernel, F, J, T),
@@ -485,9 +487,9 @@
             pltpu.VMEM((2, 4 * span, C // 2), f32),
             pltpu.SemaphoreType.DMA((3,)),
         ],
-        2 * 54 * span * C * C, 2 * 27 * C * C, "svvvhvvvv" + "vv",
+        2 * 54 * span * C * C, 2 * 27 * C * C, "svvvhvvv" + "vv",
         limit=VMEM_LIMIT_WIDE,
-    )(place, planes, cached, under, weight, frames_copy, vectors, grad_rows, following)
+    )(place, planes, cached, under, weight, kept, grad_rows, following)
 
     def after_slab(blocks):
         shapes = [(b.shape, bf16) for b in blocks]

time: 65.2 us -> 66 us (1.012)
  waiting for transfers between devices: 12.5 us -> 13.4 us
  transfers between devices with their start and end apart: 20 -> 20, of which waited for: 5 -> 7; matrix products, arithmetic and copies ran while one was open for 3% -> 3% of each run, Pallas kernels for 11% -> 11%
where the time goes in v13:
time: 66 us; the launch traced here: 65.5 us
  starting transfers between devices  31.6 us (48%)
  waiting for transfers between devices  13.4 us (20%)
  Pallas kernels  12.2 us (18%)
  local copies, waits for them, and re-layouts  6.14 us (9%)
  other arithmetic  1.29 us (2%)
  between operations  0.86 us (1%)
    ppermute x16, starting transfers between devices, partners(): lax.ppermute(value, axis, [(source, source ^ bits) for source in range(co...  18.4 us
    all_to_all x1, starting transfers between devices, gathered_form(): lax.all_to_all(jnp.broadcast_to(own, (R,) + own.shape[1:]), 'rows', 0, 0,...  7.25 us
    all_to_all x1, waiting for transfers between devices, gathered_form(): lax.all_to_all(packed.reshape(R, slot, C), 'rows', 0, 0, tiled=True)  6.25 us
    pallas_call x1, Pallas kernels, gathered_form(): call(functools.partial(slab_kernel, F, J, R, T, slot), [((R * slot, C), b...  5.35 us
    all_to_all x1, waiting for transfers between devices, gathered_form(): lax.all_to_all(jnp.broadcast_to(own, (R,) + own.shape[1:]), 'rows', 0, 0,...  4.13 us
    unnamed x22, local copies, waits for them, and re-layouts  3.99 us
    pallas_call x1, Pallas kernels, gathered_form(): call(functools.partial(weight_kernel, F, J, R, T, part), [((27, part, C),...  3.43 us
    all_to_all x1, starting transfers between devices, gathered_form(): lax.all_to_all(packed.reshape(R, slot, C), 'rows', 0, 0, tiled=True)  3.35 us
  transfers between devices with their start and end apart: 20, of which 7 were waited for; matrix products, arithmetic and copies ran while one was open for 3% of the time, Pallas kernels for 11%

profile of v13, /device:TPU:0, one launch (start us, length us, event | category | flops | bytes accessed | tf_op | source)
XLA Modules:
  0.0 65.5 jit_solution(11473661615304019782)
XLA Ops:
  0.6 0.8 %broadcast_in_dim.7 = bf16[64,256]{1,0:T(8,128)(2,1)S(1)} reshape(bf16[4,8,2,256]{3,2,1,0:T(2,128)(2,1)} %param.9) | data formatting | bytes 65536 | tf_op jit(solution)/shard_map/broadcast_in_dim | solution.py:451
  1.4 0.7 %broadcast_in_dim.8 = bf16[8,64,256]{2,1,0:T(8,128)(2,1)} broadcast(bf16[64,256]{1,0:T(8,128)(2,1)S(1)} %broadcast_in_dim.7), dimensions={1,2} | broadcast | bytes 294912 | tf_op jit(solution)/shard_map/broadcast_in_dim | solution.py:451
  2.1 7.3 %all-to-all-start = ((bf16[8,64,256]{2,1,0:T(8,128)(2,1)}), bf16[8,64,256]{2,1,0:T(8,128)(2,1)S(1)}, u32[]{:S(2)}, u32[]{:S(2)}) async-start(bf16[8,64,256]{2,1,0:T(8,128)(2,1)} %broadcast_in_dim.8), calls=%async_computation | async-start | bytes 524288 | tf_op jit(solution)/shard_map/all_to_all | solution.py:450
  9.4 0.1 pad_add_fusion.place
  9.5 0.7 %pad_maximum_fusion.vectors = f32[2,256]{1,0:T(2,128)S(1)} fusion(f32[1,256]{1,0:T(1,128)} %bitcast.19, f32[1,256]{1,0:T(1,128)} %bitcast.20), kind=kLoop, calls=%fused_computation.1 | loop fusion | flops 512 | bytes 4096 | tf_op jit(solution)/shard_map/stack | solution.py:444
  10.2 0.9 %copy-done.8 = bf16[4,2,32,256]{3,2,1,0:T(8,128)(2,1)S(1)} copy-done((bf16[4,2,32,256]{3,2,1,0:T(8,128)(2,1)S(1)}, bf16[4,2,32,256]{3,2,1,0:T(8,128)(2,1)}, u32[]{:S(2)}) %copy-start.8) | copy-done | bytes 131096
  11.1 0.8 %shard_map.92 = (bf16[2,2,64,256]{3,2,1,0:T(8,128)(2,1)S(1)}, f32[264,256]{1,0:T(8,128)S(1)}, bf16[128,128]{1,0:T(8,128)(2,1)S(1)}, bf16[384,128]{1,0:T(8,128)(2...) custom-call(s32[2]{0:T(128)S(1)} %pad_add_fusion.place, bf16[256,256]{1,0:T(8,128)(2,1)S(1)} %bitcast.16, ...), custom_call_target="tpu_custom_call" | custom-call | flops 1179648000 | bytes 262144 | tf_op jit(solution)/shard_map/pallas_call | solution.py:455
  11.9 0.0 copy-start
  11.9 0.0 copy-start.4
  11.9 0.1 collective-permute-start
  12.0 1.6 %collective-permute-start.2 = (bf16[384,128]{1,0:T(8,128)(2,1)S(1)}, bf16[384,128]{1,0:T(8,128)(2,1)S(1)}, u32[]{:S(2)}, u32[]{:S(2)}) collective-permute-start(bf16[384,128]{1,0:T(8,128)(2,1)S(1)} %get-tuple-element.30), channel_id=1, source_target_pairs={{0,3},{1,2},{2,1},{3,0},{4,7},{5,6},{6,5},{7,4},{8,11},{9,10},{10,... | collective-permute-start | bytes 294920 | tf_op jit(solution)/shard_map/ppermute | solution.py:114
  13.7 0.5 collective-permute-start.1
  14.2 4.1 %all-to-all-done.grad_rows = bf16[8,64,256]{2,1,0:T(8,128)(2,1)S(1)} async-done(((bf16[8,64,256]{2,1,0:T(8,128)(2,1)}), bf16[8,64,256]{2,1,0:T(8,128)(2,1)S(1)}, u32[]{:S(2)}, u32[]{:S(2)}) %all-to-all-start) | async-done | bytes 262176 | tf_op jit(solution)/shard_map/all_to_all | solution.py:450
  18.3 0.0 copy-start.1
  18.3 1.3 %collective-permute-start.4 = (bf16[8,32,256]{2,1,0:T(8,128)(2,1)S(1)}, bf16[8,32,256]{2,1,0:T(8,128)(2,1)S(1)}, u32[]{:S(2)}, u32[]{:S(2)}) collective-permute-start(bf16[8,32,256]{2,1,0:T(8,128)(2,1)S(1)} %get-tuple-element.35), channel_id=1, source_target_pairs={{1,0},{2,1},{3,2},{5,4},{6,5},{7,6},{9,8},{10,9},{11,10},{13,12},{... | collective-permute-start | bytes 393224 | tf_op jit(solution)/shard_map/ppermute | solution.py:20
  19.6 0.0 collective-permute-done.1.refs_2_
  19.6 0.0 collective-permute-done.refs_1_
  19.7 0.0 collective-permute-done.2.refs_3_
  19.7 0.0 copy-done.6
  19.7 0.6 shard_map.93
  20.3 0.0 copy-start.5
  20.3 0.6 copy-done.5
  21.0 1.3 %collective-permute-start.3 = (bf16[2,96,256]{2,1,0:T(8,128)(2,1)S(1)}, bf16[2,96,256]{2,1,0:T(8,128)(2,1)S(1)}, u32[]{:S(2)}, u32[]{:S(2)}) collective-permute-start(bf16[2,96,256]{2,1,0:T(8,128)(2,1)S(1)} %get-tuple-element.32), channel_id=1, source_target_pairs={{4,0},{8,4},{12,8},{16,12},{20,16},{24,20},{28,24},{5,1},{9,5},{13... | collective-permute-start | bytes 294920 | tf_op jit(solution)/shard_map/ppermute | solution.py:20
  22.3 3.3 %collective-permute-start.7 = (bf16[2,128,256]{2,1,0:T(8,128)(2,1)S(1)}, bf16[2,128,256]{2,1,0:T(8,128)(2,1)S(1)}, u32[]{:S(2)}, u32[]{:S(2)}) collective-permute-start(bf16[2,128,256]{2,1,0:T(8,128)(2,1)S(1)} %get-tuple-element.38.refs_0_), channel_id=1, source_target_pairs={{0,16},{4,20},{8,24},{12,28},{16,0},{20,4},{24,8},{28,12},{1,17},{... | collective-permute-start | bytes 393224 | tf_op jit(solution)/shard_map/ppermute | solution.py:114
  25.5 1.5 %collective-permute-start.6 = (bf16[2,128,256]{2,1,0:T(8,128)(2,1)S(1)}, bf16[2,128,256]{2,1,0:T(8,128)(2,1)S(1)}, u32[]{:S(2)}, u32[]{:S(2)}) collective-permute-start(bf16[2,128,256]{2,1,0:T(8,128)(2,1)S(1)} %get-tuple-element.38.refs_0_), channel_id=1, source_target_pairs={{0,8},{4,12},{8,0},{12,4},{16,24},{20,28},{24,16},{28,20},{1,9},{5... | collective-permute-start | bytes 393224 | tf_op jit(solution)/shard_map/ppermute | solution.py:114
  27.0 1.5 %collective-permute-start.13 = (bf16[8,64,256]{2,1,0:T(8,128)(2,1)S(1)}, bf16[8,64,256]{2,1,0:T(8,128)(2,1)S(1)}, u32[]{:S(2)}, u32[]{:S(2)}) collective-permute-start(bf16[8,64,256]{2,1,0:T(8,128)(2,1)S(1)} %get-tuple-element.34.gathered.refs_0_), channel_id=1, source_target_pairs={{0,2},{1,3},{2,0},{3,1},{4,6},{5,7},{6,4},{7,5},{8,10},{9,11},{10,... | collective-permute-start | bytes 786440 | tf_op jit(solution)/shard_map/ppermute | solution.py:114
  28.5 0.0 collective-permute-done.3.under
  28.5 0.0 collective-permute-done.4.following
  28.5 0.0 copy-start.9
  28.6 0.6 copy-done.10
  29.2 0.1 copy-done.9
  29.2 5.3 %shard_map.95 = (bf16[128,256]{1,0:T(8,128)(2,1)}, bf16[256,256]{1,0:T(8,128)(2,1)}) custom-call(s32[2]{0:T(128)} %copy-done.6, bf16[2,2,64,256]{3,2,1,0:T(8,128)(2,1)} %copy-done.4, bf16[2,2,32,256]{3,2,1,0:T(8,128)(2,1)} %copy-done.5, bf16[2,96,256]{2,1,0:T(8,128)(2,1)} %copy-done.10, bf16[27,256,256]{2,1,0:T(8,128)(2,1)} %bitcast.17, f32[264,256]{1,0:T(8,128)} %copy-done, ...), custom_call_target="tpu_custom_call" | custom-call | flops 452984832 | bytes 3538944 | tf_op jit(solution)/shard_map/pallas_call | solution.py:480
  34.6 0.2 collective-permute-done.7.refs_2_
  34.7 0.1 collective-permute-done.6.refs_1_
  34.8 0.8 %copy-done.3 = bf16[128,256]{1,0:T(8,128)(2,1)S(1)} copy-done((bf16[128,256]{1,0:T(8,128)(2,1)S(1)}, bf16[128,256]{1,0:T(8,128)(2,1)}, u32[]{:S(2)}) %copy-start.3) | copy-done | bytes 65560
  35.7 0.7 %collective-permute-start.10 = (bf16[2,128,256]{2,1,0:T(8,128)(2,1)S(1)}, bf16[2,128,256]{2,1,0:T(8,128)(2,1)S(1)}, u32[]{:S(2)}, u32[]{:S(2)}) collective-permute-start(bf16[2,128,256]{2,1,0:T(8,128)(2,1)S(1)} %get-tuple-element.40.refs_4_), channel_id=1, source_target_pairs={{0,8},{4,12},{8,0},{12,4},{16,24},{20,28},{24,16},{28,20},{1,9},{5... | collective-permute-start | bytes 393224 | tf_op jit(solution)/shard_map/ppermute | solution.py:114
  36.4 1.8 %collective-permute-start.5 = (bf16[2,128,256]{2,1,0:T(8,128)(2,1)S(1)}, bf16[2,128,256]{2,1,0:T(8,128)(2,1)S(1)}, u32[]{:S(2)}, u32[]{:S(2)}) collective-permute-start(bf16[2,128,256]{2,1,0:T(8,128)(2,1)S(1)} %get-tuple-element.38.refs_0_), channel_id=1, source_target_pairs={{0,4},{4,0},{8,12},{12,8},{16,20},{20,16},{24,28},{28,24},{1,5},{5... | collective-permute-start | bytes 393224 | tf_op jit(solution)/shard_map/ppermute | solution.py:114
  38.3 0.2 collective-permute-start.9
  38.4 1.8 %collective-permute-start.8 = (bf16[2,128,256]{2,1,0:T(8,128)(2,1)S(1)}, bf16[2,128,256]{2,1,0:T(8,128)(2,1)S(1)}, u32[]{:S(2)}, u32[]{:S(2)}) collective-permute-start(bf16[2,128,256]{2,1,0:T(8,128)(2,1)S(1)} %get-tuple-element.39.refs_2_), channel_id=1, source_target_pairs={{0,4},{4,0},{8,12},{12,8},{16,20},{20,16},{24,28},{28,24},{1,5},{5... | collective-permute-start | bytes 393224 | tf_op jit(solution)/shard_map/ppermute | solution.py:114
  40.3 0.9 %collective-permute-done.10.refs_6_ = bf16[2,128,256]{2,1,0:T(8,128)(2,1)S(1)} collective-permute-done((bf16[2,128,256]{2,1,0:T(8,128)(2,1)S(1)}, bf16[2,128,256]{2,1,0:T(8,128)(2,1)S(1)}, u32[]{:S(2)}, u32[]{:S(2)}) %collective-permute-start.10) | collective-permute-done | bytes 131104 | tf_op jit(solution)/shard_map/ppermute | solution.py:114
  41.2 2.9 %collective-permute-start.11 = (bf16[2,128,256]{2,1,0:T(8,128)(2,1)S(1)}, bf16[2,128,256]{2,1,0:T(8,128)(2,1)S(1)}, u32[]{:S(2)}, u32[]{:S(2)}) collective-permute-start(bf16[2,128,256]{2,1,0:T(8,128)(2,1)S(1)} %collective-permute-done.10.refs_6_), channel_id=1, source_target_pairs={{0,4},{4,0},{8,12},{12,8},{16,20},{20,16},{24,28},{28,24},{1,5},{5... | collective-permute-start | bytes 393224 | tf_op jit(solution)/shard_map/ppermute | solution.py:114
  44.1 3.3 %all-to-all-start.1 = ((bf16[8,16,256]{2,1,0:T(8,128)(2,1)}), bf16[8,16,256]{2,1,0:T(8,128)(2,1)S(1)}, u32[]{:S(2)}, u32[]{:S(2)}) async-start(bf16[8,16,256]{2,1,0:T(8,128)(2,1)} %bitcast.15), calls=%async_computation.1 | async-start | bytes 131072 | tf_op jit(solution)/shard_map/all_to_all | solution.py:505
  47.5 0.0 collective-permute-done.5.refs_0_.refs_1_
  47.5 0.1 collective-permute-start.12
  47.5 0.0 collective-permute-done.13.refs_2_
  47.6 0.5 collective-permute-start.14
  48.1 6.3 %all-to-all-done.1.received = bf16[8,16,256]{2,1,0:T(8,128)(2,1)S(1)} async-done(((bf16[8,16,256]{2,1,0:T(8,128)(2,1)}), bf16[8,16,256]{2,1,0:T(8,128)(2,1)S(1)}, u32[]{:S(2)}, u32[]{:S(2)}) %all-to-all-start.1) | async-done | bytes 65568 | tf_op jit(solution)/shard_map/all_to_all | solution.py:505
  54.3 0.0 collective-permute-done.8.refs_1_.refs_3_
  54.3 0.0 collective-permute-done.9.refs_2_.refs_5_
  54.3 0.0 collective-permute-done.11.refs_3_.refs_7_
  54.3 0.1 shard_map.97
  54.4 0.0 collective-permute-start.15
  54.4 1.4 %collective-permute-start.16 = (f32[1,64]{1,0:T(1,128)S(1)}, f32[1,64]{1,0:T(1,128)S(1)}, u32[]{:S(2)}, u32[]{:S(2)}) collective-permute-start(f32[1,64]{1,0:T(1,128)S(1)} %get-tuple-element.44), channel_id=1, source_target_pairs={{0,2},{1,3},{2,0},{3,1},{4,6},{5,7},{6,4},{7,5},{8,10},{9,11},{10,... | collective-permute-start | bytes 776 | tf_op jit(solution)/shard_map/ppermute | solution.py:114
  55.8 0.4 collective-permute-start.17
  56.3 0.6 copy.14
  56.9 0.0 collective-permute-done.15
  57.0 1.1 %collective-permute-done.16 = f32[1,64]{1,0:T(1,128)S(1)} collective-permute-done((f32[1,64]{1,0:T(1,128)S(1)}, f32[1,64]{1,0:T(1,128)S(1)}, u32[]{:S(2)}, u32[]{:S(2)}) %collective-permute-start.16) | collective-permute-done | bytes 288 | tf_op jit(solution)/shard_map/ppermute | solution.py:114
  58.0 0.8 %collective-permute-done.17 = f32[1,64]{1,0:T(1,128)S(1)} collective-permute-done((f32[1,64]{1,0:T(1,128)S(1)}, f32[1,64]{1,0:T(1,128)S(1)}, u32[]{:S(2)}, u32[]{:S(2)}) %collective-permute-start.17) | collective-permute-done | bytes 288 | tf_op jit(solution)/shard_map/ppermute | solution.py:114
  58.8 0.5 add_bitcast_fusion
  59.3 0.0 collective-permute-done.12.refs_1_
  59.3 0.0 collective-permute-done.14.refs_3_
  59.3 0.9 %copy-done.2 = bf16[8,64,256]{2,1,0:T(8,128)(2,1)S(1)} copy-done((bf16[8,64,256]{2,1,0:T(8,128)(2,1)S(1)}, bf16[8,64,256]{2,1,0:T(8,128)(2,1)}, u32[]{:S(2)}) %copy-start.2) | copy-done | bytes 262168
  60.3 1.8 %shard_map.98 = (bf16[2,8,288,256]{3,2,1,0:T(8,128)(2,1)S(1)}, f32[1,64]{1,0:T(1,128)}) custom-call(s32[2]{0:T(128)S(1)} %copy-done.7, bf16[8,64,256]{2,1,0:T(8,128)(2,1)S(1)} %copy-done.2, bf16[8,64,256]{2,1,0:T(8,128)(2,1)S(1)} %collective-permute-done.12.refs_1_, bf16[8,64,256]{2,1,0:T(8,128)(2,1)S(1)} %collective-permute-done.13.refs_2_, ...), custom_call_target="tpu_custom_call" | custom-call | flops 1769472000 | bytes 1048576 | tf_op jit(solution)/shard_map/pallas_call | solution.py:516
  62.0 3.4 %shard_map.99 = f32[27,64,256]{2,1,0:T(8,128)} custom-call(s32[2]{0:T(128)S(1)} %copy-done.7, f32[1,64]{1,0:T(1,128)S(1)} %get-tuple-element.41._, bf16[2,8,288,256]{3,2,1,0:T(8,128)(2,1)S(1)} %get-tuple-element.42.grads, bf16[2,128,256]{2,1,0:T(8,128)(2,1)S(1)} %get-tuple-element.38.refs_0_, ...), custom_call_target="tpu_custom_call" | custom-call | flops 3932160000 | bytes 3538944 | tf_op jit(solution)/shard_map/pallas_call | solution.py:522
  (14 shorter events, 0.1 us)
Async XLA Ops:
  2.1 16.2 %all-to-all-start = ((bf16[8,64,256]{2,1,0:T(8,128)(2,1)}), bf16[8,64,256]{2,1,0:T(8,128)(2,1)S(1)}, u32[]{:S(2)}, u32[]{:S(2)}) async-start(bf16[8,64,256]{2,1,0:T(8,128)(2,1)} %broadcast_in_dim.8), calls=%async_computation | async-start | bytes 524288 | tf_op jit(solution)/shard_map/all_to_all | solution.py:450
  9.5 10.2 %copy-start.6 = (s32[2]{0:T(128)}, s32[2]{0:T(128)S(1)}, u32[]{:S(2)}) copy-start(s32[2]{0:T(128)S(1)} %pad_add_fusion.place) | copy-start | bytes 28
  10.2 0.9 %copy-start.8 = (bf16[4,2,32,256]{3,2,1,0:T(8,128)(2,1)S(1)}, bf16[4,2,32,256]{3,2,1,0:T(8,128)(2,1)}, u32[]{:S(2)}) copy-start(bf16[4,2,32,256]{3,2,1,0:T(8,128)(2,1)} %param.5) | copy-start | bytes 393220
  11.9 16.6 %copy-start = (f32[264,256]{1,0:T(8,128)}, f32[264,256]{1,0:T(8,128)S(1)}, u32[]{:S(2)}) copy-start(f32[264,256]{1,0:T(8,128)S(1)} %get-tuple-element.33._.kept) | copy-start | bytes 811012
  11.9 16.6 %copy-start.4 = (bf16[2,2,64,256]{3,2,1,0:T(8,128)(2,1)}, bf16[2,2,64,256]{3,2,1,0:T(8,128)(2,1)S(1)}, u32[]{:S(2)}) copy-start(bf16[2,2,64,256]{3,2,1,0:T(8,128)(2,1)S(1)} %get-tuple-element.26.planes) | copy-start | bytes 393220
  11.9 7.7 %collective-permute-start = (bf16[384,128]{1,0:T(8,128)(2,1)S(1)}, bf16[384,128]{1,0:T(8,128)(2,1)S(1)}, u32[]{:S(2)}, u32[]{:S(2)}) collective-permute-start(bf16[384,128]{1,0:T(8,128)(2,1)S(1)} %get-tuple-element.28), channel_id=1, source_target_pairs={{0,1},{1,0},{2,3},{3,2},{4,5},{5,4},{6,7},{7,6},{8,9},{9,8},{10,11... | collective-permute-start | bytes 294920 | tf_op jit(solution)/shard_map/ppermute | solution.py:114
  12.0 7.6 %collective-permute-start.2 = (bf16[384,128]{1,0:T(8,128)(2,1)S(1)}, bf16[384,128]{1,0:T(8,128)(2,1)S(1)}, u32[]{:S(2)}, u32[]{:S(2)}) collective-permute-start(bf16[384,128]{1,0:T(8,128)(2,1)S(1)} %get-tuple-element.30), channel_id=1, source_target_pairs={{0,3},{1,2},{2,1},{3,0},{4,7},{5,6},{6,5},{7,4},{8,11},{9,10},{10,... | collective-permute-start | bytes 294920 | tf_op jit(solution)/shard_map/ppermute | solution.py:114
  13.7 6.0 %collective-permute-start.1 = (bf16[128,128]{1,0:T(8,128)(2,1)S(1)}, bf16[128,128]{1,0:T(8,128)(2,1)S(1)}, u32[]{:S(2)}, u32[]{:S(2)}) collective-permute-start(bf16[128,128]{1,0:T(8,128)(2,1)S(1)} %get-tuple-element.29), channel_id=1, source_target_pairs={{0,2},{1,3},{2,0},{3,1},{4,6},{5,7},{6,4},{7,5},{8,10},{9,11},{10,... | collective-permute-start | bytes 98312 | tf_op jit(solution)/shard_map/ppermute | solution.py:114
  18.3 10.2 %copy-start.1 = (bf16[8,64,256]{2,1,0:T(8,128)(2,1)}, bf16[8,64,256]{2,1,0:T(8,128)(2,1)S(1)}, u32[]{:S(2)}) copy-start(bf16[8,64,256]{2,1,0:T(8,128)(2,1)S(1)} %get-tuple-element.34.gathered.refs_0_) | copy-start | bytes 786436
  18.3 10.2 %collective-permute-start.4 = (bf16[8,32,256]{2,1,0:T(8,128)(2,1)S(1)}, bf16[8,32,256]{2,1,0:T(8,128)(2,1)S(1)}, u32[]{:S(2)}, u32[]{:S(2)}) collective-permute-start(bf16[8,32,256]{2,1,0:T(8,128)(2,1)S(1)} %get-tuple-element.35), channel_id=1, source_target_pairs={{1,0},{2,1},{3,2},{5,4},{6,5},{7,6},{9,8},{10,9},{11,10},{13,12},{... | collective-permute-start | bytes 393224 | tf_op jit(solution)/shard_map/ppermute | solution.py:20
  20.3 0.6 copy-start.5
  21.0 7.6 %collective-permute-start.3 = (bf16[2,96,256]{2,1,0:T(8,128)(2,1)S(1)}, bf16[2,96,256]{2,1,0:T(8,128)(2,1)S(1)}, u32[]{:S(2)}, u32[]{:S(2)}) collective-permute-start(bf16[2,96,256]{2,1,0:T(8,128)(2,1)S(1)} %get-tuple-element.32), channel_id=1, source_target_pairs={{4,0},{8,4},{12,8},{16,12},{20,16},{24,20},{28,24},{5,1},{9,5},{13... | collective-permute-start | bytes 294920 | tf_op jit(solution)/shard_map/ppermute | solution.py:20
  22.3 12.5 %collective-permute-start.7 = (bf16[2,128,256]{2,1,0:T(8,128)(2,1)S(1)}, bf16[2,128,256]{2,1,0:T(8,128)(2,1)S(1)}, u32[]{:S(2)}, u32[]{:S(2)}) collective-permute-start(bf16[2,128,256]{2,1,0:T(8,128)(2,1)S(1)} %get-tuple-element.38.refs_0_), channel_id=1, source_target_pairs={{0,16},{4,20},{8,24},{12,28},{16,0},{20,4},{24,8},{28,12},{1,17},{... | collective-permute-start | bytes 393224 | tf_op jit(solution)/shard_map/ppermute | solution.py:114
  25.5 9.3 %collective-permute-start.6 = (bf16[2,128,256]{2,1,0:T(8,128)(2,1)S(1)}, bf16[2,128,256]{2,1,0:T(8,128)(2,1)S(1)}, u32[]{:S(2)}, u32[]{:S(2)}) collective-permute-start(bf16[2,128,256]{2,1,0:T(8,128)(2,1)S(1)} %get-tuple-element.38.refs_0_), channel_id=1, source_target_pairs={{0,8},{4,12},{8,0},{12,4},{16,24},{20,28},{24,16},{28,20},{1,9},{5... | collective-permute-start | bytes 393224 | tf_op jit(solution)/shard_map/ppermute | solution.py:114
  27.0 20.6 %collective-permute-start.13 = (bf16[8,64,256]{2,1,0:T(8,128)(2,1)S(1)}, bf16[8,64,256]{2,1,0:T(8,128)(2,1)S(1)}, u32[]{:S(2)}, u32[]{:S(2)}) collective-permute-start(bf16[8,64,256]{2,1,0:T(8,128)(2,1)S(1)} %get-tuple-element.34.gathered.refs_0_), channel_id=1, source_target_pairs={{0,2},{1,3},{2,0},{3,1},{4,6},{5,7},{6,4},{7,5},{8,10},{9,11},{10,... | collective-permute-start | bytes 786440 | tf_op jit(solution)/shard_map/ppermute | solution.py:114
  28.5 0.6 copy-start.10
  28.5 0.7 %copy-start.9 = (bf16[8,32,256]{2,1,0:T(8,128)(2,1)}, bf16[8,32,256]{2,1,0:T(8,128)(2,1)S(1)}, u32[]{:S(2)}) copy-start(bf16[8,32,256]{2,1,0:T(8,128)(2,1)S(1)} %collective-permute-done.4.following) | copy-start | bytes 393220
  29.2 30.1 %copy-start.7 = (s32[2]{0:T(128)S(1)}, s32[2]{0:T(128)}, u32[]{:S(2)}) copy-start(s32[2]{0:T(128)} %copy-done.6) | copy-start | bytes 28
  34.8 0.8 %copy-start.3 = (bf16[128,256]{1,0:T(8,128)(2,1)S(1)}, bf16[128,256]{1,0:T(8,128)(2,1)}, u32[]{:S(2)}) copy-start(bf16[128,256]{1,0:T(8,128)(2,1)} %get-tuple-element.36.refs_0_) | copy-start | bytes 196612
  35.7 5.5 %collective-permute-start.10 = (bf16[2,128,256]{2,1,0:T(8,128)(2,1)S(1)}, bf16[2,128,256]{2,1,0:T(8,128)(2,1)S(1)}, u32[]{:S(2)}, u32[]{:S(2)}) collective-permute-start(bf16[2,128,256]{2,1,0:T(8,128)(2,1)S(1)} %get-tuple-element.40.refs_4_), channel_id=1, source_target_pairs={{0,8},{4,12},{8,0},{12,4},{16,24},{20,28},{24,16},{28,20},{1,9},{5... | collective-permute-start | bytes 393224 | tf_op jit(solution)/shard_map/ppermute | solution.py:114
  36.4 11.1 %collective-permute-start.5 = (bf16[2,128,256]{2,1,0:T(8,128)(2,1)S(1)}, bf16[2,128,256]{2,1,0:T(8,128)(2,1)S(1)}, u32[]{:S(2)}, u32[]{:S(2)}) collective-permute-start(bf16[2,128,256]{2,1,0:T(8,128)(2,1)S(1)} %get-tuple-element.38.refs_0_), channel_id=1, source_target_pairs={{0,4},{4,0},{8,12},{12,8},{16,20},{20,16},{24,28},{28,24},{1,5},{5... | collective-permute-start | bytes 393224 | tf_op jit(solution)/shard_map/ppermute | solution.py:114
  38.3 16.1 %collective-permute-start.9 = (bf16[2,128,256]{2,1,0:T(8,128)(2,1)S(1)}, bf16[2,128,256]{2,1,0:T(8,128)(2,1)S(1)}, u32[]{:S(2)}, u32[]{:S(2)}) collective-permute-start(bf16[2,128,256]{2,1,0:T(8,128)(2,1)S(1)} %get-tuple-element.40.refs_4_), channel_id=1, source_target_pairs={{0,4},{4,0},{8,12},{12,8},{16,20},{20,16},{24,28},{28,24},{1,5},{5... | collective-permute-start | bytes 393224 | tf_op jit(solution)/shard_map/ppermute | solution.py:114
  38.4 15.9 %collective-permute-start.8 = (bf16[2,128,256]{2,1,0:T(8,128)(2,1)S(1)}, bf16[2,128,256]{2,1,0:T(8,128)(2,1)S(1)}, u32[]{:S(2)}, u32[]{:S(2)}) collective-permute-start(bf16[2,128,256]{2,1,0:T(8,128)(2,1)S(1)} %get-tuple-element.39.refs_2_), channel_id=1, source_target_pairs={{0,4},{4,0},{8,12},{12,8},{16,20},{20,16},{24,28},{28,24},{1,5},{5... | collective-permute-start | bytes 393224 | tf_op jit(solution)/shard_map/ppermute | solution.py:114
  41.2 13.1 %collective-permute-start.11 = (bf16[2,128,256]{2,1,0:T(8,128)(2,1)S(1)}, bf16[2,128,256]{2,1,0:T(8,128)(2,1)S(1)}, u32[]{:S(2)}, u32[]{:S(2)}) collective-permute-start(bf16[2,128,256]{2,1,0:T(8,128)(2,1)S(1)} %collective-permute-done.10.refs_6_), channel_id=1, source_target_pairs={{0,4},{4,0},{8,12},{12,8},{16,20},{20,16},{24,28},{28,24},{1,5},{5... | collective-permute-start | bytes 393224 | tf_op jit(solution)/shard_map/ppermute | solution.py:114
  44.1 10.2 %all-to-all-start.1 = ((bf16[8,16,256]{2,1,0:T(8,128)(2,1)}), bf16[8,16,256]{2,1,0:T(8,128)(2,1)S(1)}, u32[]{:S(2)}, u32[]{:S(2)}) async-start(bf16[8,16,256]{2,1,0:T(8,128)(2,1)} %bitcast.15), calls=%async_computation.1 | async-start | bytes 131072 | tf_op jit(solution)/shard_map/all_to_all | solution.py:505
  47.5 11.8 %collective-permute-start.12 = (bf16[8,64,256]{2,1,0:T(8,128)(2,1)}, bf16[8,64,256]{2,1,0:T(8,128)(2,1)S(1)}, u32[]{:S(2)}, u32[]{:S(2)}) collective-permute-start(bf16[8,64,256]{2,1,0:T(8,128)(2,1)} %copy-done.1), channel_id=1, source_target_pairs={{0,1},{1,0},{2,3},{3,2},{4,5},{5,4},{6,7},{7,6},{8,9},{9,8},{10,11... | collective-permute-start | bytes 786440 | tf_op jit(solution)/shard_map/ppermute | solution.py:114
  47.6 11.8 %collective-permute-start.14 = (bf16[8,64,256]{2,1,0:T(8,128)(2,1)S(1)}, bf16[8,64,256]{2,1,0:T(8,128)(2,1)S(1)}, u32[]{:S(2)}, u32[]{:S(2)}) collective-permute-start(bf16[8,64,256]{2,1,0:T(8,128)(2,1)S(1)} %collective-permute-done.13.refs_2_), channel_id=1, source_target_pairs={{0,1},{1,0},{2,3},{3,2},{4,5},{5,4},{6,7},{7,6},{8,9},{9,8},{10,11... | collective-permute-start | bytes 786440 | tf_op jit(solution)/shard_map/ppermute | solution.py:114
  54.4 2.5 %collective-permute-start.15 = (f32[1,64]{1,0:T(1,128)S(1)}, f32[1,64]{1,0:T(1,128)S(1)}, u32[]{:S(2)}, u32[]{:S(2)}) collective-permute-start(f32[1,64]{1,0:T(1,128)S(1)} %get-tuple-element.43), channel_id=1, source_target_pairs={{0,1},{1,0},{2,3},{3,2},{4,5},{5,4},{6,7},{7,6},{8,9},{9,8},{10,11... | collective-permute-start | bytes 776 | tf_op jit(solution)/shard_map/ppermute | solution.py:114
  54.4 3.6 %collective-permute-start.16 = (f32[1,64]{1,0:T(1,128)S(1)}, f32[1,64]{1,0:T(1,128)S(1)}, u32[]{:S(2)}, u32[]{:S(2)}) collective-permute-start(f32[1,64]{1,0:T(1,128)S(1)} %get-tuple-element.44), channel_id=1, source_target_pairs={{0,2},{1,3},{2,0},{3,1},{4,6},{5,7},{6,4},{7,5},{8,10},{9,11},{10,... | collective-permute-start | bytes 776 | tf_op jit(solution)/shard_map/ppermute | solution.py:114
  55.8 3.0 %collective-permute-start.17 = (f32[1,64]{1,0:T(1,128)S(1)}, f32[1,64]{1,0:T(1,128)S(1)}, u32[]{:S(2)}, u32[]{:S(2)}) collective-permute-start(f32[1,64]{1,0:T(1,128)S(1)} %get-tuple-element.45), channel_id=1, source_target_pairs={{0,3},{1,2},{2,1},{3,0},{4,7},{5,6},{6,5},{7,4},{8,11},{9,10},{10,... | collective-permute-start | bytes 776 | tf_op jit(solution)/shard_map/ppermute | solution.py:114
  59.3 1.0 %copy-start.2 = (bf16[8,64,256]{2,1,0:T(8,128)(2,1)S(1)}, bf16[8,64,256]{2,1,0:T(8,128)(2,1)}, u32[]{:S(2)}) copy-start(bf16[8,64,256]{2,1,0:T(8,128)(2,1)} %copy-done.1) | copy-start | bytes 786436

commit v14 on v13

--- a/solution.py
+++ b/solution.py
@@ -150,9 +150,14 @@
 def hidden_kernel(F, J, T, place, frames, vectors, planes, kept, *rest):
     sends, tmp = rest[:T], rest[T]
     count = frames.shape[0]
-    kept[:count] = frames[...].astype(jnp.float32)
-    kept[count:] = jnp.zeros((kept.shape[0] - count, kept.shape[1]), jnp.float32)
-    kept[count : count + 2] = vectors[...]
+    kept[:count] = frames[...]
+    line = lax.broadcasted_iota(jnp.int32, (16, 1), 0)
+    rest, tail = vectors[...], jnp.zeros((16, kept.shape[1]), jnp.float32)
+    for n in range(3):
+        term = rest.astype(jnp.bfloat16).astype(jnp.float32)
+        rest = rest - term
+        tail = jnp.where(line == n, term[0:1], jnp.where(line == 3 + n, term[1:2], tail))
+    kept[count:] = tail.astype(jnp.bfloat16)
     channels = frames.shape[1]
     part = channels // T
     _, _, normed = normalised(frames[...], vectors[0:1])
@@ -268,7 +273,9 @@
     row, block = place[0], place[1]
     channels = kept.shape[1]
     span = F * J
-    gain, bias = kept[4 * span : 4 * span + 1], kept[4 * span + 1 : 4 * span + 2]
+    tail = kept[4 * span :].astype(jnp.float32)
+    gain = tail[0:1] + tail[1:2] + tail[2:3]
+    bias = tail[3:4] + tail[4:5] + tail[5:6]
     fetches = [
         pltpu.make_async_copy(weight_hbm.at[pl.ds(a * 9, 9)], weight.at[pl.ds(a * 9, 9)], sem.at[a])
         for a in range(3)
@@ -454,7 +461,7 @@
     sizes = [(2 * span + (16 * J if k % 2 else 0), 2 * part) for k in range(T)]
     planes, kept, *sends = call(
         functools.partial(hidden_kernel, F, J, T),
-        [((2, 2, span, C), bf16), ((4 * span + 8, C), f32)]
+        [((2, 2, span, C), bf16), ((4 * span + 16, C), bf16)]
         + [(size, bf16) for size in sizes],
         [pltpu.VMEM((2, 4 * span, C // 2), f32)],
         60 * WORK * span * C, 16 * span * C, "svv" + "v" * (T + 2),

time: 66 us -> 66 us (level)
  no operation moved by 1% of the time
where the time goes in v14:
time: 66 us; the launch traced here: 65.5 us
  starting transfers between devices  31.6 us (48%)
  waiting for transfers between devices  13.5 us (20%)
  Pallas kernels  12.1 us (18%)
  local copies, waits for them, and re-layouts  6.14 us (9%)
  other arithmetic  1.29 us (2%)
  between operations  0.86 us (1%)
    ppermute x16, starting transfers between devices, partners(): lax.ppermute(value, axis, [(source, source ^ bits) for source in range(co...  18.4 us
    all_to_all x1, starting transfers between devices, gathered_form(): lax.all_to_all(jnp.broadcast_to(own, (R,) + own.shape[1:]), 'rows', 0, 0,...  7.25 us
    all_to_all x1, waiting for transfers between devices, gathered_form(): lax.all_to_all(packed.reshape(R, slot, C), 'rows', 0, 0, tiled=True)  6.25 us
    pallas_call x1, Pallas kernels, gathered_form(): call(functools.partial(slab_kernel, F, J, R, T, slot), [((R * slot, C), b...  5.33 us
    all_to_all x1, waiting for transfers between devices, gathered_form(): lax.all_to_all(jnp.broadcast_to(own, (R,) + own.shape[1:]), 'rows', 0, 0,...  4.13 us
    unnamed x22, local copies, waits for them, and re-layouts  3.97 us
    pallas_call x1, Pallas kernels, gathered_form(): call(functools.partial(weight_kernel, F, J, R, T, part), [((27, part, C),...  3.43 us
    all_to_all x1, starting transfers between devices, gathered_form(): lax.all_to_all(packed.reshape(R, slot, C), 'rows', 0, 0, tiled=True)  3.35 us
  transfers between devices with their start and end apart: 20, of which 7 were waited for; matrix products, arithmetic and copies ran while one was open for 3% of the time, Pallas kernels for 11%

profile of v14, /device:TPU:0, one launch (start us, length us, event | category | flops | bytes accessed | tf_op | source)
XLA Modules:
  0.0 65.5 jit_solution(17209521815588948125)
XLA Ops:
  0.6 0.8 %broadcast_in_dim.7 = bf16[64,256]{1,0:T(8,128)(2,1)S(1)} reshape(bf16[4,8,2,256]{3,2,1,0:T(2,128)(2,1)} %param.9) | data formatting | bytes 65536 | tf_op jit(solution)/shard_map/broadcast_in_dim | solution.py:458
  1.4 0.7 %broadcast_in_dim.8 = bf16[8,64,256]{2,1,0:T(8,128)(2,1)} broadcast(bf16[64,256]{1,0:T(8,128)(2,1)S(1)} %broadcast_in_dim.7), dimensions={1,2} | broadcast | bytes 294912 | tf_op jit(solution)/shard_map/broadcast_in_dim | solution.py:458
  2.1 7.3 %all-to-all-start = ((bf16[8,64,256]{2,1,0:T(8,128)(2,1)}), bf16[8,64,256]{2,1,0:T(8,128)(2,1)S(1)}, u32[]{:S(2)}, u32[]{:S(2)}) async-start(bf16[8,64,256]{2,1,0:T(8,128)(2,1)} %broadcast_in_dim.8), calls=%async_computation | async-start | bytes 524288 | tf_op jit(solution)/shard_map/all_to_all | solution.py:457
  9.4 0.1 pad_add_fusion.place
  9.5 0.7 %pad_maximum_fusion.vectors = f32[2,256]{1,0:T(2,128)S(1)} fusion(f32[1,256]{1,0:T(1,128)} %bitcast.19, f32[1,256]{1,0:T(1,128)} %bitcast.20), kind=kLoop, calls=%fused_computation.1 | loop fusion | flops 512 | bytes 4096 | tf_op jit(solution)/shard_map/stack | solution.py:451
  10.2 0.9 %copy-done.8 = bf16[4,2,32,256]{3,2,1,0:T(8,128)(2,1)S(1)} copy-done((bf16[4,2,32,256]{3,2,1,0:T(8,128)(2,1)S(1)}, bf16[4,2,32,256]{3,2,1,0:T(8,128)(2,1)}, u32[]{:S(2)}) %copy-start.8) | copy-done | bytes 131096
  11.1 0.8 %shard_map.92 = (bf16[2,2,64,256]{3,2,1,0:T(8,128)(2,1)S(1)}, bf16[272,256]{1,0:T(8,128)(2,1)S(1)}, bf16[128,128]{1,0:T(8,128)(2,1)S(1)}, bf16[384,128]{1,0:T(8,...) custom-call(s32[2]{0:T(128)S(1)} %pad_add_fusion.place, bf16[256,256]{1,0:T(8,128)(2,1)S(1)} %bitcast.16, ...), custom_call_target="tpu_custom_call" | custom-call | flops 1179648000 | bytes 262144 | tf_op jit(solution)/shard_map/pallas_call | solution.py:462
  11.9 0.0 copy-start
  11.9 0.0 copy-start.4
  11.9 0.1 collective-permute-start
  12.0 1.6 %collective-permute-start.2 = (bf16[384,128]{1,0:T(8,128)(2,1)S(1)}, bf16[384,128]{1,0:T(8,128)(2,1)S(1)}, u32[]{:S(2)}, u32[]{:S(2)}) collective-permute-start(bf16[384,128]{1,0:T(8,128)(2,1)S(1)} %get-tuple-element.30), channel_id=1, source_target_pairs={{0,3},{1,2},{2,1},{3,0},{4,7},{5,6},{6,5},{7,4},{8,11},{9,10},{10,... | collective-permute-start | bytes 294920 | tf_op jit(solution)/shard_map/ppermute | solution.py:114
  13.7 0.5 collective-permute-start.1
  14.2 4.1 %all-to-all-done.grad_rows = bf16[8,64,256]{2,1,0:T(8,128)(2,1)S(1)} async-done(((bf16[8,64,256]{2,1,0:T(8,128)(2,1)}), bf16[8,64,256]{2,1,0:T(8,128)(2,1)S(1)}, u32[]{:S(2)}, u32[]{:S(2)}) %all-to-all-start) | async-done | bytes 262176 | tf_op jit(solution)/shard_map/all_to_all | solution.py:457
  18.3 0.0 copy-start.1
  18.3 1.3 %collective-permute-start.4 = (bf16[8,32,256]{2,1,0:T(8,128)(2,1)S(1)}, bf16[8,32,256]{2,1,0:T(8,128)(2,1)S(1)}, u32[]{:S(2)}, u32[]{:S(2)}) collective-permute-start(bf16[8,32,256]{2,1,0:T(8,128)(2,1)S(1)} %get-tuple-element.35), channel_id=1, source_target_pairs={{1,0},{2,1},{3,2},{5,4},{6,5},{7,6},{9,8},{10,9},{11,10},{13,12},{... | collective-permute-start | bytes 393224 | tf_op jit(solution)/shard_map/ppermute | solution.py:20
  19.6 0.0 collective-permute-done.1.refs_2_
  19.7 0.0 collective-permute-done.refs_1_
  19.7 0.0 collective-permute-done.2.refs_3_
  19.7 0.0 copy-done.6
  19.7 0.6 shard_map.93
  20.3 0.0 copy-start.5
  20.3 0.6 copy-done.5
  21.0 1.3 %collective-permute-start.3 = (bf16[2,96,256]{2,1,0:T(8,128)(2,1)S(1)}, bf16[2,96,256]{2,1,0:T(8,128)(2,1)S(1)}, u32[]{:S(2)}, u32[]{:S(2)}) collective-permute-start(bf16[2,96,256]{2,1,0:T(8,128)(2,1)S(1)} %get-tuple-element.32), channel_id=1, source_target_pairs={{4,0},{8,4},{12,8},{16,12},{20,16},{24,20},{28,24},{5,1},{9,5},{13... | collective-permute-start | bytes 294920 | tf_op jit(solution)/shard_map/ppermute | solution.py:20
  22.2 3.3 %collective-permute-start.7 = (bf16[2,128,256]{2,1,0:T(8,128)(2,1)S(1)}, bf16[2,128,256]{2,1,0:T(8,128)(2,1)S(1)}, u32[]{:S(2)}, u32[]{:S(2)}) collective-permute-start(bf16[2,128,256]{2,1,0:T(8,128)(2,1)S(1)} %get-tuple-element.38.refs_0_), channel_id=1, source_target_pairs={{0,16},{4,20},{8,24},{12,28},{16,0},{20,4},{24,8},{28,12},{1,17},{... | collective-permute-start | bytes 393224 | tf_op jit(solution)/shard_map/ppermute | solution.py:114
  25.5 1.5 %collective-permute-start.6 = (bf16[2,128,256]{2,1,0:T(8,128)(2,1)S(1)}, bf16[2,128,256]{2,1,0:T(8,128)(2,1)S(1)}, u32[]{:S(2)}, u32[]{:S(2)}) collective-permute-start(bf16[2,128,256]{2,1,0:T(8,128)(2,1)S(1)} %get-tuple-element.38.refs_0_), channel_id=1, source_target_pairs={{0,8},{4,12},{8,0},{12,4},{16,24},{20,28},{24,16},{28,20},{1,9},{5... | collective-permute-start | bytes 393224 | tf_op jit(solution)/shard_map/ppermute | solution.py:114
  27.0 1.5 %collective-permute-start.13 = (bf16[8,64,256]{2,1,0:T(8,128)(2,1)S(1)}, bf16[8,64,256]{2,1,0:T(8,128)(2,1)S(1)}, u32[]{:S(2)}, u32[]{:S(2)}) collective-permute-start(bf16[8,64,256]{2,1,0:T(8,128)(2,1)S(1)} %get-tuple-element.34.gathered.refs_0_), channel_id=1, source_target_pairs={{0,2},{1,3},{2,0},{3,1},{4,6},{5,7},{6,4},{7,5},{8,10},{9,11},{10,... | collective-permute-start | bytes 786440 | tf_op jit(solution)/shard_map/ppermute | solution.py:114
  28.5 0.0 collective-permute-done.3.under
  28.5 0.0 collective-permute-done.4.following
  28.6 0.6 copy-done.10
  29.2 0.1 copy-done.9
  29.2 5.3 %shard_map.95 = (bf16[128,256]{1,0:T(8,128)(2,1)}, bf16[256,256]{1,0:T(8,128)(2,1)}) custom-call(s32[2]{0:T(128)} %copy-done.6, bf16[2,2,64,256]{3,2,1,0:T(8,128)(2,1)} %copy-done.4, bf16[2,2,32,256]{3,2,1,0:T(8,128)(2,1)} %copy-done.5, bf16[2,96,256]{2,1,0:T(8,128)(2,1)} %copy-done.10, bf16[27,256,256]{2,1,0:T(8,128)(2,1)} %bitcast.17, ...), custom_call_target="tpu_custom_call" | custom-call | flops 452984832 | bytes 3538944 | tf_op jit(solution)/shard_map/pallas_call | solution.py:487
  34.6 0.2 collective-permute-done.7.refs_2_
  34.7 0.1 collective-permute-done.6.refs_1_
  34.8 0.8 %copy-done.3 = bf16[128,256]{1,0:T(8,128)(2,1)S(1)} copy-done((bf16[128,256]{1,0:T(8,128)(2,1)S(1)}, bf16[128,256]{1,0:T(8,128)(2,1)}, u32[]{:S(2)}) %copy-start.3) | copy-done | bytes 65560
  35.7 0.7 %collective-permute-start.10 = (bf16[2,128,256]{2,1,0:T(8,128)(2,1)S(1)}, bf16[2,128,256]{2,1,0:T(8,128)(2,1)S(1)}, u32[]{:S(2)}, u32[]{:S(2)}) collective-permute-start(bf16[2,128,256]{2,1,0:T(8,128)(2,1)S(1)} %get-tuple-element.40.refs_4_), channel_id=1, source_target_pairs={{0,8},{4,12},{8,0},{12,4},{16,24},{20,28},{24,16},{28,20},{1,9},{5... | collective-permute-start | bytes 393224 | tf_op jit(solution)/shard_map/ppermute | solution.py:114
  36.4 1.8 %collective-permute-start.5 = (bf16[2,128,256]{2,1,0:T(8,128)(2,1)S(1)}, bf16[2,128,256]{2,1,0:T(8,128)(2,1)S(1)}, u32[]{:S(2)}, u32[]{:S(2)}) collective-permute-start(bf16[2,128,256]{2,1,0:T(8,128)(2,1)S(1)} %get-tuple-element.38.refs_0_), channel_id=1, source_target_pairs={{0,4},{4,0},{8,12},{12,8},{16,20},{20,16},{24,28},{28,24},{1,5},{5... | collective-permute-start | bytes 393224 | tf_op jit(solution)/shard_map/ppermute | solution.py:114
  38.2 0.2 collective-permute-start.9
  38.4 1.8 %collective-permute-start.8 = (bf16[2,128,256]{2,1,0:T(8,128)(2,1)S(1)}, bf16[2,128,256]{2,1,0:T(8,128)(2,1)S(1)}, u32[]{:S(2)}, u32[]{:S(2)}) collective-permute-start(bf16[2,128,256]{2,1,0:T(8,128)(2,1)S(1)} %get-tuple-element.39.refs_2_), channel_id=1, source_target_pairs={{0,4},{4,0},{8,12},{12,8},{16,20},{20,16},{24,28},{28,24},{1,5},{5... | collective-permute-start | bytes 393224 | tf_op jit(solution)/shard_map/ppermute | solution.py:114
  40.3 0.9 %collective-permute-done.10.refs_6_ = bf16[2,128,256]{2,1,0:T(8,128)(2,1)S(1)} collective-permute-done((bf16[2,128,256]{2,1,0:T(8,128)(2,1)S(1)}, bf16[2,128,256]{2,1,0:T(8,128)(2,1)S(1)}, u32[]{:S(2)}, u32[]{:S(2)}) %collective-permute-start.10) | collective-permute-done | bytes 131104 | tf_op jit(solution)/shard_map/ppermute | solution.py:114
  41.2 2.9 %collective-permute-start.11 = (bf16[2,128,256]{2,1,0:T(8,128)(2,1)S(1)}, bf16[2,128,256]{2,1,0:T(8,128)(2,1)S(1)}, u32[]{:S(2)}, u32[]{:S(2)}) collective-permute-start(bf16[2,128,256]{2,1,0:T(8,128)(2,1)S(1)} %collective-permute-done.10.refs_6_), channel_id=1, source_target_pairs={{0,4},{4,0},{8,12},{12,8},{16,20},{20,16},{24,28},{28,24},{1,5},{5... | collective-permute-start | bytes 393224 | tf_op jit(solution)/shard_map/ppermute | solution.py:114
  44.1 3.3 %all-to-all-start.1 = ((bf16[8,16,256]{2,1,0:T(8,128)(2,1)}), bf16[8,16,256]{2,1,0:T(8,128)(2,1)S(1)}, u32[]{:S(2)}, u32[]{:S(2)}) async-start(bf16[8,16,256]{2,1,0:T(8,128)(2,1)} %bitcast.15), calls=%async_computation.1 | async-start | bytes 131072 | tf_op jit(solution)/shard_map/all_to_all | solution.py:512
  47.4 0.0 collective-permute-done.5.refs_0_.refs_1_
  47.4 0.1 collective-permute-start.12
  47.5 0.0 collective-permute-done.13.refs_2_
  47.5 0.5 collective-permute-start.14
  48.0 6.3 %all-to-all-done.1.received = bf16[8,16,256]{2,1,0:T(8,128)(2,1)S(1)} async-done(((bf16[8,16,256]{2,1,0:T(8,128)(2,1)}), bf16[8,16,256]{2,1,0:T(8,128)(2,1)S(1)}, u32[]{:S(2)}, u32[]{:S(2)}) %all-to-all-start.1) | async-done | bytes 65568 | tf_op jit(solution)/shard_map/all_to_all | solution.py:512
  54.3 0.0 collective-permute-done.8.refs_1_.refs_3_
  54.3 0.0 collective-permute-done.9.refs_2_.refs_5_
  54.3 0.0 collective-permute-done.11.refs_3_.refs_7_
  54.3 0.1 shard_map.97
  54.4 0.0 collective-permute-start.15
  54.4 1.4 %collective-permute-start.16 = (f32[1,64]{1,0:T(1,128)S(1)}, f32[1,64]{1,0:T(1,128)S(1)}, u32[]{:S(2)}, u32[]{:S(2)}) collective-permute-start(f32[1,64]{1,0:T(1,128)S(1)} %get-tuple-element.44), channel_id=1, source_target_pairs={{0,2},{1,3},{2,0},{3,1},{4,6},{5,7},{6,4},{7,5},{8,10},{9,11},{10,... | collective-permute-start | bytes 776 | tf_op jit(solution)/shard_map/ppermute | solution.py:114
  55.8 0.4 collective-permute-start.17
  56.3 0.6 copy.14
  56.9 0.0 collective-permute-done.15
  56.9 1.1 %collective-permute-done.16 = f32[1,64]{1,0:T(1,128)S(1)} collective-permute-done((f32[1,64]{1,0:T(1,128)S(1)}, f32[1,64]{1,0:T(1,128)S(1)}, u32[]{:S(2)}, u32[]{:S(2)}) %collective-permute-start.16) | collective-permute-done | bytes 288 | tf_op jit(solution)/shard_map/ppermute | solution.py:114
  58.0 0.8 %collective-permute-done.17 = f32[1,64]{1,0:T(1,128)S(1)} collective-permute-done((f32[1,64]{1,0:T(1,128)S(1)}, f32[1,64]{1,0:T(1,128)S(1)}, u32[]{:S(2)}, u32[]{:S(2)}) %collective-permute-start.17) | collective-permute-done | bytes 288 | tf_op jit(solution)/shard_map/ppermute | solution.py:114
  58.8 0.5 add_bitcast_fusion
  59.3 0.0 collective-permute-done.12.refs_1_
  59.3 0.0 collective-permute-done.14.refs_3_
  59.3 0.0 copy-start.2
  59.3 0.9 %copy-done.2 = bf16[8,64,256]{2,1,0:T(8,128)(2,1)S(1)} copy-done((bf16[8,64,256]{2,1,0:T(8,128)(2,1)S(1)}, bf16[8,64,256]{2,1,0:T(8,128)(2,1)}, u32[]{:S(2)}) %copy-start.2) | copy-done | bytes 262168
  60.3 1.8 %shard_map.98 = (bf16[2,8,288,256]{3,2,1,0:T(8,128)(2,1)S(1)}, f32[1,64]{1,0:T(1,128)}) custom-call(s32[2]{0:T(128)S(1)} %copy-done.7, bf16[8,64,256]{2,1,0:T(8,128)(2,1)S(1)} %copy-done.2, bf16[8,64,256]{2,1,0:T(8,128)(2,1)S(1)} %collective-permute-done.12.refs_1_, bf16[8,64,256]{2,1,0:T(8,128)(2,1)S(1)} %collective-permute-done.13.refs_2_, ...), custom_call_target="tpu_custom_call" | custom-call | flops 1769472000 | bytes 1048576 | tf_op jit(solution)/shard_map/pallas_call | solution.py:523
  62.0 3.4 %shard_map.99 = f32[27,64,256]{2,1,0:T(8,128)} custom-call(s32[2]{0:T(128)S(1)} %copy-done.7, f32[1,64]{1,0:T(1,128)S(1)} %get-tuple-element.41._, bf16[2,8,288,256]{3,2,1,0:T(8,128)(2,1)S(1)} %get-tuple-element.42.grads, bf16[2,128,256]{2,1,0:T(8,128)(2,1)S(1)} %get-tuple-element.38.refs_0_, ...), custom_call_target="tpu_custom_call" | custom-call | flops 3932160000 | bytes 3538944 | tf_op jit(solution)/shard_map/pallas_call | solution.py:529
  (14 shorter events, 0.1 us)
Async XLA Ops:
  2.1 16.2 %all-to-all-start = ((bf16[8,64,256]{2,1,0:T(8,128)(2,1)}), bf16[8,64,256]{2,1,0:T(8,128)(2,1)S(1)}, u32[]{:S(2)}, u32[]{:S(2)}) async-start(bf16[8,64,256]{2,1,0:T(8,128)(2,1)} %broadcast_in_dim.8), calls=%async_computation | async-start | bytes 524288 | tf_op jit(solution)/shard_map/all_to_all | solution.py:457
  9.5 10.2 %copy-start.6 = (s32[2]{0:T(128)}, s32[2]{0:T(128)S(1)}, u32[]{:S(2)}) copy-start(s32[2]{0:T(128)S(1)} %pad_add_fusion.place) | copy-start | bytes 28
  10.2 0.9 %copy-start.8 = (bf16[4,2,32,256]{3,2,1,0:T(8,128)(2,1)S(1)}, bf16[4,2,32,256]{3,2,1,0:T(8,128)(2,1)}, u32[]{:S(2)}) copy-start(bf16[4,2,32,256]{3,2,1,0:T(8,128)(2,1)} %param.5) | copy-start | bytes 393220
  11.9 16.6 %copy-start = (bf16[272,256]{1,0:T(8,128)(2,1)}, bf16[272,256]{1,0:T(8,128)(2,1)S(1)}, u32[]{:S(2)}) copy-start(bf16[272,256]{1,0:T(8,128)(2,1)S(1)} %get-tuple-element.33._.kept) | copy-start | bytes 417796
  11.9 16.6 %copy-start.4 = (bf16[2,2,64,256]{3,2,1,0:T(8,128)(2,1)}, bf16[2,2,64,256]{3,2,1,0:T(8,128)(2,1)S(1)}, u32[]{:S(2)}) copy-start(bf16[2,2,64,256]{3,2,1,0:T(8,128)(2,1)S(1)} %get-tuple-element.26.planes) | copy-start | bytes 393220
  11.9 7.7 %collective-permute-start = (bf16[384,128]{1,0:T(8,128)(2,1)S(1)}, bf16[384,128]{1,0:T(8,128)(2,1)S(1)}, u32[]{:S(2)}, u32[]{:S(2)}) collective-permute-start(bf16[384,128]{1,0:T(8,128)(2,1)S(1)} %get-tuple-element.28), channel_id=1, source_target_pairs={{0,1},{1,0},{2,3},{3,2},{4,5},{5,4},{6,7},{7,6},{8,9},{9,8},{10,11... | collective-permute-start | bytes 294920 | tf_op jit(solution)/shard_map/ppermute | solution.py:114
  12.0 7.6 %collective-permute-start.2 = (bf16[384,128]{1,0:T(8,128)(2,1)S(1)}, bf16[384,128]{1,0:T(8,128)(2,1)S(1)}, u32[]{:S(2)}, u32[]{:S(2)}) collective-permute-start(bf16[384,128]{1,0:T(8,128)(2,1)S(1)} %get-tuple-element.30), channel_id=1, source_target_pairs={{0,3},{1,2},{2,1},{3,0},{4,7},{5,6},{6,5},{7,4},{8,11},{9,10},{10,... | collective-permute-start | bytes 294920 | tf_op jit(solution)/shard_map/ppermute | solution.py:114
  13.7 6.0 %collective-permute-start.1 = (bf16[128,128]{1,0:T(8,128)(2,1)S(1)}, bf16[128,128]{1,0:T(8,128)(2,1)S(1)}, u32[]{:S(2)}, u32[]{:S(2)}) collective-permute-start(bf16[128,128]{1,0:T(8,128)(2,1)S(1)} %get-tuple-element.29), channel_id=1, source_target_pairs={{0,2},{1,3},{2,0},{3,1},{4,6},{5,7},{6,4},{7,5},{8,10},{9,11},{10,... | collective-permute-start | bytes 98312 | tf_op jit(solution)/shard_map/ppermute | solution.py:114
  18.3 10.2 %copy-start.1 = (bf16[8,64,256]{2,1,0:T(8,128)(2,1)}, bf16[8,64,256]{2,1,0:T(8,128)(2,1)S(1)}, u32[]{:S(2)}) copy-start(bf16[8,64,256]{2,1,0:T(8,128)(2,1)S(1)} %get-tuple-element.34.gathered.refs_0_) | copy-start | bytes 786436
  18.3 10.2 %collective-permute-start.4 = (bf16[8,32,256]{2,1,0:T(8,128)(2,1)S(1)}, bf16[8,32,256]{2,1,0:T(8,128)(2,1)S(1)}, u32[]{:S(2)}, u32[]{:S(2)}) collective-permute-start(bf16[8,32,256]{2,1,0:T(8,128)(2,1)S(1)} %get-tuple-element.35), channel_id=1, source_target_pairs={{1,0},{2,1},{3,2},{5,4},{6,5},{7,6},{9,8},{10,9},{11,10},{13,12},{... | collective-permute-start | bytes 393224 | tf_op jit(solution)/shard_map/ppermute | solution.py:20
  20.3 0.6 copy-start.5
  21.0 7.6 %collective-permute-start.3 = (bf16[2,96,256]{2,1,0:T(8,128)(2,1)S(1)}, bf16[2,96,256]{2,1,0:T(8,128)(2,1)S(1)}, u32[]{:S(2)}, u32[]{:S(2)}) collective-permute-start(bf16[2,96,256]{2,1,0:T(8,128)(2,1)S(1)} %get-tuple-element.32), channel_id=1, source_target_pairs={{4,0},{8,4},{12,8},{16,12},{20,16},{24,20},{28,24},{5,1},{9,5},{13... | collective-permute-start | bytes 294920 | tf_op jit(solution)/shard_map/ppermute | solution.py:20
  22.2 12.5 %collective-permute-start.7 = (bf16[2,128,256]{2,1,0:T(8,128)(2,1)S(1)}, bf16[2,128,256]{2,1,0:T(8,128)(2,1)S(1)}, u32[]{:S(2)}, u32[]{:S(2)}) collective-permute-start(bf16[2,128,256]{2,1,0:T(8,128)(2,1)S(1)} %get-tuple-element.38.refs_0_), channel_id=1, source_target_pairs={{0,16},{4,20},{8,24},{12,28},{16,0},{20,4},{24,8},{28,12},{1,17},{... | collective-permute-start | bytes 393224 | tf_op jit(solution)/shard_map/ppermute | solution.py:114
  25.5 9.3 %collective-permute-start.6 = (bf16[2,128,256]{2,1,0:T(8,128)(2,1)S(1)}, bf16[2,128,256]{2,1,0:T(8,128)(2,1)S(1)}, u32[]{:S(2)}, u32[]{:S(2)}) collective-permute-start(bf16[2,128,256]{2,1,0:T(8,128)(2,1)S(1)} %get-tuple-element.38.refs_0_), channel_id=1, source_target_pairs={{0,8},{4,12},{8,0},{12,4},{16,24},{20,28},{24,16},{28,20},{1,9},{5... | collective-permute-start | bytes 393224 | tf_op jit(solution)/shard_map/ppermute | solution.py:114
  27.0 20.5 %collective-permute-start.13 = (bf16[8,64,256]{2,1,0:T(8,128)(2,1)S(1)}, bf16[8,64,256]{2,1,0:T(8,128)(2,1)S(1)}, u32[]{:S(2)}, u32[]{:S(2)}) collective-permute-start(bf16[8,64,256]{2,1,0:T(8,128)(2,1)S(1)} %get-tuple-element.34.gathered.refs_0_), channel_id=1, source_target_pairs={{0,2},{1,3},{2,0},{3,1},{4,6},{5,7},{6,4},{7,5},{8,10},{9,11},{10,... | collective-permute-start | bytes 786440 | tf_op jit(solution)/shard_map/ppermute | solution.py:114
  28.5 0.6 copy-start.10
  28.5 0.7 %copy-start.9 = (bf16[8,32,256]{2,1,0:T(8,128)(2,1)}, bf16[8,32,256]{2,1,0:T(8,128)(2,1)S(1)}, u32[]{:S(2)}) copy-start(bf16[8,32,256]{2,1,0:T(8,128)(2,1)S(1)} %collective-permute-done.4.following) | copy-start | bytes 393220
  29.2 30.1 %copy-start.7 = (s32[2]{0:T(128)S(1)}, s32[2]{0:T(128)}, u32[]{:S(2)}) copy-start(s32[2]{0:T(128)} %copy-done.6) | copy-start | bytes 28
  34.8 0.8 %copy-start.3 = (bf16[128,256]{1,0:T(8,128)(2,1)S(1)}, bf16[128,256]{1,0:T(8,128)(2,1)}, u32[]{:S(2)}) copy-start(bf16[128,256]{1,0:T(8,128)(2,1)} %get-tuple-element.36.refs_0_) | copy-start | bytes 196612
  35.7 5.5 %collective-permute-start.10 = (bf16[2,128,256]{2,1,0:T(8,128)(2,1)S(1)}, bf16[2,128,256]{2,1,0:T(8,128)(2,1)S(1)}, u32[]{:S(2)}, u32[]{:S(2)}) collective-permute-start(bf16[2,128,256]{2,1,0:T(8,128)(2,1)S(1)} %get-tuple-element.40.refs_4_), channel_id=1, source_target_pairs={{0,8},{4,12},{8,0},{12,4},{16,24},{20,28},{24,16},{28,20},{1,9},{5... | collective-permute-start | bytes 393224 | tf_op jit(solution)/shard_map/ppermute | solution.py:114
  36.4 11.1 %collective-permute-start.5 = (bf16[2,128,256]{2,1,0:T(8,128)(2,1)S(1)}, bf16[2,128,256]{2,1,0:T(8,128)(2,1)S(1)}, u32[]{:S(2)}, u32[]{:S(2)}) collective-permute-start(bf16[2,128,256]{2,1,0:T(8,128)(2,1)S(1)} %get-tuple-element.38.refs_0_), channel_id=1, source_target_pairs={{0,4},{4,0},{8,12},{12,8},{16,20},{20,16},{24,28},{28,24},{1,5},{5... | collective-permute-start | bytes 393224 | tf_op jit(solution)/shard_map/ppermute | solution.py:114
  38.2 16.1 %collective-permute-start.9 = (bf16[2,128,256]{2,1,0:T(8,128)(2,1)S(1)}, bf16[2,128,256]{2,1,0:T(8,128)(2,1)S(1)}, u32[]{:S(2)}, u32[]{:S(2)}) collective-permute-start(bf16[2,128,256]{2,1,0:T(8,128)(2,1)S(1)} %get-tuple-element.40.refs_4_), channel_id=1, source_target_pairs={{0,4},{4,0},{8,12},{12,8},{16,20},{20,16},{24,28},{28,24},{1,5},{5... | collective-permute-start | bytes 393224 | tf_op jit(solution)/shard_map/ppermute | solution.py:114
  38.4 15.9 %collective-permute-start.8 = (bf16[2,128,256]{2,1,0:T(8,128)(2,1)S(1)}, bf16[2,128,256]{2,1,0:T(8,128)(2,1)S(1)}, u32[]{:S(2)}, u32[]{:S(2)}) collective-permute-start(bf16[2,128,256]{2,1,0:T(8,128)(2,1)S(1)} %get-tuple-element.39.refs_2_), channel_id=1, source_target_pairs={{0,4},{4,0},{8,12},{12,8},{16,20},{20,16},{24,28},{28,24},{1,5},{5... | collective-permute-start | bytes 393224 | tf_op jit(solution)/shard_map/ppermute | solution.py:114
  41.2 13.1 %collective-permute-start.11 = (bf16[2,128,256]{2,1,0:T(8,128)(2,1)S(1)}, bf16[2,128,256]{2,1,0:T(8,128)(2,1)S(1)}, u32[]{:S(2)}, u32[]{:S(2)}) collective-permute-start(bf16[2,128,256]{2,1,0:T(8,128)(2,1)S(1)} %collective-permute-done.10.refs_6_), channel_id=1, source_target_pairs={{0,4},{4,0},{8,12},{12,8},{16,20},{20,16},{24,28},{28,24},{1,5},{5... | collective-permute-start | bytes 393224 | tf_op jit(solution)/shard_map/ppermute | solution.py:114
  44.1 10.2 %all-to-all-start.1 = ((bf16[8,16,256]{2,1,0:T(8,128)(2,1)}), bf16[8,16,256]{2,1,0:T(8,128)(2,1)S(1)}, u32[]{:S(2)}, u32[]{:S(2)}) async-start(bf16[8,16,256]{2,1,0:T(8,128)(2,1)} %bitcast.15), calls=%async_computation.1 | async-start | bytes 131072 | tf_op jit(solution)/shard_map/all_to_all | solution.py:512
  47.4 11.8 %collective-permute-start.12 = (bf16[8,64,256]{2,1,0:T(8,128)(2,1)}, bf16[8,64,256]{2,1,0:T(8,128)(2,1)S(1)}, u32[]{:S(2)}, u32[]{:S(2)}) collective-permute-start(bf16[8,64,256]{2,1,0:T(8,128)(2,1)} %copy-done.1), channel_id=1, source_target_pairs={{0,1},{1,0},{2,3},{3,2},{4,5},{5,4},{6,7},{7,6},{8,9},{9,8},{10,11... | collective-permute-start | bytes 786440 | tf_op jit(solution)/shard_map/ppermute | solution.py:114
  47.5 11.8 %collective-permute-start.14 = (bf16[8,64,256]{2,1,0:T(8,128)(2,1)S(1)}, bf16[8,64,256]{2,1,0:T(8,128)(2,1)S(1)}, u32[]{:S(2)}, u32[]{:S(2)}) collective-permute-start(bf16[8,64,256]{2,1,0:T(8,128)(2,1)S(1)} %collective-permute-done.13.refs_2_), channel_id=1, source_target_pairs={{0,1},{1,0},{2,3},{3,2},{4,5},{5,4},{6,7},{7,6},{8,9},{9,8},{10,11... | collective-permute-start | bytes 786440 | tf_op jit(solution)/shard_map/ppermute | solution.py:114
  54.4 2.5 %collective-permute-start.15 = (f32[1,64]{1,0:T(1,128)S(1)}, f32[1,64]{1,0:T(1,128)S(1)}, u32[]{:S(2)}, u32[]{:S(2)}) collective-permute-start(f32[1,64]{1,0:T(1,128)S(1)} %get-tuple-element.43), channel_id=1, source_target_pairs={{0,1},{1,0},{2,3},{3,2},{4,5},{5,4},{6,7},{7,6},{8,9},{9,8},{10,11... | collective-permute-start | bytes 776 | tf_op jit(solution)/shard_map/ppermute | solution.py:114
  54.4 3.6 %collective-permute-start.16 = (f32[1,64]{1,0:T(1,128)S(1)}, f32[1,64]{1,0:T(1,128)S(1)}, u32[]{:S(2)}, u32[]{:S(2)}) collective-permute-start(f32[1,64]{1,0:T(1,128)S(1)} %get-tuple-element.44), channel_id=1, source_target_pairs={{0,2},{1,3},{2,0},{3,1},{4,6},{5,7},{6,4},{7,5},{8,10},{9,11},{10,... | collective-permute-start | bytes 776 | tf_op jit(solution)/shard_map/ppermute | solution.py:114
  55.8 3.0 %collective-permute-start.17 = (f32[1,64]{1,0:T(1,128)S(1)}, f32[1,64]{1,0:T(1,128)S(1)}, u32[]{:S(2)}, u32[]{:S(2)}) collective-permute-start(f32[1,64]{1,0:T(1,128)S(1)} %get-tuple-element.45), channel_id=1, source_target_pairs={{0,3},{1,2},{2,1},{3,0},{4,7},{5,6},{6,5},{7,4},{8,11},{9,10},{10,... | collective-permute-start | bytes 776 | tf_op jit(solution)/shard_map/ppermute | solution.py:114
  59.3 1.0 %copy-start.2 = (bf16[8,64,256]{2,1,0:T(8,128)(2,1)S(1)}, bf16[8,64,256]{2,1,0:T(8,128)(2,1)}, u32[]{:S(2)}) copy-start(bf16[8,64,256]{2,1,0:T(8,128)(2,1)} %copy-done.1) | copy-start | bytes 786436
